TPU v7x, 32 devices: a whole 2x2x4 slice. The times are simulated.
32 devices in a mesh: dp: 2 (over core), hid: 4 (over y, x), wid: 4 (over z).
Axes of the slice: x: 2, y: 2, z: 4, core: 2. Of those that a mesh axis runs over, the one named last changes fastest.
Arguments:
- inputs: float32 [12544, 768], P(('dp', 'hid', 'wid')), may hold values from -6 to 6
- grid_sizes: int32 [64], P('dp'), may hold values from 7 to 12
- cotangent: float32 [12544, 768], P(('dp', 'hid', 'wid')), may hold values from -6 to 6
- window_convkernel: float32 [9, 768], replicated, may hold values from -2 to 2
- window_convbias: float32 [768], replicated, may hold values from -2 to 2
- window_gainone: float32 [768], replicated, may hold values from 0.5 to 1.5
- window_shiftone: float32 [768], replicated, may hold values from -2 to 2
- window_inweights: bfloat16 [3, 768, 768], P(None, ('hid', 'wid')), may hold values from -0.21875 to 0.21875
- window_inbias: float32 [2, 768], P(None, 'hid'), may hold values from -3 to 3
- window_outweights: bfloat16 [768, 768], P(('hid', 'wid')), may hold values from -0.4375 to 0.4375
- window_outbias: float32 [768], replicated, may hold values from -2 to 2
- window_gaintwo: float32 [768], replicated, may hold values from 0.5 to 1.5
- window_shifttwo: float32 [768], replicated, may hold values from -2 to 2
- window_upweights: bfloat16 [3072, 768], P(('hid', 'wid')), may hold values from -0.21875 to 0.21875
- window_upbias: float32 [3072], P('hid'), may hold values from -3 to 3
- window_downweights: bfloat16 [3072, 768], P(('hid', 'wid')), may hold values from -0.15625 to 0.15625
- window_downbias: float32 [768], replicated, may hold values from -2 to 2
- channel_convkernel: float32 [9, 768], replicated, may hold values from -2 to 2
- channel_convbias: float32 [768], replicated, may hold values from -2 to 2
- channel_gainone: float32 [768], replicated, may hold values from 0.5 to 1.5
- channel_shiftone: float32 [768], replicated, may hold values from -2 to 2
- channel_inweights: bfloat16 [3, 768, 768], P(None, ('hid', 'wid')), may hold values from -0.21875 to 0.21875
- channel_inbias: float32 [3, 768], P(None, 'hid'), may hold values from -3 to 3
- channel_outweights: bfloat16 [768, 768], P(('hid', 'wid')), may hold values from -0.4375 to 0.4375
- channel_outbias: float32 [768], replicated, may hold values from -2 to 2
- channel_gaintwo: float32 [768], replicated, may hold values from 0.5 to 1.5
- channel_shifttwo: float32 [768], replicated, may hold values from -2 to 2
- channel_upweights: bfloat16 [3072, 768], P(('hid', 'wid')), may hold values from -0.21875 to 0.21875
- channel_upbias: float32 [3072], P('hid'), may hold values from -3 to 3
- channel_downweights: bfloat16 [3072, 768], P(('hid', 'wid')), may hold values from -0.15625 to 0.15625
- channel_downbias: float32 [768], replicated, may hold values from -2 to 2
Outputs:
- outputs: float32 [12544, 768], P(('dp', 'hid', 'wid'))
- input_grad: float32 [12544, 768], P(('dp', 'hid', 'wid'))
- window_convkernel_grad: float32 [9, 768], replicated
- window_convbias_grad: float32 [768], replicated
- window_gainone_grad: float32 [768], replicated
- window_shiftone_grad: float32 [768], replicated
- window_inweights_grad: float32 [3, 768, 768], P(None, ('hid', 'wid'))
- window_inbias_grad: float32 [2, 768], P(None, 'hid')
- window_outweights_grad: float32 [768, 768], P(('hid', 'wid'))
- window_outbias_grad: float32 [768], replicated
- window_gaintwo_grad: float32 [768], replicated
- window_shifttwo_grad: float32 [768], replicated
- window_upweights_grad: float32 [3072, 768], P(('hid', 'wid'))
- window_upbias_grad: float32 [3072], P('hid')
- window_downweights_grad: float32 [3072, 768], P(('hid', 'wid'))
- window_downbias_grad: float32 [768], replicated
- channel_convkernel_grad: float32 [9, 768], replicated
- channel_convbias_grad: float32 [768], replicated
- channel_gainone_grad: float32 [768], replicated
- channel_shiftone_grad: float32 [768], replicated
- channel_inweights_grad: float32 [3, 768, 768], P(None, ('hid', 'wid'))
- channel_inbias_grad: float32 [3, 768], P(None, 'hid')
- channel_outweights_grad: float32 [768, 768], P(('hid', 'wid'))
- channel_outbias_grad: float32 [768], replicated
- channel_gaintwo_grad: float32 [768], replicated
- channel_shifttwo_grad: float32 [768], replicated
- channel_upweights_grad: float32 [3072, 768], P(('hid', 'wid'))
- channel_upbias_grad: float32 [3072], P('hid')
- channel_downweights_grad: float32 [3072, 768], P(('hid', 'wid'))
- channel_downbias_grad: float32 [768], replicated
Inputs may be any that keep to these rules, and one draw needn't show every extreme that they name: `grid_sizes`: section-four grid side of images of 224 to 384 pixels; the slot is 14 x 14.
All inputs are finite; a program needn't handle non-finite values.
Results may differ from a plain program's by a relative error of at most 0.03.
Values may be sent and summed in bfloat16 or wider, within the bound.
No kernel may reach another device: no remote copies, remote signals or barrier semaphores. Data moves between devices by JAX's collectives and lax.ppermute only.
A program may use at most 192 MiB of HBM per device.

v0:
```python
from functools import partial

import jax
import jax.numpy as jnp
from jax import lax
from jax.sharding import PartitionSpec as P

HD = 32
WINDOW = 7
PADDED = 14


EPSILON = 1e-05


def presence(sizes):
    cells = jnp.arange(PADDED, dtype=jnp.int32)
    inside = (cells[None, :, None] < sizes[:, None, None]) & (
        cells[None, None, :] < sizes[:, None, None]
    )
    return inside.astype(jnp.float32).reshape(-1, 1)


def depthwise(values, kernel, bias):
    images = values.shape[0] // (PADDED * PADDED)
    grid_cells = values.reshape(images, PADDED, PADDED, values.shape[1])
    padded = jnp.pad(grid_cells, ((0, 0), (1, 1), (1, 1), (0, 0)))
    total = jnp.zeros_like(grid_cells)
    for offset in range(9):
        across = offset // 3
        along = offset % 3
        total = (
            total + padded[:, across : across + PADDED, along : along + PADDED, :] * kernel[offset]
        )
    return total.reshape(values.shape) + bias


def to_windows(values):
    images = values.shape[0] // (PADDED * PADDED)
    window_side = PADDED // WINDOW
    grid_cells = values.reshape(images, window_side, WINDOW, window_side, WINDOW, values.shape[1])
    return grid_cells.transpose(0, 1, 3, 2, 4, 5).reshape(
        images * window_side * window_side, WINDOW * WINDOW, values.shape[1]
    )


def from_windows(values):
    window_side = PADDED // WINDOW
    images = values.shape[0] // (window_side * window_side)
    grid_cells = values.reshape(images, window_side, window_side, WINDOW, WINDOW, values.shape[2])
    return grid_cells.transpose(0, 1, 3, 2, 4, 5).reshape(images * PADDED * PADDED, values.shape[2])


def split_heads(values):
    return values.reshape(values.shape[0], values.shape[1], values.shape[2] // HD, HD)


def image_heads(values):
    return values.reshape(
        values.shape[0] // (PADDED * PADDED), PADDED * PADDED, values.shape[1] // HD, HD
    )


def outer(left, right):
    return lax.dot_general(
        left, right, (((0,), (0,)), ((), ())), preferred_element_type=jnp.float32
    )


def times_transposed(left, right):
    return lax.dot_general(
        left, right, (((1,), (1,)), ((), ())), preferred_element_type=jnp.float32
    )


def norm_forward(values, norm_gain, bias_shift):
    center = jnp.mean(values, axis=1, keepdims=True)
    scaled = lax.rsqrt(jnp.mean(values * values, axis=1, keepdims=True) - center * center + EPSILON)
    normal = (values - center) * scaled
    return ((normal * norm_gain + bias_shift).astype(jnp.bfloat16), normal, scaled)


def norm_backward(grad_normed, normal, scaled, norm_gain):
    grad_normal = grad_normed * norm_gain
    first_mean = jnp.mean(grad_normal, axis=1, keepdims=True)
    second_mean = jnp.mean(grad_normal * normal, axis=1, keepdims=True)
    grad_in = scaled * (grad_normal - first_mean - normal * second_mean)
    return (grad_in, jnp.sum(grad_normed * normal, axis=0), jnp.sum(grad_normed, axis=0))


def gather_rows(normed):
    return lax.all_gather(normed, "hid", axis=0, tiled=True)


def reduce_rows(operand, weight):
    row_count = operand.shape[0] // lax.axis_size("hid")

    def term(first_row, length):
        return jnp.dot(operand, weight, preferred_element_type=jnp.float32)

    return lax.psum_scatter(
        term(jnp.int32(0), row_count * lax.axis_size("hid")), "hid", scatter_dimension=0, tiled=True
    )


def project_heads(mixed_rows, outweights):
    return reduce_rows(mixed_rows, outweights)


def gather_grads(grads):
    return lax.all_gather(grads, "hid", axis=0, tiled=True)


def reduce_back(operand, weight):
    row_count = operand.shape[0] // lax.axis_size("hid")

    def term(first_row, length):
        return jnp.dot(operand, weight, preferred_element_type=jnp.float32)

    return lax.psum_scatter(
        term(jnp.int32(0), row_count * lax.axis_size("hid")).astype(jnp.bfloat16),
        "hid",
        scatter_dimension=0,
        tiled=True,
    ).astype(jnp.float32)


def window_scores(query_rows, key_rows, present):
    queries = split_heads(to_windows(query_rows))
    keyset = split_heads(to_windows(key_rows))
    scores = jnp.einsum(
        "wqhd,wkhd->whqk", queries, keyset, preferred_element_type=jnp.float32
    ) * HD ** (-0.5)
    keep_mask = to_windows(present)[:, None, None, :, 0] > 0.5
    return (jnp.where(keep_mask, scores, -1000000000.0), keep_mask)


def window_forward(query_rows, key_rows, value_rows, present):
    scores, keep_mask = window_scores(query_rows, key_rows, present)
    totals = jax.nn.logsumexp(scores, axis=-1, keepdims=True)
    weights = jnp.exp(scores - totals).astype(jnp.bfloat16)
    valueset = split_heads(to_windows(value_rows))
    mixed_rows = jnp.einsum(
        "whqk,wkhd->wqhd", weights, valueset, preferred_element_type=jnp.float32
    )
    return (
        from_windows(mixed_rows.reshape(mixed_rows.shape[0], mixed_rows.shape[1], -1)).astype(
            jnp.bfloat16
        ),
        totals,
    )


def window_backward(grad_mixed, query_rows, key_rows, value_rows, totals, present):
    scores, keep_mask = window_scores(query_rows, key_rows, present)
    probabilities = jnp.exp(scores - totals)
    weights = probabilities.astype(jnp.bfloat16)
    incoming = split_heads(to_windows(grad_mixed))
    queries = split_heads(to_windows(query_rows))
    keyset = split_heads(to_windows(key_rows))
    valueset = split_heads(to_windows(value_rows))
    grad_probs = jnp.einsum(
        "wqhd,wkhd->whqk", incoming, valueset, preferred_element_type=jnp.float32
    )
    grad_scores = probabilities * (
        grad_probs - jnp.sum(probabilities * grad_probs, axis=-1, keepdims=True)
    )
    grad_scores = jnp.where(keep_mask, grad_scores, 0.0).astype(jnp.bfloat16)
    grad_query = jnp.einsum(
        "whqk,wkhd->wqhd", grad_scores, keyset, preferred_element_type=jnp.float32
    ) * HD ** (-0.5)
    grad_keys = jnp.einsum(
        "whqk,wqhd->wkhd", grad_scores, queries, preferred_element_type=jnp.float32
    ) * HD ** (-0.5)
    grad_values = jnp.einsum(
        "whqk,wqhd->wkhd", weights, incoming, preferred_element_type=jnp.float32
    )

    def restore(grads):
        return from_windows(grads.reshape(grads.shape[0], grads.shape[1], -1))

    return (restore(grad_query), restore(grad_keys), restore(grad_values))


def channel_forward(query_rows, key_rows, value_rows, present):
    keyset = image_heads(key_rows * present.astype(jnp.bfloat16))
    valueset = image_heads(value_rows)
    scores = jnp.einsum(
        "nthi,nthj->nhij", keyset, valueset, preferred_element_type=jnp.float32
    ) * HD ** (-0.5)
    probabilities = jax.nn.softmax(scores, axis=-1)
    mixed_rows = jnp.einsum(
        "nhij,nthj->nthi",
        probabilities.astype(jnp.bfloat16),
        image_heads(query_rows),
        preferred_element_type=jnp.float32,
    )
    return (mixed_rows.reshape(query_rows.shape).astype(jnp.bfloat16), probabilities)


def channel_backward(grad_mixed, query_rows, key_rows, value_rows, probabilities, present):
    incoming = image_heads(grad_mixed)
    queries = image_heads(query_rows)
    keyset = image_heads(key_rows * present.astype(jnp.bfloat16))
    valueset = image_heads(value_rows)
    token_mask = image_heads(jnp.broadcast_to(present, (present.shape[0], HD)))
    grad_probs = jnp.einsum(
        "nthi,nthj->nhij", incoming, queries, preferred_element_type=jnp.float32
    )
    grad_query = jnp.einsum(
        "nhij,nthi->nthj",
        probabilities.astype(jnp.bfloat16),
        incoming,
        preferred_element_type=jnp.float32,
    )
    grad_scores = probabilities * (
        grad_probs - jnp.sum(probabilities * grad_probs, axis=-1, keepdims=True)
    )
    grad_scores = grad_scores.astype(jnp.bfloat16)
    grad_keys = jnp.einsum(
        "nhij,nthj->nthi", grad_scores, valueset, preferred_element_type=jnp.float32
    )
    grad_keys = grad_keys * HD ** (-0.5) * token_mask
    grad_values = jnp.einsum(
        "nhij,nthi->nthj", grad_scores, keyset, preferred_element_type=jnp.float32
    ) * HD ** (-0.5)
    row_shape = query_rows.shape
    return (
        grad_query.reshape(row_shape),
        grad_keys.reshape(row_shape),
        grad_values.reshape(row_shape),
    )


def conv_backward(grad_values, values, kernel, bias, present):
    pullback = jax.vjp(depthwise, values, kernel, bias)[1]
    grad_in, grad_kernel, grad_bias = pullback(grad_values * present)
    return (grad_values + grad_in, grad_kernel, grad_bias)


def attention_forward(
    values,
    present,
    group_present,
    norm_gain,
    bias_shift,
    inweights,
    inbias,
    outweights,
    outbias,
    windowed,
):
    normed, normal, scaled = norm_forward(values, norm_gain, bias_shift)
    gathered = gather_rows(normed)
    stacked = inweights.reshape(-1, inweights.shape[2])
    projected = times_transposed(gathered, stacked)
    head_width = inweights.shape[1]
    query_rows = (projected[:, :head_width] + inbias[0]).astype(jnp.bfloat16)
    key_part = projected[:, head_width : 2 * head_width]
    if not windowed:
        key_part = key_part + inbias[1]
    key_rows = key_part.astype(jnp.bfloat16)
    value_rows = (projected[:, 2 * head_width :] + inbias[inbias.shape[0] - 1]).astype(jnp.bfloat16)
    if windowed:
        mixed_rows, saved_stat = window_forward(query_rows, key_rows, value_rows, group_present)
    else:
        mixed_rows, saved_stat = channel_forward(query_rows, key_rows, value_rows, group_present)
    branch = project_heads(mixed_rows, outweights) + outbias
    saved = (
        gathered,
        normal,
        scaled,
        stacked,
        query_rows,
        key_rows,
        value_rows,
        saved_stat,
        mixed_rows,
    )
    return (values + present * branch, saved)


def attention_backward(grad_values, saved, present, group_present, norm_gain, outweights, windowed):
    gathered, normal, scaled, stacked, query_rows, key_rows, value_rows, saved_stat, mixed_rows = (
        saved
    )
    grad_branch = grad_values * present
    full_grads = gather_grads(grad_branch.astype(jnp.bfloat16))
    grad_outweights = outer(mixed_rows, full_grads)
    grad_mixed = times_transposed(full_grads, outweights).astype(jnp.bfloat16)
    if windowed:
        grad_query, grad_keys, grad_value_rows = window_backward(
            grad_mixed, query_rows, key_rows, value_rows, saved_stat, group_present
        )
    else:
        grad_query, grad_keys, grad_value_rows = channel_backward(
            grad_mixed, query_rows, key_rows, value_rows, saved_stat, group_present
        )
    rounded = jnp.concatenate([grad_query, grad_keys, grad_value_rows], axis=1).astype(jnp.bfloat16)
    column_sums = jnp.sum(rounded, axis=0, dtype=jnp.float32).reshape(3, -1)
    if windowed:
        grad_inbias = jnp.stack([column_sums[0], column_sums[2]])
    else:
        grad_inbias = column_sums
    grad_stacked = outer(rounded, gathered)
    grad_inweights = grad_stacked.reshape(3, -1, grad_stacked.shape[1])
    grad_in, grad_gain, grad_shift = norm_backward(
        reduce_back(rounded, stacked), normal, scaled, norm_gain
    )
    little_grads = (grad_gain, grad_shift, jnp.sum(grad_branch, axis=0))
    return (grad_values + grad_in, little_grads, grad_inbias, grad_inweights, grad_outweights)


def gelu_back(hidden, grad_acted):
    pullback = jax.vjp(partial(jax.nn.gelu, approximate=False), hidden)[1]
    return pullback(grad_acted)[0].astype(jnp.bfloat16)


def mlp_forward(values, norm_gain, bias_shift, upward, upbias, downward, downbias, present):
    normed, normal, scaled = norm_forward(values, norm_gain, bias_shift)
    gathered = gather_rows(normed)
    hidden = times_transposed(gathered, upward) + upbias
    acted = jax.nn.gelu(hidden, approximate=False).astype(jnp.bfloat16)
    branch = reduce_rows(acted, downward) + downbias
    return (values + present * branch, (gathered, hidden, acted, normal, scaled))


def mlp_backward(grad_values, saved, norm_gain, upward, downward, present):
    gathered, hidden, acted, normal, scaled = saved
    grad_branch = grad_values * present
    full_grads = gather_grads(grad_branch.astype(jnp.bfloat16))
    grad_down = outer(acted, full_grads)
    grad_hidden = gelu_back(hidden, times_transposed(full_grads, downward))
    grad_upbias = jnp.sum(grad_hidden, axis=0, dtype=jnp.float32)
    grad_up = outer(grad_hidden, gathered)
    grad_in, grad_gain, grad_shift = norm_backward(
        reduce_back(grad_hidden, upward), normal, scaled, norm_gain
    )
    little_grads = (grad_gain, grad_shift, jnp.sum(grad_branch, axis=0))
    return (grad_values + grad_in, little_grads, grad_upbias, grad_up, grad_down)


def body(
    inputs,
    grid_sizes,
    cotangent,
    window_convkernel,
    window_convbias,
    window_gainone,
    window_shiftone,
    window_inweights,
    window_inbias,
    window_outweights,
    window_outbias,
    window_gaintwo,
    window_shifttwo,
    window_upweights,
    window_upbias,
    window_downweights,
    window_downbias,
    channel_convkernel,
    channel_convbias,
    channel_gainone,
    channel_shiftone,
    channel_inweights,
    channel_inbias,
    channel_outweights,
    channel_outbias,
    channel_gaintwo,
    channel_shifttwo,
    channel_upweights,
    channel_upbias,
    channel_downweights,
    channel_downbias,
):
    image_count = inputs.shape[0] // (PADDED * PADDED)
    size_table = grid_sizes.reshape(lax.axis_size("hid"), lax.axis_size("wid"), image_count)
    own_sizes = lax.dynamic_index_in_dim(
        lax.dynamic_index_in_dim(size_table, lax.axis_index("hid"), 0, keepdims=False),
        lax.axis_index("wid"),
        0,
        keepdims=False,
    )
    group_sizes = lax.dynamic_index_in_dim(
        size_table, lax.axis_index("wid"), 1, keepdims=False
    ).reshape(-1)
    present = presence(own_sizes)
    group_present = presence(group_sizes)
    local = (
        lax.all_gather(window_inweights, "wid", axis=1, tiled=True),
        lax.all_gather(window_outweights, "wid", axis=0, tiled=True),
        lax.all_gather(window_upweights, "wid", axis=0, tiled=True),
        lax.all_gather(window_downweights, "wid", axis=0, tiled=True),
        lax.all_gather(channel_inweights, "wid", axis=1, tiled=True),
        lax.all_gather(channel_outweights, "wid", axis=0, tiled=True),
        lax.all_gather(channel_upweights, "wid", axis=0, tiled=True),
        lax.all_gather(channel_downweights, "wid", axis=0, tiled=True),
    )
    start = inputs * present
    after_conv = start + present * depthwise(start, window_convkernel, window_convbias)
    after_attn, saved_one = attention_forward(
        after_conv,
        present,
        group_present,
        window_gainone,
        window_shiftone,
        local[0],
        window_inbias,
        local[1],
        window_outbias,
        True,
    )
    after_mlp, saved_two = mlp_forward(
        after_attn,
        window_gaintwo,
        window_shifttwo,
        local[2],
        window_upbias,
        local[3],
        window_downbias,
        present,
    )
    after_conv_c = after_mlp + present * depthwise(after_mlp, channel_convkernel, channel_convbias)
    after_attn_c, saved_three = attention_forward(
        after_conv_c,
        present,
        group_present,
        channel_gainone,
        channel_shiftone,
        local[4],
        channel_inbias,
        local[5],
        channel_outbias,
        False,
    )
    outputs, saved_four = mlp_forward(
        after_attn_c,
        channel_gaintwo,
        channel_shifttwo,
        local[6],
        channel_upbias,
        local[7],
        channel_downbias,
        present,
    )
    flowing, little_four, upbias_four, up_four, down_four = mlp_backward(
        cotangent, saved_four, channel_gaintwo, local[6], local[7], present
    )
    flowing, little_three, inbias_three, in_three, out_three = attention_backward(
        flowing, saved_three, present, group_present, channel_gainone, local[5], False
    )
    flowing, kernel_three, convbias_three = conv_backward(
        flowing, after_mlp, channel_convkernel, channel_convbias, present
    )
    flowing, little_two, upbias_two, up_two, down_two = mlp_backward(
        flowing, saved_two, window_gaintwo, local[2], local[3], present
    )
    flowing, little_one, inbias_one, in_one, out_one = attention_backward(
        flowing, saved_one, present, group_present, window_gainone, local[1], True
    )
    flowing, kernel_one, convbias_one = conv_backward(
        flowing, start, window_convkernel, window_convbias, present
    )
    input_grad = flowing * present
    tokens = lax.psum(
        (
            kernel_one,
            convbias_one,
            little_one[0],
            little_one[1],
            little_one[2],
            little_two[0],
            little_two[1],
            little_two[2],
            kernel_three,
            convbias_three,
            little_three[0],
            little_three[1],
            little_three[2],
            little_four[0],
            little_four[1],
            little_four[2],
        ),
        ("dp", "hid", "wid"),
    )
    heads = lax.psum((inbias_one, upbias_two, inbias_three, upbias_four), ("dp", "wid"))
    summed = (
        lax.psum(in_one.astype(jnp.bfloat16), "dp").astype(jnp.float32),
        lax.psum(out_one.astype(jnp.bfloat16), "dp").astype(jnp.float32),
        lax.psum(up_two.astype(jnp.bfloat16), "dp").astype(jnp.float32),
        lax.psum(down_two.astype(jnp.bfloat16), "dp").astype(jnp.float32),
        lax.psum(in_three.astype(jnp.bfloat16), "dp").astype(jnp.float32),
        lax.psum(out_three.astype(jnp.bfloat16), "dp").astype(jnp.float32),
        lax.psum(up_four.astype(jnp.bfloat16), "dp").astype(jnp.float32),
        lax.psum(down_four.astype(jnp.bfloat16), "dp").astype(jnp.float32),
    )
    weights = (
        lax.psum_scatter(
            summed[0].astype(jnp.bfloat16), "wid", scatter_dimension=1, tiled=True
        ).astype(jnp.float32),
        lax.psum_scatter(
            summed[1].astype(jnp.bfloat16), "wid", scatter_dimension=0, tiled=True
        ).astype(jnp.float32),
        lax.psum_scatter(
            summed[2].astype(jnp.bfloat16), "wid", scatter_dimension=0, tiled=True
        ).astype(jnp.float32),
        lax.psum_scatter(
            summed[3].astype(jnp.bfloat16), "wid", scatter_dimension=0, tiled=True
        ).astype(jnp.float32),
        lax.psum_scatter(
            summed[4].astype(jnp.bfloat16), "wid", scatter_dimension=1, tiled=True
        ).astype(jnp.float32),
        lax.psum_scatter(
            summed[5].astype(jnp.bfloat16), "wid", scatter_dimension=0, tiled=True
        ).astype(jnp.float32),
        lax.psum_scatter(
            summed[6].astype(jnp.bfloat16), "wid", scatter_dimension=0, tiled=True
        ).astype(jnp.float32),
        lax.psum_scatter(
            summed[7].astype(jnp.bfloat16), "wid", scatter_dimension=0, tiled=True
        ).astype(jnp.float32),
    )
    return (
        outputs,
        input_grad,
        tokens[0],
        tokens[1],
        tokens[2],
        tokens[3],
        weights[0],
        heads[0],
        weights[1],
        tokens[4],
        tokens[5],
        tokens[6],
        weights[2],
        heads[1],
        weights[3],
        tokens[7],
        tokens[8],
        tokens[9],
        tokens[10],
        tokens[11],
        weights[4],
        heads[2],
        weights[5],
        tokens[12],
        tokens[13],
        tokens[14],
        weights[6],
        heads[3],
        weights[7],
        tokens[15],
    )


def solution(mesh):
    placed = (
        P(("dp", "hid", "wid"), None),
        P("dp"),
        P(("dp", "hid", "wid"), None),
        P(),
        P(),
        P(),
        P(),
        P(None, ("hid", "wid"), None),
        P(None, "hid"),
        P(("hid", "wid"), None),
        P(),
        P(),
        P(),
        P(("hid", "wid"), None),
        P("hid"),
        P(("hid", "wid"), None),
        P(),
        P(),
        P(),
        P(),
        P(),
        P(None, ("hid", "wid"), None),
        P(None, "hid"),
        P(("hid", "wid"), None),
        P(),
        P(),
        P(),
        P(("hid", "wid"), None),
        P("hid"),
        P(("hid", "wid"), None),
        P(),
    )
    return jax.shard_map(
        body,
        mesh=mesh,
        in_specs=placed,
        out_specs=(
            P(("dp", "hid", "wid"), None),
            P(("dp", "hid", "wid"), None),
            P(),
            P(),
            P(),
            P(),
            P(None, ("hid", "wid"), None),
            P(None, "hid"),
            P(("hid", "wid"), None),
            P(),
            P(),
            P(),
            P(("hid", "wid"), None),
            P("hid"),
            P(("hid", "wid"), None),
            P(),
            P(),
            P(),
            P(),
            P(),
            P(None, ("hid", "wid"), None),
            P(None, "hid"),
            P(("hid", "wid"), None),
            P(),
            P(),
            P(),
            P(("hid", "wid"), None),
            P("hid"),
            P(("hid", "wid"), None),
            P(),
        ),
        check_vma=False,
    )
```

profile of v0, /device:TPU:1, one launch (start us, length us, event | category | flops | bytes accessed | tf_op | source)
XLA Modules:
  0.0 1465.9 jit_solution(7516293531572891777)
XLA Ops:
  20.0 13.1 all_gather.50
  33.1 16.0 %all_gather.49 = bf16[3,192,768]{2,1,0:T(8,128)(2,1)S(1)} all-gather(bf16[3,48,768]{2,1,0:T(8,128)(2,1)S(1)} %copy-done.54), channel_id=1, replica_groups=mesh['dp'=2,'hid'=4,'wid'=4] {'wid'}, dimensions={1}, use_global_device_ids=true | all-gather | bytes 1105920 | tf_op jit(solution)/shard_map/all_gather | solution.py:390
  49.1 10.5 all-gather.13.cloned.1.call-done
  139.9 57.4 %reduce-scatter.49.cloned.1.call-done = f32[392,768]{1,0:T(8,128)} async-done(((f32[1568,768]{1,0:T(8,128)}), f32[392,768]{1,0:T(8,128)}) %reduce-scatter.49.cloned.1.call-update) | async-done | bytes 1204240
  200.8 37.1 %all-gather.15.cloned.1.call-done = bf16[1568,768]{1,0:T(8,128)(2,1)} async-done(((bf16[392,768]{1,0:T(8,128)(2,1)}), bf16[1568,768]{1,0:T(8,128)(2,1)}) %all-gather.15.cloned.1.call-update) | async-done | bytes 2408464 | tf_op jit(solution)/shard_map/all_gather | solution.py:92
  237.9 15.5 %multiply_convert_fusion.1 = (bf16[1568,768]{1,0:T(8,128)(2,1)}, f32[1568,768]{1,0:T(8,128)}, f32[1568,768]{1,0:T(8,128)}) fusion(f32[768]{0:T(1024)S(1)} %copy-done.131, bf16[1568,768]{1,0:T(8,128)(2,1)} %all-gather.15.cloned.1.call-done, bf16[768,768]{1,0:T(8,128)(2,1)} %all-gather.17.cloned.1.call-done), kind=kOutput, calls=%fused_computation.26 | convolution fusion | flops 1929166848 | bytes 15633408 | tf_op jit(solution)/shard_map/dot_general | solution.py:71
  253.4 15.7 %all-gather.19.cloned.1.call-done = bf16[768,768]{1,0:T(8,128)(2,1)} async-done(((bf16[192,768]{1,0:T(8,128)(2,1)}), bf16[768,768]{1,0:T(8,128)(2,1)}) %all-gather.19.cloned.1.call-update) | async-done | bytes 1179664 | tf_op jit(solution)/shard_map/all_gather | solution.py:393
  276.2 56.7 %reduce-scatter.51.cloned.1.call-done = f32[392,768]{1,0:T(8,128)} async-done(((f32[1568,768]{1,0:T(8,128)}), f32[392,768]{1,0:T(8,128)}) %reduce-scatter.51.cloned.1.call-update) | async-done | bytes 1204240
  335.7 8.5 multiply_add_fusion
  351.4 12.1 all_gather.56
  363.5 15.5 %all_gather.55 = bf16[3,192,768]{2,1,0:T(8,128)(2,1)} all-gather(bf16[3,48,768]{2,1,0:T(8,128)(2,1)S(1)} %copy-done.55), channel_id=1, replica_groups=mesh['dp'=2,'hid'=4,'wid'=4] {'wid'}, dimensions={1}, use_global_device_ids=true | all-gather | bytes 1105920 | tf_op jit(solution)/shard_map/all_gather | solution.py:394
  379.0 10.1 all-gather.21.cloned.1.call-done
  419.6 56.6 %reduce-scatter.53.cloned.1.call-done = f32[392,768]{1,0:T(8,128)} async-done(((f32[1568,768]{1,0:T(8,128)}), f32[392,768]{1,0:T(8,128)}) %reduce-scatter.53.cloned.1.call-update) | async-done | bytes 1204240
  482.4 25.2 %all-gather.25.cloned.1.call-done = bf16[768,768]{1,0:T(8,128)(2,1)} async-done(((bf16[192,768]{1,0:T(8,128)(2,1)}), bf16[768,768]{1,0:T(8,128)(2,1)}) %all-gather.25.cloned.1.call-update) | async-done | bytes 1179664 | tf_op jit(solution)/shard_map/all_gather | solution.py:396
  507.5 39.1 %all-gather.23.cloned.1.call-done = bf16[1568,768]{1,0:T(8,128)(2,1)} async-done(((bf16[392,768]{1,0:T(8,128)(2,1)}), bf16[1568,768]{1,0:T(8,128)(2,1)}) %all-gather.23.cloned.1.call-update) | async-done | bytes 2408464 | tf_op jit(solution)/shard_map/all_gather | solution.py:92
  552.9 25.0 %all-gather.27.cloned.1.call-done = bf16[768,768]{1,0:T(8,128)(2,1)} async-done(((bf16[192,768]{1,0:T(8,128)(2,1)}), bf16[768,768]{1,0:T(8,128)(2,1)}) %all-gather.27.cloned.1.call-update) | async-done | bytes 1179664 | tf_op jit(solution)/shard_map/all_gather | solution.py:397
  577.8 39.2 %all-gather.29.cloned.1.call-done = bf16[1568,768]{1,0:T(8,128)(2,1)} async-done(((bf16[392,768]{1,0:T(8,128)(2,1)}), bf16[1568,768]{1,0:T(8,128)(2,1)}) %all-gather.29.cloned.1.call-update) | async-done | bytes 2408464 | tf_op jit(solution)/shard_map/all_gather | solution.py:111
  617.0 16.3 %convert_reduce_fusion = (f32[768]{0:T(1024)}, bf16[1568,768]{1,0:T(8,128)(2,1)S(1)}, f32[1568,768]{1,0:T(8,128)}) fusion(f32[1568,768]{1,0:T(8,128)} %fusion.134, f32[768]{0:T(1024)S(1)} %copy-done.119, bf16[1568,768]{1,0:T(8,128)(2,1)} %all-gather.29.cloned.1.call-done, bf16[768,768]{1,0:T(8,128)(2,1)} %all-gather.27.cloned.1.call-done), kind=kOutput, calls=%fused_computation.6 | convolution fusion | flops 1940004096 | bytes 15636480 | tf_op jit(solution)/shard_map/dot_general | solution.py:71
  648.7 27.9 %reduce-scatter.57.cloned.1.call-done = bf16[392,768]{1,0:T(8,128)(2,1)} async-done(((bf16[1568,768]{1,0:T(8,128)(2,1)}), bf16[392,768]{1,0:T(8,128)(2,1)}) %reduce-scatter.57.cloned.1.call-update) | async-done | bytes 602128
  679.2 58.4 %reduce-scatter.55.cloned.1.call-done = f32[392,768]{1,0:T(8,128)} async-done(((f32[1568,768]{1,0:T(8,128)}), f32[392,768]{1,0:T(8,128)}) %reduce-scatter.55.cloned.1.call-update) | async-done | bytes 1204240
  742.5 37.6 %all-gather.31.cloned.1.call-done = bf16[1568,768]{1,0:T(8,128)(2,1)} async-done(((bf16[392,768]{1,0:T(8,128)(2,1)}), bf16[1568,768]{1,0:T(8,128)(2,1)}) %all-gather.31.cloned.1.call-update) | async-done | bytes 2408464 | tf_op jit(solution)/shard_map/all_gather | solution.py:111
  815.7 37.9 %reduce-scatter.59.cloned.1.call-done = bf16[392,768]{1,0:T(8,128)(2,1)} async-done(((bf16[1568,768]{1,0:T(8,128)(2,1)}), bf16[392,768]{1,0:T(8,128)(2,1)}) %reduce-scatter.59.cloned.1.call-update) | async-done | bytes 602128
  876.7 37.7 %all-gather.33.cloned.1.call-done = bf16[1568,768]{1,0:T(8,128)(2,1)} async-done(((bf16[392,768]{1,0:T(8,128)(2,1)}), bf16[1568,768]{1,0:T(8,128)(2,1)}) %all-gather.33.cloned.1.call-update) | async-done | bytes 2408464 | tf_op jit(solution)/shard_map/all_gather | solution.py:111
  914.3 9.0 convert_reduce_fusion.1
  928.4 38.3 %reduce-scatter.61.cloned.1.call-done = bf16[392,768]{1,0:T(8,128)(2,1)} async-done(((bf16[1568,768]{1,0:T(8,128)(2,1)}), bf16[392,768]{1,0:T(8,128)(2,1)}) %reduce-scatter.61.cloned.1.call-update) | async-done | bytes 602128
  1041.3 55.7 %select_convert_fusion = bf16[32,6,49,49]{3,0,2,1:T(8,128)(2,1)S(1)} fusion(f32[32,6,49,49]{3,0,2,1:T(8,128)S(1)} %copy-done.23, f32[32,6,49,49]{3,0,2,1:T(8,128)} %copy.171, f32[32,6,49]{0,2,1:T(8,128)S(1)} %copy-done.49, pred[32,49]{1,0:T(8,128)(4,1)S(1)} %copy-done.59), kind=kOutput, calls=%fused_computation.8 | output fusion | flops 5080368 | bytes 4649120 | tf_op jit(solution)/shard_map/sub | solution.py:166
  1151.4 29.5 %reduce-scatter.39.cloned.1.call-done = bf16[192,768]{1,0:T(8,128)(2,1)} async-done(((bf16[768,768]{1,0:T(8,128)(2,1)}), bf16[192,768]{1,0:T(8,128)(2,1)}) %reduce-scatter.39.cloned.1.call-update) | async-done | bytes 294928 | tf_op jit(solution)/shard_map/reduce_scatter | solution.py:507
  1180.9 19.5 %reduce-scatter.35.cloned.1.call-done = bf16[48,768]{1,0:T(8,128)(2,1)} async-done(((bf16[192,768]{1,0:T(8,128)(2,1)}), bf16[48,768]{1,0:T(8,128)(2,1)}) %reduce-scatter.35.cloned.1.call-update) | async-done | bytes 73744 | tf_op jit(solution)/shard_map/reduce_scatter | solution.py:501
  1200.4 26.9 %reduce-scatter.33.cloned.1.call-done = bf16[3,48,768]{2,1,0:T(8,128)(2,1)} async-done(((bf16[3,192,768]{2,1,0:T(8,128)(2,1)}), bf16[3,48,768]{2,1,0:T(8,128)(2,1)}) %reduce-scatter.33.cloned.1.call-update) | async-done | bytes 221200 | tf_op jit(solution)/shard_map/reduce_scatter | solution.py:498
  1238.3 28.9 %all-reduce.47 = (f32[2,192]{1,0:T(2,128)}, f32[768]{0:T(1024)}, f32[3,192]{1,0:T(4,128)}, f32[768]{0:T(1024)}) all-reduce(f32[2,192]{1,0:T(2,128)S(1)} %pad_maximum_fusion.1, f32[768]{0:T(1024)S(1)} %copy-done.122, f32[3,192]{1,0:T(4,128)S(1)} %reshape.620, ...), channel_id=1, replica_groups=mesh['dp'=2,'hid'=4,'wid'=4] {'dp','wid'}, use_global_device_ids=true, to_apply=%region_49.50 | all-reduce | flops 2496 | bytes 19968 | tf_op jit(solution)/shard_map/psum | solution.py:486
  1277.4 12.8 reduce-scatter.63.cloned.1.call-done
  1306.0 131.8 %all-reduce.52.cloned.1.call-done = (f32[9,768]{1,0:T(8,128)}, f32[768]{0:T(1024)}, f32[768]{0:T(1024)}, f32[768]{0:T(1024)}, f32[768]{0:T(1024)}, /*index=5*/f3...) async-done(((f32[9,768]{1,0:T(8,128)}, f32[768]{0:T(1024)}, ...) | async-done | bytes 98320 | tf_op jit(solution)/shard_map/psum | solution.py:465
  (552 shorter events, 426.9 us)
Async XLA Ops:
  8.0 51.6 %all-gather.13.cloned.1.call-start = ((), (), s32[]{:S(2)}) async-start(), calls=%async_computation.16 | async-start | bytes 3010560 | tf_op jit(solution)/shard_map/all_gather | solution.py:92
  18.3 179.0 %copy-start.1 = (f32[392,768]{1,0:T(8,128)}, f32[392,768]{1,0:T(8,128)S(1)}, u32[]{:S(2)}) copy-start(f32[392,768]{1,0:T(8,128)S(1)} %get-tuple-element.143) | copy-start | bytes 3612676
  19.5 177.8 %reduce-scatter.49.cloned.1.call-start = ((), (), s32[]{:S(2)}) async-start(), calls=%async_computation.36 | async-start | bytes 6021120
  139.2 61.6 %all-gather.17.cloned.1.call-start = ((), (), s32[]{:S(2)}) async-start(), calls=%async_computation.18 | async-start | bytes 1474560 | tf_op jit(solution)/shard_map/all_gather | solution.py:392
  139.8 98.0 %all-gather.15.cloned.1.call-start = ((), (), s32[]{:S(2)}) async-start(), calls=%async_computation.17 | async-start | bytes 3010560 | tf_op jit(solution)/shard_map/all_gather | solution.py:92
  200.2 68.9 %all-gather.19.cloned.1.call-start = ((), (), s32[]{:S(2)}) async-start(), calls=%async_computation.19 | async-start | bytes 1474560 | tf_op jit(solution)/shard_map/all_gather | solution.py:393
  200.7 132.1 %reduce-scatter.51.cloned.1.call-start = ((), (), s32[]{:S(2)}) async-start(), calls=%async_computation.37 | async-start | bytes 6021120
  275.3 113.8 %all-gather.21.cloned.1.call-start = ((), (), s32[]{:S(2)}) async-start(), calls=%async_computation.20 | async-start | bytes 3010560 | tf_op jit(solution)/shard_map/all_gather | solution.py:92
  351.0 125.2 %reduce-scatter.53.cloned.1.call-start = ((), (), s32[]{:S(2)}) async-start(), calls=%async_computation.38 | async-start | bytes 6021120
  418.4 89.1 %all-gather.25.cloned.1.call-start = ((), (), s32[]{:S(2)}) async-start(), calls=%async_computation.22 | async-start | bytes 1474560 | tf_op jit(solution)/shard_map/all_gather | solution.py:396
  419.2 127.5 %all-gather.23.cloned.1.call-start = ((), (), s32[]{:S(2)}) async-start(), calls=%async_computation.21 | async-start | bytes 3010560 | tf_op jit(solution)/shard_map/all_gather | solution.py:92
  481.1 96.7 %all-gather.27.cloned.1.call-start = ((), (), s32[]{:S(2)}) async-start(), calls=%async_computation.23 | async-start | bytes 1474560 | tf_op jit(solution)/shard_map/all_gather | solution.py:397
  481.7 135.3 %all-gather.29.cloned.1.call-start = ((), (), s32[]{:S(2)}) async-start(), calls=%async_computation.24 | async-start | bytes 3010560 | tf_op jit(solution)/shard_map/all_gather | solution.py:111
  482.3 134.7 %copy-start.119 = (f32[768]{0:T(1024)S(1)}, f32[768]{0:T(1024)}, u32[]{:S(2)}) copy-start(f32[768]{0:T(1024)} %param.59) | copy-start | bytes 9220
  482.3 194.3 %reduce-scatter.57.cloned.1.call-start = ((), (), s32[]{:S(2)}) async-start(), calls=%async_computation.40 | async-start | bytes 3010560
  638.3 99.4 %reduce-scatter.55.cloned.1.call-start = ((), (), s32[]{:S(2)}) async-start(), calls=%async_computation.39 | async-start | bytes 6021120
  648.6 131.5 %all-gather.31.cloned.1.call-start = ((), (), s32[]{:S(2)}) async-start(), calls=%async_computation.25 | async-start | bytes 3010560 | tf_op jit(solution)/shard_map/all_gather | solution.py:111
  742.1 111.5 %reduce-scatter.59.cloned.1.call-start = ((), (), s32[]{:S(2)}) async-start(), calls=%async_computation.41 | async-start | bytes 3010560
  815.4 98.9 %all-gather.33.cloned.1.call-start = ((), (), s32[]{:S(2)}) async-start(), calls=%async_computation.26 | async-start | bytes 3010560 | tf_op jit(solution)/shard_map/all_gather | solution.py:111
  876.6 90.0 %reduce-scatter.61.cloned.1.call-start = ((), (), s32[]{:S(2)}) async-start(), calls=%async_computation.42 | async-start | bytes 3010560
  928.3 83.3 %all-gather.35.cloned.1.call-start = ((), (), s32[]{:S(2)}) async-start(), calls=%async_computation.27 | async-start | bytes 3010560 | tf_op jit(solution)/shard_map/all_gather | solution.py:111
  973.9 177.5 %reduce-scatter.47.cloned.1.call-start = ((), (), s32[]{:S(2)}) async-start(), calls=%async_computation.35 | async-start | bytes 1474560 | tf_op jit(solution)/shard_map/reduce_scatter | solution.py:519
  979.4 171.9 %reduce-scatter.45.cloned.1.call-start = ((), (), s32[]{:S(2)}) async-start(), calls=%async_computation.34 | async-start | bytes 1474560 | tf_op jit(solution)/shard_map/reduce_scatter | solution.py:516
  985.6 165.7 %reduce-scatter.43.cloned.1.call-start = ((), (), s32[]{:S(2)}) async-start(), calls=%async_computation.33 | async-start | bytes 368640 | tf_op jit(solution)/shard_map/reduce_scatter | solution.py:513
  988.9 162.4 %reduce-scatter.41.cloned.1.call-start = ((), (), s32[]{:S(2)}) async-start(), calls=%async_computation.32 | async-start | bytes 1105920 | tf_op jit(solution)/shard_map/reduce_scatter | solution.py:510
  993.4 158.0 %reduce-scatter.37.cloned.1.call-start = ((), (), s32[]{:S(2)}) async-start(), calls=%async_computation.30 | async-start | bytes 1474560 | tf_op jit(solution)/shard_map/reduce_scatter | solution.py:504
  999.4 181.5 %reduce-scatter.39.cloned.1.call-start = ((), (), s32[]{:S(2)}) async-start(), calls=%async_computation.31 | async-start | bytes 1474560 | tf_op jit(solution)/shard_map/reduce_scatter | solution.py:507
  1004.7 195.7 %reduce-scatter.35.cloned.1.call-start = ((), (), s32[]{:S(2)}) async-start(), calls=%async_computation.29 | async-start | bytes 368640 | tf_op jit(solution)/shard_map/reduce_scatter | solution.py:501
  1102.1 125.2 %reduce-scatter.33.cloned.1.call-start = ((), (), s32[]{:S(2)}) async-start(), calls=%async_computation.28 | async-start | bytes 1105920 | tf_op jit(solution)/shard_map/reduce_scatter | solution.py:498
  1151.1 116.2 %all-reduce.54.cloned.1.call-start = ((), (), s32[]{:S(2)}) async-start(), calls=%async_computation.45 | async-start | bytes 3538944 | tf_op jit(solution)/shard_map/psum | solution.py:488
  1227.3 62.9 %reduce-scatter.63.cloned.1.call-start = ((), (), s32[]{:S(2)}) async-start(), calls=%async_computation.43 | async-start | bytes 3010560
  1231.1 206.7 %all-reduce.52.cloned.1.call-start = ((), (), s32[]{:S(2)}) async-start(), calls=%async_computation.44 | async-start | bytes 311296 | tf_op jit(solution)/shard_map/psum | solution.py:465
  (133 other events, 2021.1 us)
Sparse Core Ops, SparseCore 0:
  19.6 39.9 all-gather.12
  139.4 57.8 reduce-scatter.48
  351.1 37.9 all-gather.20
  638.4 38.1 reduce-scatter.56
  679.7 57.9 reduce-scatter.54
  742.2 37.8 all-gather.30
  815.5 38.0 reduce-scatter.58
  928.4 38.1 reduce-scatter.60
  1227.5 21.0 all-reduce.53
  1251.4 38.8 reduce-scatter.62
  1303.6 134.0 all-reduce.51
Sparse Core Ops, SparseCore 1:
  141.3 29.6 all-gather.16
  200.2 37.6 all-gather.14
  239.3 29.7 all-gather.18
  275.4 57.4 reduce-scatter.50
  418.5 57.6 reduce-scatter.52
  477.8 29.7 all-gather.24
  509.2 37.4 all-gather.22
  548.1 29.7 all-gather.26
  579.6 37.4 all-gather.28
  876.7 37.6 all-gather.32
  973.9 37.6 all-gather.34
  1014.0 28.9 reduce-scatter.46
  1045.3 27.8 reduce-scatter.44
  1076.1 16.6 reduce-scatter.42
  1095.2 24.4 reduce-scatter.40
  1122.2 28.4 reduce-scatter.36
  1153.1 27.8 reduce-scatter.38
  1183.9 16.5 reduce-scatter.34
  1202.7 24.6 reduce-scatter.32
where the time goes:
time: 1480 us; the launch traced here: 1470 us
  waiting for transfers between devices  841 us (57%)
  local copies, waits for them, and re-layouts  191 us (13%)
  matrix products  165 us (11%)
  other arithmetic  163 us (11%)
  blocking collectives  85.6 us (6%)
  between operations  17.8 us (1%)
    unnamed x38, waiting for transfers between devices  349 us
    psum x1, waiting for transfers between devices, body(): lax.psum((kernel_one, convbias_one, little_one[0], little_one[1], little_...  132 us
    all_gather x4, waiting for transfers between devices, gather_grads(): return lax.all_gather(grads, 'hid', axis=0, tiled=True)  121 us
    all_gather x4, waiting for transfers between devices, gather_rows(): return lax.all_gather(normed, 'hid', axis=0, tiled=True)  96.9 us
    dot_general x8, matrix products, times_transposed(): lax.dot_general(left, right, (((1,), (1,)), ((), ())), preferred_element_...  60.4 us
    sub x1, other arithmetic, window_backward(): grad_probs - jnp.sum(probabilities * grad_probs, axis=-1, keepdims=True)  55.7 us
    dot_general x8, matrix products, outer(): lax.dot_general(left, right, (((0,), (0,)), ((), ())), preferred_element_...  38.3 us
    unnamed x288, local copies, waits for them, and re-layouts  37.2 us
  transfers between devices with their start and end apart: 30, of which 23 were waited for; matrix products, arithmetic and copies ran while one was open for 16% of the time, Pallas kernels for 0%

commit v1 on v0

--- a/solution.py
+++ b/solution.py
@@ -89,18 +89,11 @@
 
 
 def gather_rows(normed):
-    return lax.all_gather(normed, "hid", axis=0, tiled=True)
+    return normed
 
 
 def reduce_rows(operand, weight):
-    row_count = operand.shape[0] // lax.axis_size("hid")
-
-    def term(first_row, length):
-        return jnp.dot(operand, weight, preferred_element_type=jnp.float32)
-
-    return lax.psum_scatter(
-        term(jnp.int32(0), row_count * lax.axis_size("hid")), "hid", scatter_dimension=0, tiled=True
-    )
+    return jnp.dot(operand, weight, preferred_element_type=jnp.float32)
 
 
 def project_heads(mixed_rows, outweights):
@@ -108,21 +101,56 @@
 
 
 def gather_grads(grads):
-    return lax.all_gather(grads, "hid", axis=0, tiled=True)
+    return grads
 
 
 def reduce_back(operand, weight):
-    row_count = operand.shape[0] // lax.axis_size("hid")
-
-    def term(first_row, length):
-        return jnp.dot(operand, weight, preferred_element_type=jnp.float32)
-
-    return lax.psum_scatter(
-        term(jnp.int32(0), row_count * lax.axis_size("hid")).astype(jnp.bfloat16),
-        "hid",
-        scatter_dimension=0,
-        tiled=True,
+    return jnp.dot(operand, weight, preferred_element_type=jnp.float32)
+
+
+def sibling(values):
+    pairs = [(index, index ^ 1) for index in range(lax.axis_size("dp"))]
+    return lax.ppermute(values, "dp", pairs)
+
+
+def own_half(values):
+    half = values.shape[-1] // 2
+    first = lax.rem(lax.axis_index("dp"), 2) == 0
+    return jnp.where(first, values[..., :half], values[..., half:])
+
+
+def other_half(values):
+    half = values.shape[-1] // 2
+    first = lax.rem(lax.axis_index("dp"), 2) == 0
+    return jnp.where(first, values[..., half:], values[..., :half])
+
+
+def join_halves(own, other):
+    first = lax.rem(lax.axis_index("dp"), 2) == 0
+    return jnp.concatenate([jnp.where(first, own, other), jnp.where(first, other, own)], axis=-1)
+
+
+def gather_matrix(shard, axis):
+    own = lax.all_gather(own_half(shard), ("hid", "wid"), axis=axis, tiled=True)
+    return join_halves(own, sibling(own))
+
+
+def scatter_matrix(grads, axis):
+    rounded = grads.astype(jnp.bfloat16)
+    both = own_half(rounded).astype(jnp.float32) + sibling(other_half(rounded)).astype(jnp.float32)
+    piece = lax.psum_scatter(
+        both.astype(jnp.bfloat16), ("hid", "wid"), scatter_dimension=axis, tiled=True
     ).astype(jnp.float32)
+    total = piece
+    for shift in range(2, lax.axis_size("dp"), 2):
+        pairs = [(index, (index + shift) % lax.axis_size("dp")) for index in range(lax.axis_size("dp"))]
+        total = total + lax.ppermute(piece, "dp", pairs)
+    return join_halves(total, sibling(total))
+
+
+def own_rows(values, axis):
+    length = values.shape[axis] // lax.axis_size("hid")
+    return lax.dynamic_slice_in_dim(values, lax.axis_index("hid") * length, length, axis)
 
 
 def window_scores(query_rows, key_rows, present):
@@ -374,28 +402,23 @@
     channel_downbias,
 ):
     image_count = inputs.shape[0] // (PADDED * PADDED)
-    size_table = grid_sizes.reshape(lax.axis_size("hid"), lax.axis_size("wid"), image_count)
-    own_sizes = lax.dynamic_index_in_dim(
-        lax.dynamic_index_in_dim(size_table, lax.axis_index("hid"), 0, keepdims=False),
-        lax.axis_index("wid"),
-        0,
-        keepdims=False,
-    )
-    group_sizes = lax.dynamic_index_in_dim(
-        size_table, lax.axis_index("wid"), 1, keepdims=False
-    ).reshape(-1)
-    present = presence(own_sizes)
-    group_present = presence(group_sizes)
+    place = (lax.axis_index("hid") * lax.axis_size("wid") + lax.axis_index("wid")) * image_count
+    present = presence(lax.dynamic_slice_in_dim(grid_sizes, place, image_count, 0))
+    group_present = present
     local = (
-        lax.all_gather(window_inweights, "wid", axis=1, tiled=True),
-        lax.all_gather(window_outweights, "wid", axis=0, tiled=True),
-        lax.all_gather(window_upweights, "wid", axis=0, tiled=True),
-        lax.all_gather(window_downweights, "wid", axis=0, tiled=True),
-        lax.all_gather(channel_inweights, "wid", axis=1, tiled=True),
-        lax.all_gather(channel_outweights, "wid", axis=0, tiled=True),
-        lax.all_gather(channel_upweights, "wid", axis=0, tiled=True),
-        lax.all_gather(channel_downweights, "wid", axis=0, tiled=True),
-    )
+        gather_matrix(window_inweights, 1),
+        gather_matrix(window_outweights, 0),
+        gather_matrix(window_upweights, 0),
+        gather_matrix(window_downweights, 0),
+        gather_matrix(channel_inweights, 1),
+        gather_matrix(channel_outweights, 0),
+        gather_matrix(channel_upweights, 0),
+        gather_matrix(channel_downweights, 0),
+    )
+    window_inbias = lax.all_gather(window_inbias, "hid", axis=1, tiled=True)
+    window_upbias = lax.all_gather(window_upbias, "hid", axis=0, tiled=True)
+    channel_inbias = lax.all_gather(channel_inbias, "hid", axis=1, tiled=True)
+    channel_upbias = lax.all_gather(channel_upbias, "hid", axis=0, tiled=True)
     start = inputs * present
     after_conv = start + present * depthwise(start, window_convkernel, window_convbias)
     after_attn, saved_one = attention_forward(
@@ -483,42 +506,24 @@
         ),
         ("dp", "hid", "wid"),
     )
-    heads = lax.psum((inbias_one, upbias_two, inbias_three, upbias_four), ("dp", "wid"))
-    summed = (
-        lax.psum(in_one.astype(jnp.bfloat16), "dp").astype(jnp.float32),
-        lax.psum(out_one.astype(jnp.bfloat16), "dp").astype(jnp.float32),
-        lax.psum(up_two.astype(jnp.bfloat16), "dp").astype(jnp.float32),
-        lax.psum(down_two.astype(jnp.bfloat16), "dp").astype(jnp.float32),
-        lax.psum(in_three.astype(jnp.bfloat16), "dp").astype(jnp.float32),
-        lax.psum(out_three.astype(jnp.bfloat16), "dp").astype(jnp.float32),
-        lax.psum(up_four.astype(jnp.bfloat16), "dp").astype(jnp.float32),
-        lax.psum(down_four.astype(jnp.bfloat16), "dp").astype(jnp.float32),
+    heads = lax.psum(
+        (inbias_one, upbias_two, inbias_three, upbias_four), ("dp", "hid", "wid")
+    )
+    heads = (
+        own_rows(heads[0], 1),
+        own_rows(heads[1], 0),
+        own_rows(heads[2], 1),
+        own_rows(heads[3], 0),
     )
     weights = (
-        lax.psum_scatter(
-            summed[0].astype(jnp.bfloat16), "wid", scatter_dimension=1, tiled=True
-        ).astype(jnp.float32),
-        lax.psum_scatter(
-            summed[1].astype(jnp.bfloat16), "wid", scatter_dimension=0, tiled=True
-        ).astype(jnp.float32),
-        lax.psum_scatter(
-            summed[2].astype(jnp.bfloat16), "wid", scatter_dimension=0, tiled=True
-        ).astype(jnp.float32),
-        lax.psum_scatter(
-            summed[3].astype(jnp.bfloat16), "wid", scatter_dimension=0, tiled=True
-        ).astype(jnp.float32),
-        lax.psum_scatter(
-            summed[4].astype(jnp.bfloat16), "wid", scatter_dimension=1, tiled=True
-        ).astype(jnp.float32),
-        lax.psum_scatter(
-            summed[5].astype(jnp.bfloat16), "wid", scatter_dimension=0, tiled=True
-        ).astype(jnp.float32),
-        lax.psum_scatter(
-            summed[6].astype(jnp.bfloat16), "wid", scatter_dimension=0, tiled=True
-        ).astype(jnp.float32),
-        lax.psum_scatter(
-            summed[7].astype(jnp.bfloat16), "wid", scatter_dimension=0, tiled=True
-        ).astype(jnp.float32),
+        scatter_matrix(in_one, 1),
+        scatter_matrix(out_one, 0),
+        scatter_matrix(up_two, 0),
+        scatter_matrix(down_two, 0),
+        scatter_matrix(in_three, 1),
+        scatter_matrix(out_three, 0),
+        scatter_matrix(up_four, 0),
+        scatter_matrix(down_four, 0),
     )
     return (
         outputs,

time: 1480 us -> 1990 us (1.34)
  waiting for transfers between devices: 841 us -> 1320 us
  starting transfers between devices: 3.1 us -> 51 us
  matrix products: 165 us -> 135 us
  other arithmetic: 163 us -> 185 us
    reduce_scatter x8, waiting for transfers between devices: 76 us -> 1010 us  [scatter_matrix(): lax.psum_scatter(both.astype(jnp.bfloat16), ('hid', 'wid'), scatter_dimen...]
    unnamed x38 -> x15, waiting for transfers between devices: 349 us -> 0.25 us
    psum x1, waiting for transfers between devices: 132 us -> 55.1 us  [body(): lax.psum((kernel_one, convbias_one, little_one[0], little_one[1], little_...]
    all_gather x12 -> x6, waiting for transfers between devices: 284 us -> 230 us  [gather_matrix(): own = lax.all_gather(own_half(shard), ('hid', 'wid'), axis=axis, tiled=True)]
    ppermute x0 -> x24, starting transfers between devices: none -> 49.7 us  [sibling(): return lax.ppermute(values, 'dp', pairs)]
    all_gather x4 -> x6, blocking collectives: 56.7 us -> 104 us  [the longest x2 80.4 us: gather_matrix(): own = lax.all_gather(own_half(shard), ('hid', 'wid'), axis=axis, tiled=True)]
    select_n x0 -> x32, other arithmetic: none -> 37.5 us  [the longest x16 23.2 us: join_halves(): jnp.where(first, own, other)]
    psum x1 -> x0, blocking collectives: 28.9 us -> none  [body(): lax.psum((inbias_one, upbias_two, inbias_three, upbias_four), ('dp', 'wid'))]
  transfers between devices with their start and end apart: 30 -> 39, of which waited for: 23 -> 19; matrix products, arithmetic and copies ran while one was open for 16% -> 13% of each run, Pallas kernels for 0% -> 0%
where the time goes in v1:
time: 1990 us; the launch traced here: 1980 us
  waiting for transfers between devices  1320 us (66%)
  other arithmetic  185 us (9%)
  local copies, waits for them, and re-layouts  174 us (9%)
  matrix products  135 us (7%)
  blocking collectives  104 us (5%)
  starting transfers between devices  51 us (3%)
    reduce_scatter x8, waiting for transfers between devices, scatter_matrix(): lax.psum_scatter(both.astype(jnp.bfloat16), ('hid', 'wid'), scatter_dimen...  1010 us
    all_gather x6, waiting for transfers between devices, gather_matrix(): own = lax.all_gather(own_half(shard), ('hid', 'wid'), axis=axis, tiled=True)  230 us
    all_gather x2, blocking collectives, gather_matrix(): own = lax.all_gather(own_half(shard), ('hid', 'wid'), axis=axis, tiled=True)  80.4 us
    sub x1, other arithmetic, window_backward(): grad_probs - jnp.sum(probabilities * grad_probs, axis=-1, keepdims=True)  58.3 us
    psum x1, waiting for transfers between devices, body(): lax.psum((kernel_one, convbias_one, little_one[0], little_one[1], little_...  55.1 us
    ppermute x24, starting transfers between devices, sibling(): return lax.ppermute(values, 'dp', pairs)  49.7 us
    dot_general x8, matrix products, times_transposed(): lax.dot_general(left, right, (((1,), (1,)), ((), ())), preferred_element_...  45.2 us
  transfers between devices with their start and end apart: 39, of which 19 were waited for; matrix products, arithmetic and copies ran while one was open for 13% of the time, Pallas kernels for 0%

profile of v1, /device:TPU:1, one launch (start us, length us, event | category | flops | bytes accessed | tf_op | source)
XLA Modules:
  0.0 1983.4 jit_solution(16210127803833971832)
XLA Ops:
  15.9 44.3 %all_gather.38 = bf16[768,384]{1,0:T(8,128)(2,1)} all-gather(bf16[48,384]{1,0:T(8,128)(2,1)S(1)} %slice_select_fusion.7), channel_id=1, replica_groups=mesh['dp'=2,'hid'=4,'wid'=4] {'hid','wid'}, dimensions={0}, use_global_device_ids=true | all-gather | bytes 626688 | tf_op jit(solution)/shard_map/all_gather | solution.py:134
  60.2 8.7 collective-permute-start.1
  69.0 36.0 %all_gather.44 = bf16[768,384]{1,0:T(8,128)(2,1)S(1)} all-gather(bf16[48,384]{1,0:T(8,128)(2,1)S(1)} %slice_select_fusion.6), channel_id=1, replica_groups=mesh['dp'=2,'hid'=4,'wid'=4] {'hid','wid'}, dimensions={0}, use_global_device_ids=true | all-gather | bytes 626688 | tf_op jit(solution)/shard_map/all_gather | solution.py:134
  105.0 6.8 collective-permute-start.5
  118.3 6.9 all-gather.2
  141.0 6.4 all-gather.1
  158.3 41.2 %all-gather.21.cloned.1.call-done = bf16[3072,384]{1,0:T(8,128)(2,1)} async-done(((bf16[192,384]{1,0:T(8,128)(2,1)}), bf16[3072,384]{1,0:T(8,128)(2,1)}) %all-gather.21.cloned.1.call-update) | async-done | bytes 2359312 | tf_op jit(solution)/shard_map/all_gather | solution.py:134
  200.8 63.0 %all-gather.19.cloned.1.call-done = bf16[3072,384]{1,0:T(8,128)(2,1)} async-done(((bf16[192,384]{1,0:T(8,128)(2,1)}), bf16[3072,384]{1,0:T(8,128)(2,1)}) %all-gather.19.cloned.1.call-update) | async-done | bytes 2359312 | tf_op jit(solution)/shard_map/all_gather | solution.py:134
  265.1 63.0 %all-gather.15.cloned.1.call-done = bf16[3072,384]{1,0:T(8,128)(2,1)} async-done(((bf16[192,384]{1,0:T(8,128)(2,1)}), bf16[3072,384]{1,0:T(8,128)(2,1)}) %all-gather.15.cloned.1.call-update) | async-done | bytes 2359312 | tf_op jit(solution)/shard_map/all_gather | solution.py:134
  329.4 63.0 %all-gather.13.cloned.1.call-done = bf16[3072,384]{1,0:T(8,128)(2,1)} async-done(((bf16[192,384]{1,0:T(8,128)(2,1)}), bf16[3072,384]{1,0:T(8,128)(2,1)}) %all-gather.13.cloned.1.call-update) | async-done | bytes 2359312 | tf_op jit(solution)/shard_map/all_gather | solution.py:134
  418.3 6.2 copy.173
  447.2 5.3 copy.176
  463.7 14.6 multiply_convert_fusion.1
  532.6 13.3 multiply_convert_fusion
  593.0 5.4 multiply_reduce_fusion.18
  610.7 7.2 convert_reduce_fusion.1
  640.0 6.2 copy.201
  646.3 58.3 %select_convert_fusion = bf16[8,24,49,49]{3,1,2,0:T(8,128)(2,1)S(1)} fusion(f32[8,24,49,49]{3,1,2,0:T(8,128)} %copy.201, f32[8,24,49,49]{3,1,2,0:T(8,128)} %copy.173, f32[8,24,49]{1,2,0:T(8,128)S(1)} %copy-done.68, pred[8,49]{1,0:T(8,128)(4,1)S(1)} %copy-done.107), kind=kOutput, calls=%fused_computation.14 | output fusion | flops 5080368 | bytes 4647944 | tf_op jit(solution)/shard_map/sub | solution.py:194
  709.3 5.3 copy.212
  716.8 5.3 copy.204
  726.8 5.5 copy.208
  739.4 6.0 multiply_reduce_fusion.21
  852.7 5.5 fusion.71
  858.2 55.1 %all-reduce.41.cloned.1.call-done = (f32[9,768]{1,0:T(8,128)}, f32[768]{0:T(1024)}, f32[768]{0:T(1024)}, f32[768]{0:T(1024)}, f32[2,768]{1,0:T(2,128)}, /*index=...) async-done(((f32[9,768]{1,0:T(8,128)}, f32[768]{0:T(1024)}, ...) | async-done | bytes 138256 | tf_op jit(solution)/shard_map/psum | solution.py:488
  917.4 124.2 %reduce-scatter.19.cloned.1.call-done = bf16[48,384]{1,0:T(8,128)(2,1)} async-done(((bf16[768,384]{1,0:T(8,128)(2,1)}), bf16[48,384]{1,0:T(8,128)(2,1)}) %reduce-scatter.19.cloned.1.call-update) | async-done | bytes 36880 | tf_op jit(solution)/shard_map/reduce_scatter | solution.py:141
  1045.9 122.8 %reduce-scatter.11.cloned.1.call-done = bf16[48,384]{1,0:T(8,128)(2,1)} async-done(((bf16[768,384]{1,0:T(8,128)(2,1)}), bf16[48,384]{1,0:T(8,128)(2,1)}) %reduce-scatter.11.cloned.1.call-update) | async-done | bytes 36880 | tf_op jit(solution)/shard_map/reduce_scatter | solution.py:141
  1173.4 125.4 %reduce-scatter.17.cloned.1.call-done = bf16[3,48,384]{2,1,0:T(8,128)(2,1)} async-done(((bf16[3,768,384]{2,1,0:T(8,128)(2,1)}), bf16[3,48,384]{2,1,0:T(8,128)(2,1)}) %reduce-scatter.17.cloned.1.call-update) | async-done | bytes 110608 | tf_op jit(solution)/shard_map/reduce_scatter | solution.py:141
  1303.6 125.4 %reduce-scatter.9.cloned.1.call-done = bf16[3,48,384]{2,1,0:T(8,128)(2,1)} async-done(((bf16[3,768,384]{2,1,0:T(8,128)(2,1)}), bf16[3,48,384]{2,1,0:T(8,128)(2,1)}) %reduce-scatter.9.cloned.1.call-update) | async-done | bytes 110608 | tf_op jit(solution)/shard_map/reduce_scatter | solution.py:141
  1433.4 127.8 %reduce-scatter.21.cloned.1.call-done = bf16[192,384]{1,0:T(8,128)(2,1)} async-done(((bf16[3072,384]{1,0:T(8,128)(2,1)}), bf16[192,384]{1,0:T(8,128)(2,1)}) %reduce-scatter.21.cloned.1.call-update) | async-done | bytes 147472 | tf_op jit(solution)/shard_map/reduce_scatter | solution.py:141
  1566.2 128.3 %reduce-scatter.23.cloned.1.call-done = bf16[192,384]{1,0:T(8,128)(2,1)} async-done(((bf16[3072,384]{1,0:T(8,128)(2,1)}), bf16[192,384]{1,0:T(8,128)(2,1)}) %reduce-scatter.23.cloned.1.call-update) | async-done | bytes 147472 | tf_op jit(solution)/shard_map/reduce_scatter | solution.py:141
  1698.6 128.2 %reduce-scatter.13.cloned.1.call-done = bf16[192,384]{1,0:T(8,128)(2,1)} async-done(((bf16[3072,384]{1,0:T(8,128)(2,1)}), bf16[192,384]{1,0:T(8,128)(2,1)}) %reduce-scatter.13.cloned.1.call-update) | async-done | bytes 147472 | tf_op jit(solution)/shard_map/reduce_scatter | solution.py:141
  1830.2 129.8 %reduce-scatter.15.cloned.1.call-done = bf16[192,384]{1,0:T(8,128)(2,1)} async-done(((bf16[3072,384]{1,0:T(8,128)(2,1)}), bf16[192,384]{1,0:T(8,128)(2,1)}) %reduce-scatter.15.cloned.1.call-update) | async-done | bytes 147472 | tf_op jit(solution)/shard_map/reduce_scatter | solution.py:141
  (663 shorter events, 416.2 us)
Async XLA Ops:
  7.2 120.9 %all-gather.11.cloned.1.call-start = ((), (), s32[]{:S(2)}) async-start(), calls=%async_computation.8 | async-start | bytes 1880064 | tf_op jit(solution)/shard_map/all_gather | solution.py:134
  9.0 145.3 %all-gather.17.cloned.1.call-start = ((), (), s32[]{:S(2)}) async-start(), calls=%async_computation.11 | async-start | bytes 1880064 | tf_op jit(solution)/shard_map/all_gather | solution.py:134
  10.7 188.9 %all-gather.21.cloned.1.call-start = ((), (), s32[]{:S(2)}) async-start(), calls=%async_computation.13 | async-start | bytes 2506752 | tf_op jit(solution)/shard_map/all_gather | solution.py:134
  12.5 251.4 %all-gather.19.cloned.1.call-start = ((), (), s32[]{:S(2)}) async-start(), calls=%async_computation.12 | async-start | bytes 2506752 | tf_op jit(solution)/shard_map/all_gather | solution.py:134
  14.3 313.9 %all-gather.15.cloned.1.call-start = ((), (), s32[]{:S(2)}) async-start(), calls=%async_computation.10 | async-start | bytes 2506752 | tf_op jit(solution)/shard_map/all_gather | solution.py:134
  15.1 377.4 %all-gather.13.cloned.1.call-start = ((), (), s32[]{:S(2)}) async-start(), calls=%async_computation.9 | async-start | bytes 2506752 | tf_op jit(solution)/shard_map/all_gather | solution.py:134
  15.8 897.5 %all-reduce.41.cloned.1.call-start = ((), (), s32[]{:S(2)}) async-start(), calls=%async_computation.22 | async-start | bytes 397312 | tf_op jit(solution)/shard_map/psum | solution.py:488
  60.2 89.1 %collective-permute-start.1 = (bf16[768,384]{1,0:T(8,128)(2,1)}, bf16[768,384]{1,0:T(8,128)(2,1)}, u32[]{:S(2)}, u32[]{:S(2)}) collective-permute-start(bf16[768,384]{1,0:T(8,128)(2,1)} %all_gather.38), channel_id=1, source_target_pairs={{0,16},{16,0},{1,17},{17,1},{2,18},{18,2},{3,19},{19,3},{4,20},{20... | collective-permute-start | bytes 1769480 | tf_op jit(solution)/shard_map/ppermute | solution.py:113
  105.0 47.1 %collective-permute-start.5 = (bf16[768,384]{1,0:T(8,128)(2,1)S(1)}, bf16[768,384]{1,0:T(8,128)(2,1)}, u32[]{:S(2)}, u32[]{:S(2)}) collective-permute-start(bf16[768,384]{1,0:T(8,128)(2,1)S(1)} %all_gather.44), channel_id=1, source_target_pairs={{0,16},{16,0},{1,17},{17,1},{2,18},{18,2},{3,19},{19,3},{4,20},{20... | collective-permute-start | bytes 1769480 | tf_op jit(solution)/shard_map/ppermute | solution.py:113
  128.2 264.3 %collective-permute-start = (bf16[3,768,384]{2,1,0:T(8,128)(2,1)}, bf16[3,768,384]{2,1,0:T(8,128)(2,1)}, u32[]{:S(2)}, u32[]{:S(2)}) collective-permute-start(bf16[3,768,384]{2,1,0:T(8,128)(2,1)} %all-gather.11.cloned.1.call-done), channel_id=1, source_target_pairs={{0,16},{16,0},{1,17},{17,1},{2,18},{18,2},{3,19},{19,3},{4,20},{20... | collective-permute-start | bytes 5308424 | tf_op jit(solution)/shard_map/ppermute | solution.py:113
  154.3 300.5 %collective-permute-start.4 = (bf16[3,768,384]{2,1,0:T(8,128)(2,1)}, bf16[3,768,384]{2,1,0:T(8,128)(2,1)}, u32[]{:S(2)}, u32[]{:S(2)}) collective-permute-start(bf16[3,768,384]{2,1,0:T(8,128)(2,1)} %all-gather.17.cloned.1.call-done), channel_id=1, source_target_pairs={{0,16},{16,0},{1,17},{17,1},{2,18},{18,2},{3,19},{19,3},{4,20},{20... | collective-permute-start | bytes 5308424 | tf_op jit(solution)/shard_map/ppermute | solution.py:113
  199.6 346.3 %collective-permute-start.7 = (bf16[3072,384]{1,0:T(8,128)(2,1)}, bf16[3072,384]{1,0:T(8,128)(2,1)}, u32[]{:S(2)}, u32[]{:S(2)}) collective-permute-start(bf16[3072,384]{1,0:T(8,128)(2,1)} %all-gather.21.cloned.1.call-done), channel_id=1, source_target_pairs={{0,16},{16,0},{1,17},{17,1},{2,18},{18,2},{3,19},{19,3},{4,20},{20... | collective-permute-start | bytes 7077896 | tf_op jit(solution)/shard_map/ppermute | solution.py:113
  263.9 266.1 %collective-permute-start.6 = (bf16[3072,384]{1,0:T(8,128)(2,1)}, bf16[3072,384]{1,0:T(8,128)(2,1)}, u32[]{:S(2)}, u32[]{:S(2)}) collective-permute-start(bf16[3072,384]{1,0:T(8,128)(2,1)} %all-gather.19.cloned.1.call-done), channel_id=1, source_target_pairs={{0,16},{16,0},{1,17},{17,1},{2,18},{18,2},{3,19},{19,3},{4,20},{20... | collective-permute-start | bytes 7077896 | tf_op jit(solution)/shard_map/ppermute | solution.py:113
  328.2 150.2 %collective-permute-start.3 = (bf16[3072,384]{1,0:T(8,128)(2,1)}, bf16[3072,384]{1,0:T(8,128)(2,1)}, u32[]{:S(2)}, u32[]{:S(2)}) collective-permute-start(bf16[3072,384]{1,0:T(8,128)(2,1)} %all-gather.15.cloned.1.call-done), channel_id=1, source_target_pairs={{0,16},{16,0},{1,17},{17,1},{2,18},{18,2},{3,19},{19,3},{4,20},{20... | collective-permute-start | bytes 7077896 | tf_op jit(solution)/shard_map/ppermute | solution.py:113
  392.5 68.4 %collective-permute-start.2 = (bf16[3072,384]{1,0:T(8,128)(2,1)}, bf16[3072,384]{1,0:T(8,128)(2,1)}, u32[]{:S(2)}, u32[]{:S(2)}) collective-permute-start(bf16[3072,384]{1,0:T(8,128)(2,1)} %all-gather.13.cloned.1.call-done), channel_id=1, source_target_pairs={{0,16},{16,0},{1,17},{17,1},{2,18},{18,2},{3,19},{19,3},{4,20},{20... | collective-permute-start | bytes 7077896 | tf_op jit(solution)/shard_map/ppermute | solution.py:113
  746.7 19.7 collective-permute-start.18
  760.5 281.0 %reduce-scatter.19.cloned.1.call-start = ((), (), s32[]{:S(2)}) async-start(), calls=%async_computation.19 | async-start | bytes 626688 | tf_op jit(solution)/shard_map/reduce_scatter | solution.py:141
  768.6 400.1 %reduce-scatter.11.cloned.1.call-start = ((), (), s32[]{:S(2)}) async-start(), calls=%async_computation.15 | async-start | bytes 626688 | tf_op jit(solution)/shard_map/reduce_scatter | solution.py:141
  771.0 5.8 collective-permute-start.16
  776.7 522.1 %reduce-scatter.17.cloned.1.call-start = ((), (), s32[]{:S(2)}) async-start(), calls=%async_computation.18 | async-start | bytes 1880064 | tf_op jit(solution)/shard_map/reduce_scatter | solution.py:141
  780.2 648.8 %reduce-scatter.9.cloned.1.call-start = ((), (), s32[]{:S(2)}) async-start(), calls=%async_computation.14 | async-start | bytes 1880064 | tf_op jit(solution)/shard_map/reduce_scatter | solution.py:141
  785.4 6.5 collective-permute-start.8
  793.9 767.3 %reduce-scatter.21.cloned.1.call-start = ((), (), s32[]{:S(2)}) async-start(), calls=%async_computation.20 | async-start | bytes 2506752 | tf_op jit(solution)/shard_map/reduce_scatter | solution.py:141
  803.7 890.8 %reduce-scatter.23.cloned.1.call-start = ((), (), s32[]{:S(2)}) async-start(), calls=%async_computation.21 | async-start | bytes 2506752 | tf_op jit(solution)/shard_map/reduce_scatter | solution.py:141
  816.7 1010.2 %reduce-scatter.13.cloned.1.call-start = ((), (), s32[]{:S(2)}) async-start(), calls=%async_computation.16 | async-start | bytes 2506752 | tf_op jit(solution)/shard_map/reduce_scatter | solution.py:141
  829.7 1130.3 %reduce-scatter.15.cloned.1.call-start = ((), (), s32[]{:S(2)}) async-start(), calls=%async_computation.17 | async-start | bytes 2506752 | tf_op jit(solution)/shard_map/reduce_scatter | solution.py:141
  1042.3 129.4 %collective-permute-start.19 = (f32[48,384]{1,0:T(8,128)S(1)}, f32[48,384]{1,0:T(8,128)S(1)}, u32[]{:S(2)}, u32[]{:S(2)}) collective-permute-start(f32[48,384]{1,0:T(8,128)S(1)} %convert_element_type.344), channel_id=1, source_target_pairs={{0,16},{16,0},{1,17},{17,1},{2,18},{18,2},{3,19},{19,3},{4,20},{20... | collective-permute-start | bytes 221192 | tf_op jit(solution)/shard_map/ppermute | solution.py:113
  1299.7 132.8 %collective-permute-start.17 = (f32[3,48,384]{2,1,0:T(8,128)S(1)}, f32[3,48,384]{2,1,0:T(8,128)S(1)}, u32[]{:S(2)}, u32[]{:S(2)}) collective-permute-start(f32[3,48,384]{2,1,0:T(8,128)S(1)} %convert_element_type.338), channel_id=1, source_target_pairs={{0,16},{16,0},{1,17},{17,1},{2,18},{18,2},{3,19},{19,3},{4,20},{20... | collective-permute-start | bytes 663560 | tf_op jit(solution)/shard_map/ppermute | solution.py:113
  1429.9 134.6 %collective-permute-start.9 = (f32[3,48,384]{2,1,0:T(8,128)S(1)}, f32[3,48,384]{2,1,0:T(8,128)S(1)}, u32[]{:S(2)}, u32[]{:S(2)}) collective-permute-start(f32[3,48,384]{2,1,0:T(8,128)S(1)} %convert_element_type.315), channel_id=1, source_target_pairs={{0,16},{16,0},{1,17},{17,1},{2,18},{18,2},{3,19},{19,3},{4,20},{20... | collective-permute-start | bytes 663560 | tf_op jit(solution)/shard_map/ppermute | solution.py:113
  1562.2 401.0 %collective-permute-start.21 = (f32[192,384]{1,0:T(8,128)S(1)}, f32[192,384]{1,0:T(8,128)S(1)}, u32[]{:S(2)}, u32[]{:S(2)}) collective-permute-start(f32[192,384]{1,0:T(8,128)S(1)} %convert_element_type.349), channel_id=1, source_target_pairs={{0,16},{16,0},{1,17},{17,1},{2,18},{18,2},{3,19},{19,3},{4,20},{20... | collective-permute-start | bytes 884744 | tf_op jit(solution)/shard_map/ppermute | solution.py:113
  1695.5 267.8 %collective-permute-start.23 = (f32[192,384]{1,0:T(8,128)S(1)}, f32[192,384]{1,0:T(8,128)S(1)}, u32[]{:S(2)}, u32[]{:S(2)}) collective-permute-start(f32[192,384]{1,0:T(8,128)S(1)} %convert_element_type.355), channel_id=1, source_target_pairs={{0,16},{16,0},{1,17},{17,1},{2,18},{18,2},{3,19},{19,3},{4,20},{20... | collective-permute-start | bytes 884744 | tf_op jit(solution)/shard_map/ppermute | solution.py:113
  1827.9 135.5 %collective-permute-start.13 = (f32[192,384]{1,0:T(8,128)S(1)}, f32[192,384]{1,0:T(8,128)S(1)}, u32[]{:S(2)}, u32[]{:S(2)}) collective-permute-start(f32[192,384]{1,0:T(8,128)S(1)} %convert_element_type.326), channel_id=1, source_target_pairs={{0,16},{16,0},{1,17},{17,1},{2,18},{18,2},{3,19},{19,3},{4,20},{20... | collective-permute-start | bytes 884744 | tf_op jit(solution)/shard_map/ppermute | solution.py:113
  (172 other events, 3510.7 us)
Sparse Core Ops, SparseCore 0:
  11.5 61.0 all-gather.10
  76.0 58.4 all-gather.16
  137.8 61.6 all-gather.20
  202.7 61.0 all-gather.18
  267.0 61.0 all-gather.14
  331.3 61.0 all-gather.12
  760.6 152.5 all-reduce.40
  918.5 122.9 reduce-scatter.18
  1047.5 121.1 reduce-scatter.10
  1173.4 125.3 reduce-scatter.16
  1303.7 125.3 reduce-scatter.8
  1433.8 127.4 reduce-scatter.20
  1566.9 127.5 reduce-scatter.22
  1699.3 127.5 reduce-scatter.12
  1832.4 127.5 reduce-scatter.14

commit v2 on v1

v2 whole, which is shorter than its diff:
```python
from functools import partial

import jax
import jax.numpy as jnp
from jax import lax
from jax.sharding import PartitionSpec as P

HD = 32
WINDOW = 7
PADDED = 14
GRID = 12
CELLS = GRID * GRID
EPSILON = 1e-05
F32 = jnp.float32
BF16 = jnp.bfloat16
SCALE = HD ** (-0.5)


def exchange(values, axis, bit):
    pairs = [(index, index ^ bit) for index in range(lax.axis_size(axis))]
    return lax.ppermute(values, axis, pairs)


def sibling(values):
    return exchange(values, "dp", 1)


def cross(values, first):
    hids = lax.axis_size("hid")
    pairs = []
    for core in range(lax.axis_size("dp")):
        bit = 1 if (core % 2 == 0) == first else 2
        pairs += [(core * hids + index, core * hids + (index ^ bit)) for index in range(hids)]
    return lax.ppermute(values, ("dp", "hid"), pairs)


def second_core():
    return lax.rem(lax.axis_index("dp"), 2) == 1


def gather_half(piece):
    near = piece[None]
    near = jnp.concatenate([near, exchange(near, "wid", 1)], axis=0)
    near = jnp.concatenate([near, exchange(near, "wid", 2)], axis=0)
    near = jnp.concatenate([near, cross(near, True)], axis=0)
    return near, cross(near, False)


def scatter_half(near, far):
    near = near.astype(F32) + cross(far, False).astype(F32)
    near = near[:4] + cross(near[4:].astype(BF16), True).astype(F32)
    near = near[:2] + exchange(near[2:].astype(BF16), "wid", 2).astype(F32)
    total = near[0] + exchange(near[1].astype(BF16), "wid", 1).astype(F32)
    bit = 2
    while bit < lax.axis_size("dp"):
        total = total + exchange(total, "dp", bit)
        bit *= 2
    return total


def sum_everywhere(values):
    for axis in ("dp", "hid", "wid"):
        bit = 1
        while bit < lax.axis_size(axis):
            values = values + exchange(values, axis, bit)
            bit *= 2
    return values


def by_core(own, other, axis):
    second = second_core()
    return jnp.concatenate(
        [jnp.where(second, other, own), jnp.where(second, own, other)], axis=axis
    )


def half_of(values, axis, mine):
    half = values.shape[axis] // 2
    first = lax.slice_in_dim(values, 0, half, axis=axis)
    last = lax.slice_in_dim(values, half, 2 * half, axis=axis)
    second = second_core()
    return jnp.where(second, last, first) if mine else jnp.where(second, first, last)


def flip(values, axis, by):
    for bit in (1, 2):
        length = values.shape[axis]
        parts = [lax.slice_in_dim(values, i, i + 1, axis=axis) for i in range(length)]
        swapped = jnp.concatenate([parts[i ^ bit] for i in range(length)], axis=axis)
        values = jnp.where((by & bit) != 0, swapped, values)
    return values


def hid_turn(core_is_second):
    return core_is_second


def relative_hid(values, axis, second):
    values = flip(values, axis, lax.axis_index("hid"))
    parts = [lax.slice_in_dim(values, i, i + 1, axis=axis) for i in range(4)]
    swapped = jnp.concatenate([parts[0], parts[2], parts[1], parts[3]], axis=axis)
    return jnp.where(second, swapped, values)


def absolute_hid(values, axis, second):
    parts = [lax.slice_in_dim(values, i, i + 1, axis=axis) for i in range(4)]
    swapped = jnp.concatenate([parts[0], parts[2], parts[1], parts[3]], axis=axis)
    return flip(jnp.where(second, swapped, values), axis, lax.axis_index("hid"))


def gather_bias(bias):
    other = exchange(bias, "hid", 1)
    pair = jnp.stack([bias, other], axis=-2)
    both = jnp.concatenate([pair, exchange(pair, "hid", 2)], axis=-2)
    return flip(both, both.ndim - 2, lax.axis_index("hid"))


def hidden_order(bias):
    table = bias.reshape(4, 4, 2, -1)
    table = flip(table, 1, lax.axis_index("wid"))
    second = second_core()
    own = jnp.where(second, table[:, :, 1], table[:, :, 0])
    other = jnp.where(second, table[:, :, 0], table[:, :, 1])
    own = relative_hid(own, 0, second)
    other = relative_hid(other, 0, jnp.logical_not(second))
    return jnp.concatenate([own.reshape(-1), other.reshape(-1)])


def hidden_back(grads):
    table = grads.reshape(2, 4, 4, -1)
    second = second_core()
    own = absolute_hid(table[0], 0, second)
    other = absolute_hid(table[1], 0, jnp.logical_not(second))
    both = jnp.stack([jnp.where(second, other, own), jnp.where(second, own, other)], axis=2)
    return flip(both, 1, lax.axis_index("wid")).reshape(4, -1)


def gather_hidden(weights):
    near, far = gather_half(half_of(weights, 0, True))
    width = weights.shape[1]
    other_near, other_far = sibling(near), sibling(far)
    return jnp.concatenate([part.reshape(-1, width) for part in (near, far, other_near, other_far)])


def scatter_hidden(grads):
    rows = grads.shape[0] // 16
    pieces = grads.reshape(2, 8, rows, grads.shape[1])
    total = scatter_half(pieces[0], pieces[1])
    return by_core(total, sibling(total), 0)


def gather_attention(inweights, outweights):
    piece = half_of(jnp.concatenate([inweights, outweights[None]], axis=0), 2, True)
    near, far = gather_half(piece)
    second = second_core()

    def arrange(near, far, second):
        table = jnp.concatenate([near, far]).reshape((4, 4) + piece.shape)
        table = flip(table, 1, lax.axis_index("wid"))
        parts = [table[i : i + 1] for i in range(4)]
        swapped = jnp.concatenate([parts[0], parts[2], parts[1], parts[3]])
        table = jnp.where(second, swapped, table)
        return table.transpose(2, 0, 1, 3, 4).reshape(4, -1, piece.shape[2])

    own = arrange(near, far, second)
    other = arrange(sibling(near), sibling(far), jnp.logical_not(second))
    return by_core(own, other, 2)


def scatter_attention(grads):
    second = second_core()
    table = grads.reshape(4, 4, 4, -1, grads.shape[2]).transpose(1, 2, 0, 3, 4)
    parts = [table[i : i + 1] for i in range(4)]
    swapped = jnp.concatenate([parts[0], parts[2], parts[1], parts[3]])
    table = flip(jnp.where(second, swapped, table), 1, lax.axis_index("wid"))
    table = table.reshape((2, 8) + table.shape[2:])
    total = scatter_half(table[0], table[1])
    return by_core(total, sibling(total), 2)


def compact(values):
    slots = values.reshape(-1, PADDED, PADDED, values.shape[1])
    return slots[:, :GRID, :GRID].reshape(-1, values.shape[1])


def expand(values):
    slots = values.reshape(-1, GRID, GRID, values.shape[1])
    rest = PADDED - GRID
    return jnp.pad(slots, ((0, 0), (0, rest), (0, rest), (0, 0))).reshape(-1, values.shape[1])


def presence(sizes):
    cells = jnp.arange(GRID, dtype=jnp.int32)
    inside = (cells[None, :, None] < sizes[:, None, None]) & (
        cells[None, None, :] < sizes[:, None, None]
    )
    return inside.astype(F32).reshape(-1, 1)


def depthwise(values, kernel, bias):
    images = values.shape[0] // CELLS
    grid_cells = values.reshape(images, GRID, GRID, values.shape[1])
    padded = jnp.pad(grid_cells, ((0, 0), (1, 1), (1, 1), (0, 0)))
    total = jnp.zeros_like(grid_cells)
    for offset in range(9):
        across = offset // 3
        along = offset % 3
        total = total + padded[:, across : across + GRID, along : along + GRID, :] * kernel[offset]
    return total.reshape(values.shape) + bias


def conv_backward(grad_values, values, kernel, bias, present):
    pullback = jax.vjp(depthwise, values, kernel, bias)[1]
    grad_in, grad_kernel, grad_bias = pullback(grad_values * present)
    return (grad_values + grad_in, grad_kernel, grad_bias)


def image_heads(values):
    return values.reshape(values.shape[0] // CELLS, CELLS, values.shape[1] // HD, HD)


def outer(left, right):
    return lax.dot_general(left, right, (((0,), (0,)), ((), ())), preferred_element_type=F32)


def times(left, right):
    return jnp.dot(left, right, preferred_element_type=F32)


def times_transposed(left, right):
    return lax.dot_general(left, right, (((1,), (1,)), ((), ())), preferred_element_type=F32)


def norm_forward(values, norm_gain, bias_shift):
    center = jnp.mean(values, axis=1, keepdims=True)
    scaled = lax.rsqrt(jnp.mean(values * values, axis=1, keepdims=True) - center * center + EPSILON)
    normal = (values - center) * scaled
    return ((normal * norm_gain + bias_shift).astype(BF16), normal, scaled)


def norm_backward(grad_normed, normal, scaled, norm_gain):
    grad_normal = grad_normed * norm_gain
    first_mean = jnp.mean(grad_normal, axis=1, keepdims=True)
    second_mean = jnp.mean(grad_normal * normal, axis=1, keepdims=True)
    grad_in = scaled * (grad_normal - first_mean - normal * second_mean)
    return (grad_in, jnp.sum(grad_normed * normal, axis=0), jnp.sum(grad_normed, axis=0))


def window_scores(query_rows, key_rows, keep_mask):
    scores = jnp.einsum(
        "nqhd,nkhd->nhqk", image_heads(query_rows), image_heads(key_rows), preferred_element_type=F32
    )
    return jnp.where(keep_mask, scores * SCALE, -1000000000.0)


def window_mask(present):
    cell = jnp.arange(CELLS, dtype=jnp.int32)
    window = (cell // GRID // WINDOW) * 2 + cell % GRID // WINDOW
    same = window[:, None] == window[None, :]
    return same[None, None] & (present.reshape(-1, 1, 1, CELLS) > 0.5)


def window_forward(query_rows, key_rows, value_rows, present):
    scores = window_scores(query_rows, key_rows, window_mask(present))
    totals = jax.nn.logsumexp(scores, axis=-1, keepdims=True)
    weights = jnp.exp(scores - totals).astype(BF16)
    mixed = jnp.einsum("nhqk,nkhd->nqhd", weights, image_heads(value_rows), preferred_element_type=F32)
    return mixed.reshape(query_rows.shape).astype(BF16), totals


def window_backward(grad_mixed, query_rows, key_rows, value_rows, totals, present):
    keep_mask = window_mask(present)
    scores = window_scores(query_rows, key_rows, keep_mask)
    probabilities = jnp.exp(scores - totals)
    weights = probabilities.astype(BF16)
    incoming = image_heads(grad_mixed)
    grad_probs = jnp.einsum("nqhd,nkhd->nhqk", incoming, image_heads(value_rows), preferred_element_type=F32)
    grad_scores = probabilities * (
        grad_probs - jnp.sum(probabilities * grad_probs, axis=-1, keepdims=True)
    )
    grad_scores = jnp.where(keep_mask, grad_scores, 0.0).astype(BF16)
    grad_query = jnp.einsum("nhqk,nkhd->nqhd", grad_scores, image_heads(key_rows), preferred_element_type=F32)
    grad_keys = jnp.einsum("nhqk,nqhd->nkhd", grad_scores, image_heads(query_rows), preferred_element_type=F32)
    grad_values = jnp.einsum("nhqk,nqhd->nkhd", weights, incoming, preferred_element_type=F32)
    shape = query_rows.shape
    return (
        (grad_query * SCALE).reshape(shape),
        (grad_keys * SCALE).reshape(shape),
        grad_values.reshape(shape),
    )


def channel_forward(query_rows, key_rows, value_rows, present):
    keyset = image_heads(key_rows * present.astype(BF16))
    scores = jnp.einsum("nthi,nthj->nhij", keyset, image_heads(value_rows), preferred_element_type=F32)
    probabilities = jax.nn.softmax(scores * SCALE, axis=-1)
    mixed = jnp.einsum(
        "nhij,nthj->nthi", probabilities.astype(BF16), image_heads(query_rows), preferred_element_type=F32
    )
    return (mixed.reshape(query_rows.shape).astype(BF16), probabilities)


def channel_backward(grad_mixed, query_rows, key_rows, value_rows, probabilities, present):
    incoming = image_heads(grad_mixed)
    queries = image_heads(query_rows)
    keyset = image_heads(key_rows * present.astype(BF16))
    valueset = image_heads(value_rows)
    grad_probs = jnp.einsum("nthi,nthj->nhij", incoming, queries, preferred_element_type=F32)
    grad_query = jnp.einsum("nhij,nthi->nthj", probabilities.astype(BF16), incoming, preferred_element_type=F32)
    grad_scores = probabilities * (
        grad_probs - jnp.sum(probabilities * grad_probs, axis=-1, keepdims=True)
    )
    grad_scores = grad_scores.astype(BF16)
    grad_keys = jnp.einsum("nhij,nthj->nthi", grad_scores, valueset, preferred_element_type=F32)
    grad_values = jnp.einsum("nhij,nthi->nthj", grad_scores, keyset, preferred_element_type=F32)
    shape = query_rows.shape
    return (
        grad_query.reshape(shape),
        grad_keys.reshape(shape) * SCALE * present,
        grad_values.reshape(shape) * SCALE,
    )


def attention_forward(values, present, gain, shift, weights, biases, outbias, windowed):
    normed, normal, scaled = norm_forward(values, gain, shift)
    query_rows = (times_transposed(normed, weights[0]) + biases[0]).astype(BF16)
    key_part = times_transposed(normed, weights[1])
    if not windowed:
        key_part = key_part + biases[1]
    key_rows = key_part.astype(BF16)
    value_rows = (times_transposed(normed, weights[2]) + biases[-1]).astype(BF16)
    attend = window_forward if windowed else channel_forward
    mixed, stat = attend(query_rows, key_rows, value_rows, present)
    branch = times(mixed, weights[3]) + outbias
    return values + present * branch, (normed, normal, scaled, query_rows, key_rows, value_rows, stat, mixed)


def attention_backward(grad_values, saved, present, gain, weights, windowed):
    normed, normal, scaled, query_rows, key_rows, value_rows, stat, mixed = saved
    grad_branch = grad_values * present
    low_branch = grad_branch.astype(BF16)
    grad_mixed = times_transposed(low_branch, weights[3]).astype(BF16)
    attend = window_backward if windowed else channel_backward
    grads = attend(grad_mixed, query_rows, key_rows, value_rows, stat, present)
    rounded = [item.astype(BF16) for item in grads]
    sums = [jnp.sum(item, axis=0, dtype=F32) for item in rounded]
    stacked = jnp.concatenate(rounded, axis=1)
    grad_normed = times(stacked, weights[:3].reshape(-1, weights.shape[2]))
    left = jnp.concatenate([stacked, mixed], axis=1)
    other_left = sibling(left)
    normed_half = jnp.concatenate([half_of(normed, 1, True), sibling(half_of(normed, 1, False))])
    branch_half = jnp.concatenate([half_of(low_branch, 1, True), sibling(half_of(low_branch, 1, False))])
    left = jnp.concatenate([left, other_left])
    cut = stacked.shape[1]
    grad_weights = jnp.concatenate([outer(left[:, :cut], normed_half), outer(left[:, cut:], branch_half)])
    grad_weights = grad_weights.astype(BF16).reshape(4, -1, grad_weights.shape[1])
    grad_in, grad_gain, grad_shift = norm_backward(grad_normed.astype(BF16).astype(F32), normal, scaled, gain)
    little = [grad_gain, grad_shift, jnp.sum(grad_branch, axis=0)]
    biases = [sums[0], sums[2]] if windowed else sums
    return grad_values + grad_in, little, biases, grad_weights


def mlp_forward(values, present, gain, shift, upward, upbias, downward, downbias):
    normed, normal, scaled = norm_forward(values, gain, shift)
    hidden = times_transposed(normed, upward) + upbias
    acted = jax.nn.gelu(hidden, approximate=False).astype(BF16)
    branch = times(acted, downward) + downbias
    return values + present * branch, (normed, normal, scaled, hidden, acted)


def gelu_back(hidden, grad_acted):
    pullback = jax.vjp(partial(jax.nn.gelu, approximate=False), hidden)[1]
    return pullback(grad_acted)[0].astype(BF16)


def mlp_backward(grad_values, saved, present, gain, upward, downward):
    normed, normal, scaled, hidden, acted = saved
    grad_branch = grad_values * present
    low_branch = grad_branch.astype(BF16)
    half = acted.shape[1] // 2
    branches = jnp.concatenate([low_branch, sibling(low_branch)])
    grad_down = outer(jnp.concatenate([acted[:, :half], sibling(acted[:, half:])]), branches)
    grad_hidden = gelu_back(hidden, times_transposed(low_branch, downward))
    grad_upbias = jnp.sum(grad_hidden, axis=0, dtype=F32)
    both_hidden = jnp.concatenate([grad_hidden[:, :half], sibling(grad_hidden[:, half:])])
    grad_up = outer(both_hidden, jnp.concatenate([normed, sibling(normed)]))
    grad_normed = times(grad_hidden, upward).astype(BF16).astype(F32)
    grad_in, grad_gain, grad_shift = norm_backward(grad_normed, normal, scaled, gain)
    little = [grad_gain, grad_shift, jnp.sum(grad_branch, axis=0)]
    return grad_values + grad_in, little, grad_upbias, grad_up.astype(BF16), grad_down.astype(BF16)


def head_order(bias):
    return flip(bias, 1, lax.axis_index("hid")).reshape(bias.shape[0], -1)


def body(
    inputs, grid_sizes, cotangent,
    wkernel, wcbias, wgain, wshift, winw, winb, woutw, woutb,
    wgain_two, wshift_two, wupw, wupb, wdownw, wdownb,
    ckernel, ccbias, cgain, cshift, cinw, cinb, coutw, coutb,
    cgain_two, cshift_two, cupw, cupb, cdownw, cdownb,
):
    image_count = inputs.shape[0] // (PADDED * PADDED)
    place = (lax.axis_index("hid") * lax.axis_size("wid") + lax.axis_index("wid")) * image_count
    present = presence(lax.dynamic_slice_in_dim(grid_sizes, place, image_count, 0))
    attention_one = gather_attention(winw, woutw)
    up_two = gather_hidden(wupw)
    down_two = gather_hidden(wdownw)
    attention_three = gather_attention(cinw, coutw)
    up_four = gather_hidden(cupw)
    down_four = gather_hidden(cdownw)

    table = jnp.concatenate([winb, wupb.reshape(4, -1), cinb, cupb.reshape(4, -1)])
    table = gather_bias(table)
    winb = head_order(table[0:2])
    wupb = hidden_order(table[2:6].transpose(1, 0, 2).reshape(4, -1))
    cinb = head_order(table[6:9])
    cupb = hidden_order(table[9:13].transpose(1, 0, 2).reshape(4, -1))

    start = compact(inputs) * present
    after_conv = start + present * depthwise(start, wkernel, wcbias)
    after_attn, saved_one = attention_forward(
        after_conv, present, wgain, wshift, attention_one, winb, woutb, True
    )
    after_mlp, saved_two = mlp_forward(
        after_attn, present, wgain_two, wshift_two, up_two, wupb, down_two, wdownb
    )
    after_conv_c = after_mlp + present * depthwise(after_mlp, ckernel, ccbias)
    after_attn_c, saved_three = attention_forward(
        after_conv_c, present, cgain, cshift, attention_three, cinb, coutb, False
    )
    outputs, saved_four = mlp_forward(
        after_attn_c, present, cgain_two, cshift_two, up_four, cupb, down_four, cdownb
    )

    flowing, little_four, upb_four, gup_four, gdown_four = mlp_backward(
        compact(cotangent), saved_four, present, cgain_two, up_four, down_four
    )
    gdown_four = scatter_hidden(gdown_four)
    gup_four = scatter_hidden(gup_four)
    flowing, little_three, inb_three, gatt_three = attention_backward(
        flowing, saved_three, present, cgain, attention_three, False
    )
    gatt_three = scatter_attention(gatt_three)
    flowing, kernel_three, cbias_three = conv_backward(flowing, after_mlp, ckernel, ccbias, present)
    flowing, little_two, upb_two, gup_two, gdown_two = mlp_backward(
        flowing, saved_two, present, wgain_two, up_two, down_two
    )
    gdown_two = scatter_hidden(gdown_two)
    gup_two = scatter_hidden(gup_two)
    flowing, little_one, inb_one, gatt_one = attention_backward(
        flowing, saved_one, present, wgain, attention_one, True
    )
    gatt_one = scatter_attention(gatt_one)
    flowing, kernel_one, cbias_one = conv_backward(flowing, start, wkernel, wcbias, present)

    def bias_rows(sums):
        rows = jnp.stack(sums).reshape(len(sums), 4, -1)
        return flip(rows, 1, lax.axis_index("hid")).reshape(len(sums), -1)

    early = sum_everywhere(
        jnp.concatenate(
            [kernel_three, jnp.stack([cbias_three] + little_two + little_three + little_four),
             bias_rows(inb_three), hidden_back(upb_two), hidden_back(upb_four)]
        )
    )
    late = sum_everywhere(
        jnp.concatenate([kernel_one, jnp.stack([cbias_one] + little_one), bias_rows(inb_one)])
    )

    def own_hid(rows, axis):
        length = rows.shape[axis] // 4
        return lax.dynamic_slice_in_dim(rows, lax.axis_index("hid") * length, length, axis)

    return (
        expand(outputs), expand(flowing * present),
        late[0:9], late[9], late[10], late[11], gatt_one[:3], own_hid(late[13:15], 1), gatt_one[3], late[12],
        early[10], early[11], gup_two, own_hid(early[22:26], 0).reshape(-1), gdown_two, early[12],
        early[0:9], early[9], early[13], early[14], gatt_three[:3], own_hid(early[19:22], 1), gatt_three[3], early[15],
        early[16], early[17], gup_four, own_hid(early[26:30], 0).reshape(-1), gdown_four, early[18],
    )


def solution(mesh):
    tokens, everywhere = P(("dp", "hid", "wid"), None), P()
    stacked, rows = P(None, ("hid", "wid"), None), P(("hid", "wid"), None)
    block = (
        everywhere, everywhere, everywhere, everywhere, stacked, P(None, "hid"), rows, everywhere,
        everywhere, everywhere, rows, P("hid"), rows, everywhere,
    )
    return jax.shard_map(
        body,
        mesh=mesh,
        in_specs=(tokens, P("dp"), tokens) + block + block,
        out_specs=(tokens, tokens) + block + block,
        check_vma=False,
    )
```

time: 1990 us -> 890 us (0.45)
  waiting for transfers between devices: 1320 us -> 192 us
  blocking collectives: 104 us -> 0 us
  local copies, waits for them, and re-layouts: 174 us -> 252 us
  matrix products: 135 us -> 173 us
  starting transfers between devices: 51 us -> 77.7 us
    reduce_scatter x8 -> x0, waiting for transfers between devices: 1010 us -> none  [scatter_matrix(): lax.psum_scatter(both.astype(jnp.bfloat16), ('hid', 'wid'), scatter_dimen...]
    all_gather x6 -> x0, waiting for transfers between devices: 230 us -> none  [gather_matrix(): own = lax.all_gather(own_half(shard), ('hid', 'wid'), axis=axis, tiled=True)]
    ppermute x24 -> x92, waiting for transfers between devices: 20.7 us -> 192 us  [the longest x68 127 us: exchange(): return lax.ppermute(values, axis, pairs)]
    all_gather x6 -> x0, blocking collectives: 104 us -> none  [the longest x2 80.4 us: gather_matrix(): own = lax.all_gather(own_half(shard), ('hid', 'wid'), axis=axis, tiled=True)]
    sub x2 -> x1, other arithmetic: 59.3 us -> 1.09 us  [channel_forward(): probabilities = jax.nn.softmax(scores * SCALE, axis=-1)]
    psum x1 -> x0, waiting for transfers between devices: 55.1 us -> none  [body(): lax.psum((kernel_one, convbias_one, little_one[0], little_one[1], little_...]
    concatenate x10 -> x49, other arithmetic: 8.69 us -> 52.8 us  [the longest x1 11 us: attention_backward(): left = jnp.concatenate([left, other_left])]
    slice x6 -> x100, local copies, waits for them, and re-layouts: 0.13 us -> 39.4 us  [the longest x40 14 us: flip(): lax.slice_in_dim(values, i, i + 1, axis=axis)]
  transfers between devices with their start and end apart: 39 -> 92, of which waited for: 19 -> 27; matrix products, arithmetic and copies ran while one was open for 13% -> 66% of each run, Pallas kernels for 0% -> 0%
where the time goes in v2:
time: 890 us; the launch traced here: 875 us
  local copies, waits for them, and re-layouts  252 us (28%)
  waiting for transfers between devices  192 us (22%)
  other arithmetic  175 us (20%)
  matrix products  173 us (19%)
  starting transfers between devices  77.7 us (9%)
    ppermute x68, waiting for transfers between devices, exchange(): return lax.ppermute(values, axis, pairs)  127 us
    ppermute x24, waiting for transfers between devices, cross(): return lax.ppermute(values, ('dp', 'hid'), pairs)  64.7 us
    ppermute x68, starting transfers between devices, exchange(): return lax.ppermute(values, axis, pairs)  63 us
    dot_general x12, matrix products, times_transposed(): lax.dot_general(left, right, (((1,), (1,)), ((), ())), preferred_element_...  60.9 us
    dot_general x8, matrix products, times(): return jnp.dot(left, right, preferred_element_type=F32)  31.5 us
    unnamed x523, local copies, waits for them, and re-layouts  23.8 us
    select_n x32, other arithmetic, flip(): values = jnp.where(by & bit != 0, swapped, values)  22.4 us
    reshape x8, local copies, waits for them, and re-layouts, image_heads(): values.reshape(values.shape[0] // CELLS, CELLS, values.shape[1] // HD, HD)  21.7 us
  transfers between devices with their start and end apart: 92, of which 27 were waited for; matrix products, arithmetic and copies ran while one was open for 66% of the time, Pallas kernels for 0%

profile of v2, /device:TPU:1, one launch (start us, length us, event | category | flops | bytes accessed | tf_op | source)
XLA Modules:
  0.0 875.5 jit_solution(5911537281523189358)
XLA Ops:
  130.6 26.7 %collective-permute-done.21 = bf16[2,4,48,384]{3,2,1,0:T(8,128)(2,1)S(1)} collective-permute-done((bf16[2,4,48,384]{3,2,1,0:T(8,128)(2,1)S(1)}, bf16[2,4,48,384]{3,2,1,0:T(8,128)(2,1)S(1)}, u32[]{:S(2)}, u32[]{:S(2)}) %collective-permute-start.21) | collective-permute-done | bytes 294944 | tf_op jit(solution)/shard_map/ppermute | solution.py:21
  158.3 8.4 collective-permute-done.1
  168.1 8.1 collective-permute-done.9
  177.5 5.0 collective-permute-done.15
  183.8 5.0 collective-permute-done.27
  190.1 5.1 collective-permute-done.33
  206.9 10.6 %collective-permute-start.3 = (bf16[8,4,48,384]{3,2,1,0:T(8,128)(2,1)S(1)}, bf16[8,4,48,384]{3,2,1,0:T(8,128)(2,1)S(1)}, u32[]{:S(2)}, u32[]{:S(2)}) collective-permute-start(bf16[8,4,48,384]{3,2,1,0:T(8,128)(2,1)S(1)} %pad_maximum_fusion.12), channel_id=1, source_target_pairs={{0,16},{16,0},{1,17},{17,1},{2,18},{18,2},{3,19},{19,3},{4,20},{20... | collective-permute-start | bytes 3538952 | tf_op jit(solution)/shard_map/ppermute | solution.py:21
  224.8 6.5 collective-permute-start.12
  232.8 7.2 collective-permute-done.4
  285.6 4.9 fusion.81
  301.9 15.7 %multiply_convert_fusion.1 = (bf16[288,3072]{1,0:T(8,128)(2,1)S(1)}, f32[288,3072]{1,0:T(8,128)}, f32[288,3072]{1,0:T(8,128)}) fusion(f32[3072]{0:T(1024)S(1)} %copy-done.216, bf16[288,768]{1,0:T(8,128)(2,1)S(1)} %add_convert_fusion.6, bf16[768,768]{1,0:T(8,128)(2,1)} %bitcast.19, bf16[768,768]{1,0:T(8,128)(2,1)} %bitcast.18, ...), kind=kOutput, calls=%fused_computation.64 | convolution fusion | flops 1436221440 | bytes 14020608 | tf_op jit(solution)/shard_map/dot_general | solution.py:231
  327.2 7.6 multiply_add_fusion
  380.2 15.7 %multiply_convert_fusion = (bf16[288,3072]{1,0:T(8,128)(2,1)}, f32[288,3072]{1,0:T(8,128)S(1)}, f32[288,3072]{1,0:T(8,128)S(1)}) fusion(f32[3072]{0:T(1024)S(1)} %copy-done.215, bf16[288,768]{1,0:T(8,128)(2,1)} %add_convert_fusion.4, bf16[768,768]{1,0:T(8,128)(2,1)} %bitcast.63, bf16[768,768]{1,0:T(8,128)(2,1)} %bitcast.62, bf16[768,768]{1,0:T(8,128)(2,1)} %bitcast.61, ...), kind=kOutput, calls=%fused_computation.51 | convolution fusion | flops 1436221440 | bytes 14020608 | tf_op jit(solution)/shard_map/dot_general | solution.py:231
  399.3 7.5 convert_reduce_fusion
  458.1 9.1 %convert_reduce_fusion.1 = (f32[3072]{0:T(1024)S(1)}, bf16[288,3072]{1,0:T(8,128)(2,1)S(1)}) fusion(f32[288,3072]{1,0:T(8,128)} %get-tuple-element.139, f32[288,3072]{1,0:T(8,128)} %get-tuple-element.464, bf16[288,768]{1,0:T(8,128)(2,1)} %get-tuple-element.129, bf16[768,768]{1,0:T(8,128)(2,1)S(1)} %bitcast.448, bf16[768,768]{1,0:T(8,128)(2,1)} %bitcast.44, ...), kind=kOutput, calls=%fused_computation.46 | convolution fusion | flops 1391981568 | bytes 14020608 | tf_op jit(solution)/shard_map/dot_general | solution.py:231
  467.2 5.3 fusion.163
  479.1 5.4 fusion.180
  484.5 14.2 %convert_reduce_fusion.6 = (f32[24,32]{1,0:T(8,128)S(1)}, bf16[2,24,32,144]{3,2,1,0:T(8,128)(2,1)}) fusion(f32[2,24,144,144]{2,3,1,0:T(8,128)} %fusion.180, f32[2,24,144,144]{2,3,1,0:T(8,128)} %copy-done.11, f32[2,24,144]{2,1,0:T(8,128)S(1)} %copy-done.130, pred[2,144,144]{1,2,0:T(8,128)(4,1)S(1)} %copy-done.106, bf16[2,144,24,32]{1,0,3,2:T(2,128)(2,1)} %reshape.2229), kind=kOutput, calls=%fused_computation.155 | convolution fusion | flops 75540624 | bytes 8919552 | tf_op jit(solution)/shard_map/nhqk,nkhd->nqhd/dot_general | solution.py:282
  498.7 14.5 %fusion.82 = bf16[2,144,24,32]{1,3,2,0:T(8,128)(2,1)} fusion(f32[2,24,144,144]{2,3,1,0:T(8,128)} %fusion.180, f32[2,24,144,144]{2,3,1,0:T(8,128)} %copy-done.11, f32[2,24,144]{2,1,0:T(8,128)S(1)} %copy-done.130, pred[2,144,144]{1,2,0:T(8,128)(4,1)S(1)} %copy-done.106, bf16[2,144,24,32]{1,0,3,2:T(2,128)(2,1)} %reshape.2228), kind=kOutput, calls=%fused_computation.211 | convolution fusion | flops 75099024 | bytes 8916480 | tf_op jit(solution)/shard_map/nhqk,nqhd->nkhd/dot_general | solution.py:283
  513.2 6.1 convert_reduce_fusion.5
  564.5 4.8 fusion.164
  573.9 5.8 multiply_reduce_fusion.18
  591.6 5.4 fusion.86
  614.1 7.0 concatenate.836
  689.5 11.0 %pad_maximum_fusion.4 = bf16[576,3072]{0,1:T(8,128)(2,1)S(1)} fusion(bf16[288,3072]{0,1:T(8,128)(2,1)S(1)} %copy.456, bf16[288,768]{0,1:T(8,128)(2,1)S(1)} %copy-done.21, bf16[288,768]{0,1:T(8,128)(2,1)} %copy-done.56, bf16[288,768]{0,1:T(8,128)(2,1)} %copy-done.58, bf16[288,768]{0,1:T(8,128)(2,1)S(1)} %copy-done.55), kind=kLoop, calls=%fused_computation.37 | loop fusion | flops 17694720 | bytes 7077888 | tf_op jit(solution)/shard_map/concatenate | solution.py:353
  737.4 5.7 collective-permute-done.80
  746.4 20.3 %collective-permute-done.58 = bf16[8,96,768]{2,1,0:T(8,128)(2,1)S(1)} collective-permute-done((bf16[8,96,768]{2,1,0:T(8,128)(2,1)}, bf16[8,96,768]{2,1,0:T(8,128)(2,1)S(1)}, u32[]{:S(2)}, u32[]{:S(2)}) %collective-permute-start.58) | collective-permute-done | bytes 1179680 | tf_op jit(solution)/shard_map/ppermute | solution.py:34
  769.0 13.1 %collective-permute-done.81 = bf16[4,96,768]{2,1,0:T(8,128)(2,1)S(1)} collective-permute-done((bf16[4,96,768]{2,1,0:T(8,128)(2,1)S(1)}, bf16[4,96,768]{2,1,0:T(8,128)(2,1)S(1)}, u32[]{:S(2)}, u32[]{:S(2)}) %collective-permute-start.81) | collective-permute-done | bytes 589856 | tf_op jit(solution)/shard_map/ppermute | solution.py:34
  782.3 12.5 %collective-permute-done.59 = bf16[4,96,768]{2,1,0:T(8,128)(2,1)S(1)} collective-permute-done((bf16[4,96,768]{2,1,0:T(8,128)(2,1)S(1)}, bf16[4,96,768]{2,1,0:T(8,128)(2,1)S(1)}, u32[]{:S(2)}, u32[]{:S(2)}) %collective-permute-start.59) | collective-permute-done | bytes 589856 | tf_op jit(solution)/shard_map/ppermute | solution.py:34
  797.6 18.6 %collective-permute-done.82 = bf16[2,96,768]{2,1,0:T(8,128)(2,1)S(1)} collective-permute-done((bf16[2,96,768]{2,1,0:T(8,128)(2,1)S(1)}, bf16[2,96,768]{2,1,0:T(8,128)(2,1)S(1)}, u32[]{:S(2)}, u32[]{:S(2)}) %collective-permute-start.82) | collective-permute-done | bytes 294944 | tf_op jit(solution)/shard_map/ppermute | solution.py:21
  839.3 19.4 %collective-permute-done.75 = bf16[2,4,48,384]{3,2,1,0:T(8,128)(2,1)S(1)} collective-permute-done((bf16[2,4,48,384]{3,2,1,0:T(8,128)(2,1)S(1)}, bf16[2,4,48,384]{3,2,1,0:T(8,128)(2,1)S(1)}, u32[]{:S(2)}, u32[]{:S(2)}) %collective-permute-start.75) | collective-permute-done | bytes 294944 | tf_op jit(solution)/shard_map/ppermute | solution.py:21
  858.9 6.2 collective-permute-done.48
  (1212 shorter events, 551.3 us)
Async XLA Ops:
  2.4 113.7 %collective-permute-start.20 = (bf16[1,4,48,384]{3,2,1,0:T(8,128)(2,1)}, bf16[1,4,48,384]{3,2,1,0:T(8,128)(2,1)}, u32[]{:S(2)}, u32[]{:S(2)}) collective-permute-start(bf16[1,4,48,384]{3,2,1,0:T(8,128)(2,1)} %get-tuple-element.136), channel_id=1, source_target_pairs={{0,1},{1,0},{2,3},{3,2},{4,5},{5,4},{6,7},{7,6},{8,9},{9,8},{10,11... | collective-permute-start | bytes 442376 | tf_op jit(solution)/shard_map/ppermute | solution.py:21
  6.2 111.0 %collective-permute-start = (bf16[1,4,48,384]{3,2,1,0:T(8,128)(2,1)}, bf16[1,4,48,384]{3,2,1,0:T(8,128)(2,1)}, u32[]{:S(2)}, u32[]{:S(2)}) collective-permute-start(bf16[1,4,48,384]{3,2,1,0:T(8,128)(2,1)} %get-tuple-element.143), channel_id=1, source_target_pairs={{0,1},{1,0},{2,3},{3,2},{4,5},{5,4},{6,7},{7,6},{8,9},{9,8},{10,11... | collective-permute-start | bytes 442376 | tf_op jit(solution)/shard_map/ppermute | solution.py:21
  9.1 36.6 %collective-permute-start.6 = (f32[13,192]{1,0:T(8,128)}, f32[13,192]{1,0:T(8,128)}, u32[]{:S(2)}, u32[]{:S(2)}) collective-permute-start(f32[13,192]{1,0:T(8,128)} %get-tuple-element.328), channel_id=1, source_target_pairs={{0,4},{4,0},{8,12},{12,8},{1,5},{5,1},{9,13},{13,9},{2,6},{6,2},{1... | collective-permute-start | bytes 29960 | tf_op jit(solution)/shard_map/ppermute | solution.py:21
  12.1 108.5 %collective-permute-start.8 = (bf16[1,96,768]{2,1,0:T(8,128)(2,1)}, bf16[1,96,768]{2,1,0:T(8,128)(2,1)}, u32[]{:S(2)}, u32[]{:S(2)}) collective-permute-start(bf16[1,96,768]{2,1,0:T(8,128)(2,1)} %select_bitcast_fusion.3), channel_id=1, source_target_pairs={{0,1},{1,0},{2,3},{3,2},{4,5},{5,4},{6,7},{7,6},{8,9},{9,8},{10,11... | collective-permute-start | bytes 442376 | tf_op jit(solution)/shard_map/ppermute | solution.py:21
  15.1 106.7 %collective-permute-start.14 = (bf16[1,96,768]{2,1,0:T(8,128)(2,1)}, bf16[1,96,768]{2,1,0:T(8,128)(2,1)}, u32[]{:S(2)}, u32[]{:S(2)}) collective-permute-start(bf16[1,96,768]{2,1,0:T(8,128)(2,1)} %select_bitcast_fusion.2), channel_id=1, source_target_pairs={{0,1},{1,0},{2,3},{3,2},{4,5},{5,4},{6,7},{7,6},{8,9},{9,8},{10,11... | collective-permute-start | bytes 442376 | tf_op jit(solution)/shard_map/ppermute | solution.py:21
  57.1 68.2 %collective-permute-start.26 = (bf16[1,96,768]{2,1,0:T(8,128)(2,1)S(1)}, bf16[1,96,768]{2,1,0:T(8,128)(2,1)}, u32[]{:S(2)}, u32[]{:S(2)}) collective-permute-start(bf16[1,96,768]{2,1,0:T(8,128)(2,1)S(1)} %select_bitcast_fusion.1), channel_id=1, source_target_pairs={{0,1},{1,0},{2,3},{3,2},{4,5},{5,4},{6,7},{7,6},{8,9},{9,8},{10,11... | collective-permute-start | bytes 442376 | tf_op jit(solution)/shard_map/ppermute | solution.py:21
  117.3 40.0 %collective-permute-start.21 = (bf16[2,4,48,384]{3,2,1,0:T(8,128)(2,1)S(1)}, bf16[2,4,48,384]{3,2,1,0:T(8,128)(2,1)S(1)}, u32[]{:S(2)}, u32[]{:S(2)}) collective-permute-start(bf16[2,4,48,384]{3,2,1,0:T(8,128)(2,1)S(1)} %pad_maximum_fusion.45), channel_id=1, source_target_pairs={{0,2},{1,3},{2,0},{3,1},{4,6},{5,7},{6,4},{7,5},{8,10},{9,11},{10,... | collective-permute-start | bytes 884744 | tf_op jit(solution)/shard_map/ppermute | solution.py:21
  120.7 46.0 %collective-permute-start.1 = (bf16[2,4,48,384]{3,2,1,0:T(8,128)(2,1)S(1)}, bf16[2,4,48,384]{3,2,1,0:T(8,128)(2,1)S(1)}, u32[]{:S(2)}, u32[]{:S(2)}) collective-permute-start(bf16[2,4,48,384]{3,2,1,0:T(8,128)(2,1)S(1)} %pad_maximum_fusion.42), channel_id=1, source_target_pairs={{0,2},{1,3},{2,0},{3,1},{4,6},{5,7},{6,4},{7,5},{8,10},{9,11},{10,... | collective-permute-start | bytes 884744 | tf_op jit(solution)/shard_map/ppermute | solution.py:21
  121.8 54.4 %collective-permute-start.9 = (bf16[2,96,768]{2,1,0:T(8,128)(2,1)S(1)}, bf16[2,96,768]{2,1,0:T(8,128)(2,1)S(1)}, u32[]{:S(2)}, u32[]{:S(2)}) collective-permute-start(bf16[2,96,768]{2,1,0:T(8,128)(2,1)S(1)} %pad_maximum_fusion.43), channel_id=1, source_target_pairs={{0,2},{1,3},{2,0},{3,1},{4,6},{5,7},{6,4},{7,5},{8,10},{9,11},{10,... | collective-permute-start | bytes 884744 | tf_op jit(solution)/shard_map/ppermute | solution.py:21
  125.2 57.3 %collective-permute-start.15 = (bf16[2,96,768]{2,1,0:T(8,128)(2,1)S(1)}, bf16[2,96,768]{2,1,0:T(8,128)(2,1)S(1)}, u32[]{:S(2)}, u32[]{:S(2)}) collective-permute-start(bf16[2,96,768]{2,1,0:T(8,128)(2,1)S(1)} %pad_maximum_fusion.44), channel_id=1, source_target_pairs={{0,2},{1,3},{2,0},{3,1},{4,6},{5,7},{6,4},{7,5},{8,10},{9,11},{10,... | collective-permute-start | bytes 884744 | tf_op jit(solution)/shard_map/ppermute | solution.py:21
  126.3 62.5 %collective-permute-start.27 = (bf16[2,96,768]{2,1,0:T(8,128)(2,1)S(1)}, bf16[2,96,768]{2,1,0:T(8,128)(2,1)S(1)}, u32[]{:S(2)}, u32[]{:S(2)}) collective-permute-start(bf16[2,96,768]{2,1,0:T(8,128)(2,1)S(1)} %pad_maximum_fusion.46), channel_id=1, source_target_pairs={{0,2},{1,3},{2,0},{3,1},{4,6},{5,7},{6,4},{7,5},{8,10},{9,11},{10,... | collective-permute-start | bytes 884744 | tf_op jit(solution)/shard_map/ppermute | solution.py:21
  157.2 37.9 %collective-permute-start.33 = (bf16[2,96,768]{2,1,0:T(8,128)(2,1)S(1)}, bf16[2,96,768]{2,1,0:T(8,128)(2,1)S(1)}, u32[]{:S(2)}, u32[]{:S(2)}) collective-permute-start(bf16[2,96,768]{2,1,0:T(8,128)(2,1)S(1)} %pad_maximum_fusion.47), channel_id=1, source_target_pairs={{0,2},{1,3},{2,0},{3,1},{4,6},{5,7},{6,4},{7,5},{8,10},{9,11},{10,... | collective-permute-start | bytes 884744 | tf_op jit(solution)/shard_map/ppermute | solution.py:21
  199.5 52.4 %collective-permute-start.23 = (bf16[8,4,48,384]{3,2,1,0:T(8,128)(2,1)S(1)}, bf16[8,4,48,384]{3,2,1,0:T(8,128)(2,1)S(1)}, u32[]{:S(2)}, u32[]{:S(2)}) collective-permute-start(bf16[8,4,48,384]{3,2,1,0:T(8,128)(2,1)S(1)} %pad_maximum_fusion.15), channel_id=1, source_target_pairs={{0,16},{16,0},{1,17},{17,1},{2,18},{18,2},{3,19},{19,3},{4,20},{20... | collective-permute-start | bytes 3538952 | tf_op jit(solution)/shard_map/ppermute | solution.py:21
  204.8 35.2 %collective-permute-start.4 = (bf16[8,4,48,384]{3,2,1,0:T(8,128)(2,1)S(1)}, bf16[8,4,48,384]{3,2,1,0:T(8,128)(2,1)S(1)}, u32[]{:S(2)}, u32[]{:S(2)}) collective-permute-start(bf16[8,4,48,384]{3,2,1,0:T(8,128)(2,1)S(1)} %pad_maximum_fusion.12), channel_id=1, source_target_pairs={{0,8},{4,12},{8,0},{12,4},{16,20},{20,16},{24,28},{28,24},{1,9},{5... | collective-permute-start | bytes 3538952 | tf_op jit(solution)/shard_map/ppermute | solution.py:34
  206.9 39.6 %collective-permute-start.3 = (bf16[8,4,48,384]{3,2,1,0:T(8,128)(2,1)S(1)}, bf16[8,4,48,384]{3,2,1,0:T(8,128)(2,1)S(1)}, u32[]{:S(2)}, u32[]{:S(2)}) collective-permute-start(bf16[8,4,48,384]{3,2,1,0:T(8,128)(2,1)S(1)} %pad_maximum_fusion.12), channel_id=1, source_target_pairs={{0,16},{16,0},{1,17},{17,1},{2,18},{18,2},{3,19},{19,3},{4,20},{20... | collective-permute-start | bytes 3538952 | tf_op jit(solution)/shard_map/ppermute | solution.py:21
  224.8 75.9 %collective-permute-start.12 = (bf16[8,96,768]{2,1,0:T(8,128)(2,1)}, bf16[8,96,768]{2,1,0:T(8,128)(2,1)}, u32[]{:S(2)}, u32[]{:S(2)}) collective-permute-start(bf16[8,96,768]{2,1,0:T(8,128)(2,1)} %pad_maximum_fusion.13), channel_id=1, source_target_pairs={{0,16},{16,0},{1,17},{17,1},{2,18},{18,2},{3,19},{19,3},{4,20},{20... | collective-permute-start | bytes 3538952 | tf_op jit(solution)/shard_map/ppermute | solution.py:21
  246.5 54.3 %collective-permute-start.17 = (bf16[8,96,768]{2,1,0:T(8,128)(2,1)}, bf16[8,96,768]{2,1,0:T(8,128)(2,1)}, u32[]{:S(2)}, u32[]{:S(2)}) collective-permute-start(bf16[8,96,768]{2,1,0:T(8,128)(2,1)} %pad_maximum_fusion.14), channel_id=1, source_target_pairs={{0,8},{4,12},{8,0},{12,4},{16,20},{20,16},{24,28},{28,24},{1,9},{5... | collective-permute-start | bytes 3538952 | tf_op jit(solution)/shard_map/ppermute | solution.py:34
  251.9 68.5 %collective-permute-start.18 = (bf16[8,96,768]{2,1,0:T(8,128)(2,1)}, bf16[8,96,768]{2,1,0:T(8,128)(2,1)}, u32[]{:S(2)}, u32[]{:S(2)}) collective-permute-start(bf16[8,96,768]{2,1,0:T(8,128)(2,1)} %pad_maximum_fusion.14), channel_id=1, source_target_pairs={{0,16},{16,0},{1,17},{17,1},{2,18},{18,2},{3,19},{19,3},{4,20},{20... | collective-permute-start | bytes 3538952 | tf_op jit(solution)/shard_map/ppermute | solution.py:21
  252.6 67.8 %collective-permute-start.29 = (bf16[8,96,768]{2,1,0:T(8,128)(2,1)}, bf16[8,96,768]{2,1,0:T(8,128)(2,1)}, u32[]{:S(2)}, u32[]{:S(2)}) collective-permute-start(bf16[8,96,768]{2,1,0:T(8,128)(2,1)} %pad_maximum_fusion.16), channel_id=1, source_target_pairs={{0,8},{4,12},{8,0},{12,4},{16,20},{20,16},{24,28},{28,24},{1,9},{5... | collective-permute-start | bytes 3538952 | tf_op jit(solution)/shard_map/ppermute | solution.py:34
  253.4 48.0 %collective-permute-start.13 = (bf16[8,96,768]{2,1,0:T(8,128)(2,1)}, bf16[8,96,768]{2,1,0:T(8,128)(2,1)}, u32[]{:S(2)}, u32[]{:S(2)}) collective-permute-start(bf16[8,96,768]{2,1,0:T(8,128)(2,1)} %collective-permute-done.11), channel_id=1, source_target_pairs={{0,16},{16,0},{1,17},{17,1},{2,18},{18,2},{3,19},{19,3},{4,20},{20... | collective-permute-start | bytes 3538952 | tf_op jit(solution)/shard_map/ppermute | solution.py:21
  300.7 79.5 %collective-permute-start.30 = (bf16[8,96,768]{2,1,0:T(8,128)(2,1)}, bf16[8,96,768]{2,1,0:T(8,128)(2,1)}, u32[]{:S(2)}, u32[]{:S(2)}) collective-permute-start(bf16[8,96,768]{2,1,0:T(8,128)(2,1)} %pad_maximum_fusion.16), channel_id=1, source_target_pairs={{0,16},{16,0},{1,17},{17,1},{2,18},{18,2},{3,19},{19,3},{4,20},{20... | collective-permute-start | bytes 3538952 | tf_op jit(solution)/shard_map/ppermute | solution.py:21
  320.3 78.9 %collective-permute-start.36 = (bf16[8,96,768]{2,1,0:T(8,128)(2,1)}, bf16[8,96,768]{2,1,0:T(8,128)(2,1)}, u32[]{:S(2)}, u32[]{:S(2)}) collective-permute-start(bf16[8,96,768]{2,1,0:T(8,128)(2,1)} %pad_maximum_fusion.17), channel_id=1, source_target_pairs={{0,16},{16,0},{1,17},{17,1},{2,18},{18,2},{3,19},{19,3},{4,20},{20... | collective-permute-start | bytes 3538952 | tf_op jit(solution)/shard_map/ppermute | solution.py:21
  320.5 59.7 %collective-permute-start.31 = (bf16[8,96,768]{2,1,0:T(8,128)(2,1)}, bf16[8,96,768]{2,1,0:T(8,128)(2,1)}, u32[]{:S(2)}, u32[]{:S(2)}) collective-permute-start(bf16[8,96,768]{2,1,0:T(8,128)(2,1)} %collective-permute-done.29), channel_id=1, source_target_pairs={{0,16},{16,0},{1,17},{17,1},{2,18},{18,2},{3,19},{19,3},{4,20},{20... | collective-permute-start | bytes 3538952 | tf_op jit(solution)/shard_map/ppermute | solution.py:21
  320.8 78.4 %collective-permute-start.37 = (bf16[8,96,768]{2,1,0:T(8,128)(2,1)}, bf16[8,96,768]{2,1,0:T(8,128)(2,1)}, u32[]{:S(2)}, u32[]{:S(2)}) collective-permute-start(bf16[8,96,768]{2,1,0:T(8,128)(2,1)} %collective-permute-done.35), channel_id=1, source_target_pairs={{0,16},{16,0},{1,17},{17,1},{2,18},{18,2},{3,19},{19,3},{4,20},{20... | collective-permute-start | bytes 3538952 | tf_op jit(solution)/shard_map/ppermute | solution.py:21
  376.7 284.9 %collective-permute-start.86 = (bf16[288,768]{1,0:T(8,128)(2,1)}, bf16[288,768]{1,0:T(8,128)(2,1)}, u32[]{:S(2)}, u32[]{:S(2)}) collective-permute-start(bf16[288,768]{1,0:T(8,128)(2,1)} %get-tuple-element.452), channel_id=1, source_target_pairs={{0,16},{16,0},{1,17},{17,1},{2,18},{18,2},{3,19},{19,3},{4,20},{20... | collective-permute-start | bytes 1327112 | tf_op jit(solution)/shard_map/ppermute | solution.py:21
  457.9 210.6 %collective-permute-start.64 = (bf16[288,768]{1,0:T(8,128)(2,1)}, bf16[288,768]{1,0:T(8,128)(2,1)}, u32[]{:S(2)}, u32[]{:S(2)}) collective-permute-start(bf16[288,768]{1,0:T(8,128)(2,1)} %get-tuple-element.129), channel_id=1, source_target_pairs={{0,16},{16,0},{1,17},{17,1},{2,18},{18,2},{3,19},{19,3},{4,20},{20... | collective-permute-start | bytes 1327112 | tf_op jit(solution)/shard_map/ppermute | solution.py:21
  542.3 121.8 %collective-permute-start.85 = (bf16[288,1536]{1,0:T(8,128)(2,1)}, bf16[288,1536]{1,0:T(8,128)(2,1)}, u32[]{:S(2)}, u32[]{:S(2)}) collective-permute-start(bf16[288,1536]{1,0:T(8,128)(2,1)} %get-tuple-element.219), channel_id=1, source_target_pairs={{0,16},{16,0},{1,17},{17,1},{2,18},{18,2},{3,19},{19,3},{4,20},{20... | collective-permute-start | bytes 2654216 | tf_op jit(solution)/shard_map/ppermute | solution.py:21
  672.4 45.5 %collective-permute-start.44 = (bf16[288,384]{1,0:T(8,128)(2,1)}, bf16[288,384]{1,0:T(8,128)(2,1)}, u32[]{:S(2)}, u32[]{:S(2)}) collective-permute-start(bf16[288,384]{1,0:T(8,128)(2,1)} %get-tuple-element.265), channel_id=1, source_target_pairs={{0,16},{16,0},{1,17},{17,1},{2,18},{18,2},{3,19},{19,3},{4,20},{20... | collective-permute-start | bytes 663560 | tf_op jit(solution)/shard_map/ppermute | solution.py:21
  686.5 35.6 %collective-permute-start.45 = (bf16[288,384]{1,0:T(8,128)(2,1)}, bf16[288,384]{1,0:T(8,128)(2,1)}, u32[]{:S(2)}, u32[]{:S(2)}) collective-permute-start(bf16[288,384]{1,0:T(8,128)(2,1)} %get-tuple-element.267), channel_id=1, source_target_pairs={{0,16},{16,0},{1,17},{17,1},{2,18},{18,2},{3,19},{19,3},{4,20},{20... | collective-permute-start | bytes 663560 | tf_op jit(solution)/shard_map/ppermute | solution.py:21
  718.0 48.7 %collective-permute-start.58 = (bf16[8,96,768]{2,1,0:T(8,128)(2,1)}, bf16[8,96,768]{2,1,0:T(8,128)(2,1)S(1)}, u32[]{:S(2)}, u32[]{:S(2)}) collective-permute-start(bf16[8,96,768]{2,1,0:T(8,128)(2,1)} %bitcast.420), channel_id=1, source_target_pairs={{0,8},{4,12},{8,0},{12,4},{16,20},{20,16},{24,28},{28,24},{1,9},{5... | collective-permute-start | bytes 3538952 | tf_op jit(solution)/shard_map/ppermute | solution.py:34
  730.5 85.9 %collective-permute-start.73 = (bf16[8,4,48,384]{3,2,1,0:T(8,128)(2,1)S(1)}, bf16[8,4,48,384]{3,2,1,0:T(8,128)(2,1)S(1)}, u32[]{:S(2)}, u32[]{:S(2)}) collective-permute-start(bf16[8,4,48,384]{3,2,1,0:T(8,128)(2,1)S(1)} %bitcast.419), channel_id=1, source_target_pairs={{0,8},{4,12},{8,0},{12,4},{16,20},{20,16},{24,28},{28,24},{1,9},{5... | collective-permute-start | bytes 3538952 | tf_op jit(solution)/shard_map/ppermute | solution.py:34
  732.0 92.0 %collective-permute-start.46 = (bf16[8,4,48,384]{3,2,1,0:T(8,128)(2,1)S(1)}, bf16[8,4,48,384]{3,2,1,0:T(8,128)(2,1)S(1)}, u32[]{:S(2)}, u32[]{:S(2)}) collective-permute-start(bf16[8,4,48,384]{3,2,1,0:T(8,128)(2,1)S(1)} %bitcast.418), channel_id=1, source_target_pairs={{0,8},{4,12},{8,0},{12,4},{16,20},{20,16},{24,28},{28,24},{1,9},{5... | collective-permute-start | bytes 3538952 | tf_op jit(solution)/shard_map/ppermute | solution.py:34
  (315 other events, 2696.8 us)

commit v3 on v2

v3 whole, which is shorter than its diff:
```python
from functools import partial

import jax
import jax.numpy as jnp
from jax import lax
from jax.experimental import pallas as pl
from jax.experimental.pallas import tpu as pltpu
from jax.sharding import PartitionSpec as P

HD = 32
WINDOW = 7
PADDED = 14
GRID = 12
CELLS = GRID * GRID
EPSILON = 1e-05
F32 = jnp.float32
BF16 = jnp.bfloat16
SCALE = HD ** (-0.5)


def exchange(values, axis, bit):
    pairs = [(index, index ^ bit) for index in range(lax.axis_size(axis))]
    return lax.ppermute(values, axis, pairs)


def sibling(values):
    return exchange(values, "dp", 1)


def cross(values, first):
    hids = lax.axis_size("hid")
    pairs = []
    for core in range(lax.axis_size("dp")):
        bit = 1 if (core % 2 == 0) == first else 2
        pairs += [(core * hids + index, core * hids + (index ^ bit)) for index in range(hids)]
    return lax.ppermute(values, ("dp", "hid"), pairs)


def second_core():
    return lax.rem(lax.axis_index("dp"), 2) == 1


def sum_everywhere(values):
    for axis in ("dp", "hid", "wid"):
        bit = 1
        while bit < lax.axis_size(axis):
            values = values + exchange(values, axis, bit)
            bit *= 2
    return values


def by_core(own, other, axis):
    second = second_core()
    return jnp.concatenate(
        [jnp.where(second, other, own), jnp.where(second, own, other)], axis=axis
    )


def half_of(values, axis, mine):
    half = values.shape[axis] // 2
    first = lax.slice_in_dim(values, 0, half, axis=axis)
    last = lax.slice_in_dim(values, half, 2 * half, axis=axis)
    second = second_core()
    return jnp.where(second, last, first) if mine else jnp.where(second, first, last)


def flip(values, axis, by):
    for bit in (1, 2):
        length = values.shape[axis]
        parts = [lax.slice_in_dim(values, i, i + 1, axis=axis) for i in range(length)]
        swapped = jnp.concatenate([parts[i ^ bit] for i in range(length)], axis=axis)
        values = jnp.where((by & bit) != 0, swapped, values)
    return values


def relative_hid(values, axis, second):
    values = flip(values, axis, lax.axis_index("hid"))
    parts = [lax.slice_in_dim(values, i, i + 1, axis=axis) for i in range(4)]
    swapped = jnp.concatenate([parts[0], parts[2], parts[1], parts[3]], axis=axis)
    return jnp.where(second, swapped, values)


def absolute_hid(values, axis, second):
    parts = [lax.slice_in_dim(values, i, i + 1, axis=axis) for i in range(4)]
    swapped = jnp.concatenate([parts[0], parts[2], parts[1], parts[3]], axis=axis)
    return flip(jnp.where(second, swapped, values), axis, lax.axis_index("hid"))


def gather_bias(bias):
    other = exchange(bias, "hid", 1)
    pair = jnp.stack([bias, other], axis=-2)
    both = jnp.concatenate([pair, exchange(pair, "hid", 2)], axis=-2)
    return flip(both, both.ndim - 2, lax.axis_index("hid"))


def hidden_order(bias):
    table = bias.reshape(4, 4, 2, -1)
    table = flip(table, 1, lax.axis_index("wid"))
    second = second_core()
    own = jnp.where(second, table[:, :, 1], table[:, :, 0])
    other = jnp.where(second, table[:, :, 0], table[:, :, 1])
    own = relative_hid(own, 0, second)
    other = relative_hid(other, 0, jnp.logical_not(second))
    return jnp.concatenate([own.reshape(-1), other.reshape(-1)])


def hidden_back(grads):
    table = grads.reshape(2, 4, 4, -1)
    second = second_core()
    own = absolute_hid(table[0], 0, second)
    other = absolute_hid(table[1], 0, jnp.logical_not(second))
    both = jnp.stack([jnp.where(second, other, own), jnp.where(second, own, other)], axis=2)
    return flip(both, 1, lax.axis_index("wid")).reshape(4, -1)


VMEM_LIMIT = 56 * 1024 * 1024
GROUP = 256
HEADS = GROUP // HD


def call(kernel, outs, operands, spaces=(), scratch=(), flops=0, limit=VMEM_LIMIT):
    vmem = pl.BlockSpec(memory_space=pltpu.VMEM)
    specs = [vmem] * len(operands)
    for index, space in spaces:
        specs[index] = pl.BlockSpec(memory_space=space)
    moved = sum(item.size * item.dtype.itemsize for item in list(operands) + list(outs))
    return pl.pallas_call(
        kernel,
        out_shape=list(outs),
        in_specs=specs,
        out_specs=[vmem] * len(outs),
        scratch_shapes=list(scratch),
        compiler_params=pltpu.CompilerParams(vmem_limit_bytes=limit),
        cost_estimate=pl.CostEstimate(flops=flops, bytes_accessed=moved, transcendentals=0),
    )(*operands)


def struct(shape, dtype):
    return jax.ShapeDtypeStruct(shape, dtype)


def mm(left, right):
    return jnp.dot(left, right, preferred_element_type=F32)


def mm_nt(left, right):
    return lax.dot_general(left, right, (((1,), (1,)), ((), ())), preferred_element_type=F32)


def mm_tn(left, right):
    return lax.dot_general(left, right, (((0,), (0,)), ((), ())), preferred_element_type=F32)


def normalize(values):
    center = jnp.mean(values, axis=1, keepdims=True)
    spread = jnp.mean(values * values, axis=1, keepdims=True) - center * center
    scaled = lax.rsqrt(spread + EPSILON)
    return (values - center) * scaled, scaled


def cells_of(rows):
    cell = lax.broadcasted_iota(jnp.int32, (rows, 1), 0)
    column = lax.rem(cell, GRID)
    line = lax.rem(lax.div(cell, GRID), GRID)
    return line, column


def shift_columns(values):
    rows = values.shape[0]
    _, column = cells_of(rows)
    before = jnp.where(column != 0, pltpu.roll(values, 1, 0), 0.0)
    after = jnp.where(column != GRID - 1, pltpu.roll(values, rows - 1, 0), 0.0)
    return before, after


def shift_lines(values, ahead):
    rows = values.shape[0]
    line, _ = cells_of(rows)
    if ahead:
        return jnp.where(line != GRID - 1, pltpu.roll(values, rows - GRID, 0), 0.0)
    return jnp.where(line != 0, pltpu.roll(values, GRID, 0), 0.0)


def convolve(values, taps):
    before, after = shift_columns(values)
    lines = [
        before * taps[3 * a] + values * taps[3 * a + 1] + after * taps[3 * a + 2] for a in range(3)
    ]
    return shift_lines(lines[0], False) + lines[1] + shift_lines(lines[2], True)


LANES = 256


def pack_cells(slots_ref, cells_ref):
    for image in range(cells_ref.shape[0] // CELLS):
        for line in range(GRID):
            cells_ref[pl.ds(image * CELLS + line * GRID, GRID), :] = slots_ref[
                pl.ds((image * PADDED + line) * PADDED, GRID), :
            ]


def unpack_cells(cells_ref, slots_ref):
    slots_ref[...] = jnp.zeros_like(slots_ref)
    for image in range(cells_ref.shape[0] // CELLS):
        for line in range(GRID):
            slots_ref[pl.ds((image * PADDED + line) * PADDED, GRID), :] = cells_ref[
                pl.ds(image * CELLS + line * GRID, GRID), :
            ]


def conv_kernel(values_ref, present_ref, kernel_ref, bias_ref, out_ref):
    present = present_ref[...]
    for lane in range(0, values_ref.shape[1], LANES):
        cut = pl.ds(lane, LANES)
        values = values_ref[:, cut]
        taps = [kernel_ref[pl.ds(i, 1), cut] for i in range(9)]
        out_ref[:, cut] = values + present * (convolve(values, taps) + bias_ref[:, cut])


def first_conv_kernel(slots_ref, present_ref, kernel_ref, bias_ref, start_ref, out_ref):
    pack_cells(slots_ref, start_ref)
    present = present_ref[...]
    for lane in range(0, start_ref.shape[1], LANES):
        cut = pl.ds(lane, LANES)
        values = start_ref[:, cut] * present
        start_ref[:, cut] = values
        taps = [kernel_ref[pl.ds(i, 1), cut] for i in range(9)]
        out_ref[:, cut] = values + present * (convolve(values, taps) + bias_ref[:, cut])


def conv_back_kernel(grads_ref, values_ref, present_ref, kernel_ref, out_ref, sums_ref, *rest):
    present = present_ref[...]
    target = rest[0] if rest else out_ref
    for lane in range(0, grads_ref.shape[1], LANES):
        cut = pl.ds(lane, LANES)
        grads = grads_ref[:, cut]
        masked = grads * present
        taps = [kernel_ref[pl.ds(8 - i, 1), cut] for i in range(9)]
        flowing = grads + convolve(masked, taps)
        target[:, cut] = flowing * present if rest else flowing
        values = values_ref[:, cut]
        before, after = shift_columns(values)
        behind = shift_lines(masked, False)
        ahead = shift_lines(masked, True)
        for a, moved in enumerate((ahead, masked, behind)):
            for e, source in enumerate((before, values, after)):
                sums_ref[pl.ds(3 * a + e, 1), cut] = jnp.sum(moved * source, axis=0, keepdims=True)
        sums_ref[pl.ds(9, 1), cut] = jnp.sum(masked, axis=0, keepdims=True)
    if rest:
        unpack_cells(target, out_ref)


def conv(values, present, kernel, bias):
    return call(conv_kernel, [struct(values.shape, F32)], [values, present, kernel, bias[None]])[0]


def first_conv(slots, present, kernel, bias):
    cells = struct((present.shape[0], slots.shape[1]), F32)
    return call(first_conv_kernel, [cells, cells], [slots, present, kernel, bias[None]])


def conv_back(grads, values, present, kernel, last):
    rows, width = grads.shape
    images = rows // CELLS
    out = struct((images * PADDED * PADDED if last else rows, width), F32)
    scratch = [pltpu.VMEM((rows, width), F32)] if last else []
    return call(
        conv_back_kernel, [out, struct((10, width), F32)], [grads, values, present, kernel], scratch=scratch
    )


UNITS = 768
TILE = 256


def mlp_kernel(
    values_ref, present_ref, gain_ref, shift_ref, upbias_ref, downbias_ref,
    u0, u1, u2, u3, d0, d1, d2, d3,
    *rest,
):
    packed = len(rest) == 6
    out_ref, acted_ref, send_ref, deriv_ref, total_ref = rest[0], rest[1], rest[2], rest[3], rest[4]
    values = values_ref[...]
    normal, _ = normalize(values)
    half = 2 * UNITS
    send_ref[:, half:] = (normal * gain_ref[...] + shift_ref[...]).astype(BF16)
    for index, (up, down) in enumerate(zip((u0, u1, u2, u3), (d0, d1, d2, d3))):
        target = acted_ref if index < 2 else send_ref
        base = (index % 2) * UNITS

        def step(part, _, up=up, target=target, base=base, index=index):
            first = pl.multiple_of(part * TILE, TILE)
            here = pl.ds(pl.multiple_of(index * UNITS + part * TILE, TILE), TILE)
            hidden = mm_nt(send_ref[:, half:], up[pl.ds(first, TILE), :]) + upbias_ref[:, here]
            below = 0.5 + 0.5 * lax.erf(hidden * (0.5**0.5))
            there = pl.ds(pl.multiple_of(base + part * TILE, TILE), TILE)
            target[:, there] = (hidden * below).astype(BF16)
            bell = jnp.exp(hidden * hidden * -0.5) * 0.3989422804014327
            deriv_ref[:, here] = below + hidden * bell
            return 0

        lax.fori_loop(0, UNITS // TILE, step, 0)
        term = mm(target[:, base : base + UNITS], down[...])
        total_ref[...] = term if index == 0 else total_ref[...] + term
    result = values + present_ref[...] * (total_ref[...] + downbias_ref[...])
    if packed:
        rest[5][...] = result
        unpack_cells(rest[5], out_ref)
    else:
        out_ref[...] = result


def mlp(values, present, gain, shift, upbias, downbias, ups, downs, last):
    rows, width = values.shape
    images = rows // CELLS
    half = 2 * UNITS
    outs = [
        struct((images * PADDED * PADDED if last else rows, width), F32),
        struct((rows, half), BF16),
        struct((rows, half + width), BF16),
        struct((rows, 2 * half), F32),
    ]
    scratch = [pltpu.VMEM((rows, width), F32)] * (2 if last else 1)
    operands = [values, present, gain[None], shift[None], upbias[None], downbias[None], *ups, *downs]
    return call(mlp_kernel, outs, operands, scratch=scratch, flops=4 * rows * width * 2 * half)


def norm_back(dn, values, gain, little_ref):
    normal, scaled = normalize(values)
    little_ref[0:1, :] = jnp.sum(dn * normal, axis=0, keepdims=True)
    little_ref[1:2, :] = jnp.sum(dn, axis=0, keepdims=True)
    grad_normal = dn * gain
    first = jnp.mean(grad_normal, axis=1, keepdims=True)
    second = jnp.mean(grad_normal * normal, axis=1, keepdims=True)
    return scaled * (grad_normal - first - normal * second)


def mlp_back_kernel(
    grads_ref, values_ref, present_ref, gain_ref, deriv_ref,
    u0, u1, u2, u3, d0, d1, d2, d3,
    out_ref, hidden_ref, send_ref, little_ref, bias_ref, total_ref, *rest,
):
    half = 2 * UNITS
    if rest:
        pack_cells(grads_ref, rest[0])
        grads_ref = rest[0]
    branch = grads_ref[...] * present_ref[...]
    little_ref[2:3, :] = jnp.sum(branch, axis=0, keepdims=True)
    send_ref[:, half:] = branch.astype(BF16)
    for index, (up, down) in enumerate(zip((u0, u1, u2, u3), (d0, d1, d2, d3))):
        target = hidden_ref if index < 2 else send_ref
        base = (index % 2) * UNITS

        def step(part, _, down=down, target=target, base=base, index=index):
            first = pl.multiple_of(part * TILE, TILE)
            here = pl.ds(pl.multiple_of(index * UNITS + part * TILE, TILE), TILE)
            acted = mm_nt(send_ref[:, half:], down[pl.ds(first, TILE), :])
            hidden = (acted * deriv_ref[:, here]).astype(BF16)
            there = pl.ds(pl.multiple_of(base + part * TILE, TILE), TILE)
            target[:, there] = hidden
            bias_ref[:, here] = jnp.sum(hidden.astype(F32), axis=0, keepdims=True)
            return 0

        lax.fori_loop(0, UNITS // TILE, step, 0)
        term = mm(target[:, base : base + UNITS], up[...])
        total_ref[...] = term if index == 0 else total_ref[...] + term
    grad_in = norm_back(total_ref[...], values_ref[...], gain_ref[...], little_ref)
    out_ref[...] = grads_ref[...] + grad_in


def mlp_back(grads, values, present, gain, deriv, ups, downs):
    rows, width = values.shape
    half = 2 * UNITS
    outs = [
        struct((rows, width), F32),
        struct((rows, half), BF16),
        struct((rows, half + width), BF16),
        struct((3, width), F32),
        struct((1, 2 * half), F32),
    ]
    scratch = [pltpu.VMEM((rows, width), F32)] * (2 if grads.shape[0] != rows else 1)
    operands = [grads, values, present, gain[None], deriv, *ups, *downs]
    return call(mlp_back_kernel, outs, operands, scratch=scratch, flops=4 * rows * width * 2 * half)


def pair_grads_kernel(wide_ref, wide_send_ref, thin_ref, thin_send_ref, near_ref, far_ref):
    half = 2 * UNITS
    for index, out_ref in enumerate((near_ref, far_ref)):
        cut = pl.ds(index * UNITS, UNITS)
        total = mm_tn(wide_ref[:, cut], thin_ref[:, half:])
        total = total + mm_tn(wide_send_ref[:, cut], thin_send_ref[:, half:])
        out_ref[...] = total.astype(BF16)


def pair_grads(wide, wide_send, thin, thin_send):
    width = thin.shape[1] - 2 * UNITS
    out = struct((UNITS, width), BF16)
    flops = 8 * wide.shape[0] * UNITS * width
    return call(pair_grads_kernel, [out, out], [wide, wide_send, thin, thin_send], flops=flops)


MATS = 4


def load_weights(place_ref, parts, weights_ref, sems):
    core, wid = place_ref[0], place_ref[1]
    copies = []
    for index, part in enumerate(parts):
        side = index // 2
        turn = core if side == 0 else 1 - core
        columns = pl.ds(pl.multiple_of(turn * 384, 384), 384)
        for i in range(2):
            line = 2 * (index % 2) + i
            order = line if line in (0, 3) else jnp.where(turn == 1, 3 - line, line)
            for j in range(4):
                first = pl.multiple_of(order * 192 + jnp.bitwise_xor(wid, j) * 48, 16)
                copies.append(
                    pltpu.make_async_copy(
                        part.at[i * 4 + j],
                        weights_ref.at[:, pl.ds(first, 48), columns],
                        sems.at[len(copies)],
                    )
                )
    for copy in copies:
        copy.start()
    return copies


def spread_heads(block):
    lane_head = lax.broadcasted_iota(jnp.int32, (1, GROUP), 1) // HD
    zero = jnp.zeros_like(block)
    return jnp.concatenate([jnp.where(lane_head == h, block, zero) for h in range(HEADS)], axis=0)


def gather_heads(wide):
    lane_head = lax.broadcasted_iota(jnp.int32, (1, GROUP), 1) // HD
    rows = wide.shape[0] // HEADS
    total = jnp.where(lane_head == 0, wide[:rows], 0.0)
    for h in range(1, HEADS):
        total = jnp.where(lane_head == h, wide[h * rows : (h + 1) * rows], total)
    return total


def window_probabilities(queries, keys, mask):
    scores = mm_nt(queries, keys) * SCALE
    scores = scores.reshape(HEADS, CELLS, CELLS)
    scores = jnp.where(mask[None] > 0.5, scores, -1000000000.0)
    raised = jnp.exp(scores - jnp.max(scores, axis=-1, keepdims=True))
    return raised * (1.0 / jnp.sum(raised, axis=-1, keepdims=True))


def channel_probabilities(keys, values):
    scores = mm_tn(keys, values) * SCALE
    line = lax.broadcasted_iota(jnp.int32, (GROUP, GROUP), 0) // HD
    column = lax.broadcasted_iota(jnp.int32, (GROUP, GROUP), 1) // HD
    scores = jnp.where(line == column, scores, -jnp.inf)
    raised = jnp.exp(scores - jnp.max(scores, axis=-1, keepdims=True))
    return raised * (1.0 / jnp.sum(raised, axis=-1, keepdims=True))


def unit_cuts(unit, width):
    groups = width // GROUP
    image = unit // groups
    rows = pl.ds(pl.multiple_of(image * CELLS, 16), CELLS)
    lane = pl.multiple_of(lax.rem(unit, groups) * GROUP, GROUP)
    return rows, lane


def attention_kernel(
    windowed, place_ref, values_ref, present_ref, mask_ref, gain_ref, shift_ref, bias_ref, outbias_ref,
    p0, p1, p2, p3, out_ref, normed_ref, qkv_ref, mixed_ref, weights_ref, sems,
):
    copies = load_weights(place_ref, (p0, p1, p2, p3), weights_ref, sems)
    rows_all, width = values_ref.shape
    normal, _ = normalize(values_ref[...])
    normed_ref[...] = (normal * gain_ref[...] + shift_ref[...]).astype(BF16)
    for copy in copies:
        copy.wait()
    for m in range(3):
        projected = mm_nt(normed_ref[...], weights_ref[m]) + bias_ref[m : m + 1, :]
        qkv_ref[:, m * width : (m + 1) * width] = projected.astype(BF16)

    def step(unit, _):
        rows, lane = unit_cuts(unit, width)
        queries = qkv_ref[rows, pl.ds(lane, GROUP)]
        keys = qkv_ref[rows, pl.ds(lane + width, GROUP)]
        values = qkv_ref[rows, pl.ds(lane + 2 * width, GROUP)]
        if windowed:
            probs = window_probabilities(spread_heads(queries), keys, mask_ref[rows, :])
            weights = probs.reshape(HEADS * CELLS, CELLS).astype(BF16)
            mixed = gather_heads(mm(weights, values))
        else:
            kept = keys * present_ref[rows, :].astype(BF16)
            weights = channel_probabilities(kept, values).astype(BF16)
            mixed = mm_nt(queries, weights)
        mixed_ref[rows, pl.ds(lane, GROUP)] = mixed.astype(BF16)
        return 0

    lax.fori_loop(0, rows_all // CELLS * (width // GROUP), step, 0)
    branch = mm(mixed_ref[...], weights_ref[3]) + outbias_ref[...]
    out_ref[...] = values_ref[...] + present_ref[...] * branch


def attention(windowed, place, values, present, mask, gain, shift, bias, outbias, parts):
    rows, width = values.shape
    outs = [
        struct((rows, width), F32),
        struct((rows, width), BF16),
        struct((rows, 3 * width), BF16),
        struct((rows, width), BF16),
    ]
    operands = [place, values, present, mask, gain[None], shift[None], bias, outbias[None], *parts]
    spaces = [(0, pltpu.SMEM)] + [(8 + i, pl.ANY) for i in range(4)]
    scratch = [pltpu.VMEM((MATS, width, width), BF16), pltpu.SemaphoreType.DMA((32,))]
    return call(
        partial(attention_kernel, windowed), outs, operands, spaces=spaces, scratch=scratch,
        flops=8 * rows * width * width,
    )


def attention_back_kernel(
    windowed, place_ref, grads_ref, values_ref, present_ref, mask_ref, gain_ref, normed_ref, qkv_ref, mixed_ref,
    p0, p1, p2, p3, out_ref, left_ref, mine_ref, theirs_ref, little_ref, bias_ref,
    weights_ref, low_ref, mix_ref, sems,
):
    copies = load_weights(place_ref, (p0, p1, p2, p3), weights_ref, sems)
    rows_all, width = values_ref.shape
    half = width // 2
    core = place_ref[0]
    own = pl.ds(pl.multiple_of(core * half, half), half)
    other = pl.ds(pl.multiple_of((1 - core) * half, half), half)
    branch = grads_ref[...] * present_ref[...]
    little_ref[2:3, :] = jnp.sum(branch, axis=0, keepdims=True)
    low_ref[...] = branch.astype(BF16)
    mine_ref[:, :half] = normed_ref[:, own]
    mine_ref[:, half:] = low_ref[:, own]
    theirs_ref[:, :half] = normed_ref[:, other]
    theirs_ref[:, half:] = low_ref[:, other]
    left_ref[:, 3 * width :] = mixed_ref[...]
    for copy in copies:
        copy.wait()
    mix_ref[...] = mm_nt(low_ref[...], weights_ref[3]).astype(BF16)

    def step(unit, _):
        rows, lane = unit_cuts(unit, width)
        queries = qkv_ref[rows, pl.ds(lane, GROUP)]
        keys = qkv_ref[rows, pl.ds(lane + width, GROUP)]
        values = qkv_ref[rows, pl.ds(lane + 2 * width, GROUP)]
        incoming = mix_ref[rows, pl.ds(lane, GROUP)]
        if windowed:
            mask = mask_ref[rows, :]
            wide_queries = spread_heads(queries)
            wide_incoming = spread_heads(incoming)
            probs = window_probabilities(wide_queries, keys, mask)
            weights = probs.reshape(HEADS * CELLS, CELLS).astype(BF16)
            grad_probs = mm_nt(wide_incoming, values).reshape(HEADS, CELLS, CELLS)
            inner = jnp.sum(probs * grad_probs, axis=-1, keepdims=True)
            grad_scores = jnp.where(mask[None] > 0.5, probs * (grad_probs - inner), 0.0)
            grad_scores = grad_scores.reshape(HEADS * CELLS, CELLS).astype(BF16)
            grad_query = gather_heads(mm(grad_scores, keys)) * SCALE
            grad_keys = mm_tn(grad_scores, wide_queries) * SCALE
            grad_values = mm_tn(weights, wide_incoming)
        else:
            present = present_ref[rows, :]
            kept = keys * present.astype(BF16)
            probs = channel_probabilities(kept, values)
            grad_probs = mm_tn(incoming, queries)
            inner = jnp.sum(probs * grad_probs, axis=-1, keepdims=True)
            grad_scores = (probs * (grad_probs - inner)).astype(BF16)
            grad_query = mm(incoming, probs.astype(BF16))
            grad_keys = mm_nt(values, grad_scores) * SCALE * present
            grad_values = mm(kept, grad_scores) * SCALE
        for m, item in enumerate((grad_query, grad_keys, grad_values)):
            left_ref[rows, pl.ds(lane + m * width, GROUP)] = item.astype(BF16)
        return 0

    lax.fori_loop(0, rows_all // CELLS * (width // GROUP), step, 0)
    total = None
    for m in range(3):
        rounded = left_ref[:, m * width : (m + 1) * width]
        bias_ref[m : m + 1, :] = jnp.sum(rounded.astype(F32), axis=0, keepdims=True)
        term = mm(rounded, weights_ref[m])
        total = term if total is None else total + term
    out_ref[...] = grads_ref[...] + norm_back(total, values_ref[...], gain_ref[...], little_ref)


def attention_back(windowed, place, grads, values, present, mask, gain, normed, qkv, mixed, parts):
    rows, width = values.shape
    outs = [
        struct((rows, width), F32),
        struct((rows, 4 * width), BF16),
        struct((rows, width), BF16),
        struct((rows, width), BF16),
        struct((3, width), F32),
        struct((3, width), F32),
    ]
    operands = [place, grads, values, present, mask, gain[None], normed, qkv, mixed, *parts]
    spaces = [(0, pltpu.SMEM)] + [(9 + i, pl.ANY) for i in range(4)]
    scratch = [
        pltpu.VMEM((MATS, width, width), BF16),
        pltpu.VMEM((rows, width), BF16),
        pltpu.VMEM((rows, width), BF16),
        pltpu.SemaphoreType.DMA((32,)),
    ]
    return call(
        partial(attention_back_kernel, windowed), outs, operands, spaces=spaces, scratch=scratch,
        flops=10 * rows * width * width,
    )


def head_grads_kernel(place_ref, left_ref, left_send_ref, right_ref, right_send_ref, near_ref, far_ref, table_ref):
    core, wid = place_ref[0], place_ref[1]
    width = left_ref.shape[1] // MATS
    half = width // 2
    for m in range(MATS):
        cut = slice(m * width, (m + 1) * width)
        side = slice(0, half) if m < 3 else slice(half, width)
        table_ref[...] = mm_tn(left_ref[:, cut], right_ref[:, side])
        table_ref[...] = table_ref[...] + mm_tn(left_send_ref[:, cut], right_send_ref[:, side])
        for line in range(4):
            order = line if line in (0, 3) else jnp.where(core == 1, 3 - line, line)
            out_ref = near_ref if line < 2 else far_ref
            for j in range(4):
                first = pl.multiple_of(order * 192 + jnp.bitwise_xor(wid, j) * 48, 16)
                out_ref[(line % 2) * 4 + j, m] = table_ref[pl.ds(first, 48), :].astype(BF16)


def head_grads(place, left, left_send, right, right_send):
    width = right.shape[1]
    out = struct((8, MATS, width // 16, width // 2), BF16)
    return call(
        head_grads_kernel, [out, out], [place, left, left_send, right, right_send],
        spaces=[(0, pltpu.SMEM)], scratch=[pltpu.VMEM((width, width // 2), F32)],
        flops=8 * left.shape[0] * width * width,
    )


class Line:
    def __init__(self, mark):
        self.mark = mark

    def gate(self, tree):
        tree, self.mark = lax.optimization_barrier((tree, self.mark))
        return tree

    def run(self, function, *operands):
        return self.gate(function(*self.gate(operands)))


class Gather:
    def __init__(self, line, piece):
        self.line, self.near, self.step, self.flight = line, piece[None], 0, ()

    def advance(self):
        gate = self.line.gate
        if self.step in (1, 2, 3):
            arrived = gate(self.flight[0])
            self.near = jnp.concatenate([self.near, arrived], axis=0)
        elif self.step == 4:
            self.far, self.other_near = gate(self.flight)
        elif self.step == 5:
            self.other_far = gate(self.flight[0])
        if self.step < 4:
            self.near = gate(self.near)
        if self.step == 0:
            self.flight = (exchange(self.near, "wid", 1),)
        elif self.step == 1:
            self.flight = (exchange(self.near, "wid", 2),)
        elif self.step == 2:
            self.flight = (cross(self.near, True),)
        elif self.step == 3:
            self.flight = (cross(self.near, False), sibling(self.near))
        elif self.step == 4:
            self.far = gate(self.far)
            self.flight = (sibling(self.far),)
        self.step += 1

    def parts(self):
        return [self.near, self.far, self.other_near, self.other_far]

    def rows(self):
        return [part.reshape(-1, part.shape[-1]) for part in self.parts()]


class Scatter:
    def __init__(self, line, near, far, axis):
        self.line, self.kept, self.sent, self.axis, self.step = line, near, far, axis, 0

    def advance(self):
        gate = self.line.gate
        if self.step in (1, 2, 3):
            arrived = gate(self.flight)
            half = arrived.shape[0] // 2
            self.sent = (self.kept[half:].astype(F32) + arrived[half:].astype(F32)).astype(BF16)
            self.kept = self.kept[:half].astype(F32) + arrived[:half].astype(F32)
        elif self.step == 4:
            total = self.kept[0] + gate(self.flight)[0].astype(F32)
            bit = 2
            while bit < lax.axis_size("dp"):
                total = total + exchange(total, "dp", bit)
                bit *= 2
            self.kept = total
        elif self.step == 5:
            self.total = by_core(self.kept, gate(self.flight), self.axis)
        if self.step < 4:
            self.sent = gate(self.sent)
        if self.step == 0:
            self.flight = cross(self.sent, False)
        elif self.step == 1:
            self.flight = cross(self.sent, True)
        elif self.step == 2:
            self.flight = exchange(self.sent, "wid", 2)
        elif self.step == 3:
            self.flight = exchange(self.sent, "wid", 1)
        elif self.step == 4:
            self.flight = sibling(gate(self.kept))
        self.step += 1


def presence(sizes):
    cells = jnp.arange(GRID, dtype=jnp.int32)
    inside = (cells[None, :, None] < sizes[:, None, None]) & (
        cells[None, None, :] < sizes[:, None, None]
    )
    return inside.astype(F32).reshape(-1, 1)


def window_mask(present):
    cell = jnp.arange(CELLS, dtype=jnp.int32)
    window = (cell // GRID // WINDOW) * 2 + cell % GRID // WINDOW
    same = window[:, None] == window[None, :]
    return (same[None] & (present.reshape(-1, 1, CELLS) > 0.5)).astype(F32).reshape(-1, CELLS)


def head_order(bias):
    return flip(bias, 1, lax.axis_index("hid")).reshape(bias.shape[0], -1)


def attention_piece(inweights, outweights):
    return half_of(jnp.concatenate([inweights, outweights[None]], axis=0), 2, True)


def body(
    inputs, grid_sizes, cotangent,
    wkernel, wcbias, wgain, wshift, winw, winb, woutw, woutb,
    wgain_two, wshift_two, wupw, wupb, wdownw, wdownb,
    ckernel, ccbias, cgain, cshift, cinw, cinb, coutw, coutb,
    cgain_two, cshift_two, cupw, cupb, cdownw, cdownb,
):
    image_count = inputs.shape[0] // (PADDED * PADDED)
    wid = lax.axis_index("wid")
    own_place = (lax.axis_index("hid") * lax.axis_size("wid") + wid) * image_count
    present = presence(lax.dynamic_slice_in_dim(grid_sizes, own_place, image_count, 0))
    mask = window_mask(present)
    place = jnp.stack([lax.rem(lax.axis_index("dp"), 2), wid]).astype(jnp.int32)
    line = Line(winb[0, 0])

    groups = [
        Gather(line, piece)
        for piece in (
            attention_piece(winw, woutw), half_of(wupw, 0, True), half_of(wdownw, 0, True),
            attention_piece(cinw, coutw), half_of(cupw, 0, True), half_of(cdownw, 0, True),
        )
    ]
    done = 0

    def gather_step():
        nonlocal done
        for index, group in enumerate(groups):
            if index <= done and done - index < 6:
                group.advance()
        done += 1

    table = jnp.concatenate([winb, wupb.reshape(4, -1), cinb, cupb.reshape(4, -1)])
    table = gather_bias(table)
    winb = head_order(table[0:2])
    winb = jnp.stack([winb[0], jnp.zeros_like(winb[0]), winb[1]])
    wupb = hidden_order(table[2:6].transpose(1, 0, 2).reshape(4, -1))
    cinb = head_order(table[6:9])
    cupb = hidden_order(table[9:13].transpose(1, 0, 2).reshape(4, -1))

    gather_step()
    start, after_conv = line.run(first_conv, inputs, present, wkernel, wcbias)
    for _ in range(5):
        gather_step()
    att_one = groups[0].parts()
    after_attn, normed_one, qkv_one, mixed_one = line.run(
        partial(attention, True), place, after_conv, present, mask, wgain, wshift, winb, woutb, att_one
    )
    gather_step()
    gather_step()
    ups_two, downs_two = groups[1].rows(), groups[2].rows()
    after_mlp, acted_two, fpack_two, deriv_two = line.run(
        partial(mlp, last=False),
        after_attn, present, wgain_two, wshift_two, wupb, wdownb, ups_two, downs_two,
    )
    fpack_two_other = sibling(fpack_two)
    gather_step()
    after_conv_c = line.run(conv, after_mlp, present, ckernel, ccbias)
    att_three = groups[3].parts()
    after_attn_c, normed_three, qkv_three, mixed_three = line.run(
        partial(attention, False), place, after_conv_c, present, mask, cgain, cshift, cinb, coutb, att_three
    )
    gather_step()
    fpack_two_other = line.gate(fpack_two_other)
    gather_step()
    ups_four, downs_four = groups[4].rows(), groups[5].rows()
    outputs, acted_four, fpack_four, deriv_four = line.run(
        partial(mlp, last=True),
        after_attn_c, present, cgain_two, cshift_two, cupb, cdownb, ups_four, downs_four,
    )

    fpack_four_other = sibling(fpack_four)
    flowing, gh_four, bpack_four, little_four, upb_four = line.run(
        mlp_back, cotangent, after_attn_c, present, cgain_two, deriv_four, ups_four, downs_four
    )
    bpack_four_other = sibling(bpack_four)
    fpack_four_other, bpack_four_other = line.gate((fpack_four_other, bpack_four_other))

    def mlp_scatter(wide, wide_send, thin, thin_send):
        near, far = line.run(pair_grads, wide, wide_send, thin, thin_send)
        group = Scatter(line, near.reshape(8, -1, near.shape[1]), far.reshape(8, -1, far.shape[1]), 0)
        group.advance()
        return group

    d_four = mlp_scatter(acted_four, fpack_four_other, bpack_four, bpack_four_other)
    u_four = mlp_scatter(gh_four, bpack_four_other, fpack_four, fpack_four_other)
    flowing, left_three, mine_three, theirs_three, little_three, inb_three = line.run(
        partial(attention_back, False),
        place, flowing, after_conv_c, present, mask, cgain, normed_three, qkv_three, mixed_three, att_three,
    )
    sent_three = sibling(left_three), sibling(theirs_three)
    d_four.advance()
    u_four.advance()
    sent_three = line.gate(sent_three)
    a_three = Scatter(line, *line.run(head_grads, place, left_three, sent_three[0], mine_three, sent_three[1]), 2)
    a_three.advance()
    d_four.advance()
    flowing, sums_three = line.run(
        partial(conv_back, last=False), flowing, after_mlp, present, ckernel
    )
    u_four.advance()
    flowing, gh_two, bpack_two, little_two, upb_two = line.run(
        mlp_back, flowing, after_attn, present, wgain_two, deriv_two, ups_two, downs_two
    )
    bpack_two_other = sibling(bpack_two)
    d_four.advance()
    a_three.advance()
    bpack_two_other = line.gate(bpack_two_other)
    d_two = mlp_scatter(acted_two, fpack_two_other, bpack_two, bpack_two_other)
    u_two = mlp_scatter(gh_two, bpack_two_other, fpack_two, fpack_two_other)
    u_four.advance()
    a_three.advance()
    d_four.advance()
    flowing, left_one, mine_one, theirs_one, little_one, inb_one = line.run(
        partial(attention_back, True),
        place, flowing, after_conv, present, mask, wgain, normed_one, qkv_one, mixed_one, att_one,
    )
    sent_one = sibling(left_one), sibling(theirs_one)
    d_two.advance()
    u_two.advance()
    sent_one = line.gate(sent_one)
    a_one = Scatter(line, *line.run(head_grads, place, left_one, sent_one[0], mine_one, sent_one[1]), 2)
    a_one.advance()
    u_four.advance()
    a_three.advance()
    d_four.advance()
    input_grad, sums_one = line.run(partial(conv_back, last=True), flowing, start, present, wkernel)
    d_two.advance()
    u_two.advance()
    u_four.advance()
    a_three.advance()

    def bias_rows(rows):
        rows = rows.reshape(rows.shape[0], 4, -1)
        return flip(rows, 1, lax.axis_index("hid")).reshape(rows.shape[0], -1)

    early = jnp.concatenate(
        [sums_three, little_two, little_three, little_four,
         bias_rows(inb_three), hidden_back(upb_two), hidden_back(upb_four)]
    )
    late = jnp.concatenate([sums_one, little_one, bias_rows(inb_one)])
    small = sum_everywhere(jnp.concatenate([early, late]))
    early, late = small[:30], small[30:]
    a_one.advance()
    d_two.advance()
    u_two.advance()
    a_three.advance()
    a_one.advance()
    d_two.advance()
    u_two.advance()
    a_one.advance()
    d_two.advance()
    u_two.advance()
    a_one.advance()
    a_one.advance()

    def own_hid(rows, axis):
        length = rows.shape[axis] // 4
        return lax.dynamic_slice_in_dim(rows, lax.axis_index("hid") * length, length, axis)

    for group in (d_two, u_two, a_one, d_four, u_four, a_three):
        while group.step < 6:
            group.advance()
    gatt_one, gatt_three = a_one.total, a_three.total
    return (
        outputs, input_grad,
        late[0:9], late[9], late[10], late[11], gatt_one[:3], own_hid(late[13:16:2], 1), gatt_one[3], late[12],
        early[10], early[11], u_two.total, own_hid(early[22:26], 0).reshape(-1), d_two.total, early[12],
        early[0:9], early[9], early[13], early[14], gatt_three[:3], own_hid(early[19:22], 1), gatt_three[3], early[15],
        early[16], early[17], u_four.total, own_hid(early[26:30], 0).reshape(-1), d_four.total, early[18],
    )


def solution(mesh):
    tokens, everywhere = P(("dp", "hid", "wid"), None), P()
    stacked, rows = P(None, ("hid", "wid"), None), P(("hid", "wid"), None)
    block = (
        everywhere, everywhere, everywhere, everywhere, stacked, P(None, "hid"), rows, everywhere,
        everywhere, everywhere, rows, P("hid"), rows, everywhere,
    )
    return jax.shard_map(
        body,
        mesh=mesh,
        in_specs=(tokens, P("dp"), tokens) + block + block,
        out_specs=(tokens, tokens) + block + block,
        check_vma=False,
    )
```

time: 890 us -> 592 us (0.67)
  matrix products: 173 us -> 0 us
  Pallas kernels: 0 us -> 166 us
  local copies, waits for them, and re-layouts: 252 us -> 89.2 us
  other arithmetic: 175 us -> 63.7 us
  starting transfers between devices: 77.7 us -> 59.2 us
  waiting for transfers between devices: 192 us -> 201 us
    dot_general x40 -> x0, matrix products: 173 us -> none  [the longest x12 60.9 us: times_transposed(): lax.dot_general(left, right, (((1,), (1,)), ((), ())), preferred_element_...]
    pallas_call x0 -> x18, Pallas kernels: none -> 166 us  [call(): pl.pallas_call(kernel, out_shape=list(outs), in_specs=specs, out_specs=[v...]
    reshape x26 -> x3, local copies, waits for them, and re-layouts: 51.2 us -> 2.97 us  [the longest x2 1.58 us: bias_rows(): rows = rows.reshape(rows.shape[0], 4, -1)]
    ppermute x68 -> x57, waiting for transfers between devices: 127 us -> 171 us  [exchange(): return lax.ppermute(values, axis, pairs)]
    convert_element_type x30 -> x0, local copies, waits for them, and re-layouts: 43.7 us -> none  [the longest x10 17.5 us: attention_backward(): rounded = [item.astype(BF16) for item in grads]]
    ppermute x24, waiting for transfers between devices: 64.7 us -> 30 us  [cross(): return lax.ppermute(values, ('dp', 'hid'), pairs)]
    reduce_sum x8 -> x0, other arithmetic: 23.1 us -> none  [the longest x2 9.7 us: depthwise(): padded[:, across:across + GRID, along:along + GRID, :] * kernel[offset]]
    ppermute x68 -> x57, starting transfers between devices: 63 us -> 43.3 us  [exchange(): return lax.ppermute(values, axis, pairs)]
  transfers between devices with their start and end apart: 92 -> 81, of which waited for: 27 -> 29; matrix products, arithmetic and copies ran while one was open for 66% -> 21% of each run, Pallas kernels for 0% -> 17%
where the time goes in v3:
time: 592 us; the launch traced here: 582 us
  waiting for transfers between devices  201 us (34%)
  Pallas kernels  166 us (28%)
  local copies, waits for them, and re-layouts  89.2 us (15%)
  other arithmetic  63.7 us (11%)
  starting transfers between devices  59.2 us (10%)
    ppermute x57, waiting for transfers between devices, exchange(): return lax.ppermute(values, axis, pairs)  171 us
    pallas_call x18, Pallas kernels, call(): pl.pallas_call(kernel, out_shape=list(outs), in_specs=specs, out_specs=[v...  166 us
    ppermute x57, starting transfers between devices, exchange(): return lax.ppermute(values, axis, pairs)  43.3 us
    ppermute x24, waiting for transfers between devices, cross(): return lax.ppermute(values, ('dp', 'hid'), pairs)  30 us
    ppermute x24, starting transfers between devices, cross(): return lax.ppermute(values, ('dp', 'hid'), pairs)  15.9 us
    concatenate x18, other arithmetic, advance(): self.near = jnp.concatenate([self.near, arrived], axis=0)  13.8 us
    concatenate x18, local copies, waits for them, and re-layouts, flip(): jnp.concatenate([parts[i ^ bit] for i in range(length)], axis=axis)  12.1 us
  transfers between devices with their start and end apart: 81, of which 29 were waited for; matrix products, arithmetic and copies ran while one was open for 21% of the time, Pallas kernels for 17%

profile of v3, /device:TPU:1, one launch (start us, length us, event | category | flops | bytes accessed | tf_op | source)
XLA Modules:
  0.0 582.4 jit_solution(4248166392955073544)
XLA Ops:
  23.5 13.7 %collective-permute-done.3 = bf16[2,4,48,384]{3,2,1,0:T(8,128)(2,1)S(1)} collective-permute-done((bf16[2,4,48,384]{3,2,1,0:T(8,128)(2,1)S(1)}, bf16[2,4,48,384]{3,2,1,0:T(8,128)(2,1)S(1)}, u32[]{:S(2)}, u32[]{:S(2)}) %collective-permute-start.3) | collective-permute-done | bytes 294944 | tf_op jit(solution)/shard_map/ppermute | solution.py:23
  40.0 4.5 collective-permute-done.5
  49.1 11.7 %collective-permute-done.9 = bf16[2,96,768]{2,1,0:T(8,128)(2,1)S(1)} collective-permute-done((bf16[2,96,768]{2,1,0:T(8,128)(2,1)S(1)}, bf16[2,96,768]{2,1,0:T(8,128)(2,1)S(1)}, u32[]{:S(2)}, u32[]{:S(2)}) %collective-permute-start.9) | collective-permute-done | bytes 294944 | tf_op jit(solution)/shard_map/ppermute | solution.py:23
  63.7 4.7 collective-permute-done.8
  75.1 8.3 %collective-permute-done.12 = bf16[2,96,768]{2,1,0:T(8,128)(2,1)S(1)} collective-permute-done((bf16[2,96,768]{2,1,0:T(8,128)(2,1)S(1)}, bf16[2,96,768]{2,1,0:T(8,128)(2,1)S(1)}, u32[]{:S(2)}, u32[]{:S(2)}) %collective-permute-start.12) | collective-permute-done | bytes 294944 | tf_op jit(solution)/shard_map/ppermute | solution.py:23
  102.4 10.8 %collective-permute-done.15 = bf16[2,4,48,384]{3,2,1,0:T(8,128)(2,1)S(1)} collective-permute-done((bf16[2,4,48,384]{3,2,1,0:T(8,128)(2,1)S(1)}, bf16[2,4,48,384]{3,2,1,0:T(8,128)(2,1)S(1)}, u32[]{:S(2)}, u32[]{:S(2)}) %collective-permute-start.15) | collective-permute-done | bytes 294944 | tf_op jit(solution)/shard_map/ppermute | solution.py:23
  125.1 12.8 %shard_map.527 = (f32[288,768]{1,0:T(8,128)}, bf16[288,768]{1,0:T(8,128)(2,1)}, bf16[288,2304]{1,0:T(8,128)(2,1)}, bf16[288,768]{1,0:T(8,128)(2,1)}) custom-call(s32[2]{0:T(128)} %pad_add_fusion.place_ref, f32[288,768]{1,0:T(8,128)} %get-tuple-element.971.values_ref, f32[288,1]{1,0:T(8,128)} %copy.133.present_ref, f32[288,144]{1,0:T(8,128)} %bitcast.233, ...), custom_call_target="tpu_custom_call" | custom-call | flops 1358954496 | bytes 8885384 | tf_op jit(solution)/shard_map/pallas_call | solution.py:127
  144.0 10.2 %collective-permute-done.24 = bf16[2,96,768]{2,1,0:T(8,128)(2,1)S(1)} collective-permute-done((bf16[2,96,768]{2,1,0:T(8,128)(2,1)S(1)}, bf16[2,96,768]{2,1,0:T(8,128)(2,1)S(1)}, u32[]{:S(2)}, u32[]{:S(2)}) %collective-permute-start.24) | collective-permute-done | bytes 294944 | tf_op jit(solution)/shard_map/ppermute | solution.py:23
  182.6 8.8 %collective-permute-done.26 = bf16[2,96,768]{2,1,0:T(8,128)(2,1)} collective-permute-done((bf16[2,96,768]{2,1,0:T(8,128)(2,1)}, bf16[2,96,768]{2,1,0:T(8,128)(2,1)}, u32[]{:S(2)}, u32[]{:S(2)}) %collective-permute-start.26) | collective-permute-done | bytes 294944 | tf_op jit(solution)/shard_map/ppermute | solution.py:23
  199.9 13.4 %shard_map.528 = (f32[288,768]{1,0:T(8,128)}, bf16[288,1536]{1,0:T(8,128)(2,1)}, bf16[288,2304]{1,0:T(8,128)(2,1)}, f32[288,3072]{1,0:T(8,128)}) custom-call(f32[288,768]{1,0:T(8,128)} %get-tuple-element.899.values_ref, f32[288,1]{1,0:T(8,128)} %copy.149.present_ref, f32[1,768]{1,0:T(1,128)} %broadcast_in_dim.103.gain_ref, ...), custom_call_target="tpu_custom_call" | custom-call | flops 2717908992 | bytes 16980096 | tf_op jit(solution)/shard_map/pallas_call | solution.py:127
  231.2 11.3 %shard_map.530 = (f32[288,768]{1,0:T(8,128)}, bf16[288,768]{1,0:T(8,128)(2,1)}, bf16[288,2304]{1,0:T(8,128)(2,1)}, bf16[288,768]{1,0:T(8,128)(2,1)}) custom-call(s32[2]{0:T(128)} %pad_add_fusion.place_ref, f32[288,768]{1,0:T(8,128)} %shard_map.529.values_ref, f32[288,1]{1,0:T(8,128)} %copy.151.present_ref, f32[288,144]{1,0:T(8,128)} %bitcast.234, ...), custom_call_target="tpu_custom_call" | custom-call | flops 1358954496 | bytes 8885384 | tf_op jit(solution)/shard_map/pallas_call | solution.py:127
  260.0 13.5 %shard_map.531 = (f32[392,768]{1,0:T(8,128)}, bf16[288,1536]{1,0:T(8,128)(2,1)}, bf16[288,2304]{1,0:T(8,128)(2,1)}, f32[288,3072]{1,0:T(8,128)}) custom-call(f32[288,768]{1,0:T(8,128)} %get-tuple-element.781.values_ref, f32[288,1]{1,0:T(8,128)} %copy.170.present_ref, f32[1,768]{1,0:T(1,128)} %broadcast_in_dim.111.gain_ref, ...), custom_call_target="tpu_custom_call" | custom-call | flops 2717908992 | bytes 17299584 | tf_op jit(solution)/shard_map/pallas_call | solution.py:127
  274.9 13.1 %shard_map.532 = (f32[288,768]{1,0:T(8,128)}, bf16[288,1536]{1,0:T(8,128)(2,1)}, bf16[288,2304]{1,0:T(8,128)(2,1)}, f32[3,768]{1,0:T(4,128)}, f32[1,3072]{1,0:T(1,128)}) custom-call(f32[392,768]{1,0:T(8,128)} %grads_ref, f32[288,768]{1,0:T(8,128)} %get-tuple-element.781.values_ref, f32[288,1]{1,0:T(8,128)} %copy.171.present_ref, ...), custom_call_target="tpu_custom_call" | custom-call | flops 2717908992 | bytes 18187392 | tf_op jit(solution)/shard_map/pallas_call | solution.py:127
  296.8 6.0 %shard_map.533 = (bf16[768,768]{1,0:T(8,128)(2,1)}, bf16[768,768]{1,0:T(8,128)(2,1)}) custom-call(bf16[288,1536]{1,0:T(8,128)(2,1)} %get-tuple-element.811.wide_ref, bf16[288,2304]{1,0:T(8,128)(2,1)} %collective-permute-done.39.wide_send_ref.thin_send_ref, bf16[288,2304]{1,0:T(8,128)(2,1)} %get-tuple-element.813.thin_ref, bf16[288,2304]{1,0:T(8,128)(2,1)} %copy-done.79), custom_call_target="tpu_custom_call" | custom-call | flops 1358954496 | bytes 7225344 | tf_op jit(solution)/shard_map/pallas_call | solution.py:127
  302.9 6.1 %shard_map.534 = (bf16[768,768]{1,0:T(8,128)(2,1)}, bf16[768,768]{1,0:T(8,128)(2,1)}) custom-call(bf16[288,1536]{1,0:T(8,128)(2,1)} %get-tuple-element.821.wide_ref, bf16[288,2304]{1,0:T(8,128)(2,1)} %copy-done.79, bf16[288,2304]{1,0:T(8,128)(2,1)} %get-tuple-element.823.thin_ref, bf16[288,2304]{1,0:T(8,128)(2,1)} %collective-permute-done.39.wide_send_ref.thin_send_ref), custom_call_target="tpu_custom_call" | custom-call | flops 1358954496 | bytes 7225344 | tf_op jit(solution)/shard_map/pallas_call | solution.py:127
  310.3 13.0 %shard_map.535 = (f32[288,768]{1,0:T(8,128)}, bf16[288,3072]{1,0:T(8,128)(2,1)}, bf16[288,768]{1,0:T(8,128)(2,1)}, bf16[288,768]{1,0:T(8,128)(2,1)}, f32[3,768]{1,0:T(4,128)}, /*index=5*/f32[3,768]{1,0:T(4,128)}) custom-call(s32[2]{0:T(128)} %pad_add_fusion.place_ref, f32[288,768]{1,0:T(8,128)} %get-tuple-element.832.grads_ref, ...), custom_call_target="tpu_custom_call" | custom-call | flops 1698693120 | bytes 12427400 | tf_op jit(solution)/shard_map/pallas_call | solution.py:127
  330.1 8.9 %collective-permute-done.41 = bf16[8,96,768]{2,1,0:T(8,128)(2,1)S(1)} collective-permute-done((bf16[8,96,768]{2,1,0:T(8,128)(2,1)}, bf16[8,96,768]{2,1,0:T(8,128)(2,1)S(1)}, u32[]{:S(2)}, u32[]{:S(2)}) %collective-permute-start.41) | collective-permute-done | bytes 1179680 | tf_op jit(solution)/shard_map/ppermute | solution.py:36
  339.2 12.4 %collective-permute-done.45 = bf16[8,96,768]{2,1,0:T(8,128)(2,1)S(1)} collective-permute-done((bf16[8,96,768]{2,1,0:T(8,128)(2,1)}, bf16[8,96,768]{2,1,0:T(8,128)(2,1)S(1)}, u32[]{:S(2)}, u32[]{:S(2)}) %collective-permute-start.45) | collective-permute-done | bytes 1179680 | tf_op jit(solution)/shard_map/ppermute | solution.py:36
  354.0 6.8 %shard_map.536 = (bf16[8,4,48,384]{3,2,1,0:T(8,128)(2,1)}, bf16[8,4,48,384]{3,2,1,0:T(8,128)(2,1)}) custom-call(s32[2]{0:T(128)} %pad_add_fusion.place_ref, bf16[288,3072]{1,0:T(8,128)(2,1)} %get-tuple-element.871.left_ref, bf16[288,3072]{1,0:T(8,128)(2,1)} %collective-permute-done.43.left_send_ref, bf16[288,768]{1,0:T(8,128)(2,1)} %get-tuple-element.873.right_ref, ...), custom_call_target="tpu_custom_call" | custom-call | flops 1358954496 | bytes 6782984 | tf_op jit(solution)/shard_map/pallas_call | solution.py:127
  362.4 5.5 shard_map.537
  370.1 13.3 %shard_map.538 = (f32[288,768]{1,0:T(8,128)}, bf16[288,1536]{1,0:T(8,128)(2,1)}, bf16[288,2304]{1,0:T(8,128)(2,1)}, f32[3,768]{1,0:T(4,128)}, f32[1,3072]{1,0:T(1,128)}) custom-call(f32[288,768]{1,0:T(8,128)} %get-tuple-element.898.grads_ref, f32[288,768]{1,0:T(8,128)} %get-tuple-element.899.values_ref, f32[288,1]{1,0:T(8,128)} %copy.174.present_ref, ...), custom_call_target="tpu_custom_call" | custom-call | flops 2717908992 | bytes 17867904 | tf_op jit(solution)/shard_map/pallas_call | solution.py:127
  392.1 15.3 %collective-permute-done.47 = bf16[2,96,768]{2,1,0:T(8,128)(2,1)S(1)} collective-permute-done((bf16[2,96,768]{2,1,0:T(8,128)(2,1)S(1)}, bf16[2,96,768]{2,1,0:T(8,128)(2,1)S(1)}, u32[]{:S(2)}, u32[]{:S(2)}) %collective-permute-start.47) | collective-permute-done | bytes 294944 | tf_op jit(solution)/shard_map/ppermute | solution.py:23
  412.3 6.0 %shard_map.539 = (bf16[768,768]{1,0:T(8,128)(2,1)}, bf16[768,768]{1,0:T(8,128)(2,1)}) custom-call(bf16[288,1536]{1,0:T(8,128)(2,1)} %get-tuple-element.940.wide_ref, bf16[288,2304]{1,0:T(8,128)(2,1)} %collective-permute-done.38.wide_send_ref.thin_send_ref, bf16[288,2304]{1,0:T(8,128)(2,1)} %get-tuple-element.942.thin_ref, ...), custom_call_target="tpu_custom_call" | custom-call | flops 1358954496 | bytes 7225344 | tf_op jit(solution)/shard_map/pallas_call | solution.py:127
  418.3 6.1 %shard_map.540 = (bf16[768,768]{1,0:T(8,128)(2,1)}, bf16[768,768]{1,0:T(8,128)(2,1)}) custom-call(bf16[288,1536]{1,0:T(8,128)(2,1)} %get-tuple-element.950.wide_ref, bf16[288,2304]{1,0:T(8,128)(2,1)} %collective-permute-done.52.thin_send_ref.wide_send_ref, bf16[288,2304]{1,0:T(8,128)(2,1)} %get-tuple-element.952.thin_ref, ...), custom_call_target="tpu_custom_call" | custom-call | flops 1358954496 | bytes 7225344 | tf_op jit(solution)/shard_map/pallas_call | solution.py:127
  431.5 17.2 %shard_map.541 = (f32[288,768]{1,0:T(8,128)}, bf16[288,3072]{1,0:T(8,128)(2,1)}, bf16[288,768]{1,0:T(8,128)(2,1)}, bf16[288,768]{1,0:T(8,128)(2,1)}, f32[3,768]{1,0:T(4,128)}, /*index=5*/f32[3,768]{1,0:T(4,128)}) custom-call(s32[2]{0:T(128)} %pad_add_fusion.place_ref, f32[288,768]{1,0:T(8,128)} %get-tuple-element.970.grads_ref, ...), custom_call_target="tpu_custom_call" | custom-call | flops 1698693120 | bytes 12427400 | tf_op jit(solution)/shard_map/pallas_call | solution.py:127
  453.6 6.2 %shard_map.543 = (f32[392,768]{1,0:T(8,128)}, f32[10,768]{1,0:T(8,128)}) custom-call(f32[288,768]{1,0:T(8,128)} %get-tuple-element.1029.grads_ref, f32[288,768]{1,0:T(8,128)} %get-tuple-element.1030.values_ref, f32[288,1]{1,0:T(8,128)} %copy.176.present_ref, f32[9,768]{1,0:T(8,128)} %kernel_ref.3), custom_call_target="tpu_custom_call" | custom-call | bytes 3033216 | tf_op jit(solution)/shard_map/pallas_call | solution.py:127
  464.7 16.8 %collective-permute-done.61 = f32[46,768]{1,0:T(8,128)S(1)} collective-permute-done((f32[46,768]{1,0:T(8,128)S(1)}, f32[46,768]{1,0:T(8,128)S(1)}, u32[]{:S(2)}, u32[]{:S(2)}) %collective-permute-start.61) | collective-permute-done | bytes 141344 | tf_op jit(solution)/shard_map/ppermute | solution.py:23
  492.9 7.2 %collective-permute-done.64 = f32[46,768]{1,0:T(8,128)S(1)} collective-permute-done((f32[46,768]{1,0:T(8,128)S(1)}, f32[46,768]{1,0:T(8,128)S(1)}, u32[]{:S(2)}, u32[]{:S(2)}) %collective-permute-start.64) | collective-permute-done | bytes 141344 | tf_op jit(solution)/shard_map/ppermute | solution.py:23
  510.8 6.8 %shard_map.542 = (bf16[8,4,48,384]{3,2,1,0:T(8,128)(2,1)}, bf16[8,4,48,384]{3,2,1,0:T(8,128)(2,1)}) custom-call(s32[2]{0:T(128)} %pad_add_fusion.place_ref, bf16[288,3072]{1,0:T(8,128)(2,1)} %get-tuple-element.1012.left_ref, bf16[288,3072]{1,0:T(8,128)(2,1)} %collective-permute-done.56.left_send_ref, bf16[288,768]{1,0:T(8,128)(2,1)} %get-tuple-element.1014.right_ref, ...), custom_call_target="tpu_custom_call" | custom-call | flops 1358954496 | bytes 6782984 | tf_op jit(solution)/shard_map/pallas_call | solution.py:127
  523.3 17.3 %collective-permute-done.75 = bf16[2,96,768]{2,1,0:T(8,128)(2,1)S(1)} collective-permute-done((bf16[2,96,768]{2,1,0:T(8,128)(2,1)S(1)}, bf16[2,96,768]{2,1,0:T(8,128)(2,1)S(1)}, u32[]{:S(2)}, u32[]{:S(2)}) %collective-permute-start.75) | collective-permute-done | bytes 294944 | tf_op jit(solution)/shard_map/ppermute | solution.py:23
  540.7 6.2 %collective-permute-done.74 = bf16[2,96,768]{2,1,0:T(8,128)(2,1)S(1)} collective-permute-done((bf16[2,96,768]{2,1,0:T(8,128)(2,1)S(1)}, bf16[2,96,768]{2,1,0:T(8,128)(2,1)S(1)}, u32[]{:S(2)}, u32[]{:S(2)}) %collective-permute-start.74) | collective-permute-done | bytes 294944 | tf_op jit(solution)/shard_map/ppermute | solution.py:23
  559.8 11.7 %collective-permute-done.71 = bf16[2,4,48,384]{3,2,1,0:T(8,128)(2,1)S(1)} collective-permute-done((bf16[2,4,48,384]{3,2,1,0:T(8,128)(2,1)S(1)}, bf16[2,4,48,384]{3,2,1,0:T(8,128)(2,1)S(1)}, u32[]{:S(2)}, u32[]{:S(2)}) %collective-permute-start.71) | collective-permute-done | bytes 294944 | tf_op jit(solution)/shard_map/ppermute | solution.py:23
  (617 shorter events, 253.7 us)
Async XLA Ops:
  46.5 21.9 %collective-permute-start.6 = (bf16[8,4,48,384]{3,2,1,0:T(8,128)(2,1)S(1)}, bf16[8,4,48,384]{3,2,1,0:T(8,128)(2,1)}, u32[]{:S(2)}, u32[]{:S(2)}) collective-permute-start(bf16[8,4,48,384]{3,2,1,0:T(8,128)(2,1)S(1)} %pad_maximum_fusion.p0), channel_id=1, source_target_pairs={{0,8},{4,12},{8,0},{12,4},{16,20},{20,16},{24,28},{28,24},{1,9},{5... | collective-permute-start | bytes 3538952 | tf_op jit(solution)/shard_map/ppermute | solution.py:36
  46.9 21.6 %collective-permute-start.7 = (bf16[8,4,48,384]{3,2,1,0:T(8,128)(2,1)S(1)}, bf16[8,4,48,384]{3,2,1,0:T(8,128)(2,1)S(1)}, u32[]{:S(2)}, u32[]{:S(2)}) collective-permute-start(bf16[8,4,48,384]{3,2,1,0:T(8,128)(2,1)S(1)} %pad_maximum_fusion.p0), channel_id=1, source_target_pairs={{0,16},{16,0},{1,17},{17,1},{2,18},{18,2},{3,19},{19,3},{4,20},{20... | collective-permute-start | bytes 3538952 | tf_op jit(solution)/shard_map/ppermute | solution.py:23
  70.8 26.4 %collective-permute-start.17 = (bf16[8,96,768]{2,1,0:T(8,128)(2,1)S(1)}, bf16[8,96,768]{2,1,0:T(8,128)(2,1)S(1)}, u32[]{:S(2)}, u32[]{:S(2)}) collective-permute-start(bf16[8,96,768]{2,1,0:T(8,128)(2,1)S(1)} %pad_maximum_fusion.1), channel_id=1, source_target_pairs={{0,8},{4,12},{8,0},{12,4},{16,20},{20,16},{24,28},{28,24},{1,9},{5... | collective-permute-start | bytes 3538952 | tf_op jit(solution)/shard_map/ppermute | solution.py:36
  70.8 26.3 %collective-permute-start.18 = (bf16[8,96,768]{2,1,0:T(8,128)(2,1)S(1)}, bf16[8,96,768]{2,1,0:T(8,128)(2,1)S(1)}, u32[]{:S(2)}, u32[]{:S(2)}) collective-permute-start(bf16[8,96,768]{2,1,0:T(8,128)(2,1)S(1)} %pad_maximum_fusion.1), channel_id=1, source_target_pairs={{0,16},{16,0},{1,17},{17,1},{2,18},{18,2},{3,19},{19,3},{4,20},{20... | collective-permute-start | bytes 3538952 | tf_op jit(solution)/shard_map/ppermute | solution.py:23
  73.9 23.2 %collective-permute-start.10 = (bf16[8,4,48,384]{3,2,1,0:T(8,128)(2,1)}, bf16[8,4,48,384]{3,2,1,0:T(8,128)(2,1)}, u32[]{:S(2)}, u32[]{:S(2)}) collective-permute-start(bf16[8,4,48,384]{3,2,1,0:T(8,128)(2,1)} %collective-permute-done.6.p1), channel_id=1, source_target_pairs={{0,16},{16,0},{1,17},{17,1},{2,18},{18,2},{3,19},{19,3},{4,20},{20... | collective-permute-start | bytes 3538952 | tf_op jit(solution)/shard_map/ppermute | solution.py:23
  100.7 37.4 %collective-permute-start.20 = (bf16[8,96,768]{2,1,0:T(8,128)(2,1)S(1)}, bf16[8,96,768]{2,1,0:T(8,128)(2,1)}, u32[]{:S(2)}, u32[]{:S(2)}) collective-permute-start(bf16[8,96,768]{2,1,0:T(8,128)(2,1)S(1)} %pad_maximum_fusion.2), channel_id=1, source_target_pairs={{0,8},{4,12},{8,0},{12,4},{16,20},{20,16},{24,28},{28,24},{1,9},{5... | collective-permute-start | bytes 3538952 | tf_op jit(solution)/shard_map/ppermute | solution.py:36
  100.8 37.4 %collective-permute-start.21 = (bf16[8,96,768]{2,1,0:T(8,128)(2,1)S(1)}, bf16[8,96,768]{2,1,0:T(8,128)(2,1)S(1)}, u32[]{:S(2)}, u32[]{:S(2)}) collective-permute-start(bf16[8,96,768]{2,1,0:T(8,128)(2,1)S(1)} %pad_maximum_fusion.2), channel_id=1, source_target_pairs={{0,16},{16,0},{1,17},{17,1},{2,18},{18,2},{3,19},{19,3},{4,20},{20... | collective-permute-start | bytes 3538952 | tf_op jit(solution)/shard_map/ppermute | solution.py:23
  101.8 36.3 %collective-permute-start.19 = (bf16[8,96,768]{2,1,0:T(8,128)(2,1)S(1)}, bf16[8,96,768]{2,1,0:T(8,128)(2,1)}, u32[]{:S(2)}, u32[]{:S(2)}) collective-permute-start(bf16[8,96,768]{2,1,0:T(8,128)(2,1)S(1)} %copy-done.7), channel_id=1, source_target_pairs={{0,16},{16,0},{1,17},{17,1},{2,18},{18,2},{3,19},{19,3},{4,20},{20... | collective-permute-start | bytes 3538952 | tf_op jit(solution)/shard_map/ppermute | solution.py:23
  114.1 25.0 %collective-permute-start.25 = (bf16[4,4,48,384]{3,2,1,0:T(8,128)(2,1)}, bf16[4,4,48,384]{3,2,1,0:T(8,128)(2,1)}, u32[]{:S(2)}, u32[]{:S(2)}) collective-permute-start(bf16[4,4,48,384]{3,2,1,0:T(8,128)(2,1)} %pad_maximum_fusion.9), channel_id=1, source_target_pairs={{0,4},{4,0},{8,12},{12,8},{16,24},{20,28},{24,16},{28,20},{1,5},{5... | collective-permute-start | bytes 1769480 | tf_op jit(solution)/shard_map/ppermute | solution.py:36
  140.6 30.7 %collective-permute-start.28 = (bf16[8,4,48,384]{3,2,1,0:T(8,128)(2,1)S(1)}, bf16[8,4,48,384]{3,2,1,0:T(8,128)(2,1)}, u32[]{:S(2)}, u32[]{:S(2)}) collective-permute-start(bf16[8,4,48,384]{3,2,1,0:T(8,128)(2,1)S(1)} %pad_maximum_fusion.3.p0), channel_id=1, source_target_pairs={{0,8},{4,12},{8,0},{12,4},{16,20},{20,16},{24,28},{28,24},{1,9},{5... | collective-permute-start | bytes 3538952 | tf_op jit(solution)/shard_map/ppermute | solution.py:36
  140.7 30.6 %collective-permute-start.29 = (bf16[8,4,48,384]{3,2,1,0:T(8,128)(2,1)S(1)}, bf16[8,4,48,384]{3,2,1,0:T(8,128)(2,1)S(1)}, u32[]{:S(2)}, u32[]{:S(2)}) collective-permute-start(bf16[8,4,48,384]{3,2,1,0:T(8,128)(2,1)S(1)} %pad_maximum_fusion.3.p0), channel_id=1, source_target_pairs={{0,16},{16,0},{1,17},{17,1},{2,18},{18,2},{3,19},{19,3},{4,20},{20... | collective-permute-start | bytes 3538952 | tf_op jit(solution)/shard_map/ppermute | solution.py:23
  142.0 29.3 %collective-permute-start.22 = (bf16[8,96,768]{2,1,0:T(8,128)(2,1)}, bf16[8,96,768]{2,1,0:T(8,128)(2,1)S(1)}, u32[]{:S(2)}, u32[]{:S(2)}) collective-permute-start(bf16[8,96,768]{2,1,0:T(8,128)(2,1)} %collective-permute-done.20), channel_id=1, source_target_pairs={{0,16},{16,0},{1,17},{17,1},{2,18},{18,2},{3,19},{19,3},{4,20},{20... | collective-permute-start | bytes 3538952 | tf_op jit(solution)/shard_map/ppermute | solution.py:23
  173.7 39.7 %collective-permute-start.31 = (bf16[8,96,768]{2,1,0:T(8,128)(2,1)S(1)}, bf16[8,96,768]{2,1,0:T(8,128)(2,1)}, u32[]{:S(2)}, u32[]{:S(2)}) collective-permute-start(bf16[8,96,768]{2,1,0:T(8,128)(2,1)S(1)} %pad_maximum_fusion.4), channel_id=1, source_target_pairs={{0,8},{4,12},{8,0},{12,4},{16,20},{20,16},{24,28},{28,24},{1,9},{5... | collective-permute-start | bytes 3538952 | tf_op jit(solution)/shard_map/ppermute | solution.py:36
  173.8 39.6 %collective-permute-start.32 = (bf16[8,96,768]{2,1,0:T(8,128)(2,1)S(1)}, bf16[8,96,768]{2,1,0:T(8,128)(2,1)S(1)}, u32[]{:S(2)}, u32[]{:S(2)}) collective-permute-start(bf16[8,96,768]{2,1,0:T(8,128)(2,1)S(1)} %pad_maximum_fusion.4), channel_id=1, source_target_pairs={{0,16},{16,0},{1,17},{17,1},{2,18},{18,2},{3,19},{19,3},{4,20},{20... | collective-permute-start | bytes 3538952 | tf_op jit(solution)/shard_map/ppermute | solution.py:23
  175.7 37.7 %collective-permute-start.33 = (bf16[8,4,48,384]{3,2,1,0:T(8,128)(2,1)}, bf16[8,4,48,384]{3,2,1,0:T(8,128)(2,1)S(1)}, u32[]{:S(2)}, u32[]{:S(2)}) collective-permute-start(bf16[8,4,48,384]{3,2,1,0:T(8,128)(2,1)} %collective-permute-done.28.p1), channel_id=1, source_target_pairs={{0,16},{16,0},{1,17},{17,1},{2,18},{18,2},{3,19},{19,3},{4,20},{20... | collective-permute-start | bytes 3538952 | tf_op jit(solution)/shard_map/ppermute | solution.py:23
  215.8 26.7 %collective-permute-start.35 = (bf16[8,96,768]{2,1,0:T(8,128)(2,1)S(1)}, bf16[8,96,768]{2,1,0:T(8,128)(2,1)S(1)}, u32[]{:S(2)}, u32[]{:S(2)}) collective-permute-start(bf16[8,96,768]{2,1,0:T(8,128)(2,1)S(1)} %pad_maximum_fusion.5), channel_id=1, source_target_pairs={{0,8},{4,12},{8,0},{12,4},{16,20},{20,16},{24,28},{28,24},{1,9},{5... | collective-permute-start | bytes 3538952 | tf_op jit(solution)/shard_map/ppermute | solution.py:36
  216.4 26.1 %collective-permute-start.36 = (bf16[8,96,768]{2,1,0:T(8,128)(2,1)S(1)}, bf16[8,96,768]{2,1,0:T(8,128)(2,1)S(1)}, u32[]{:S(2)}, u32[]{:S(2)}) collective-permute-start(bf16[8,96,768]{2,1,0:T(8,128)(2,1)S(1)} %pad_maximum_fusion.5), channel_id=1, source_target_pairs={{0,16},{16,0},{1,17},{17,1},{2,18},{18,2},{3,19},{19,3},{4,20},{20... | collective-permute-start | bytes 3538952 | tf_op jit(solution)/shard_map/ppermute | solution.py:23
  217.5 25.0 %collective-permute-start.34 = (bf16[8,96,768]{2,1,0:T(8,128)(2,1)}, bf16[8,96,768]{2,1,0:T(8,128)(2,1)}, u32[]{:S(2)}, u32[]{:S(2)}) collective-permute-start(bf16[8,96,768]{2,1,0:T(8,128)(2,1)} %collective-permute-done.31), channel_id=1, source_target_pairs={{0,16},{16,0},{1,17},{17,1},{2,18},{18,2},{3,19},{19,3},{4,20},{20... | collective-permute-start | bytes 3538952 | tf_op jit(solution)/shard_map/ppermute | solution.py:23
  220.5 35.3 %collective-permute-start.38 = (bf16[288,2304]{1,0:T(8,128)(2,1)}, bf16[288,2304]{1,0:T(8,128)(2,1)}, u32[]{:S(2)}, u32[]{:S(2)}) collective-permute-start(bf16[288,2304]{1,0:T(8,128)(2,1)} %get-tuple-element.952.thin_ref), channel_id=1, source_target_pairs={{0,16},{16,0},{1,17},{17,1},{2,18},{18,2},{3,19},{19,3},{4,20},{20... | collective-permute-start | bytes 3981320 | tf_op jit(solution)/shard_map/ppermute | solution.py:23
  324.3 27.3 %collective-permute-start.45 = (bf16[8,96,768]{2,1,0:T(8,128)(2,1)}, bf16[8,96,768]{2,1,0:T(8,128)(2,1)S(1)}, u32[]{:S(2)}, u32[]{:S(2)}) collective-permute-start(bf16[8,96,768]{2,1,0:T(8,128)(2,1)} %bitcast.59), channel_id=1, source_target_pairs={{0,8},{4,12},{8,0},{12,4},{16,20},{20,16},{24,28},{28,24},{1,9},{5... | collective-permute-start | bytes 3538952 | tf_op jit(solution)/shard_map/ppermute | solution.py:36
  324.8 29.1 %collective-permute-start.43 = (bf16[288,3072]{1,0:T(8,128)(2,1)}, bf16[288,3072]{1,0:T(8,128)(2,1)}, u32[]{:S(2)}, u32[]{:S(2)}) collective-permute-start(bf16[288,3072]{1,0:T(8,128)(2,1)} %get-tuple-element.871.left_ref), channel_id=1, source_target_pairs={{0,16},{16,0},{1,17},{17,1},{2,18},{18,2},{3,19},{19,3},{4,20},{20... | collective-permute-start | bytes 5308424 | tf_op jit(solution)/shard_map/ppermute | solution.py:23
  325.8 28.2 %collective-permute-start.44 = (bf16[288,768]{1,0:T(8,128)(2,1)}, bf16[288,768]{1,0:T(8,128)(2,1)}, u32[]{:S(2)}, u32[]{:S(2)}) collective-permute-start(bf16[288,768]{1,0:T(8,128)(2,1)} %get-tuple-element.859), channel_id=1, source_target_pairs={{0,16},{16,0},{1,17},{17,1},{2,18},{18,2},{3,19},{19,3},{4,20},{20... | collective-permute-start | bytes 1327112 | tf_op jit(solution)/shard_map/ppermute | solution.py:23
  387.7 24.6 %collective-permute-start.52 = (bf16[288,2304]{1,0:T(8,128)(2,1)}, bf16[288,2304]{1,0:T(8,128)(2,1)}, u32[]{:S(2)}, u32[]{:S(2)}) collective-permute-start(bf16[288,2304]{1,0:T(8,128)(2,1)} %get-tuple-element.942.thin_ref), channel_id=1, source_target_pairs={{0,16},{16,0},{1,17},{17,1},{2,18},{18,2},{3,19},{19,3},{4,20},{20... | collective-permute-start | bytes 3981320 | tf_op jit(solution)/shard_map/ppermute | solution.py:23
  389.3 35.1 %collective-permute-start.51 = (bf16[2,96,768]{2,1,0:T(8,128)(2,1)}, bf16[2,96,768]{2,1,0:T(8,128)(2,1)}, u32[]{:S(2)}, u32[]{:S(2)}) collective-permute-start(bf16[2,96,768]{2,1,0:T(8,128)(2,1)} %get-tuple-element.932), channel_id=1, source_target_pairs={{0,2},{1,3},{2,0},{3,1},{4,6},{5,7},{6,4},{7,5},{8,10},{9,11},{10,... | collective-permute-start | bytes 884744 | tf_op jit(solution)/shard_map/ppermute | solution.py:23
  426.0 78.6 %collective-permute-start.59 = (bf16[8,96,768]{2,1,0:T(8,128)(2,1)}, bf16[8,96,768]{2,1,0:T(8,128)(2,1)}, u32[]{:S(2)}, u32[]{:S(2)}) collective-permute-start(bf16[8,96,768]{2,1,0:T(8,128)(2,1)} %bitcast.64), channel_id=1, source_target_pairs={{0,8},{4,12},{8,0},{12,4},{16,20},{20,16},{24,28},{28,24},{1,9},{5... | collective-permute-start | bytes 3538952 | tf_op jit(solution)/shard_map/ppermute | solution.py:36
  428.3 53.2 %collective-permute-start.53 = (f32[96,768]{1,0:T(8,128)}, f32[96,768]{1,0:T(8,128)}, u32[]{:S(2)}, u32[]{:S(2)}) collective-permute-start(f32[96,768]{1,0:T(8,128)} %fusion.29), channel_id=1, source_target_pairs={{0,16},{16,0},{1,17},{17,1},{2,18},{18,2},{3,19},{19,3},{4,20},{20... | collective-permute-start | bytes 884744 | tf_op jit(solution)/shard_map/ppermute | solution.py:23
  448.7 34.0 %collective-permute-start.54 = (bf16[2,4,48,384]{3,2,1,0:T(8,128)(2,1)}, bf16[2,4,48,384]{3,2,1,0:T(8,128)(2,1)}, u32[]{:S(2)}, u32[]{:S(2)}) collective-permute-start(bf16[2,4,48,384]{3,2,1,0:T(8,128)(2,1)} %get-tuple-element.992), channel_id=1, source_target_pairs={{0,2},{1,3},{2,0},{3,1},{4,6},{5,7},{6,4},{7,5},{8,10},{9,11},{10,... | collective-permute-start | bytes 884744 | tf_op jit(solution)/shard_map/ppermute | solution.py:23
  463.0 43.7 %collective-permute-start.58 = (bf16[8,96,768]{2,1,0:T(8,128)(2,1)}, bf16[8,96,768]{2,1,0:T(8,128)(2,1)}, u32[]{:S(2)}, u32[]{:S(2)}) collective-permute-start(bf16[8,96,768]{2,1,0:T(8,128)(2,1)} %bitcast.65), channel_id=1, source_target_pairs={{0,8},{4,12},{8,0},{12,4},{16,20},{20,16},{24,28},{28,24},{1,9},{5... | collective-permute-start | bytes 3538952 | tf_op jit(solution)/shard_map/ppermute | solution.py:36
  481.5 65.5 %collective-permute-start.55 = (bf16[1,96,768]{2,1,0:T(8,128)(2,1)}, bf16[1,96,768]{2,1,0:T(8,128)(2,1)}, u32[]{:S(2)}, u32[]{:S(2)}) collective-permute-start(bf16[1,96,768]{2,1,0:T(8,128)(2,1)} %fusion.26), channel_id=1, source_target_pairs={{0,1},{1,0},{2,3},{3,2},{4,5},{5,4},{6,7},{7,6},{8,9},{9,8},{10,11... | collective-permute-start | bytes 442376 | tf_op jit(solution)/shard_map/ppermute | solution.py:23
  489.4 21.5 %collective-permute-start.56 = (bf16[288,3072]{1,0:T(8,128)(2,1)}, bf16[288,3072]{1,0:T(8,128)(2,1)}, u32[]{:S(2)}, u32[]{:S(2)}) collective-permute-start(bf16[288,3072]{1,0:T(8,128)(2,1)} %get-tuple-element.1012.left_ref), channel_id=1, source_target_pairs={{0,16},{16,0},{1,17},{17,1},{2,18},{18,2},{3,19},{19,3},{4,20},{20... | collective-permute-start | bytes 5308424 | tf_op jit(solution)/shard_map/ppermute | solution.py:23
  517.7 29.4 %collective-permute-start.65 = (bf16[8,4,48,384]{3,2,1,0:T(8,128)(2,1)}, bf16[8,4,48,384]{3,2,1,0:T(8,128)(2,1)S(1)}, u32[]{:S(2)}, u32[]{:S(2)}) collective-permute-start(bf16[8,4,48,384]{3,2,1,0:T(8,128)(2,1)} %get-tuple-element.1048), channel_id=1, source_target_pairs={{0,8},{4,12},{8,0},{12,4},{16,20},{20,16},{24,28},{28,24},{1,9},{5... | collective-permute-start | bytes 3538952 | tf_op jit(solution)/shard_map/ppermute | solution.py:36
  522.5 24.4 %collective-permute-start.74 = (bf16[2,96,768]{2,1,0:T(8,128)(2,1)S(1)}, bf16[2,96,768]{2,1,0:T(8,128)(2,1)S(1)}, u32[]{:S(2)}, u32[]{:S(2)}) collective-permute-start(bf16[2,96,768]{2,1,0:T(8,128)(2,1)S(1)} %get-tuple-element.1067), channel_id=1, source_target_pairs={{0,2},{1,3},{2,0},{3,1},{4,6},{5,7},{6,4},{7,5},{8,10},{9,11},{10,... | collective-permute-start | bytes 884744 | tf_op jit(solution)/shard_map/ppermute | solution.py:23
  (130 other events, 1398.0 us)

commit v4 on v3

v4 whole, which is shorter than its diff:
```python
from functools import partial

import jax
import jax.numpy as jnp
from jax import lax
from jax.experimental import pallas as pl
from jax.experimental.pallas import tpu as pltpu
from jax.sharding import PartitionSpec as P

HD = 32
WINDOW = 7
PADDED = 14
GRID = 12
CELLS = GRID * GRID
EPSILON = 1e-05
F32 = jnp.float32
BF16 = jnp.bfloat16
SCALE = HD ** (-0.5)


def exchange(values, axis, bit):
    pairs = [(index, index ^ bit) for index in range(lax.axis_size(axis))]
    return lax.ppermute(values, axis, pairs)


def sibling(values):
    return exchange(values, "dp", 1)


def cross(values, first):
    hids = lax.axis_size("hid")
    pairs = []
    for core in range(lax.axis_size("dp")):
        bit = 1 if (core % 2 == 0) == first else 2
        pairs += [(core * hids + index, core * hids + (index ^ bit)) for index in range(hids)]
    return lax.ppermute(values, ("dp", "hid"), pairs)


def second_core():
    return lax.rem(lax.axis_index("dp"), 2) == 1


def by_core(own, other, axis):
    second = second_core()
    return jnp.concatenate(
        [jnp.where(second, other, own), jnp.where(second, own, other)], axis=axis
    )


VMEM_LIMIT = 56 * 1024 * 1024
GROUP = 256
HEADS = GROUP // HD


def call(kernel, outs, operands, spaces=(), scratch=(), flops=0, limit=VMEM_LIMIT):
    vmem = pl.BlockSpec(memory_space=pltpu.VMEM)
    specs = [vmem] * len(operands)
    for index, space in spaces:
        specs[index] = pl.BlockSpec(memory_space=space)
    moved = sum(item.size * item.dtype.itemsize for item in list(operands) + list(outs))
    return pl.pallas_call(
        kernel,
        out_shape=list(outs),
        in_specs=specs,
        out_specs=[vmem] * len(outs),
        scratch_shapes=list(scratch),
        compiler_params=pltpu.CompilerParams(vmem_limit_bytes=limit),
        cost_estimate=pl.CostEstimate(flops=1, bytes_accessed=1, transcendentals=0),
    )(*operands)


def struct(shape, dtype):
    return jax.ShapeDtypeStruct(shape, dtype)


def mm(left, right):
    return jnp.dot(left, right, preferred_element_type=F32)


def mm_nt(left, right):
    return lax.dot_general(left, right, (((1,), (1,)), ((), ())), preferred_element_type=F32)


def mm_tn(left, right):
    return lax.dot_general(left, right, (((0,), (0,)), ((), ())), preferred_element_type=F32)


def normalize(values):
    center = jnp.mean(values, axis=1, keepdims=True)
    spread = jnp.mean(values * values, axis=1, keepdims=True) - center * center
    scaled = lax.rsqrt(spread + EPSILON)
    return (values - center) * scaled, scaled


def cells_of(rows):
    cell = lax.broadcasted_iota(jnp.int32, (rows, 1), 0)
    column = lax.rem(cell, GRID)
    line = lax.rem(lax.div(cell, GRID), GRID)
    return line, column


def shift_columns(values):
    rows = values.shape[0]
    _, column = cells_of(rows)
    before = jnp.where(column != 0, pltpu.roll(values, 1, 0), 0.0)
    after = jnp.where(column != GRID - 1, pltpu.roll(values, rows - 1, 0), 0.0)
    return before, after


def shift_lines(values, ahead):
    rows = values.shape[0]
    line, _ = cells_of(rows)
    if ahead:
        return jnp.where(line != GRID - 1, pltpu.roll(values, rows - GRID, 0), 0.0)
    return jnp.where(line != 0, pltpu.roll(values, GRID, 0), 0.0)


def convolve(values, taps):
    before, after = shift_columns(values)
    lines = [
        before * taps[3 * a] + values * taps[3 * a + 1] + after * taps[3 * a + 2] for a in range(3)
    ]
    return shift_lines(lines[0], False) + lines[1] + shift_lines(lines[2], True)


def presence(place_ref, rows, image=None):
    line, column = cells_of(rows)
    if image is not None:
        side = place_ref[3 + image]
    else:
        cell = lax.broadcasted_iota(jnp.int32, (rows, 1), 0)
        side = jnp.zeros((rows, 1), jnp.int32) + place_ref[3]
        for index in range(1, rows // CELLS):
            side = jnp.where(cell >= index * CELLS, place_ref[3 + index], side)
    return jnp.where((line < side) & (column < side), 1.0, 0.0).astype(F32)


def window_mask(place_ref, image):
    side = place_ref[3 + image]
    query = lax.broadcasted_iota(jnp.int32, (CELLS, 1), 0)
    key = lax.broadcasted_iota(jnp.int32, (1, CELLS), 1)
    line, column = lax.div(key, GRID), lax.rem(key, GRID)
    kept = (line < side) & (column < side)

    def window(cell):
        below = lax.div(cell, GRID) >= WINDOW
        right = lax.rem(cell, GRID) >= WINDOW
        return jnp.where(below, 2, 0) + jnp.where(right, 1, 0)

    own = jnp.where(kept, window(key), -1)
    return window(query) == own


LANES = 256


def pack_cells(slots_ref, cells_ref):
    for image in range(cells_ref.shape[0] // CELLS):
        for line in range(GRID):
            cells_ref[pl.ds(image * CELLS + line * GRID, GRID), :] = slots_ref[
                pl.ds((image * PADDED + line) * PADDED, GRID), :
            ]


def unpack_cells(cells_ref, slots_ref):
    slots_ref[...] = jnp.zeros_like(slots_ref)
    for image in range(cells_ref.shape[0] // CELLS):
        for line in range(GRID):
            slots_ref[pl.ds((image * PADDED + line) * PADDED, GRID), :] = cells_ref[
                pl.ds(image * CELLS + line * GRID, GRID), :
            ]


def conv_lanes(values, present, table_ref, base, cut):
    taps = [table_ref[pl.ds(base + i, 1), cut] for i in range(9)]
    return values + present * (convolve(values, taps) + table_ref[pl.ds(base + 9, 1), cut])


def conv_kernel(base, place_ref, values_ref, table_ref, out_ref):
    present = presence(place_ref, values_ref.shape[0])
    for lane in range(0, values_ref.shape[1], LANES):
        cut = pl.ds(lane, LANES)
        out_ref[:, cut] = conv_lanes(values_ref[:, cut], present, table_ref, base, cut)


def first_conv_kernel(base, place_ref, slots_ref, table_ref, start_ref, out_ref):
    pack_cells(slots_ref, start_ref)
    present = presence(place_ref, start_ref.shape[0])
    for lane in range(0, start_ref.shape[1], LANES):
        cut = pl.ds(lane, LANES)
        values = start_ref[:, cut] * present
        start_ref[:, cut] = values
        out_ref[:, cut] = conv_lanes(values, present, table_ref, base, cut)


def conv_back_kernel(base, place_ref, grads_ref, values_ref, table_ref, out_ref, sums_ref, *rest):
    present = presence(place_ref, grads_ref.shape[0])
    target = rest[0] if rest else out_ref
    for lane in range(0, grads_ref.shape[1], LANES):
        cut = pl.ds(lane, LANES)
        grads = grads_ref[:, cut]
        masked = grads * present
        taps = [table_ref[pl.ds(base + 8 - i, 1), cut] for i in range(9)]
        flowing = grads + convolve(masked, taps)
        target[:, cut] = flowing * present if rest else flowing
        values = values_ref[:, cut]
        before, after = shift_columns(values)
        behind = shift_lines(masked, False)
        ahead = shift_lines(masked, True)
        for a, moved in enumerate((ahead, masked, behind)):
            for e, source in enumerate((before, values, after)):
                sums_ref[pl.ds(3 * a + e, 1), cut] = jnp.sum(moved * source, axis=0, keepdims=True)
        sums_ref[pl.ds(9, 1), cut] = jnp.sum(masked, axis=0, keepdims=True)
    if rest:
        unpack_cells(target, out_ref)


SMALL = [(0, pltpu.SMEM)]


def conv(base, place, values, table):
    return call(partial(conv_kernel, base), [struct(values.shape, F32)], [place, values, table], SMALL)[0]


def first_conv(base, place, slots, table):
    cells = struct((slots.shape[0] // (PADDED * PADDED) * CELLS, slots.shape[1]), F32)
    return call(partial(first_conv_kernel, base), [cells, cells], [place, slots, table], SMALL)


def conv_back(base, last, place, grads, values, table):
    rows, width = grads.shape
    images = rows // CELLS
    out = struct((images * PADDED * PADDED if last else rows, width), F32)
    scratch = [pltpu.VMEM((rows, width), F32)] if last else []
    return call(
        partial(conv_back_kernel, base), [out, struct((10, width), F32)], [place, grads, values, table],
        SMALL, scratch=scratch,
    )


def low_kernel(place_ref, slots_ref, cells_ref, low_ref):
    pack_cells(slots_ref, cells_ref)
    low_ref[...] = (cells_ref[...] * presence(place_ref, cells_ref.shape[0])).astype(BF16)


def low_cells(place, slots):
    shape = (slots.shape[0] // (PADDED * PADDED) * CELLS, slots.shape[1])
    return call(low_kernel, [struct(shape, F32), struct(shape, BF16)], [place, slots], SMALL)


UNITS = 768
TILE = 256


def mlp_kernel(
    base_row, place_ref, values_ref, table_ref, upbias_ref,
    u0, u1, u2, u3, d0, d1, d2, d3,
    *rest,
):
    packed = len(rest) == 6
    gain, shift, downbias = (table_ref[pl.ds(base_row + i, 1), :] for i in (13, 14, 15))
    ubias = 0 if base_row == 0 else 1
    out_ref, acted_ref, send_ref, deriv_ref, total_ref = rest[0], rest[1], rest[2], rest[3], rest[4]
    values = values_ref[...]
    normal, _ = normalize(values)
    half = 2 * UNITS
    send_ref[:, half:] = (normal * gain + shift).astype(BF16)
    for index, (up, down) in enumerate(zip((u0, u1, u2, u3), (d0, d1, d2, d3))):
        target = acted_ref if index < 2 else send_ref
        base = (index % 2) * UNITS

        def step(part, _, up=up, target=target, base=base, index=index):
            first = pl.multiple_of(part * TILE, TILE)
            here = pl.ds(pl.multiple_of(index * UNITS + part * TILE, TILE), TILE)
            hidden = mm_nt(send_ref[:, half:], up[pl.ds(first, TILE), :]) + upbias_ref[ubias : ubias + 1, here]
            below = 0.5 + 0.5 * lax.erf(hidden * (0.5**0.5))
            there = pl.ds(pl.multiple_of(base + part * TILE, TILE), TILE)
            target[:, there] = (hidden * below).astype(BF16)
            bell = jnp.exp(hidden * hidden * -0.5) * 0.3989422804014327
            deriv_ref[:, here] = below + hidden * bell
            return 0

        lax.fori_loop(0, UNITS // TILE, step, 0)
        term = mm(target[:, base : base + UNITS], down[...])
        total_ref[...] = term if index == 0 else total_ref[...] + term
    result = values + presence(place_ref, values.shape[0]) * (total_ref[...] + downbias)
    if packed:
        rest[5][...] = result
        unpack_cells(rest[5], out_ref)
    else:
        out_ref[...] = result


def mlp(base, last, place, values, table, upbias, ups, downs):
    rows, width = values.shape
    images = rows // CELLS
    half = 2 * UNITS
    outs = [
        struct((images * PADDED * PADDED if last else rows, width), F32),
        struct((rows, half), BF16),
        struct((rows, half + width), BF16),
        struct((rows, 2 * half), F32),
    ]
    scratch = [pltpu.VMEM((rows, width), F32)] * (2 if last else 1)
    operands = [place, values, table, upbias, *ups, *downs]
    flops = 4 * rows * width * 2 * half
    return call(partial(mlp_kernel, base), outs, operands, SMALL, scratch=scratch, flops=flops)


def norm_back(dn, values, gain, little_ref):
    normal, scaled = normalize(values)
    little_ref[0:1, :] = jnp.sum(dn * normal, axis=0, keepdims=True)
    little_ref[1:2, :] = jnp.sum(dn, axis=0, keepdims=True)
    grad_normal = dn * gain
    first = jnp.mean(grad_normal, axis=1, keepdims=True)
    second = jnp.mean(grad_normal * normal, axis=1, keepdims=True)
    return scaled * (grad_normal - first - normal * second)


def mlp_back_kernel(
    base_row, place_ref, grads_ref, values_ref, table_ref, deriv_ref,
    u0, u1, u2, u3, d0, d1, d2, d3,
    out_ref, hidden_ref, send_ref, little_ref, bias_ref, total_ref,
):
    half = 2 * UNITS
    branch = grads_ref[...] * presence(place_ref, grads_ref.shape[0])
    little_ref[2:3, :] = jnp.sum(branch, axis=0, keepdims=True)
    send_ref[:, half:] = branch.astype(BF16)
    for index, (up, down) in enumerate(zip((u0, u1, u2, u3), (d0, d1, d2, d3))):
        target = hidden_ref if index < 2 else send_ref
        base = (index % 2) * UNITS

        def step(part, _, down=down, target=target, base=base, index=index):
            first = pl.multiple_of(part * TILE, TILE)
            here = pl.ds(pl.multiple_of(index * UNITS + part * TILE, TILE), TILE)
            acted = mm_nt(send_ref[:, half:], down[pl.ds(first, TILE), :])
            hidden = (acted * deriv_ref[:, here]).astype(BF16)
            there = pl.ds(pl.multiple_of(base + part * TILE, TILE), TILE)
            target[:, there] = hidden
            bias_ref[:, here] = jnp.sum(hidden.astype(F32), axis=0, keepdims=True)
            return 0

        lax.fori_loop(0, UNITS // TILE, step, 0)
        term = mm(target[:, base : base + UNITS], up[...])
        total_ref[...] = term if index == 0 else total_ref[...] + term
    gain = table_ref[pl.ds(base_row + 13, 1), :]
    out_ref[...] = grads_ref[...] + norm_back(total_ref[...], values_ref[...], gain, little_ref)


def mlp_back(base, place, grads, values, table, deriv, ups, downs):
    rows, width = values.shape
    half = 2 * UNITS
    outs = [
        struct((rows, width), F32),
        struct((rows, half), BF16),
        struct((rows, half + width), BF16),
        struct((3, width), F32),
        struct((1, 2 * half), F32),
    ]
    scratch = [pltpu.VMEM((rows, width), F32)]
    operands = [place, grads, values, table, deriv, *ups, *downs]
    flops = 4 * rows * width * 2 * half
    return call(partial(mlp_back_kernel, base), outs, operands, SMALL, scratch=scratch, flops=flops)


def pair_grads_kernel(wide_ref, wide_send_ref, thin_ref, thin_send_ref, near_ref, far_ref):
    half = thin_ref.shape[1] - near_ref.shape[1]
    half_send = thin_send_ref.shape[1] - near_ref.shape[1]
    for index, out_ref in enumerate((near_ref, far_ref)):
        cut = pl.ds(index * UNITS, UNITS)
        total = mm_tn(wide_ref[:, cut], thin_ref[:, half:])
        total = total + mm_tn(wide_send_ref[:, cut], thin_send_ref[:, half_send:])
        out_ref[...] = total.astype(BF16)


def pair_grads(wide, wide_send, thin, thin_send):
    width = min(thin.shape[1], UNITS)
    out = struct((UNITS, width), BF16)
    flops = 8 * wide.shape[0] * UNITS * width
    return call(pair_grads_kernel, [out, out], [wide, wide_send, thin, thin_send], flops=flops)


MATS = 4
SWAP = (0, 2, 1, 3)


def load_weights(place_ref, parts, weights_ref, sems):
    core, wid = place_ref[0], place_ref[1]
    copies = []
    for index, part in enumerate(parts):
        side = index // 2
        turn = core if side == 0 else 1 - core
        columns = pl.ds(pl.multiple_of(turn * 384, 384), 384)
        for i in range(2):
            line = 2 * (index % 2) + i
            order = line if side == 0 else SWAP[line]
            for j in range(4):
                first = pl.multiple_of(order * 192 + jnp.bitwise_xor(wid, j) * 48, 16)
                copies.append(
                    pltpu.make_async_copy(
                        part.at[i * 4 + j],
                        weights_ref.at[:, pl.ds(first, 48), columns],
                        sems.at[len(copies)],
                    )
                )
    for copy in copies:
        copy.start()
    return copies


def spread_heads(block):
    lane_head = lax.broadcasted_iota(jnp.int32, (1, GROUP), 1) // HD
    zero = jnp.zeros_like(block)
    return jnp.concatenate([jnp.where(lane_head == h, block, zero) for h in range(HEADS)], axis=0)


def gather_heads(wide):
    lane_head = lax.broadcasted_iota(jnp.int32, (1, GROUP), 1) // HD
    rows = wide.shape[0] // HEADS
    total = jnp.where(lane_head == 0, wide[:rows], 0.0)
    for h in range(1, HEADS):
        total = jnp.where(lane_head == h, wide[h * rows : (h + 1) * rows], total)
    return total


def window_probabilities(queries, keys, mask):
    scores = mm_nt(queries, keys) * SCALE
    scores = scores.reshape(HEADS, CELLS, CELLS)
    scores = jnp.where(mask[None], scores, -1000000000.0)
    raised = jnp.exp(scores - jnp.max(scores, axis=-1, keepdims=True))
    return raised * (1.0 / jnp.sum(raised, axis=-1, keepdims=True))


def channel_probabilities(keys, values):
    scores = mm_tn(keys, values) * SCALE
    line = lax.broadcasted_iota(jnp.int32, (GROUP, GROUP), 0) // HD
    column = lax.broadcasted_iota(jnp.int32, (GROUP, GROUP), 1) // HD
    scores = jnp.where(line == column, scores, -jnp.inf)
    raised = jnp.exp(scores - jnp.max(scores, axis=-1, keepdims=True))
    return raised * (1.0 / jnp.sum(raised, axis=-1, keepdims=True))


def unit_cuts(unit, width):
    groups = width // GROUP
    image = lax.div(unit, groups)
    rows = pl.ds(pl.multiple_of(image * CELLS, 16), CELLS)
    lane = pl.multiple_of(lax.rem(unit, groups) * GROUP, GROUP)
    return image, rows, lane


def attention_kernel(
    windowed, place_ref, values_ref, table_ref, bias_ref,
    p0, p1, p2, p3, out_ref, normed_ref, qkv_ref, mixed_ref, weights_ref, sems,
):
    copies = load_weights(place_ref, (p0, p1, p2, p3), weights_ref, sems)
    rows_all, width = values_ref.shape
    base = 0 if windowed else 16
    gain, shift, outbias = (table_ref[pl.ds(base + i, 1), :] for i in (10, 11, 12))
    first_bias = 0 if windowed else 3
    normal, _ = normalize(values_ref[...])
    normed_ref[...] = (normal * gain + shift).astype(BF16)
    for copy in copies:
        copy.wait()
    for m in range(3):
        projected = mm_nt(normed_ref[...], weights_ref[m])
        projected = projected + bias_ref[pl.ds(first_bias + m, 1), :]
        qkv_ref[:, m * width : (m + 1) * width] = projected.astype(BF16)

    def step(unit, _):
        image, rows, lane = unit_cuts(unit, width)
        queries = qkv_ref[rows, pl.ds(lane, GROUP)]
        keys = qkv_ref[rows, pl.ds(lane + width, GROUP)]
        values = qkv_ref[rows, pl.ds(lane + 2 * width, GROUP)]
        if windowed:
            probs = window_probabilities(spread_heads(queries), keys, window_mask(place_ref, image))
            weights = probs.reshape(HEADS * CELLS, CELLS).astype(BF16)
            mixed = gather_heads(mm(weights, values))
        else:
            kept = keys * presence(place_ref, CELLS, image).astype(BF16)
            weights = channel_probabilities(kept, values).astype(BF16)
            mixed = mm_nt(queries, weights)
        mixed_ref[rows, pl.ds(lane, GROUP)] = mixed.astype(BF16)
        return 0

    lax.fori_loop(0, rows_all // CELLS * (width // GROUP), step, 0)
    branch = mm(mixed_ref[...], weights_ref[3]) + outbias
    out_ref[...] = values_ref[...] + presence(place_ref, rows_all) * branch


def attention(windowed, place, values, table, bias, parts):
    rows, width = values.shape
    outs = [
        struct((rows, width), F32),
        struct((rows, width), BF16),
        struct((rows, 3 * width), BF16),
        struct((rows, width), BF16),
    ]
    operands = [place, values, table, bias, *parts]
    spaces = SMALL + [(4 + i, pl.ANY) for i in range(4)]
    scratch = [pltpu.VMEM((MATS, width, width), BF16), pltpu.SemaphoreType.DMA((32,))]
    return call(
        partial(attention_kernel, windowed), outs, operands, spaces=spaces, scratch=scratch,
        flops=8 * rows * width * width,
    )


def attention_back_kernel(
    windowed, place_ref, grads_ref, values_ref, table_ref, normed_ref, qkv_ref, mixed_ref,
    p0, p1, p2, p3, out_ref, left_ref, mine_ref, theirs_ref, little_ref, bias_ref,
    weights_ref, low_ref, mix_ref, sems,
):
    copies = load_weights(place_ref, (p0, p1, p2, p3), weights_ref, sems)
    rows_all, width = values_ref.shape
    half = width // 2
    core = place_ref[0]
    own = pl.ds(pl.multiple_of(core * half, half), half)
    other = pl.ds(pl.multiple_of((1 - core) * half, half), half)
    branch = grads_ref[...] * presence(place_ref, rows_all)
    little_ref[2:3, :] = jnp.sum(branch, axis=0, keepdims=True)
    low_ref[...] = branch.astype(BF16)
    mine_ref[:, :half] = normed_ref[:, own]
    mine_ref[:, half:] = low_ref[:, own]
    theirs_ref[:, :half] = normed_ref[:, other]
    theirs_ref[:, half:] = low_ref[:, other]
    left_ref[:, 3 * width :] = mixed_ref[...]
    for copy in copies:
        copy.wait()
    mix_ref[...] = mm_nt(low_ref[...], weights_ref[3]).astype(BF16)

    def step(unit, _):
        image, rows, lane = unit_cuts(unit, width)
        queries = qkv_ref[rows, pl.ds(lane, GROUP)]
        keys = qkv_ref[rows, pl.ds(lane + width, GROUP)]
        values = qkv_ref[rows, pl.ds(lane + 2 * width, GROUP)]
        incoming = mix_ref[rows, pl.ds(lane, GROUP)]
        if windowed:
            mask = window_mask(place_ref, image)
            wide_queries = spread_heads(queries)
            wide_incoming = spread_heads(incoming)
            probs = window_probabilities(wide_queries, keys, mask)
            weights = probs.reshape(HEADS * CELLS, CELLS).astype(BF16)
            grad_probs = mm_nt(wide_incoming, values).reshape(HEADS, CELLS, CELLS)
            inner = jnp.sum(probs * grad_probs, axis=-1, keepdims=True)
            grad_scores = jnp.where(mask[None], probs * (grad_probs - inner), 0.0)
            grad_scores = grad_scores.reshape(HEADS * CELLS, CELLS).astype(BF16)
            grad_query = gather_heads(mm(grad_scores, keys)) * SCALE
            grad_keys = mm_tn(grad_scores, wide_queries) * SCALE
            grad_values = mm_tn(weights, wide_incoming)
        else:
            present = presence(place_ref, CELLS, image)
            kept = keys * present.astype(BF16)
            probs = channel_probabilities(kept, values)
            grad_probs = mm_tn(incoming, queries)
            inner = jnp.sum(probs * grad_probs, axis=-1, keepdims=True)
            grad_scores = (probs * (grad_probs - inner)).astype(BF16)
            grad_query = mm(incoming, probs.astype(BF16))
            grad_keys = mm_nt(values, grad_scores) * SCALE * present
            grad_values = mm(kept, grad_scores) * SCALE
        for m, item in enumerate((grad_query, grad_keys, grad_values)):
            left_ref[rows, pl.ds(lane + m * width, GROUP)] = item.astype(BF16)
        return 0

    lax.fori_loop(0, rows_all // CELLS * (width // GROUP), step, 0)
    total = None
    for m in range(3):
        rounded = left_ref[:, m * width : (m + 1) * width]
        bias_ref[m : m + 1, :] = jnp.sum(rounded.astype(F32), axis=0, keepdims=True)
        term = mm(rounded, weights_ref[m])
        total = term if total is None else total + term
    gain = table_ref[pl.ds((0 if windowed else 16) + 10, 1), :]
    out_ref[...] = grads_ref[...] + norm_back(total, values_ref[...], gain, little_ref)


def attention_back(windowed, place, grads, values, table, normed, qkv, mixed, parts):
    rows, width = values.shape
    outs = [
        struct((rows, width), F32),
        struct((rows, 4 * width), BF16),
        struct((rows, width), BF16),
        struct((rows, width), BF16),
        struct((3, width), F32),
        struct((3, width), F32),
    ]
    operands = [place, grads, values, table, normed, qkv, mixed, *parts]
    spaces = SMALL + [(7 + i, pl.ANY) for i in range(4)]
    scratch = [
        pltpu.VMEM((MATS, width, width), BF16),
        pltpu.VMEM((rows, width), BF16),
        pltpu.VMEM((rows, width), BF16),
        pltpu.SemaphoreType.DMA((32,)),
    ]
    return call(
        partial(attention_back_kernel, windowed), outs, operands, spaces=spaces, scratch=scratch,
        flops=10 * rows * width * width,
    )


def head_grads_kernel(place_ref, left_ref, left_send_ref, right_ref, right_send_ref, near_ref, far_ref, table_ref, other_ref):
    wid = place_ref[1]
    width = left_ref.shape[1] // MATS
    half = width // 2
    for m in range(MATS):
        cut = slice(m * width, (m + 1) * width)
        side = slice(0, half) if m < 3 else slice(half, width)
        table_ref[...] = mm_tn(left_ref[:, cut], right_ref[:, side])
        other_ref[...] = mm_tn(left_send_ref[:, cut], right_send_ref[:, side])
        for line in range(4):
            out_ref = near_ref if line < 2 else far_ref
            for j in range(4):
                inner = jnp.bitwise_xor(wid, j) * 48
                mine = table_ref[pl.ds(pl.multiple_of(line * 192 + inner, 16), 48), :]
                other = other_ref[pl.ds(pl.multiple_of(SWAP[line] * 192 + inner, 16), 48), :]
                out_ref[(line % 2) * 4 + j, m] = (mine + other).astype(BF16)


def head_grads(place, left, left_send, right, right_send):
    width = right.shape[1]
    out = struct((8, MATS, width // 16, width // 2), BF16)
    return call(
        head_grads_kernel, [out, out], [place, left, left_send, right, right_send],
        SMALL, scratch=[pltpu.VMEM((width, width // 2), F32)] * 2,
        flops=8 * left.shape[0] * width * width,
    )


def pieces_kernel(place_ref, *refs):
    core = place_ref[0]
    for base in (0, 4):
        inw, outw, up, down = refs[base : base + 4]
        outs = refs[8 + base // 4 * 3 : 11 + base // 4 * 3]
        half = inw.shape[2] // 2
        columns = pl.ds(pl.multiple_of(core * half, half), half)
        for m in range(3):
            outs[0][0, m] = inw[m, :, columns]
        outs[0][0, 3] = outw[:, columns]
        rows = up.shape[0] // 2
        own = pl.ds(pl.multiple_of(core * rows, rows), rows)
        outs[1][0] = up[own, :]
        outs[2][0] = down[own, :]


def pieces(place, *weights):
    outs = []
    for base in (0, 4):
        inw, _, up, _ = weights[base : base + 4]
        outs.append(struct((1, MATS, inw.shape[1], inw.shape[2] // 2), BF16))
        outs += [struct((1, up.shape[0] // 2, up.shape[1]), BF16)] * 2
    return call(pieces_kernel, outs, [place, *weights], SMALL)


def table_kernel(*refs):
    inputs, (table_ref, bias_ref) = refs[:20], refs[20:]
    for base in (0, 1):
        kernel, cbias, gain, shift, inb, outb, gain_two, shift_two, upb, downb = inputs[base * 10 : base * 10 + 10]
        table_ref[pl.ds(base * 16, 9), :] = kernel[...]
        for index, item in enumerate((cbias, gain, shift, outb, gain_two, shift_two, downb)):
            table_ref[pl.ds(base * 16 + 9 + index, 1), :] = item[...].reshape(1, -1)
        first = 0 if base == 0 else 6
        count = inb.shape[0]
        bias_ref[pl.ds(first, count), :] = inb[...]
        wide = upb[...].reshape(1, -1)
        step = wide.shape[1] // 4
        for index in range(4):
            bias_ref[pl.ds(first + count + index, 1), :] = wide[:, index * step : (index + 1) * step]
    bias_ref[pl.ds(13, 3), :] = jnp.zeros((3, bias_ref.shape[1]), F32)


def tables(*small):
    width = small[0].shape[1]
    return call(table_kernel, [struct((32, width), F32), struct((16, small[4].shape[1]), F32)], list(small))


def order_kernel(place_ref, g0, g1, g2, head_ref, hidden_ref):
    core, wid = place_ref[0], place_ref[1]
    hids = [g0, g1, g2.at[0], g2.at[1]]
    step = g0.shape[1]
    half = step // 2
    head_ref[...] = jnp.zeros_like(head_ref)
    hidden_ref[...] = jnp.zeros_like(hidden_ref)
    for row, source in ((0, 0), (2, 1), (3, 6), (4, 7), (5, 8)):
        for i in range(4):
            head_ref[row : row + 1, i * step : (i + 1) * step] = hids[i][source : source + 1, :]
    for index, first in ((0, 2), (1, 9)):
        for side in range(2):
            for i in range(4):
                hid = hids[i if side == 0 else SWAP[i]]
                for j in range(4):
                    line = hid[pl.ds(first + jnp.bitwise_xor(wid, j), 1), :]
                    value = jnp.where(core == side, line[:, :half], line[:, half:])
                    lane = side * 16 * half + (i * 4 + j) * half
                    hidden_ref[index : index + 1, lane : lane + half] = value


def order_biases(place, g0, g1, g2):
    step = g0.shape[1]
    outs = [struct((8, 4 * step), F32), struct((8, 16 * step), F32)]
    return call(order_kernel, outs, [place, g0, g1, g2], SMALL)


BIASES = 16


def small_kernel(counts, kinds, place_ref, *refs):
    out_ref = refs[-1]
    core, wid, hid = place_ref[0], place_ref[1], place_ref[2]
    out_ref[...] = jnp.zeros_like(out_ref)
    row = 0
    for count, ref in zip(counts, refs):
        out_ref[pl.ds(row, count), :] = ref[...]
        row += count
    base = out_ref.shape[0] - BIASES
    rest = refs[len(counts) : -1]
    heads, hiddens = rest[0], rest[1:]
    step = heads.shape[1] // 4
    half = step // 2
    gap = jnp.zeros((1, 256 - step), F32)
    blank = jnp.zeros((1, half), F32)
    for i in range(4):
        owned = jnp.bitwise_xor(hid, jnp.where(core == 0, i, SWAP[i]))
        for j in range(4):
            parts = []
            for ref in hiddens:
                lane = (i * 4 + j) * half
                mine = ref[0:1, lane : lane + half]
                lane = 16 * half + (SWAP[i] * 4 + j) * half
                other = ref[0:1, lane : lane + half]
                parts += [jnp.where(core == 0, mine, other), jnp.where(core == 0, other, mine), gap]
            for _ in range(2 - len(hiddens)):
                parts += [blank, blank, gap]
            line = pl.ds(base + owned * 4 + jnp.bitwise_xor(wid, j), 1)
            out_ref[line, 0:512] = jnp.concatenate(parts, axis=1)
        for place_of, kind in enumerate(kinds):
            line = pl.ds(base + owned * 4 + place_of, 1)
            value = heads[kind : kind + 1, i * step : (i + 1) * step]
            out_ref[line, 512:768] = jnp.concatenate([value, gap], axis=1)


def small_table(kinds, place, rows, heads, hiddens):
    counts = [item.shape[0] for item in rows]
    total = (sum(counts) + 7) // 8 * 8 + BIASES
    return call(
        partial(small_kernel, counts, kinds), [struct((total, rows[0].shape[1]), F32)],
        [place, *rows, heads, *hiddens], SMALL,
    )[0]


def outputs_kernel(place_ref, early_ref, late_ref, *outs):
    hid = place_ref[2]
    early_base = early_ref.shape[0] - BIASES
    late_base = late_ref.shape[0] - BIASES
    plan = (
        (outs[:10], late_ref, 0, late_ref, 10, late_base, early_ref, 10, 0),
        (outs[10:], early_ref, 0, early_ref, 13, early_base, early_ref, 16, 1),
    )
    for refs, sums, first, one, at_one, heads_base, two, at_two, column in plan:
        kernel, cbias, gain, shift, inb, outb, gain_two, shift_two, upb, downb = refs
        heads = late_ref if column == 0 else early_ref
        kernel[...] = sums[pl.ds(first, 9), :]
        for ref, source, row in (
            (cbias, sums, 9), (gain, one, at_one), (shift, one, at_one + 1), (outb, one, at_one + 2),
            (gain_two, two, at_two), (shift_two, two, at_two + 1), (downb, two, at_two + 2),
        ):
            ref[...] = source[pl.ds(row, 1), :].reshape(-1)
        step = inb.shape[1]
        for index in range(inb.shape[0]):
            inb[pl.ds(index, 1), :] = heads[pl.ds(heads_base + hid * 4 + index, 1), :][:, 512 : 512 + step]
        for index in range(4):
            line = early_ref[pl.ds(early_base + hid * 4 + index, 1), :]
            upb[pl.ds(index * step, step)] = line[:, column * 256 : column * 256 + step].reshape(-1)


def small_outputs(place, early, late):
    width = early.shape[1]
    step = width // 4
    outs = []
    for count in (2, 3):
        flat = struct((width,), F32)
        outs += [struct((9, width), F32), flat, flat, flat, struct((count, step), F32), flat, flat, flat, flat, flat]
    return call(outputs_kernel, outs, [place, early, late], SMALL)


class Line:
    def __init__(self, mark):
        self.mark = mark

    def gate(self, tree):
        tree, self.mark = lax.optimization_barrier((tree, self.mark))
        return tree

    def run(self, function, *operands):
        return self.gate(function(*self.gate(operands)))


class Gather:
    def __init__(self, line, piece):
        self.line, self.near, self.step, self.flight = line, piece, 0, ()

    def advance(self):
        gate = self.line.gate
        if self.step in (1, 2, 3):
            arrived = gate(self.flight[0])
            self.near = jnp.concatenate([self.near, arrived], axis=0)
        elif self.step == 4:
            self.far, self.other_near = gate(self.flight)
        elif self.step == 5:
            self.other_far = gate(self.flight[0])
        if self.step < 4:
            self.near = gate(self.near)
        if self.step == 0:
            self.flight = (exchange(self.near, "wid", 1),)
        elif self.step == 1:
            self.flight = (exchange(self.near, "wid", 2),)
        elif self.step == 2:
            self.flight = (cross(self.near, True),)
        elif self.step == 3:
            self.flight = (cross(self.near, False), sibling(self.near))
        elif self.step == 4:
            self.far = gate(self.far)
            self.flight = (sibling(self.far),)
        self.step += 1

    def parts(self):
        return [self.near, self.far, self.other_near, self.other_far]

    def rows(self):
        return [part.reshape(-1, part.shape[-1]) for part in self.parts()]


class Scatter:
    def __init__(self, line, near, far, axis):
        self.line, self.kept, self.sent, self.axis, self.step = line, near, far, axis, 0

    def advance(self):
        gate = self.line.gate
        if self.step in (1, 2, 3):
            arrived = gate(self.flight)
            half = arrived.shape[0] // 2
            self.sent = (self.kept[half:].astype(F32) + arrived[half:].astype(F32)).astype(BF16)
            self.kept = self.kept[:half].astype(F32) + arrived[:half].astype(F32)
        elif self.step == 4:
            total = self.kept[0] + gate(self.flight)[0].astype(F32)
            bit = 2
            while bit < lax.axis_size("dp"):
                total = total + exchange(total, "dp", bit)
                bit *= 2
            self.kept = total
        elif self.step == 5:
            self.total = by_core(self.kept, gate(self.flight), self.axis)
        if self.step < 4:
            self.sent = gate(self.sent)
        if self.step == 0:
            self.flight = cross(self.sent, False)
        elif self.step == 1:
            self.flight = cross(self.sent, True)
        elif self.step == 2:
            self.flight = exchange(self.sent, "wid", 2)
        elif self.step == 3:
            self.flight = exchange(self.sent, "wid", 1)
        elif self.step == 4:
            self.flight = sibling(gate(self.kept))
        self.step += 1


class Small:
    def __init__(self, line, table):
        self.line, self.table, self.flight = line, table, None
        self.steps = []
        for axis in ("dp", "hid", "wid"):
            bit = 1
            while bit < lax.axis_size(axis):
                self.steps.append((axis, bit))
                bit *= 2

    def advance(self):
        if self.flight is not None:
            self.table = self.table + self.line.gate(self.flight)
            self.flight = None
        if self.steps:
            axis, bit = self.steps.pop(0)
            self.table = self.line.gate(self.table)
            self.flight = exchange(self.table, axis, bit)
            return True
        return False


def body(
    inputs, grid_sizes, cotangent,
    wkernel, wcbias, wgain, wshift, winw, winb, woutw, woutb,
    wgain_two, wshift_two, wupw, wupb, wdownw, wdownb,
    ckernel, ccbias, cgain, cshift, cinw, cinb, coutw, coutb,
    cgain_two, cshift_two, cupw, cupb, cdownw, cdownb,
):
    image_count = inputs.shape[0] // (PADDED * PADDED)
    hid, wid = lax.axis_index("hid"), lax.axis_index("wid")
    own_sizes = lax.dynamic_slice_in_dim(
        grid_sizes, (hid * lax.axis_size("wid") + wid) * image_count, image_count, 0
    )
    at = jnp.stack([lax.rem(lax.axis_index("dp"), 2), wid, hid]).astype(jnp.int32)
    place = jnp.concatenate([at, own_sizes])
    line = Line(winb[0, 0])

    groups = [
        Gather(line, piece)
        for piece in pieces(place, winw, woutw, wupw, wdownw, cinw, coutw, cupw, cdownw)
    ]

    def go(*numbers):
        for number in numbers:
            groups[number].advance()

    go(0)
    table, bias = line.run(
        tables, wkernel, wcbias, wgain, wshift, winb, woutb, wgain_two, wshift_two, wupb, wdownb,
        ckernel, ccbias, cgain, cshift, cinb, coutb, cgain_two, cshift_two, cupb, cdownb,
    )
    go(0, 1)
    bias_one = cross(bias, True)
    start, after_conv = line.run(partial(first_conv, 0), place, inputs, table)
    cotangent, low_four = line.run(low_cells, place, cotangent)
    bias_one = line.gate(bias_one)
    bias_two = cross(jnp.stack([bias, bias_one]), False)
    low_four_other = sibling(low_four)
    go(1, 2)
    go(0, 2, 3)
    bias_two, low_four_other = line.gate((bias_two, low_four_other))
    head_bias, hidden_bias = line.run(order_biases, place, bias, bias_one, bias_two)
    go(0)
    go(1, 3, 4)
    go(0, 1, 0)
    att_one = groups[0].parts()
    after_attn, normed_one, qkv_one, mixed_one = line.run(
        partial(attention, True), place, after_conv, table, head_bias, att_one
    )
    go(2, 4, 5)
    go(1, 2, 3, 5, 2, 1, 3, 2)
    ups_two, downs_two = groups[1].rows(), groups[2].rows()
    after_mlp, acted_two, fpack_two, deriv_two = line.run(
        partial(mlp, 0, False), place, after_attn, table, hidden_bias, ups_two, downs_two
    )
    fpack_two_other = sibling(fpack_two)
    go(4, 3, 4, 5)
    after_conv_c = line.run(partial(conv, 16), place, after_mlp, table)
    go(3, 5)
    att_three = groups[3].parts()
    after_attn_c, normed_three, qkv_three, mixed_three = line.run(
        partial(attention, False), place, after_conv_c, table, head_bias, att_three
    )
    fpack_two_other = line.gate(fpack_two_other)
    go(4, 5, 4, 5)
    ups_four, downs_four = groups[4].rows(), groups[5].rows()
    outputs, acted_four, fpack_four, deriv_four = line.run(
        partial(mlp, 16, True), place, after_attn_c, table, hidden_bias, ups_four, downs_four
    )

    def scatter(near, far, axis):
        group = Scatter(line, near.reshape((8, -1) + near.shape[-1:] if axis == 0 else near.shape),
                        far.reshape((8, -1) + far.shape[-1:] if axis == 0 else far.shape), axis)
        group.advance()
        return group

    fpack_four_other = line.gate(sibling(fpack_four))
    d_four = scatter(*line.run(pair_grads, acted_four, fpack_four_other, low_four, low_four_other), 0)
    flowing, gh_four, bpack_four, little_four, upb_four = line.run(
        partial(mlp_back, 16), place, cotangent, after_attn_c, table, deriv_four, ups_four, downs_four
    )
    bpack_four_other = sibling(bpack_four)
    d_four.advance()
    bpack_four_other = line.gate(bpack_four_other)
    u_four = scatter(*line.run(pair_grads, gh_four, bpack_four_other, fpack_four, fpack_four_other), 0)
    d_four.advance()
    flowing, left_three, mine_three, theirs_three, little_three, inb_three = line.run(
        partial(attention_back, False),
        place, flowing, after_conv_c, table, normed_three, qkv_three, mixed_three, att_three,
    )
    sent_three = sibling(left_three), sibling(theirs_three)
    u_four.advance()
    sent_three = line.gate(sent_three)
    a_three = scatter(*line.run(head_grads, place, left_three, sent_three[0], mine_three, sent_three[1]), 2)
    d_four.advance()
    u_four.advance()
    flowing, sums_three = line.run(partial(conv_back, 16, False), place, flowing, after_mlp, table)
    flowing, gh_two, bpack_two, little_two, upb_two = line.run(
        partial(mlp_back, 0), place, flowing, after_attn, table, deriv_two, ups_two, downs_two
    )
    bpack_two_other = sibling(bpack_two)
    a_three.advance()
    bpack_two_other = line.gate(bpack_two_other)
    d_two = scatter(*line.run(pair_grads, acted_two, fpack_two_other, bpack_two, bpack_two_other), 0)
    u_four.advance()
    d_four.advance()
    a_three.advance()
    u_two = scatter(*line.run(pair_grads, gh_two, bpack_two_other, fpack_two, fpack_two_other), 0)
    early = line.run(
        partial(small_table, (0, 1, 2)), place,
        [sums_three, little_two, little_three, little_four], inb_three, [upb_two, upb_four],
    )
    early = Small(line, early)
    early.advance()
    u_four.advance()
    flowing, left_one, mine_one, theirs_one, little_one, inb_one = line.run(
        partial(attention_back, True),
        place, flowing, after_conv, table, normed_one, qkv_one, mixed_one, att_one,
    )
    sent_one = sibling(left_one), sibling(theirs_one)
    d_two.advance()
    a_three.advance()
    early.advance()
    sent_one = line.gate(sent_one)
    a_one = scatter(*line.run(head_grads, place, left_one, sent_one[0], mine_one, sent_one[1]), 2)
    u_two.advance()
    d_two.advance()
    early.advance()
    input_grad, sums_one = line.run(partial(conv_back, 0, True), place, flowing, start, table)
    late = Small(line, line.run(partial(small_table, (0, 2)), place, [sums_one, little_one], inb_one, []))
    early.advance()
    late.advance()
    a_three.advance()
    u_two.advance()
    late.advance()
    early.advance()
    a_one.advance()
    late.advance()
    d_two.advance()
    early.advance()
    a_one.advance()
    late.advance()
    u_two.advance()
    late.advance()
    a_one.advance()
    u_two.advance()
    while late.advance():
        pass
    while early.advance():
        pass
    small = line.run(small_outputs, place, early.table, late.table)
    for group in (d_four, u_four, a_three, d_two, u_two, a_one):
        while group.step < 6:
            group.advance()
    gatt_one, gatt_three = a_one.total, a_three.total

    def ordered(small, attention, up, down):
        return (
            *small[:4], attention[:3], small[4], attention[3], *small[5:8], up.total, small[8], down.total, small[9]
        )

    return (
        outputs, input_grad,
        *ordered(small[:10], gatt_one, u_two, d_two),
        *ordered(small[10:], gatt_three, u_four, d_four),
    )


def solution(mesh):
    tokens, everywhere = P(("dp", "hid", "wid"), None), P()
    stacked, rows = P(None, ("hid", "wid"), None), P(("hid", "wid"), None)
    block = (
        everywhere, everywhere, everywhere, everywhere, stacked, P(None, "hid"), rows, everywhere,
        everywhere, everywhere, rows, P("hid"), rows, everywhere,
    )
    return jax.shard_map(
        body,
        mesh=mesh,
        in_specs=(tokens, P("dp"), tokens) + block + block,
        out_specs=(tokens, tokens) + block + block,
        check_vma=False,
    )
```

time: 592 us -> 459 us (0.78)
  local copies, waits for them, and re-layouts: 89.2 us -> 11.9 us
  waiting for transfers between devices: 201 us -> 143 us
  other arithmetic: 63.7 us -> 28.6 us
  starting transfers between devices: 59.2 us -> 91.9 us
  Pallas kernels: 166 us -> 176 us
    ppermute x57 -> x61, waiting for transfers between devices: 171 us -> 113 us  [exchange(): return lax.ppermute(values, axis, pairs)]
    ppermute x57 -> x61, starting transfers between devices: 43.3 us -> 67.5 us  [exchange(): return lax.ppermute(values, axis, pairs)]
    concatenate x39 -> x0, local copies, waits for them, and re-layouts: 19.6 us -> none  [the longest x18 12.1 us: flip(): jnp.concatenate([parts[i ^ bit] for i in range(length)], axis=axis)]
    broadcast_in_dim x18 -> x0, local copies, waits for them, and re-layouts: 18 us -> none  [the longest x2 2.53 us: attention(): shift[None]]
    slice x61 -> x0, local copies, waits for them, and re-layouts: 14.6 us -> none  [the longest x28 4.3 us: flip(): lax.slice_in_dim(values, i, i + 1, axis=axis)]
    concatenate x23 -> x1, other arithmetic: 11.7 us -> 0.61 us  [body(): place = jnp.concatenate([at, own_sizes])]
    concatenate x18, other arithmetic: 13.8 us -> 3.19 us  [advance(): self.near = jnp.concatenate([self.near, arrived], axis=0)]
    optimization_barrier x12 -> x0, local copies, waits for them, and re-layouts: 9.91 us -> none  [gate(): tree, self.mark = lax.optimization_barrier((tree, self.mark))]
  transfers between devices with their start and end apart: 81 -> 87, of which waited for: 29 -> 33; matrix products, arithmetic and copies ran while one was open for 21% -> 5% of each run, Pallas kernels for 17% -> 34%
where the time goes in v4:
time: 459 us; the launch traced here: 453 us
  Pallas kernels  176 us (38%)
  waiting for transfers between devices  143 us (31%)
  starting transfers between devices  91.9 us (20%)
  other arithmetic  28.6 us (6%)
  local copies, waits for them, and re-layouts  11.9 us (3%)
    pallas_call x25, Pallas kernels, call(): pl.pallas_call(kernel, out_shape=list(outs), in_specs=specs, out_specs=[v...  176 us
    ppermute x61, waiting for transfers between devices, exchange(): return lax.ppermute(values, axis, pairs)  113 us
    ppermute x61, starting transfers between devices, exchange(): return lax.ppermute(values, axis, pairs)  67.5 us
    ppermute x26, waiting for transfers between devices, cross(): return lax.ppermute(values, ('dp', 'hid'), pairs)  30 us
    ppermute x26, starting transfers between devices, cross(): return lax.ppermute(values, ('dp', 'hid'), pairs)  24.4 us
    unnamed x108, local copies, waits for them, and re-layouts  10.9 us
  transfers between devices with their start and end apart: 87, of which 33 were waited for; matrix products, arithmetic and copies ran while one was open for 5% of the time, Pallas kernels for 34%

profile of v4, /device:TPU:1, one launch (start us, length us, event | category | flops | bytes accessed | tf_op | source)
XLA Modules:
  0.0 453.1 jit_solution(5690489937265558611)
XLA Ops:
  16.1 4.4 shard_map.528
  43.2 11.9 %collective-permute-done.11 = bf16[2,96,768]{2,1,0:T(8,128)(2,1)S(1)} collective-permute-done((bf16[2,96,768]{2,1,0:T(8,128)(2,1)S(1)}, bf16[2,96,768]{2,1,0:T(8,128)(2,1)S(1)}, u32[]{:S(2)}, u32[]{:S(2)}) %collective-permute-start.11) | collective-permute-done | bytes 294944 | tf_op jit(solution)/shard_map/ppermute | solution.py:23
  57.5 7.4 %collective-permute-done.13 = bf16[4,96,768]{2,1,0:T(8,128)(2,1)S(1)} collective-permute-done((bf16[4,96,768]{2,1,0:T(8,128)(2,1)S(1)}, bf16[4,96,768]{2,1,0:T(8,128)(2,1)S(1)}, u32[]{:S(2)}, u32[]{:S(2)}) %collective-permute-start.13) | collective-permute-done | bytes 589856 | tf_op jit(solution)/shard_map/ppermute | solution.py:36
  68.1 12.7 %shard_map.531 = (f32[288,768]{1,0:T(8,128)}, bf16[288,768]{1,0:T(8,128)(2,1)}, bf16[288,2304]{1,0:T(8,128)(2,1)}, bf16[288,768]{1,0:T(8,128)(2,1)}) custom-call(s32[5]{0:T(128)} %pad_add_fusion.place_ref, f32[288,768]{1,0:T(8,128)} %get-tuple-element.1153.values_ref, f32[32,768]{1,0:T(8,128)} %get-tuple-element.1218.table_ref, ...), custom_call_target="tpu_custom_call" | custom-call | flops 1 | bytes 1 | tf_op jit(solution)/shard_map/pallas_call | solution.py:61
  96.3 14.9 %collective-permute-done.23 = bf16[2,4,48,384]{3,2,1,0:T(8,128)(2,1)S(1)} collective-permute-done((bf16[2,4,48,384]{3,2,1,0:T(8,128)(2,1)S(1)}, bf16[2,4,48,384]{3,2,1,0:T(8,128)(2,1)S(1)}, u32[]{:S(2)}, u32[]{:S(2)}) %collective-permute-start.23) | collective-permute-done | bytes 294944 | tf_op jit(solution)/shard_map/ppermute | solution.py:23
  112.7 4.7 %collective-permute-done.22 = bf16[1,96,768]{2,1,0:T(8,128)(2,1)S(1)} collective-permute-done((bf16[1,96,768]{2,1,0:T(8,128)(2,1)S(1)}, bf16[1,96,768]{2,1,0:T(8,128)(2,1)S(1)}, u32[]{:S(2)}, u32[]{:S(2)}) %collective-permute-start.22) | collective-permute-done | bytes 147488 | tf_op jit(solution)/shard_map/ppermute | solution.py:23
  124.2 13.3 %shard_map.532 = (f32[288,768]{1,0:T(8,128)}, bf16[288,1536]{1,0:T(8,128)(2,1)}, bf16[288,2304]{1,0:T(8,128)(2,1)}, f32[288,3072]{1,0:T(8,128)}) custom-call(s32[5]{0:T(128)} %pad_add_fusion.place_ref, f32[288,768]{1,0:T(8,128)} %get-tuple-element.1065.values_ref, f32[32,768]{1,0:T(8,128)} %get-tuple-element.1218.table_ref, ...), custom_call_target="tpu_custom_call" | custom-call | flops 1 | bytes 1 | tf_op jit(solution)/shard_map/pallas_call | solution.py:61
  142.0 5.1 %collective-permute-done.28 = bf16[4,96,768]{2,1,0:T(8,128)(2,1)S(1)} collective-permute-done((bf16[4,96,768]{2,1,0:T(8,128)(2,1)S(1)}, bf16[4,96,768]{2,1,0:T(8,128)(2,1)S(1)}, u32[]{:S(2)}, u32[]{:S(2)}) %collective-permute-start.28) | collective-permute-done | bytes 589856 | tf_op jit(solution)/shard_map/ppermute | solution.py:36
  147.3 8.2 %collective-permute-done.26 = bf16[2,96,768]{2,1,0:T(8,128)(2,1)S(1)} collective-permute-done((bf16[2,96,768]{2,1,0:T(8,128)(2,1)S(1)}, bf16[2,96,768]{2,1,0:T(8,128)(2,1)S(1)}, u32[]{:S(2)}, u32[]{:S(2)}) %collective-permute-start.26) | collective-permute-done | bytes 294944 | tf_op jit(solution)/shard_map/ppermute | solution.py:23
  161.4 6.8 %collective-permute-done.32 = bf16[4,96,768]{2,1,0:T(8,128)(2,1)} collective-permute-done((bf16[4,96,768]{2,1,0:T(8,128)(2,1)S(1)}, bf16[4,96,768]{2,1,0:T(8,128)(2,1)}, u32[]{:S(2)}, u32[]{:S(2)}) %collective-permute-start.32) | collective-permute-done | bytes 589856 | tf_op jit(solution)/shard_map/ppermute | solution.py:36
  174.4 10.4 %shard_map.534 = (f32[288,768]{1,0:T(8,128)}, bf16[288,768]{1,0:T(8,128)(2,1)}, bf16[288,2304]{1,0:T(8,128)(2,1)}, bf16[288,768]{1,0:T(8,128)(2,1)}) custom-call(s32[5]{0:T(128)} %pad_add_fusion.place_ref, f32[288,768]{1,0:T(8,128)} %shard_map.533.values_ref, f32[32,768]{1,0:T(8,128)} %get-tuple-element.1218.table_ref, ...), custom_call_target="tpu_custom_call" | custom-call | flops 1 | bytes 1 | tf_op jit(solution)/shard_map/pallas_call | solution.py:61
  185.2 5.7 %collective-permute-done.37 = bf16[8,96,768]{2,1,0:T(8,128)(2,1)S(1)} collective-permute-done((bf16[8,96,768]{2,1,0:T(8,128)(2,1)S(1)}, bf16[8,96,768]{2,1,0:T(8,128)(2,1)S(1)}, u32[]{:S(2)}, u32[]{:S(2)}) %collective-permute-start.37) | collective-permute-done | bytes 1179680 | tf_op jit(solution)/shard_map/ppermute | solution.py:36
  194.7 13.9 %shard_map.535 = (f32[392,768]{1,0:T(8,128)}, bf16[288,1536]{1,0:T(8,128)(2,1)}, bf16[288,2304]{1,0:T(8,128)(2,1)}, f32[288,3072]{1,0:T(8,128)}) custom-call(s32[5]{0:T(128)} %pad_add_fusion.place_ref, f32[288,768]{1,0:T(8,128)} %get-tuple-element.958.values_ref, f32[32,768]{1,0:T(8,128)} %get-tuple-element.1218.table_ref, ...), custom_call_target="tpu_custom_call" | custom-call | flops 1 | bytes 1 | tf_op jit(solution)/shard_map/pallas_call | solution.py:61
  213.0 5.5 %shard_map.536 = (bf16[768,768]{1,0:T(8,128)(2,1)}, bf16[768,768]{1,0:T(8,128)(2,1)}) custom-call(bf16[288,1536]{1,0:T(8,128)(2,1)} %get-tuple-element.946.wide_ref, bf16[288,2304]{1,0:T(8,128)(2,1)} %copy-done.8, bf16[288,768]{1,0:T(8,128)(2,1)} %get-tuple-element.948.thin_ref, bf16[288,768]{1,0:T(8,128)(2,1)} %copy-done.40), custom_call_target="tpu_custom_call" | custom-call | flops 1 | bytes 1 | tf_op jit(solution)/shard_map/pallas_call | solution.py:61
  219.3 12.9 %shard_map.537 = (f32[288,768]{1,0:T(8,128)}, bf16[288,1536]{1,0:T(8,128)(2,1)}, bf16[288,2304]{1,0:T(8,128)(2,1)}, f32[3,768]{1,0:T(4,128)}, f32[1,3072]{1,0:T(1,128)}) custom-call(s32[5]{0:T(128)} %pad_add_fusion.place_ref, f32[288,768]{1,0:T(8,128)} %get-tuple-element.957.grads_ref, f32[288,768]{1,0:T(8,128)} %get-tuple-element.958.values_ref, ...), custom_call_target="tpu_custom_call" | custom-call | flops 1 | bytes 1 | tf_op jit(solution)/shard_map/pallas_call | solution.py:61
  236.6 6.1 %shard_map.538 = (bf16[768,768]{1,0:T(8,128)(2,1)}, bf16[768,768]{1,0:T(8,128)(2,1)}) custom-call(bf16[288,1536]{1,0:T(8,128)(2,1)} %get-tuple-element.990.wide_ref, bf16[288,2304]{1,0:T(8,128)(2,1)} %copy-done.29, bf16[288,2304]{1,0:T(8,128)(2,1)} %get-tuple-element.992.thin_ref, bf16[288,2304]{1,0:T(8,128)(2,1)} %copy-done.8), custom_call_target="tpu_custom_call" | custom-call | flops 1 | bytes 1 | tf_op jit(solution)/shard_map/pallas_call | solution.py:61
  243.7 12.6 %shard_map.539 = (f32[288,768]{1,0:T(8,128)}, bf16[288,3072]{1,0:T(8,128)(2,1)}, bf16[288,768]{1,0:T(8,128)(2,1)}, bf16[288,768]{1,0:T(8,128)(2,1)}, f32[3,768]{1,0:T(4,128)}, /*index=5*/f32[3,768]{1,0:T(4,128)}) custom-call(s32[5]{0:T(128)} %pad_add_fusion.place_ref, f32[288,768]{1,0:T(8,128)} %get-tuple-element.1004.grads_ref, ...), custom_call_target="tpu_custom_call" | custom-call | flops 1 | bytes 1 | tf_op jit(solution)/shard_map/pallas_call | solution.py:61
  264.0 6.9 %shard_map.540 = (bf16[8,4,48,384]{3,2,1,0:T(8,128)(2,1)}, bf16[8,4,48,384]{3,2,1,0:T(8,128)(2,1)}) custom-call(s32[5]{0:T(128)} %pad_add_fusion.place_ref, bf16[288,3072]{1,0:T(8,128)(2,1)} %get-tuple-element.1037.left_ref, bf16[288,3072]{1,0:T(8,128)(2,1)} %copy-done.28, bf16[288,768]{1,0:T(8,128)(2,1)} %get-tuple-element.1039.right_ref, ...), custom_call_target="tpu_custom_call" | custom-call | flops 1 | bytes 1 | tf_op jit(solution)/shard_map/pallas_call | solution.py:61
  270.9 5.4 %collective-permute-done.46 = bf16[2,96,768]{2,1,0:T(8,128)(2,1)S(1)} collective-permute-done((bf16[2,96,768]{2,1,0:T(8,128)(2,1)S(1)}, bf16[2,96,768]{2,1,0:T(8,128)(2,1)S(1)}, u32[]{:S(2)}, u32[]{:S(2)}) %collective-permute-start.46) | collective-permute-done | bytes 294944 | tf_op jit(solution)/shard_map/ppermute | solution.py:23
  277.3 4.7 %shard_map.541 = (f32[288,768]{1,0:T(8,128)}, f32[10,768]{1,0:T(8,128)}) custom-call(s32[5]{0:T(128)} %pad_add_fusion.place_ref, f32[288,768]{1,0:T(8,128)} %get-tuple-element.1054.grads_ref, f32[288,768]{1,0:T(8,128)} %get-tuple-element.1055.values_ref, f32[32,768]{1,0:T(8,128)} %get-tuple-element.1218.table_ref), custom_call_target="tpu_custom_call" | custom-call | flops 1 | bytes 1 | tf_op jit(solution)/shard_map/pallas_call | solution.py:61
  282.0 13.2 %shard_map.542 = (f32[288,768]{1,0:T(8,128)}, bf16[288,1536]{1,0:T(8,128)(2,1)}, bf16[288,2304]{1,0:T(8,128)(2,1)}, f32[3,768]{1,0:T(4,128)}, f32[1,3072]{1,0:T(1,128)}) custom-call(s32[5]{0:T(128)} %pad_add_fusion.place_ref, f32[288,768]{1,0:T(8,128)} %get-tuple-element.1064.grads_ref, f32[288,768]{1,0:T(8,128)} %get-tuple-element.1065.values_ref, ...), custom_call_target="tpu_custom_call" | custom-call | flops 1 | bytes 1 | tf_op jit(solution)/shard_map/pallas_call | solution.py:61
  299.6 6.1 %shard_map.543 = (bf16[768,768]{1,0:T(8,128)(2,1)}, bf16[768,768]{1,0:T(8,128)(2,1)}) custom-call(bf16[288,1536]{1,0:T(8,128)(2,1)} %get-tuple-element.1098.wide_ref, bf16[288,2304]{1,0:T(8,128)(2,1)} %copy-done.6, bf16[288,2304]{1,0:T(8,128)(2,1)} %get-tuple-element.1100.thin_ref, bf16[288,2304]{1,0:T(8,128)(2,1)} %copy-done.7), custom_call_target="tpu_custom_call" | custom-call | flops 1 | bytes 1 | tf_op jit(solution)/shard_map/pallas_call | solution.py:61
  305.7 4.8 %collective-permute-done.49 = bf16[2,96,768]{2,1,0:T(8,128)(2,1)S(1)} collective-permute-done((bf16[2,96,768]{2,1,0:T(8,128)(2,1)S(1)}, bf16[2,96,768]{2,1,0:T(8,128)(2,1)S(1)}, u32[]{:S(2)}, u32[]{:S(2)}) %collective-permute-start.49) | collective-permute-done | bytes 294944 | tf_op jit(solution)/shard_map/ppermute | solution.py:23
  312.4 6.0 %shard_map.544 = (bf16[768,768]{1,0:T(8,128)(2,1)}, bf16[768,768]{1,0:T(8,128)(2,1)}) custom-call(bf16[288,1536]{1,0:T(8,128)(2,1)} %get-tuple-element.1128.wide_ref, bf16[288,2304]{1,0:T(8,128)(2,1)} %copy-done.7, bf16[288,2304]{1,0:T(8,128)(2,1)} %get-tuple-element.1130.thin_ref, bf16[288,2304]{1,0:T(8,128)(2,1)} %copy-done.6), custom_call_target="tpu_custom_call" | custom-call | flops 1 | bytes 1 | tf_op jit(solution)/shard_map/pallas_call | solution.py:61
  320.2 17.2 %shard_map.546 = (f32[288,768]{1,0:T(8,128)}, bf16[288,3072]{1,0:T(8,128)(2,1)}, bf16[288,768]{1,0:T(8,128)(2,1)}, bf16[288,768]{1,0:T(8,128)(2,1)}, f32[3,768]{1,0:T(4,128)}, /*index=5*/f32[3,768]{1,0:T(4,128)}) custom-call(s32[5]{0:T(128)} %pad_add_fusion.place_ref, f32[288,768]{1,0:T(8,128)} %get-tuple-element.1152.grads_ref, ...), custom_call_target="tpu_custom_call" | custom-call | flops 1 | bytes 1 | tf_op jit(solution)/shard_map/pallas_call | solution.py:61
  345.0 10.9 %collective-permute-done.56 = bf16[2,4,48,384]{3,2,1,0:T(8,128)(2,1)S(1)} collective-permute-done((bf16[2,4,48,384]{3,2,1,0:T(8,128)(2,1)}, bf16[2,4,48,384]{3,2,1,0:T(8,128)(2,1)S(1)}, u32[]{:S(2)}, u32[]{:S(2)}) %collective-permute-start.56) | collective-permute-done | bytes 294944 | tf_op jit(solution)/shard_map/ppermute | solution.py:23
  359.9 6.9 %shard_map.547 = (bf16[8,4,48,384]{3,2,1,0:T(8,128)(2,1)}, bf16[8,4,48,384]{3,2,1,0:T(8,128)(2,1)}) custom-call(s32[5]{0:T(128)} %pad_add_fusion.place_ref, bf16[288,3072]{1,0:T(8,128)(2,1)} %get-tuple-element.1196.left_ref, bf16[288,3072]{1,0:T(8,128)(2,1)} %copy-done.27, bf16[288,768]{1,0:T(8,128)(2,1)} %get-tuple-element.1198.right_ref, ...), custom_call_target="tpu_custom_call" | custom-call | flops 1 | bytes 1 | tf_op jit(solution)/shard_map/pallas_call | solution.py:61
  375.1 6.2 %shard_map.548 = (f32[392,768]{1,0:T(8,128)}, f32[10,768]{1,0:T(8,128)}) custom-call(s32[5]{0:T(128)} %pad_add_fusion.place_ref, f32[288,768]{1,0:T(8,128)} %get-tuple-element.1216.grads_ref, f32[288,768]{1,0:T(8,128)} %get-tuple-element.1217.values_ref, f32[32,768]{1,0:T(8,128)} %get-tuple-element.1218.table_ref), custom_call_target="tpu_custom_call" | custom-call | flops 1 | bytes 1 | tf_op jit(solution)/shard_map/pallas_call | solution.py:61
  389.2 5.5 %collective-permute-start.65 = (f32[32,768]{1,0:T(8,128)S(1)}, f32[32,768]{1,0:T(8,128)S(1)}, u32[]{:S(2)}, u32[]{:S(2)}) collective-permute-start(f32[32,768]{1,0:T(8,128)S(1)} %copy-done.41), channel_id=1, source_target_pairs={{0,16},{16,0},{1,17},{17,1},{2,18},{18,2},{3,19},{19,3},{4,20},{20... | collective-permute-start | bytes 294920 | tf_op jit(solution)/shard_map/ppermute | solution.py:23
  405.9 6.5 %collective-permute-start.84 = (f32[4,48,384]{2,1,0:T(8,128)S(1)}, f32[4,48,384]{2,1,0:T(8,128)S(1)}, u32[]{:S(2)}, u32[]{:S(2)}) collective-permute-start(f32[4,48,384]{2,1,0:T(8,128)S(1)} %fusion.22), channel_id=1, source_target_pairs={{0,16},{16,0},{1,17},{17,1},{2,18},{18,2},{3,19},{19,3},{4,20},{20... | collective-permute-start | bytes 884744 | tf_op jit(solution)/shard_map/ppermute | solution.py:23
  421.0 8.6 %collective-permute-done.77 = bf16[2,4,48,384]{3,2,1,0:T(8,128)(2,1)S(1)} collective-permute-done((bf16[2,4,48,384]{3,2,1,0:T(8,128)(2,1)S(1)}, bf16[2,4,48,384]{3,2,1,0:T(8,128)(2,1)S(1)}, u32[]{:S(2)}, u32[]{:S(2)}) %collective-permute-start.77) | collective-permute-done | bytes 294944 | tf_op jit(solution)/shard_map/ppermute | solution.py:23
  435.1 7.3 %collective-permute-done.68 = f32[40,768]{1,0:T(8,128)S(1)} collective-permute-done((f32[40,768]{1,0:T(8,128)S(1)}, f32[40,768]{1,0:T(8,128)S(1)}, u32[]{:S(2)}, u32[]{:S(2)}) %collective-permute-start.68) | collective-permute-done | bytes 122912 | tf_op jit(solution)/shard_map/ppermute | solution.py:23
  (345 shorter events, 178.2 us)
Async XLA Ops:
  37.6 19.8 %collective-permute-start.9 = (bf16[8,4,48,384]{3,2,1,0:T(8,128)(2,1)S(1)}, bf16[8,4,48,384]{3,2,1,0:T(8,128)(2,1)S(1)}, u32[]{:S(2)}, u32[]{:S(2)}) collective-permute-start(bf16[8,4,48,384]{3,2,1,0:T(8,128)(2,1)S(1)} %pad_maximum_fusion.p0), channel_id=1, source_target_pairs={{0,16},{16,0},{1,17},{17,1},{2,18},{18,2},{3,19},{19,3},{4,20},{20... | collective-permute-start | bytes 3538952 | tf_op jit(solution)/shard_map/ppermute | solution.py:23
  38.6 18.7 %collective-permute-start.8 = (bf16[8,4,48,384]{3,2,1,0:T(8,128)(2,1)S(1)}, bf16[8,4,48,384]{3,2,1,0:T(8,128)(2,1)S(1)}, u32[]{:S(2)}, u32[]{:S(2)}) collective-permute-start(bf16[8,4,48,384]{3,2,1,0:T(8,128)(2,1)S(1)} %pad_maximum_fusion.p0), channel_id=1, source_target_pairs={{0,8},{4,12},{8,0},{12,4},{16,20},{20,16},{24,28},{28,24},{1,9},{5... | collective-permute-start | bytes 3538952 | tf_op jit(solution)/shard_map/ppermute | solution.py:36
  65.0 23.3 %collective-permute-start.15 = (bf16[8,96,768]{2,1,0:T(8,128)(2,1)S(1)}, bf16[8,96,768]{2,1,0:T(8,128)(2,1)S(1)}, u32[]{:S(2)}, u32[]{:S(2)}) collective-permute-start(bf16[8,96,768]{2,1,0:T(8,128)(2,1)S(1)} %pad_maximum_fusion.1), channel_id=1, source_target_pairs={{0,16},{16,0},{1,17},{17,1},{2,18},{18,2},{3,19},{19,3},{4,20},{20... | collective-permute-start | bytes 3538952 | tf_op jit(solution)/shard_map/ppermute | solution.py:23
  66.6 21.8 %collective-permute-start.14 = (bf16[8,96,768]{2,1,0:T(8,128)(2,1)S(1)}, bf16[8,96,768]{2,1,0:T(8,128)(2,1)S(1)}, u32[]{:S(2)}, u32[]{:S(2)}) collective-permute-start(bf16[8,96,768]{2,1,0:T(8,128)(2,1)S(1)} %pad_maximum_fusion.1), channel_id=1, source_target_pairs={{0,8},{4,12},{8,0},{12,4},{16,20},{20,16},{24,28},{28,24},{1,9},{5... | collective-permute-start | bytes 3538952 | tf_op jit(solution)/shard_map/ppermute | solution.py:36
  91.9 25.5 %collective-permute-start.21 = (bf16[8,96,768]{2,1,0:T(8,128)(2,1)S(1)}, bf16[8,96,768]{2,1,0:T(8,128)(2,1)S(1)}, u32[]{:S(2)}, u32[]{:S(2)}) collective-permute-start(bf16[8,96,768]{2,1,0:T(8,128)(2,1)S(1)} %pad_maximum_fusion.2), channel_id=1, source_target_pairs={{0,16},{16,0},{1,17},{17,1},{2,18},{18,2},{3,19},{19,3},{4,20},{20... | collective-permute-start | bytes 3538952 | tf_op jit(solution)/shard_map/ppermute | solution.py:23
  93.8 23.6 %collective-permute-start.20 = (bf16[8,96,768]{2,1,0:T(8,128)(2,1)S(1)}, bf16[8,96,768]{2,1,0:T(8,128)(2,1)S(1)}, u32[]{:S(2)}, u32[]{:S(2)}) collective-permute-start(bf16[8,96,768]{2,1,0:T(8,128)(2,1)S(1)} %pad_maximum_fusion.2), channel_id=1, source_target_pairs={{0,8},{4,12},{8,0},{12,4},{16,20},{20,16},{24,28},{28,24},{1,9},{5... | collective-permute-start | bytes 3538952 | tf_op jit(solution)/shard_map/ppermute | solution.py:36
  94.8 24.3 %collective-permute-start.18 = (bf16[8,96,768]{2,1,0:T(8,128)(2,1)S(1)}, bf16[8,96,768]{2,1,0:T(8,128)(2,1)S(1)}, u32[]{:S(2)}, u32[]{:S(2)}) collective-permute-start(bf16[8,96,768]{2,1,0:T(8,128)(2,1)S(1)} %copy-done.14), channel_id=1, source_target_pairs={{0,16},{16,0},{1,17},{17,1},{2,18},{18,2},{3,19},{19,3},{4,20},{20... | collective-permute-start | bytes 3538952 | tf_op jit(solution)/shard_map/ppermute | solution.py:23
  120.5 18.5 %collective-permute-start.30 = (bf16[8,4,48,384]{3,2,1,0:T(8,128)(2,1)S(1)}, bf16[8,4,48,384]{3,2,1,0:T(8,128)(2,1)S(1)}, u32[]{:S(2)}, u32[]{:S(2)}) collective-permute-start(bf16[8,4,48,384]{3,2,1,0:T(8,128)(2,1)S(1)} %pad_maximum_fusion.3.p0), channel_id=1, source_target_pairs={{0,16},{16,0},{1,17},{17,1},{2,18},{18,2},{3,19},{19,3},{4,20},{20... | collective-permute-start | bytes 3538952 | tf_op jit(solution)/shard_map/ppermute | solution.py:23
  122.2 16.8 %collective-permute-start.29 = (bf16[8,4,48,384]{3,2,1,0:T(8,128)(2,1)S(1)}, bf16[8,4,48,384]{3,2,1,0:T(8,128)(2,1)S(1)}, u32[]{:S(2)}, u32[]{:S(2)}) collective-permute-start(bf16[8,4,48,384]{3,2,1,0:T(8,128)(2,1)S(1)} %pad_maximum_fusion.3.p0), channel_id=1, source_target_pairs={{0,8},{4,12},{8,0},{12,4},{16,20},{20,16},{24,28},{28,24},{1,9},{5... | collective-permute-start | bytes 3538952 | tf_op jit(solution)/shard_map/ppermute | solution.py:36
  139.0 22.4 %collective-permute-start.31 = (bf16[8,4,48,384]{3,2,1,0:T(8,128)(2,1)S(1)}, bf16[8,4,48,384]{3,2,1,0:T(8,128)(2,1)S(1)}, u32[]{:S(2)}, u32[]{:S(2)}) collective-permute-start(bf16[8,4,48,384]{3,2,1,0:T(8,128)(2,1)S(1)} %collective-permute-done.29.p1), channel_id=1, source_target_pairs={{0,16},{16,0},{1,17},{17,1},{2,18},{18,2},{3,19},{19,3},{4,20},{20... | collective-permute-start | bytes 3538952 | tf_op jit(solution)/shard_map/ppermute | solution.py:23
  156.4 28.5 %collective-permute-start.35 = (bf16[288,2304]{1,0:T(8,128)(2,1)}, bf16[288,2304]{1,0:T(8,128)(2,1)S(1)}, u32[]{:S(2)}, u32[]{:S(2)}) collective-permute-start(bf16[288,2304]{1,0:T(8,128)(2,1)} %get-tuple-element.1130.thin_ref), channel_id=1, source_target_pairs={{0,16},{16,0},{1,17},{17,1},{2,18},{18,2},{3,19},{19,3},{4,20},{20... | collective-permute-start | bytes 3981320 | tf_op jit(solution)/shard_map/ppermute | solution.py:23
  157.5 27.4 %collective-permute-start.34 = (bf16[8,96,768]{2,1,0:T(8,128)(2,1)S(1)}, bf16[8,96,768]{2,1,0:T(8,128)(2,1)S(1)}, u32[]{:S(2)}, u32[]{:S(2)}) collective-permute-start(bf16[8,96,768]{2,1,0:T(8,128)(2,1)S(1)} %pad_maximum_fusion.4), channel_id=1, source_target_pairs={{0,16},{16,0},{1,17},{17,1},{2,18},{18,2},{3,19},{19,3},{4,20},{20... | collective-permute-start | bytes 3538952 | tf_op jit(solution)/shard_map/ppermute | solution.py:23
  157.5 27.4 %collective-permute-start.33 = (bf16[8,96,768]{2,1,0:T(8,128)(2,1)S(1)}, bf16[8,96,768]{2,1,0:T(8,128)(2,1)}, u32[]{:S(2)}, u32[]{:S(2)}) collective-permute-start(bf16[8,96,768]{2,1,0:T(8,128)(2,1)S(1)} %pad_maximum_fusion.4), channel_id=1, source_target_pairs={{0,8},{4,12},{8,0},{12,4},{16,20},{20,16},{24,28},{28,24},{1,9},{5... | collective-permute-start | bytes 3538952 | tf_op jit(solution)/shard_map/ppermute | solution.py:36
  173.3 17.5 %collective-permute-start.37 = (bf16[8,96,768]{2,1,0:T(8,128)(2,1)S(1)}, bf16[8,96,768]{2,1,0:T(8,128)(2,1)S(1)}, u32[]{:S(2)}, u32[]{:S(2)}) collective-permute-start(bf16[8,96,768]{2,1,0:T(8,128)(2,1)S(1)} %pad_maximum_fusion.5), channel_id=1, source_target_pairs={{0,8},{4,12},{8,0},{12,4},{16,20},{20,16},{24,28},{28,24},{1,9},{5... | collective-permute-start | bytes 3538952 | tf_op jit(solution)/shard_map/ppermute | solution.py:36
  242.7 16.2 %collective-permute-start.44 = (bf16[8,96,768]{2,1,0:T(8,128)(2,1)}, bf16[8,96,768]{2,1,0:T(8,128)(2,1)S(1)}, u32[]{:S(2)}, u32[]{:S(2)}) collective-permute-start(bf16[8,96,768]{2,1,0:T(8,128)(2,1)} %bitcast.98), channel_id=1, source_target_pairs={{0,8},{4,12},{8,0},{12,4},{16,20},{20,16},{24,28},{28,24},{1,9},{5... | collective-permute-start | bytes 3538952 | tf_op jit(solution)/shard_map/ppermute | solution.py:36
  259.2 17.1 %collective-permute-start.45 = (bf16[4,96,768]{2,1,0:T(8,128)(2,1)S(1)}, bf16[4,96,768]{2,1,0:T(8,128)(2,1)S(1)}, u32[]{:S(2)}, u32[]{:S(2)}) collective-permute-start(bf16[4,96,768]{2,1,0:T(8,128)(2,1)S(1)} %get-tuple-element.1027), channel_id=1, source_target_pairs={{0,4},{4,0},{8,12},{12,8},{16,24},{20,28},{24,16},{28,20},{1,5},{5... | collective-permute-start | bytes 1769480 | tf_op jit(solution)/shard_map/ppermute | solution.py:36
  276.3 19.2 %collective-permute-start.51 = (bf16[8,4,48,384]{3,2,1,0:T(8,128)(2,1)}, bf16[8,4,48,384]{3,2,1,0:T(8,128)(2,1)S(1)}, u32[]{:S(2)}, u32[]{:S(2)}) collective-permute-start(bf16[8,4,48,384]{3,2,1,0:T(8,128)(2,1)} %get-tuple-element.1091), channel_id=1, source_target_pairs={{0,8},{4,12},{8,0},{12,4},{16,20},{20,16},{24,28},{28,24},{1,9},{5... | collective-permute-start | bytes 3538952 | tf_op jit(solution)/shard_map/ppermute | solution.py:36
  310.7 31.5 %collective-permute-start.57 = (bf16[8,96,768]{2,1,0:T(8,128)(2,1)}, bf16[8,96,768]{2,1,0:T(8,128)(2,1)}, u32[]{:S(2)}, u32[]{:S(2)}) collective-permute-start(bf16[8,96,768]{2,1,0:T(8,128)(2,1)} %bitcast.28), channel_id=1, source_target_pairs={{0,8},{4,12},{8,0},{12,4},{16,20},{20,16},{24,28},{28,24},{1,9},{5... | collective-permute-start | bytes 3538952 | tf_op jit(solution)/shard_map/ppermute | solution.py:36
  337.4 21.3 %collective-permute-start.61 = (bf16[288,3072]{1,0:T(8,128)(2,1)}, bf16[288,3072]{1,0:T(8,128)(2,1)S(1)}, u32[]{:S(2)}, u32[]{:S(2)}) collective-permute-start(bf16[288,3072]{1,0:T(8,128)(2,1)} %get-tuple-element.1196.left_ref), channel_id=1, source_target_pairs={{0,16},{16,0},{1,17},{17,1},{2,18},{18,2},{3,19},{19,3},{4,20},{20... | collective-permute-start | bytes 5308424 | tf_op jit(solution)/shard_map/ppermute | solution.py:23
  338.2 28.6 %collective-permute-start.60 = (bf16[8,96,768]{2,1,0:T(8,128)(2,1)}, bf16[8,96,768]{2,1,0:T(8,128)(2,1)}, u32[]{:S(2)}, u32[]{:S(2)}) collective-permute-start(bf16[8,96,768]{2,1,0:T(8,128)(2,1)} %bitcast.30), channel_id=1, source_target_pairs={{0,8},{4,12},{8,0},{12,4},{16,20},{20,16},{24,28},{28,24},{1,9},{5... | collective-permute-start | bytes 3538952 | tf_op jit(solution)/shard_map/ppermute | solution.py:36
  339.1 16.9 %collective-permute-start.56 = (bf16[2,4,48,384]{3,2,1,0:T(8,128)(2,1)}, bf16[2,4,48,384]{3,2,1,0:T(8,128)(2,1)S(1)}, u32[]{:S(2)}, u32[]{:S(2)}) collective-permute-start(bf16[2,4,48,384]{3,2,1,0:T(8,128)(2,1)} %get-tuple-element.1172), channel_id=1, source_target_pairs={{0,2},{1,3},{2,0},{3,1},{4,6},{5,7},{6,4},{7,5},{8,10},{9,11},{10,... | collective-permute-start | bytes 884744 | tf_op jit(solution)/shard_map/ppermute | solution.py:23
  342.0 16.5 %collective-permute-start.62 = (bf16[288,768]{1,0:T(8,128)(2,1)S(1)}, bf16[288,768]{1,0:T(8,128)(2,1)S(1)}, u32[]{:S(2)}, u32[]{:S(2)}) collective-permute-start(bf16[288,768]{1,0:T(8,128)(2,1)S(1)} %copy-done.52), channel_id=1, source_target_pairs={{0,16},{16,0},{1,17},{17,1},{2,18},{18,2},{3,19},{19,3},{4,20},{20... | collective-permute-start | bytes 1327112 | tf_op jit(solution)/shard_map/ppermute | solution.py:23
  343.8 25.2 %collective-permute-start.59 = (bf16[4,96,768]{2,1,0:T(8,128)(2,1)S(1)}, bf16[4,96,768]{2,1,0:T(8,128)(2,1)S(1)}, u32[]{:S(2)}, u32[]{:S(2)}) collective-permute-start(bf16[4,96,768]{2,1,0:T(8,128)(2,1)S(1)} %get-tuple-element.1185), channel_id=1, source_target_pairs={{0,4},{4,0},{8,12},{12,8},{16,24},{20,28},{24,16},{28,20},{1,5},{5... | collective-permute-start | bytes 1769480 | tf_op jit(solution)/shard_map/ppermute | solution.py:36
  366.8 29.2 %collective-permute-start.71 = (bf16[8,4,48,384]{3,2,1,0:T(8,128)(2,1)}, bf16[8,4,48,384]{3,2,1,0:T(8,128)(2,1)}, u32[]{:S(2)}, u32[]{:S(2)}) collective-permute-start(bf16[8,4,48,384]{3,2,1,0:T(8,128)(2,1)} %get-tuple-element.1258), channel_id=1, source_target_pairs={{0,8},{4,12},{8,0},{12,4},{16,20},{20,16},{24,28},{28,24},{1,9},{5... | collective-permute-start | bytes 3538952 | tf_op jit(solution)/shard_map/ppermute | solution.py:36
  369.0 19.3 %collective-permute-start.67 = (bf16[1,4,48,384]{3,2,1,0:T(8,128)(2,1)}, bf16[1,4,48,384]{3,2,1,0:T(8,128)(2,1)}, u32[]{:S(2)}, u32[]{:S(2)}) collective-permute-start(bf16[1,4,48,384]{3,2,1,0:T(8,128)(2,1)} %fusion.23), channel_id=1, source_target_pairs={{0,1},{1,0},{2,3},{3,2},{4,5},{5,4},{6,7},{7,6},{8,9},{9,8},{10,11... | collective-permute-start | bytes 442376 | tf_op jit(solution)/shard_map/ppermute | solution.py:23
  369.1 25.6 %collective-permute-start.66 = (bf16[4,96,768]{2,1,0:T(8,128)(2,1)S(1)}, bf16[4,96,768]{2,1,0:T(8,128)(2,1)}, u32[]{:S(2)}, u32[]{:S(2)}) collective-permute-start(bf16[4,96,768]{2,1,0:T(8,128)(2,1)S(1)} %get-tuple-element.1240), channel_id=1, source_target_pairs={{0,4},{4,0},{8,12},{12,8},{16,24},{20,28},{24,16},{28,20},{1,5},{5... | collective-permute-start | bytes 1769480 | tf_op jit(solution)/shard_map/ppermute | solution.py:36
  373.1 21.6 %collective-permute-start.69 = (bf16[2,96,768]{2,1,0:T(8,128)(2,1)}, bf16[2,96,768]{2,1,0:T(8,128)(2,1)}, u32[]{:S(2)}, u32[]{:S(2)}) collective-permute-start(bf16[2,96,768]{2,1,0:T(8,128)(2,1)} %get-tuple-element.1255), channel_id=1, source_target_pairs={{0,2},{1,3},{2,0},{3,1},{4,6},{5,7},{6,4},{7,5},{8,10},{9,11},{10,... | collective-permute-start | bytes 884744 | tf_op jit(solution)/shard_map/ppermute | solution.py:23
  396.0 17.7 %collective-permute-start.75 = (bf16[2,96,768]{2,1,0:T(8,128)(2,1)S(1)}, bf16[2,96,768]{2,1,0:T(8,128)(2,1)S(1)}, u32[]{:S(2)}, u32[]{:S(2)}) collective-permute-start(bf16[2,96,768]{2,1,0:T(8,128)(2,1)S(1)} %get-tuple-element.1279), channel_id=1, source_target_pairs={{0,2},{1,3},{2,0},{3,1},{4,6},{5,7},{6,4},{7,5},{8,10},{9,11},{10,... | collective-permute-start | bytes 884744 | tf_op jit(solution)/shard_map/ppermute | solution.py:23
  403.1 27.7 %collective-permute-start.64 = (f32[40,768]{1,0:T(8,128)S(1)}, f32[40,768]{1,0:T(8,128)S(1)}, u32[]{:S(2)}, u32[]{:S(2)}) collective-permute-start(f32[40,768]{1,0:T(8,128)S(1)} %add.209), channel_id=1, source_target_pairs={{0,1},{1,0},{2,3},{3,2},{4,5},{5,4},{6,7},{7,6},{8,9},{9,8},{10,11... | collective-permute-start | bytes 368648 | tf_op jit(solution)/shard_map/ppermute | solution.py:23
  405.9 27.7 %collective-permute-start.84 = (f32[4,48,384]{2,1,0:T(8,128)S(1)}, f32[4,48,384]{2,1,0:T(8,128)S(1)}, u32[]{:S(2)}, u32[]{:S(2)}) collective-permute-start(f32[4,48,384]{2,1,0:T(8,128)S(1)} %fusion.22), channel_id=1, source_target_pairs={{0,16},{16,0},{1,17},{17,1},{2,18},{18,2},{3,19},{19,3},{4,20},{20... | collective-permute-start | bytes 884744 | tf_op jit(solution)/shard_map/ppermute | solution.py:23
  416.8 26.3 %collective-permute-start.83 = (f32[96,768]{1,0:T(8,128)S(1)}, f32[96,768]{1,0:T(8,128)S(1)}, u32[]{:S(2)}, u32[]{:S(2)}) collective-permute-start(f32[96,768]{1,0:T(8,128)S(1)} %fusion.14), channel_id=1, source_target_pairs={{0,16},{16,0},{1,17},{17,1},{2,18},{18,2},{3,19},{19,3},{4,20},{20... | collective-permute-start | bytes 884744 | tf_op jit(solution)/shard_map/ppermute | solution.py:23
  429.6 17.3 %collective-permute-start.81 = (f32[96,768]{1,0:T(8,128)S(1)}, f32[96,768]{1,0:T(8,128)S(1)}, u32[]{:S(2)}, u32[]{:S(2)}) collective-permute-start(f32[96,768]{1,0:T(8,128)S(1)} %fusion.17), channel_id=1, source_target_pairs={{0,16},{16,0},{1,17},{17,1},{2,18},{18,2},{3,19},{19,3},{4,20},{20... | collective-permute-start | bytes 884744 | tf_op jit(solution)/shard_map/ppermute | solution.py:23
  (109 other events, 967.2 us)

commit v5 on v4

--- a/solution.py
+++ b/solution.py
@@ -47,25 +47,25 @@
     )
 
 
-VMEM_LIMIT = 56 * 1024 * 1024
+VMEM_LIMIT = 16 * 1024 * 1024
 GROUP = 256
+WAIT = 1_000_000_000
 HEADS = GROUP // HD
 
 
-def call(kernel, outs, operands, spaces=(), scratch=(), flops=0, limit=VMEM_LIMIT):
+def call(kernel, outs, operands, spaces=(), scratch=(), flops=1):
     vmem = pl.BlockSpec(memory_space=pltpu.VMEM)
     specs = [vmem] * len(operands)
     for index, space in spaces:
         specs[index] = pl.BlockSpec(memory_space=space)
-    moved = sum(item.size * item.dtype.itemsize for item in list(operands) + list(outs))
     return pl.pallas_call(
         kernel,
         out_shape=list(outs),
         in_specs=specs,
         out_specs=[vmem] * len(outs),
         scratch_shapes=list(scratch),
-        compiler_params=pltpu.CompilerParams(vmem_limit_bytes=limit),
-        cost_estimate=pl.CostEstimate(flops=1, bytes_accessed=1, transcendentals=0),
+        compiler_params=pltpu.CompilerParams(vmem_limit_bytes=VMEM_LIMIT),
+        cost_estimate=pl.CostEstimate(flops=flops, bytes_accessed=1, transcendentals=0),
     )(*operands)
 
 
@@ -238,60 +238,49 @@
     )
 
 
-def low_kernel(place_ref, slots_ref, cells_ref, low_ref):
-    pack_cells(slots_ref, cells_ref)
-    low_ref[...] = (cells_ref[...] * presence(place_ref, cells_ref.shape[0])).astype(BF16)
-
-
-def low_cells(place, slots):
+def cells(slots):
     shape = (slots.shape[0] // (PADDED * PADDED) * CELLS, slots.shape[1])
-    return call(low_kernel, [struct(shape, F32), struct(shape, BF16)], [place, slots], SMALL)
+    return call(pack_cells, [struct(shape, F32)], [slots])[0]
 
 
 UNITS = 768
-TILE = 256
-
-
-def mlp_kernel(
-    base_row, place_ref, values_ref, table_ref, upbias_ref,
-    u0, u1, u2, u3, d0, d1, d2, d3,
-    *rest,
-):
-    packed = len(rest) == 6
+
+
+def tile(part, which):
+    return part[:, which].reshape(-1, part.shape[-1])
+
+
+def mlp_kernel(base_row, place_ref, values_ref, table_ref, upbias_ref, p0, p1, p2, p3, *rest):
+    last = base_row != 0
     gain, shift, downbias = (table_ref[pl.ds(base_row + i, 1), :] for i in (13, 14, 15))
-    ubias = 0 if base_row == 0 else 1
-    out_ref, acted_ref, send_ref, deriv_ref, total_ref = rest[0], rest[1], rest[2], rest[3], rest[4]
+    ubias = 1 if last else 0
+    out_ref, acted_ref, send_ref, deriv_ref, total_ref = rest[:5]
     values = values_ref[...]
     normal, _ = normalize(values)
     half = 2 * UNITS
     send_ref[:, half:] = (normal * gain + shift).astype(BF16)
-    for index, (up, down) in enumerate(zip((u0, u1, u2, u3), (d0, d1, d2, d3))):
+    for index, part in enumerate((p0, p1, p2, p3)):
         target = acted_ref if index < 2 else send_ref
         base = (index % 2) * UNITS
-
-        def step(part, _, up=up, target=target, base=base, index=index):
-            first = pl.multiple_of(part * TILE, TILE)
-            here = pl.ds(pl.multiple_of(index * UNITS + part * TILE, TILE), TILE)
-            hidden = mm_nt(send_ref[:, half:], up[pl.ds(first, TILE), :]) + upbias_ref[ubias : ubias + 1, here]
-            below = 0.5 + 0.5 * lax.erf(hidden * (0.5**0.5))
-            there = pl.ds(pl.multiple_of(base + part * TILE, TILE), TILE)
-            target[:, there] = (hidden * below).astype(BF16)
-            bell = jnp.exp(hidden * hidden * -0.5) * 0.3989422804014327
-            deriv_ref[:, here] = below + hidden * bell
-            return 0
-
-        lax.fori_loop(0, UNITS // TILE, step, 0)
-        term = mm(target[:, base : base + UNITS], down[...])
+        here = slice(index * UNITS, (index + 1) * UNITS)
+        there = slice(base, base + UNITS)
+        hidden = mm_nt(send_ref[:, half:], tile(part, 0)) + upbias_ref[ubias : ubias + 1, here]
+        below = 0.5 + 0.5 * lax.erf(hidden * (0.5**0.5))
+        target[:, there] = (hidden * below).astype(BF16)
+        bell = jnp.exp(hidden * hidden * -0.5) * 0.3989422804014327
+        deriv_ref[:, here] = below + hidden * bell
+        term = mm(target[:, there], tile(part, 1))
         total_ref[...] = term if index == 0 else total_ref[...] + term
     result = values + presence(place_ref, values.shape[0]) * (total_ref[...] + downbias)
-    if packed:
+    if last:
         rest[5][...] = result
         unpack_cells(rest[5], out_ref)
     else:
         out_ref[...] = result
 
 
-def mlp(base, last, place, values, table, upbias, ups, downs):
+def mlp(base, place, values, table, upbias, parts):
+    last = base != 0
     rows, width = values.shape
     images = rows // CELLS
     half = 2 * UNITS
@@ -302,9 +291,8 @@
         struct((rows, 2 * half), F32),
     ]
     scratch = [pltpu.VMEM((rows, width), F32)] * (2 if last else 1)
-    operands = [place, values, table, upbias, *ups, *downs]
-    flops = 4 * rows * width * 2 * half
-    return call(partial(mlp_kernel, base), outs, operands, SMALL, scratch=scratch, flops=flops)
+    operands = [place, values, table, upbias, *parts]
+    return call(partial(mlp_kernel, base), outs, operands, SMALL, scratch=scratch)
 
 
 def norm_back(dn, values, gain, little_ref):
@@ -318,36 +306,29 @@
 
 
 def mlp_back_kernel(
-    base_row, place_ref, grads_ref, values_ref, table_ref, deriv_ref,
-    u0, u1, u2, u3, d0, d1, d2, d3,
+    base_row, place_ref, grads_ref, values_ref, table_ref, deriv_ref, p0, p1, p2, p3,
     out_ref, hidden_ref, send_ref, little_ref, bias_ref, total_ref,
 ):
     half = 2 * UNITS
     branch = grads_ref[...] * presence(place_ref, grads_ref.shape[0])
     little_ref[2:3, :] = jnp.sum(branch, axis=0, keepdims=True)
     send_ref[:, half:] = branch.astype(BF16)
-    for index, (up, down) in enumerate(zip((u0, u1, u2, u3), (d0, d1, d2, d3))):
+    for index, part in enumerate((p0, p1, p2, p3)):
         target = hidden_ref if index < 2 else send_ref
         base = (index % 2) * UNITS
-
-        def step(part, _, down=down, target=target, base=base, index=index):
-            first = pl.multiple_of(part * TILE, TILE)
-            here = pl.ds(pl.multiple_of(index * UNITS + part * TILE, TILE), TILE)
-            acted = mm_nt(send_ref[:, half:], down[pl.ds(first, TILE), :])
-            hidden = (acted * deriv_ref[:, here]).astype(BF16)
-            there = pl.ds(pl.multiple_of(base + part * TILE, TILE), TILE)
-            target[:, there] = hidden
-            bias_ref[:, here] = jnp.sum(hidden.astype(F32), axis=0, keepdims=True)
-            return 0
-
-        lax.fori_loop(0, UNITS // TILE, step, 0)
-        term = mm(target[:, base : base + UNITS], up[...])
+        here = slice(index * UNITS, (index + 1) * UNITS)
+        there = slice(base, base + UNITS)
+        acted = mm_nt(send_ref[:, half:], tile(part, 1))
+        hidden = (acted * deriv_ref[:, here]).astype(BF16)
+        target[:, there] = hidden
+        bias_ref[:, here] = jnp.sum(hidden.astype(F32), axis=0, keepdims=True)
+        term = mm(target[:, there], tile(part, 0))
         total_ref[...] = term if index == 0 else total_ref[...] + term
     gain = table_ref[pl.ds(base_row + 13, 1), :]
     out_ref[...] = grads_ref[...] + norm_back(total_ref[...], values_ref[...], gain, little_ref)
 
 
-def mlp_back(base, place, grads, values, table, deriv, ups, downs):
+def mlp_back(base, place, grads, values, table, deriv, parts):
     rows, width = values.shape
     half = 2 * UNITS
     outs = [
@@ -358,26 +339,26 @@
         struct((1, 2 * half), F32),
     ]
     scratch = [pltpu.VMEM((rows, width), F32)]
-    operands = [place, grads, values, table, deriv, *ups, *downs]
-    flops = 4 * rows * width * 2 * half
-    return call(partial(mlp_back_kernel, base), outs, operands, SMALL, scratch=scratch, flops=flops)
-
-
-def pair_grads_kernel(wide_ref, wide_send_ref, thin_ref, thin_send_ref, near_ref, far_ref):
-    half = thin_ref.shape[1] - near_ref.shape[1]
-    half_send = thin_send_ref.shape[1] - near_ref.shape[1]
+    operands = [place, grads, values, table, deriv, *parts]
+    return call(partial(mlp_back_kernel, base), outs, operands, SMALL, scratch=scratch)
+
+
+def pair_grads_kernel(acted_ref, normed_ref, normed_send_ref, hidden_ref, branch_ref, branch_send_ref, near_ref, far_ref):
+    half = 2 * UNITS
     for index, out_ref in enumerate((near_ref, far_ref)):
-        cut = pl.ds(index * UNITS, UNITS)
-        total = mm_tn(wide_ref[:, cut], thin_ref[:, half:])
-        total = total + mm_tn(wide_send_ref[:, cut], thin_send_ref[:, half_send:])
-        out_ref[...] = total.astype(BF16)
-
-
-def pair_grads(wide, wide_send, thin, thin_send):
-    width = min(thin.shape[1], UNITS)
-    out = struct((UNITS, width), BF16)
-    flops = 8 * wide.shape[0] * UNITS * width
-    return call(pair_grads_kernel, [out, out], [wide, wide_send, thin, thin_send], flops=flops)
+        cut = slice(index * UNITS, (index + 1) * UNITS)
+        for which, (wide, wide_send, thin, thin_send) in enumerate((
+            (hidden_ref, branch_send_ref, normed_ref, normed_send_ref),
+            (acted_ref, normed_send_ref, branch_ref, branch_send_ref),
+        )):
+            total = mm_tn(wide[:, cut], thin[:, half:]) + mm_tn(wide_send[:, cut], thin_send[:, half:])
+            out_ref[:, which] = total.astype(BF16).reshape(8, -1, total.shape[1])
+
+
+def pair_grads(acted, normed, normed_send, hidden, branch, branch_send):
+    width = normed.shape[1] - 2 * UNITS
+    out = struct((8, 2, UNITS // 8, width), BF16)
+    return call(pair_grads_kernel, [out, out], [acted, normed, normed_send, hidden, branch, branch_send])
 
 
 MATS = 4
@@ -496,17 +477,16 @@
         struct((rows, width), BF16),
     ]
     operands = [place, values, table, bias, *parts]
-    spaces = SMALL + [(4 + i, pl.ANY) for i in range(4)]
+    spaces = SMALL + [(4 + i, pltpu.HBM) for i in range(4)]
     scratch = [pltpu.VMEM((MATS, width, width), BF16), pltpu.SemaphoreType.DMA((32,))]
     return call(
         partial(attention_kernel, windowed), outs, operands, spaces=spaces, scratch=scratch,
-        flops=8 * rows * width * width,
     )
 
 
 def attention_back_kernel(
     windowed, place_ref, grads_ref, values_ref, table_ref, normed_ref, qkv_ref, mixed_ref,
-    p0, p1, p2, p3, out_ref, left_ref, mine_ref, theirs_ref, little_ref, bias_ref,
+    p0, p1, p2, p3, out_ref, left_ref, rest_ref, mine_ref, little_ref, bias_ref,
     weights_ref, low_ref, mix_ref, sems,
 ):
     copies = load_weights(place_ref, (p0, p1, p2, p3), weights_ref, sems)
@@ -520,9 +500,9 @@
     low_ref[...] = branch.astype(BF16)
     mine_ref[:, :half] = normed_ref[:, own]
     mine_ref[:, half:] = low_ref[:, own]
-    theirs_ref[:, :half] = normed_ref[:, other]
-    theirs_ref[:, half:] = low_ref[:, other]
-    left_ref[:, 3 * width :] = mixed_ref[...]
+    rest_ref[:, width : width + half] = normed_ref[:, other]
+    rest_ref[:, width + half :] = low_ref[:, other]
+    rest_ref[:, :width] = mixed_ref[...]
     for copy in copies:
         copy.wait()
     mix_ref[...] = mm_nt(low_ref[...], weights_ref[3]).astype(BF16)
@@ -575,14 +555,14 @@
     rows, width = values.shape
     outs = [
         struct((rows, width), F32),
-        struct((rows, 4 * width), BF16),
-        struct((rows, width), BF16),
+        struct((rows, 3 * width), BF16),
+        struct((rows, 2 * width), BF16),
         struct((rows, width), BF16),
         struct((3, width), F32),
         struct((3, width), F32),
     ]
     operands = [place, grads, values, table, normed, qkv, mixed, *parts]
-    spaces = SMALL + [(7 + i, pl.ANY) for i in range(4)]
+    spaces = SMALL + [(7 + i, pltpu.HBM) for i in range(4)]
     scratch = [
         pltpu.VMEM((MATS, width, width), BF16),
         pltpu.VMEM((rows, width), BF16),
@@ -591,19 +571,22 @@
     ]
     return call(
         partial(attention_back_kernel, windowed), outs, operands, spaces=spaces, scratch=scratch,
-        flops=10 * rows * width * width,
-    )
-
-
-def head_grads_kernel(place_ref, left_ref, left_send_ref, right_ref, right_send_ref, near_ref, far_ref, table_ref, other_ref):
+    )
+
+
+def head_grads_kernel(
+    place_ref, left_ref, rest_ref, left_send_ref, rest_send_ref, right_ref, near_ref, far_ref, table_ref, other_ref
+):
     wid = place_ref[1]
-    width = left_ref.shape[1] // MATS
+    width = right_ref.shape[1]
     half = width // 2
     for m in range(MATS):
-        cut = slice(m * width, (m + 1) * width)
+        left, left_send = (left_ref, left_send_ref) if m < 3 else (rest_ref, rest_send_ref)
+        cut = slice(m % 3 * width, (m % 3 + 1) * width)
         side = slice(0, half) if m < 3 else slice(half, width)
-        table_ref[...] = mm_tn(left_ref[:, cut], right_ref[:, side])
-        other_ref[...] = mm_tn(left_send_ref[:, cut], right_send_ref[:, side])
+        beside = slice(width + side.start, width + side.stop)
+        table_ref[...] = mm_tn(left[:, cut], right_ref[:, side])
+        other_ref[...] = mm_tn(left_send[:, cut], rest_send_ref[:, beside])
         for line in range(4):
             out_ref = near_ref if line < 2 else far_ref
             for j in range(4):
@@ -613,39 +596,44 @@
                 out_ref[(line % 2) * 4 + j, m] = (mine + other).astype(BF16)
 
 
-def head_grads(place, left, left_send, right, right_send):
+def head_grads(place, left, rest, left_send, rest_send, right):
     width = right.shape[1]
     out = struct((8, MATS, width // 16, width // 2), BF16)
     return call(
-        head_grads_kernel, [out, out], [place, left, left_send, right, right_send],
+        head_grads_kernel, [out, out], [place, left, rest, left_send, rest_send, right],
         SMALL, scratch=[pltpu.VMEM((width, width // 2), F32)] * 2,
-        flops=8 * left.shape[0] * width * width,
     )
 
 
 def pieces_kernel(place_ref, *refs):
     core = place_ref[0]
-    for base in (0, 4):
-        inw, outw, up, down = refs[base : base + 4]
-        outs = refs[8 + base // 4 * 3 : 11 + base // 4 * 3]
+    weights, outs, sems = refs[:8], refs[8:12], refs[12]
+    moves = []
+    for index in range(2):
+        inw, outw, up, down = weights[4 * index : 4 * index + 4]
+        heads, units = outs[2 * index : 2 * index + 2]
         half = inw.shape[2] // 2
         columns = pl.ds(pl.multiple_of(core * half, half), half)
-        for m in range(3):
-            outs[0][0, m] = inw[m, :, columns]
-        outs[0][0, 3] = outw[:, columns]
+        moves.append((inw.at[:, :, columns], heads.at[0, pl.ds(0, 3)]))
+        moves.append((outw.at[:, columns], heads.at[0, 3]))
         rows = up.shape[0] // 2
         own = pl.ds(pl.multiple_of(core * rows, rows), rows)
-        outs[1][0] = up[own, :]
-        outs[2][0] = down[own, :]
+        moves.append((up.at[own, :], units.at[0, 0]))
+        moves.append((down.at[own, :], units.at[0, 1]))
+    copies = [pltpu.make_async_copy(*move, sems.at[index]) for index, move in enumerate(moves)]
+    for copy in copies:
+        copy.start()
+    for copy in copies:
+        copy.wait()
 
 
 def pieces(place, *weights):
-    outs = []
-    for base in (0, 4):
-        inw, _, up, _ = weights[base : base + 4]
-        outs.append(struct((1, MATS, inw.shape[1], inw.shape[2] // 2), BF16))
-        outs += [struct((1, up.shape[0] // 2, up.shape[1]), BF16)] * 2
-    return call(pieces_kernel, outs, [place, *weights], SMALL)
+    inw, _, up, _ = weights[:4]
+    heads = struct((1, MATS, inw.shape[1], inw.shape[2] // 2), BF16)
+    units = struct((1, 2, up.shape[0] // 2, up.shape[1]), BF16)
+    spaces = SMALL + [(1 + index, pltpu.HBM) for index in range(8)]
+    scratch = [pltpu.SemaphoreType.DMA((8,))]
+    return call(pieces_kernel, [heads, units, heads, units], [place, *weights], spaces, scratch)
 
 
 def table_kernel(*refs):
@@ -700,7 +688,7 @@
 BIASES = 16
 
 
-def small_kernel(counts, kinds, place_ref, *refs):
+def small_kernel(counts, place_ref, *refs):
     out_ref = refs[-1]
     core, wid, hid = place_ref[0], place_ref[1], place_ref[2]
     out_ref[...] = jnp.zeros_like(out_ref)
@@ -708,13 +696,11 @@
     for count, ref in zip(counts, refs):
         out_ref[pl.ds(row, count), :] = ref[...]
         row += count
-    base = out_ref.shape[0] - BIASES
-    rest = refs[len(counts) : -1]
-    heads, hiddens = rest[0], rest[1:]
-    step = heads.shape[1] // 4
+    base = out_ref.shape[0] - 2 * BIASES
+    window_heads, channel_heads, *hiddens = refs[len(counts) : -1]
+    step = window_heads.shape[1] // 4
     half = step // 2
     gap = jnp.zeros((1, 256 - step), F32)
-    blank = jnp.zeros((1, half), F32)
     for i in range(4):
         owned = jnp.bitwise_xor(hid, jnp.where(core == 0, i, SWAP[i]))
         for j in range(4):
@@ -725,58 +711,118 @@
                 lane = 16 * half + (SWAP[i] * 4 + j) * half
                 other = ref[0:1, lane : lane + half]
                 parts += [jnp.where(core == 0, mine, other), jnp.where(core == 0, other, mine), gap]
-            for _ in range(2 - len(hiddens)):
-                parts += [blank, blank, gap]
             line = pl.ds(base + owned * 4 + jnp.bitwise_xor(wid, j), 1)
             out_ref[line, 0:512] = jnp.concatenate(parts, axis=1)
-        for place_of, kind in enumerate(kinds):
-            line = pl.ds(base + owned * 4 + place_of, 1)
-            value = heads[kind : kind + 1, i * step : (i + 1) * step]
-            out_ref[line, 512:768] = jnp.concatenate([value, gap], axis=1)
-
-
-def small_table(kinds, place, rows, heads, hiddens):
+        for first, heads, kinds in ((base, channel_heads, (0, 1, 2)), (base + BIASES, window_heads, (0, 2))):
+            for position, kind in enumerate(kinds):
+                value = heads[kind : kind + 1, i * step : (i + 1) * step]
+                line = pl.ds(first + owned * 4 + position, 1)
+                out_ref[line, 512:768] = jnp.concatenate([value, gap], axis=1)
+
+
+def small_table(place, rows, window_heads, channel_heads, hiddens):
     counts = [item.shape[0] for item in rows]
-    total = (sum(counts) + 7) // 8 * 8 + BIASES
+    total = (sum(counts) + 7) // 8 * 8 + 2 * BIASES
     return call(
-        partial(small_kernel, counts, kinds), [struct((total, rows[0].shape[1]), F32)],
-        [place, *rows, heads, *hiddens], SMALL,
+        partial(small_kernel, counts), [struct((total, rows[0].shape[1]), F32)],
+        [place, *rows, window_heads, channel_heads, *hiddens], SMALL,
     )[0]
 
 
-def outputs_kernel(place_ref, early_ref, late_ref, *outs):
+def outputs_kernel(place_ref, table_ref, *outs):
     hid = place_ref[2]
-    early_base = early_ref.shape[0] - BIASES
-    late_base = late_ref.shape[0] - BIASES
-    plan = (
-        (outs[:10], late_ref, 0, late_ref, 10, late_base, early_ref, 10, 0),
-        (outs[10:], early_ref, 0, early_ref, 13, early_base, early_ref, 16, 1),
-    )
-    for refs, sums, first, one, at_one, heads_base, two, at_two, column in plan:
+    base = table_ref.shape[0] - 2 * BIASES
+    plan = ((outs[:10], 0, 10, 13, base + BIASES, 0), (outs[10:], 16, 26, 29, base, 256))
+    for refs, sums, one, two, heads, lane in plan:
         kernel, cbias, gain, shift, inb, outb, gain_two, shift_two, upb, downb = refs
-        heads = late_ref if column == 0 else early_ref
-        kernel[...] = sums[pl.ds(first, 9), :]
-        for ref, source, row in (
-            (cbias, sums, 9), (gain, one, at_one), (shift, one, at_one + 1), (outb, one, at_one + 2),
-            (gain_two, two, at_two), (shift_two, two, at_two + 1), (downb, two, at_two + 2),
-        ):
-            ref[...] = source[pl.ds(row, 1), :].reshape(-1)
+        kernel[...] = table_ref[pl.ds(sums, 9), :]
+        rows = (sums + 9, one, one + 1, one + 2, two, two + 1, two + 2)
+        for ref, row in zip((cbias, gain, shift, outb, gain_two, shift_two, downb), rows):
+            ref[...] = table_ref[pl.ds(row, 1), :].reshape(-1)
         step = inb.shape[1]
         for index in range(inb.shape[0]):
-            inb[pl.ds(index, 1), :] = heads[pl.ds(heads_base + hid * 4 + index, 1), :][:, 512 : 512 + step]
+            inb[pl.ds(index, 1), :] = table_ref[pl.ds(heads + hid * 4 + index, 1), :][:, 512 : 512 + step]
         for index in range(4):
-            line = early_ref[pl.ds(early_base + hid * 4 + index, 1), :]
-            upb[pl.ds(index * step, step)] = line[:, column * 256 : column * 256 + step].reshape(-1)
-
-
-def small_outputs(place, early, late):
-    width = early.shape[1]
+            line = table_ref[pl.ds(base + hid * 4 + index, 1), :]
+            upb[pl.ds(index * step, step)] = line[:, lane : lane + step].reshape(-1)
+
+
+def small_outputs(place, table):
+    width = table.shape[1]
     step = width // 4
     outs = []
     for count in (2, 3):
         flat = struct((width,), F32)
         outs += [struct((9, width), F32), flat, flat, flat, struct((count, step), F32), flat, flat, flat, flat, flat]
-    return call(outputs_kernel, outs, [place, early, late], SMALL)
+    return call(outputs_kernel, outs, [place, table], SMALL)
+
+
+def join_kernel(first_ref, second_ref, out_ref):
+    count = first_ref.shape[0]
+    out_ref[:count] = first_ref[...]
+    out_ref[count:] = second_ref[...]
+
+
+def join(first, second, wait=5):
+    shape = (2 * first.shape[0], *first.shape[1:])
+    return call(join_kernel, [struct(shape, first.dtype)], [first, second], flops=max(wait * WAIT, 1))[0]
+
+
+def fold_kernel(kept_ref, arrived_ref, still_ref, sent_ref):
+    half = still_ref.shape[0]
+    still_ref[...] = kept_ref[:half].astype(F32) + arrived_ref[:half].astype(F32)
+    sent_ref[...] = (kept_ref[half:].astype(F32) + arrived_ref[half:].astype(F32)).astype(BF16)
+
+
+def fold(kept, arrived):
+    shape = (kept.shape[0] // 2, *kept.shape[1:])
+    return call(fold_kernel, [struct(shape, F32), struct(shape, BF16)], [kept, arrived], flops=5 * WAIT)
+
+
+def total_kernel(kept_ref, arrived_ref, out_ref):
+    out_ref[...] = kept_ref[0] + arrived_ref[0].astype(F32)
+
+
+def fold_last(kept, arrived):
+    return call(total_kernel, [struct(kept.shape[1:], F32)], [kept, arrived], flops=5 * WAIT)[0]
+
+
+def rows_kernel(place_ref, own_ref, other_ref, *outs):
+    rows = own_ref.shape[1]
+    core = place_ref[0]
+    for index, out_ref in enumerate(outs):
+        out_ref[pl.ds(pl.multiple_of(core * rows, 8), rows), :] = own_ref[index]
+        out_ref[pl.ds(pl.multiple_of((1 - core) * rows, 8), rows), :] = other_ref[index]
+
+
+def both_rows(place, own, other):
+    out = struct((2 * own.shape[1], own.shape[2]), F32)
+    return call(rows_kernel, [out, out], [place, own, other], SMALL)
+
+
+def columns_kernel(place_ref, own_ref, other_ref, in_ref, out_ref):
+    half = own_ref.shape[2]
+    core = place_ref[0]
+    for turn, ref in ((core, own_ref), (1 - core, other_ref)):
+        cut = pl.ds(pl.multiple_of(turn * half, 128), half)
+        for m in range(3):
+            in_ref[m, :, cut] = ref[m]
+        out_ref[:, cut] = ref[3]
+
+
+def both_columns(place, own, other):
+    rows, width = own.shape[1], own.shape[2] * 2
+    return call(
+        columns_kernel, [struct((3, rows, width), F32), struct((rows, width), F32)], [place, own, other], SMALL
+    )
+
+
+def add_kernel(first_ref, second_ref, out_ref):
+    out_ref[...] = first_ref[...] + second_ref[...]
+
+
+def add(first, second):
+    return call(add_kernel, [struct(first.shape, F32)], [first, second])[0]
 
 
 class Line:
@@ -791,61 +837,24 @@
         return self.gate(function(*self.gate(operands)))
 
 
-class Gather:
-    def __init__(self, line, piece):
-        self.line, self.near, self.step, self.flight = line, piece, 0, ()
+class Scatter:
+    def __init__(self, line, place, near, far, heads):
+        self.line, self.place, self.kept, self.sent = line, place, near, far
+        self.heads, self.step = heads, 0
 
     def advance(self):
         gate = self.line.gate
         if self.step in (1, 2, 3):
-            arrived = gate(self.flight[0])
-            self.near = jnp.concatenate([self.near, arrived], axis=0)
+            self.kept, self.sent = self.line.run(fold, self.kept, self.flight)
         elif self.step == 4:
-            self.far, self.other_near = gate(self.flight)
-        elif self.step == 5:
-            self.other_far = gate(self.flight[0])
-        if self.step < 4:
-            self.near = gate(self.near)
-        if self.step == 0:
-            self.flight = (exchange(self.near, "wid", 1),)
-        elif self.step == 1:
-            self.flight = (exchange(self.near, "wid", 2),)
-        elif self.step == 2:
-            self.flight = (cross(self.near, True),)
-        elif self.step == 3:
-            self.flight = (cross(self.near, False), sibling(self.near))
-        elif self.step == 4:
-            self.far = gate(self.far)
-            self.flight = (sibling(self.far),)
-        self.step += 1
-
-    def parts(self):
-        return [self.near, self.far, self.other_near, self.other_far]
-
-    def rows(self):
-        return [part.reshape(-1, part.shape[-1]) for part in self.parts()]
-
-
-class Scatter:
-    def __init__(self, line, near, far, axis):
-        self.line, self.kept, self.sent, self.axis, self.step = line, near, far, axis, 0
-
-    def advance(self):
-        gate = self.line.gate
-        if self.step in (1, 2, 3):
-            arrived = gate(self.flight)
-            half = arrived.shape[0] // 2
-            self.sent = (self.kept[half:].astype(F32) + arrived[half:].astype(F32)).astype(BF16)
-            self.kept = self.kept[:half].astype(F32) + arrived[:half].astype(F32)
-        elif self.step == 4:
-            total = self.kept[0] + gate(self.flight)[0].astype(F32)
+            self.kept = self.line.run(fold_last, self.kept, self.flight)
             bit = 2
             while bit < lax.axis_size("dp"):
-                total = total + exchange(total, "dp", bit)
+                self.kept = self.line.run(add, self.kept, exchange(self.kept, "dp", bit))
                 bit *= 2
-            self.kept = total
         elif self.step == 5:
-            self.total = by_core(self.kept, gate(self.flight), self.axis)
+            join_cores = both_columns if self.heads else both_rows
+            self.total = self.line.run(join_cores, self.place, self.kept, self.flight)
         if self.step < 4:
             self.sent = gate(self.sent)
         if self.step == 0:
@@ -873,7 +882,7 @@
 
     def advance(self):
         if self.flight is not None:
-            self.table = self.table + self.line.gate(self.flight)
+            self.table = self.line.run(add, self.table, self.flight)
             self.flight = None
         if self.steps:
             axis, bit = self.steps.pop(0)
@@ -899,154 +908,177 @@
     place = jnp.concatenate([at, own_sizes])
     line = Line(winb[0, 0])
 
-    groups = [
-        Gather(line, piece)
-        for piece in pieces(place, winw, woutw, wupw, wdownw, cinw, coutw, cupw, cdownw)
-    ]
-
-    def go(*numbers):
-        for number in numbers:
-            groups[number].advance()
-
-    go(0)
+    def send(move, values):
+        return move(line.gate(values))
+
+    def w1(values):
+        return exchange(values, "wid", 1)
+
+    def w2(values):
+        return exchange(values, "wid", 2)
+
+    def h1(values):
+        return cross(values, True)
+
+    def h2(values):
+        return cross(values, False)
+
+    gate = line.gate
+
+    def both(near, arrived, wait=5):
+        return line.run(partial(join, wait=wait), near, arrived)
+
+    own0, own1, own2, own3 = pieces(place, winw, woutw, wupw, wdownw, cinw, coutw, cupw, cdownw)
+
+    w1_0 = send(w1, own0)
     table, bias = line.run(
         tables, wkernel, wcbias, wgain, wshift, winb, woutb, wgain_two, wshift_two, wupb, wdownb,
         ckernel, ccbias, cgain, cshift, cinb, coutb, cgain_two, cshift_two, cupb, cdownb,
     )
-    go(0, 1)
-    bias_one = cross(bias, True)
+    near0 = both(own0, w1_0)
+    w2_0 = send(w2, near0)
+    w1_1 = send(w1, own1)
+    bias_one = send(h1, bias)
     start, after_conv = line.run(partial(first_conv, 0), place, inputs, table)
-    cotangent, low_four = line.run(low_cells, place, cotangent)
-    bias_one = line.gate(bias_one)
-    bias_two = cross(jnp.stack([bias, bias_one]), False)
-    low_four_other = sibling(low_four)
-    go(1, 2)
-    go(0, 2, 3)
-    bias_two, low_four_other = line.gate((bias_two, low_four_other))
+    cotangent = line.run(cells, cotangent)
+    bias_one = gate(bias_one)
+    bias_two = send(h2, jnp.stack([bias, bias_one]))
+    near1 = both(own1, w1_1)
+    bias_two = gate(bias_two)
     head_bias, hidden_bias = line.run(order_biases, place, bias, bias_one, bias_two)
-    go(0)
-    go(1, 3, 4)
-    go(0, 1, 0)
-    att_one = groups[0].parts()
+    near0 = both(near0, w2_0)
+    h1_0 = send(h1, near0)
+    w2_1 = send(w2, near1)
+    near0 = both(near0, h1_0, 0)
+    h2_0 = send(h2, near0)
+    near1 = both(near1, w2_1, 9)
+    h1_1 = send(h1, near1)
+    w1_2 = send(w1, own2)
+    far0 = gate(h2_0)
+    s_0 = send(sibling, near0), send(sibling, far0)
+    near2 = both(own2, w1_2)
+    w2_2 = send(w2, near2)
+    s_0 = gate(s_0)
+    att_one = [near0, far0, *s_0]
     after_attn, normed_one, qkv_one, mixed_one = line.run(
         partial(attention, True), place, after_conv, table, head_bias, att_one
     )
-    go(2, 4, 5)
-    go(1, 2, 3, 5, 2, 1, 3, 2)
-    ups_two, downs_two = groups[1].rows(), groups[2].rows()
+    near1 = both(near1, h1_1)
+    h2_1 = send(h2, near1)
+    near2 = both(near2, w2_2)
+    h1_2 = send(h1, near2)
+    w1_3 = send(w1, own3)
+    near3 = both(own3, w1_3)
+    w2_3 = send(w2, near3)
+    near2 = both(near2, h1_2)
+    h2_2 = send(h2, near2)
+    near3 = both(near3, w2_3)
+    h1_3 = send(h1, near3)
+    far1 = gate(h2_1)
+    far2 = gate(h2_2)
+    s_1 = send(sibling, near1), send(sibling, far1)
+    near3 = both(near3, h1_3)
+    h2_3 = send(h2, near3)
+    s_1 = gate(s_1)
+    mlp_two = [near1, far1, *s_1]
     after_mlp, acted_two, fpack_two, deriv_two = line.run(
-        partial(mlp, 0, False), place, after_attn, table, hidden_bias, ups_two, downs_two
-    )
-    fpack_two_other = sibling(fpack_two)
-    go(4, 3, 4, 5)
+        partial(mlp, 0), place, after_attn, table, hidden_bias, mlp_two
+    )
+    s_2 = send(sibling, near2), send(sibling, far2)
     after_conv_c = line.run(partial(conv, 16), place, after_mlp, table)
-    go(3, 5)
-    att_three = groups[3].parts()
+    s_2 = gate(s_2)
+    s_3 = send(sibling, near3)
+    att_three = [near2, far2, *s_2]
     after_attn_c, normed_three, qkv_three, mixed_three = line.run(
         partial(attention, False), place, after_conv_c, table, head_bias, att_three
     )
-    fpack_two_other = line.gate(fpack_two_other)
-    go(4, 5, 4, 5)
-    ups_four, downs_four = groups[4].rows(), groups[5].rows()
+    s_3 = gate(s_3)
+    fpack_two_other = gate(send(sibling, fpack_two))
+    far3 = gate(h2_3)
+    s_far3 = gate(send(sibling, far3))
+    mlp_four = [near3, far3, s_3, s_far3]
     outputs, acted_four, fpack_four, deriv_four = line.run(
-        partial(mlp, 16, True), place, after_attn_c, table, hidden_bias, ups_four, downs_four
-    )
-
-    def scatter(near, far, axis):
-        group = Scatter(line, near.reshape((8, -1) + near.shape[-1:] if axis == 0 else near.shape),
-                        far.reshape((8, -1) + far.shape[-1:] if axis == 0 else far.shape), axis)
+        partial(mlp, 16), place, after_attn_c, table, hidden_bias, mlp_four
+    )
+
+    def scatter(near, far, heads):
+        group = Scatter(line, place, near, far, heads)
         group.advance()
         return group
 
-    fpack_four_other = line.gate(sibling(fpack_four))
-    d_four = scatter(*line.run(pair_grads, acted_four, fpack_four_other, low_four, low_four_other), 0)
+    fpack_four_other = send(sibling, fpack_four)
     flowing, gh_four, bpack_four, little_four, upb_four = line.run(
-        partial(mlp_back, 16), place, cotangent, after_attn_c, table, deriv_four, ups_four, downs_four
-    )
-    bpack_four_other = sibling(bpack_four)
-    d_four.advance()
-    bpack_four_other = line.gate(bpack_four_other)
-    u_four = scatter(*line.run(pair_grads, gh_four, bpack_four_other, fpack_four, fpack_four_other), 0)
-    d_four.advance()
-    flowing, left_three, mine_three, theirs_three, little_three, inb_three = line.run(
+        partial(mlp_back, 16), place, cotangent, after_attn_c, table, deriv_four, mlp_four
+    )
+    fpack_four_other = gate(fpack_four_other)
+    bpack_four_other = gate(send(sibling, bpack_four))
+    m_four = scatter(
+        *line.run(pair_grads, acted_four, fpack_four, fpack_four_other, gh_four, bpack_four, bpack_four_other), False
+    )
+    flowing, left_three, rest_three, mine_three, little_three, inb_three = line.run(
         partial(attention_back, False),
         place, flowing, after_conv_c, table, normed_three, qkv_three, mixed_three, att_three,
     )
-    sent_three = sibling(left_three), sibling(theirs_three)
-    u_four.advance()
-    sent_three = line.gate(sent_three)
-    a_three = scatter(*line.run(head_grads, place, left_three, sent_three[0], mine_three, sent_three[1]), 2)
-    d_four.advance()
-    u_four.advance()
+    sent_three = gate((send(sibling, left_three), send(sibling, rest_three)))
+    near_far = line.run(head_grads, place, left_three, rest_three, *sent_three, mine_three)
+    m_four.advance()
+    a_three = scatter(*near_far, True)
     flowing, sums_three = line.run(partial(conv_back, 16, False), place, flowing, after_mlp, table)
     flowing, gh_two, bpack_two, little_two, upb_two = line.run(
-        partial(mlp_back, 0), place, flowing, after_attn, table, deriv_two, ups_two, downs_two
-    )
-    bpack_two_other = sibling(bpack_two)
+        partial(mlp_back, 0), place, flowing, after_attn, table, deriv_two, mlp_two
+    )
+    m_four.advance()
+    bpack_two_other = gate(send(sibling, bpack_two))
+    near_far = line.run(pair_grads, acted_two, fpack_two, fpack_two_other, gh_two, bpack_two, bpack_two_other)
     a_three.advance()
-    bpack_two_other = line.gate(bpack_two_other)
-    d_two = scatter(*line.run(pair_grads, acted_two, fpack_two_other, bpack_two, bpack_two_other), 0)
-    u_four.advance()
-    d_four.advance()
-    a_three.advance()
-    u_two = scatter(*line.run(pair_grads, gh_two, bpack_two_other, fpack_two, fpack_two_other), 0)
-    early = line.run(
-        partial(small_table, (0, 1, 2)), place,
-        [sums_three, little_two, little_three, little_four], inb_three, [upb_two, upb_four],
-    )
-    early = Small(line, early)
-    early.advance()
-    u_four.advance()
-    flowing, left_one, mine_one, theirs_one, little_one, inb_one = line.run(
+    m_two = scatter(*near_far, False)
+    flowing, left_one, rest_one, mine_one, little_one, inb_one = line.run(
         partial(attention_back, True),
         place, flowing, after_conv, table, normed_one, qkv_one, mixed_one, att_one,
     )
-    sent_one = sibling(left_one), sibling(theirs_one)
-    d_two.advance()
     a_three.advance()
-    early.advance()
-    sent_one = line.gate(sent_one)
-    a_one = scatter(*line.run(head_grads, place, left_one, sent_one[0], mine_one, sent_one[1]), 2)
-    u_two.advance()
-    d_two.advance()
-    early.advance()
+    m_four.advance()
+    sent_one = gate((send(sibling, left_one), send(sibling, rest_one)))
+    near_far = line.run(head_grads, place, left_one, rest_one, *sent_one, mine_one)
+    m_two.advance()
     input_grad, sums_one = line.run(partial(conv_back, 0, True), place, flowing, start, table)
-    late = Small(line, line.run(partial(small_table, (0, 2)), place, [sums_one, little_one], inb_one, []))
-    early.advance()
-    late.advance()
+    small = line.run(
+        small_table, place, [sums_one, little_one, little_two, sums_three, little_three, little_four],
+        inb_one, inb_three, [upb_two, upb_four],
+    )
+    m_two.advance()
+    a_one = scatter(*near_far, True)
+    m_four.advance()
     a_three.advance()
-    u_two.advance()
-    late.advance()
-    early.advance()
+    small = Small(line, small)
+    small.advance()
+    m_four.advance()
+    small.advance()
+    a_three.advance()
     a_one.advance()
-    late.advance()
-    d_two.advance()
-    early.advance()
+    small.advance()
+    a_three.advance()
     a_one.advance()
-    late.advance()
-    u_two.advance()
-    late.advance()
+    m_two.advance()
+    small.advance()
+    m_two.advance()
+    small.advance()
     a_one.advance()
-    u_two.advance()
-    while late.advance():
-        pass
-    while early.advance():
-        pass
-    small = line.run(small_outputs, place, early.table, late.table)
-    for group in (d_four, u_four, a_three, d_two, u_two, a_one):
-        while group.step < 6:
-            group.advance()
-    gatt_one, gatt_three = a_one.total, a_three.total
-
-    def ordered(small, attention, up, down):
+    m_two.advance()
+    a_one.advance()
+    small.advance()
+    a_one.advance()
+    small = line.run(small_outputs, place, small.table)
+
+    def ordered(small, attention, units):
         return (
-            *small[:4], attention[:3], small[4], attention[3], *small[5:8], up.total, small[8], down.total, small[9]
+            *small[:4], attention[0], small[4], attention[1], *small[5:8], units[0], small[8], units[1], small[9]
         )
 
     return (
         outputs, input_grad,
-        *ordered(small[:10], gatt_one, u_two, d_two),
-        *ordered(small[10:], gatt_three, u_four, d_four),
+        *ordered(small[:10], a_one.total, m_two.total),
+        *ordered(small[10:], a_three.total, m_four.total),
     )
 
 

time: 459 us -> 415 us (0.904)
  Pallas kernels: 176 us -> 102 us
  waiting for transfers between devices: 143 us -> 215 us
  other arithmetic: 28.6 us -> 0.09 us
  starting transfers between devices: 91.9 us -> 68.9 us
  local copies, waits for them, and re-layouts: 11.9 us -> 19.5 us
    pallas_call x25 -> x59, Pallas kernels: 176 us -> 102 us  [call(): pl.pallas_call(kernel, out_shape=list(outs), in_specs=specs, out_specs=[v...]
    ppermute x26 -> x18, waiting for transfers between devices: 30 us -> 79.1 us  [cross(): return lax.ppermute(values, ('dp', 'hid'), pairs)]
    ppermute x61 -> x41, waiting for transfers between devices: 113 us -> 135 us  [exchange(): return lax.ppermute(values, axis, pairs)]
    ppermute x61 -> x41, starting transfers between devices: 67.5 us -> 49.5 us  [exchange(): return lax.ppermute(values, axis, pairs)]
    add x24 -> x0, other arithmetic: 13.2 us -> none  [the longest x8 6.47 us: advance(): self.kept = self.kept[:half].astype(F32) + arrived[:half].astype(F32)]
    concatenate x24 -> x0, other arithmetic: 8.2 us -> none  [the longest x6 5 us: by_core(): jnp.concatenate([jnp.where(second, other, own), jnp.where(second, own, ot...]
    unnamed x108 -> x112, local copies, waits for them, and re-layouts: 10.9 us -> 18.8 us
    ppermute x26 -> x18, starting transfers between devices: 24.4 us -> 19.4 us  [cross(): return lax.ppermute(values, ('dp', 'hid'), pairs)]
  transfers between devices with their start and end apart: 87 -> 59, of which waited for: 33 -> 34; matrix products, arithmetic and copies ran while one was open for 5% -> 0% of each run, Pallas kernels for 34% -> 20%
where the time goes in v5:
time: 415 us; the launch traced here: 407 us
  waiting for transfers between devices  215 us (52%)
  Pallas kernels  102 us (25%)
  starting transfers between devices  68.9 us (17%)
  local copies, waits for them, and re-layouts  19.5 us (5%)
    ppermute x41, waiting for transfers between devices, exchange(): return lax.ppermute(values, axis, pairs)  135 us
    pallas_call x59, Pallas kernels, call(): pl.pallas_call(kernel, out_shape=list(outs), in_specs=specs, out_specs=[v...  102 us
    ppermute x18, waiting for transfers between devices, cross(): return lax.ppermute(values, ('dp', 'hid'), pairs)  79.1 us
    ppermute x41, starting transfers between devices, exchange(): return lax.ppermute(values, axis, pairs)  49.5 us
    ppermute x18, starting transfers between devices, cross(): return lax.ppermute(values, ('dp', 'hid'), pairs)  19.4 us
    unnamed x112, local copies, waits for them, and re-layouts  18.8 us
  transfers between devices with their start and end apart: 59, of which 34 were waited for; matrix products, arithmetic and copies ran while one was open for 0% of the time, Pallas kernels for 20%

profile of v5, /device:TPU:1, one launch (start us, length us, event | category | flops | bytes accessed | tf_op | source)
XLA Modules:
  0.0 407.2 jit_solution(6934882305903285393)
XLA Ops:
  33.2 4.5 %collective-permute-done.5.second_ref = bf16[4,4,48,384]{3,2,1,0:T(8,128)(2,1)S(1)} collective-permute-done((bf16[4,4,48,384]{3,2,1,0:T(8,128)(2,1)S(1)}, bf16[4,4,48,384]{3,2,1,0:T(8,128)(2,1)S(1)}, u32[]{:S(2)}, u32[]{:S(2)}) %collective-permute-start.5) | collective-permute-done | bytes 589856 | tf_op jit(solution)/shard_map/ppermute | solution.py:36
  39.8 19.0 %collective-permute-done.7.second_ref = bf16[2,2,96,768]{3,2,1,0:T(8,128)(2,1)S(1)} collective-permute-done((bf16[2,2,96,768]{3,2,1,0:T(8,128)(2,1)S(1)}, bf16[2,2,96,768]{3,2,1,0:T(8,128)(2,1)S(1)}, u32[]{:S(2)}, u32[]{:S(2)}) %collective-permute-start.7) | collective-permute-done | bytes 589856 | tf_op jit(solution)/shard_map/ppermute | solution.py:23
  58.9 8.4 %collective-permute-start.9 = (bf16[8,4,48,384]{3,2,1,0:T(8,128)(2,1)S(1)}, bf16[8,4,48,384]{3,2,1,0:T(8,128)(2,1)S(1)}, u32[]{:S(2)}, u32[]{:S(2)}) collective-permute-start(bf16[8,4,48,384]{3,2,1,0:T(8,128)(2,1)S(1)} %collective-permute-done.6.p1), channel_id=1, source_target_pairs={{0,16},{16,0},{1,17},{17,1},{2,18},{18,2},{3,19},{19,3},{4,20},{20... | collective-permute-start | bytes 3538952 | tf_op jit(solution)/shard_map/ppermute | solution.py:23
  67.3 4.3 %collective-permute-done.10.second_ref = bf16[1,4,48,384]{3,2,1,0:T(8,128)(2,1)S(1)} collective-permute-done((bf16[1,4,48,384]{3,2,1,0:T(8,128)(2,1)S(1)}, bf16[1,4,48,384]{3,2,1,0:T(8,128)(2,1)S(1)}, u32[]{:S(2)}, u32[]{:S(2)}) %collective-permute-start.10) | collective-permute-done | bytes 147488 | tf_op jit(solution)/shard_map/ppermute | solution.py:23
  71.8 9.6 %shard_map.537 = (f32[288,768]{1,0:T(8,128)S(1)}, bf16[288,768]{1,0:T(8,128)(2,1)S(1)}, bf16[288,2304]{1,0:T(8,128)(2,1)S(1)}, bf16[288,768]{1,0:T(8,128)(2,1)S(1)}) custom-call(s32[5]{0:T(128)S(1)} %pad_add_fusion.place_ref, f32[288,768]{1,0:T(8,128)S(1)} %get-tuple-element.1122.values_ref, f32[32,768]{1,0:T(8,128)S(1)} %get-tuple-element.1194.table_ref, ...), custom_call_target="tpu_custom_call" | custom-call | flops 1 | bytes 1 | tf_op jit(solution)/shard_map/pallas_call | solution.py:61
  91.0 4.9 %collective-permute-done.14.second_ref = bf16[1,2,96,768]{3,2,1,0:T(8,128)(2,1)S(1)} collective-permute-done((bf16[1,2,96,768]{3,2,1,0:T(8,128)(2,1)S(1)}, bf16[1,2,96,768]{3,2,1,0:T(8,128)(2,1)S(1)}, u32[]{:S(2)}, u32[]{:S(2)}) %collective-permute-start.14) | collective-permute-done | bytes 294944 | tf_op jit(solution)/shard_map/ppermute | solution.py:23
  96.0 8.8 %collective-permute-done.16.second_ref = bf16[4,4,48,384]{3,2,1,0:T(8,128)(2,1)S(1)} collective-permute-done((bf16[4,4,48,384]{3,2,1,0:T(8,128)(2,1)S(1)}, bf16[4,4,48,384]{3,2,1,0:T(8,128)(2,1)S(1)}, u32[]{:S(2)}, u32[]{:S(2)}) %collective-permute-start.16) | collective-permute-done | bytes 589856 | tf_op jit(solution)/shard_map/ppermute | solution.py:36
  106.0 27.6 %collective-permute-done.15.second_ref = bf16[2,2,96,768]{3,2,1,0:T(8,128)(2,1)S(1)} collective-permute-done((bf16[2,2,96,768]{3,2,1,0:T(8,128)(2,1)S(1)}, bf16[2,2,96,768]{3,2,1,0:T(8,128)(2,1)S(1)}, u32[]{:S(2)}, u32[]{:S(2)}) %collective-permute-start.15) | collective-permute-done | bytes 589856 | tf_op jit(solution)/shard_map/ppermute | solution.py:23
  138.4 13.9 %collective-permute-done.20.second_ref = bf16[4,2,96,768]{3,2,1,0:T(8,128)(2,1)S(1)} collective-permute-done((bf16[4,2,96,768]{3,2,1,0:T(8,128)(2,1)S(1)}, bf16[4,2,96,768]{3,2,1,0:T(8,128)(2,1)S(1)}, u32[]{:S(2)}, u32[]{:S(2)}) %collective-permute-start.20) | collective-permute-done | bytes 1179680 | tf_op jit(solution)/shard_map/ppermute | solution.py:36
  152.4 4.3 %shard_map.544 = (f32[288,768]{1,0:T(8,128)S(1)}, bf16[288,1536]{1,0:T(8,128)(2,1)S(1)}, bf16[288,2304]{1,0:T(8,128)(2,1)S(1)}, f32[288,3072]{1,0:T(8,128)S(1)}) custom-call(s32[5]{0:T(128)S(1)} %pad_add_fusion.place_ref, f32[288,768]{1,0:T(8,128)S(1)} %get-tuple-element.1062.values_ref, f32[32,768]{1,0:T(8,128)S(1)} %get-tuple-element.1194.table_ref, ...), custom_call_target="tpu_custom_call" | custom-call | flops 1 | bytes 1 | tf_op jit(solution)/shard_map/pallas_call | solution.py:61
  164.2 7.8 %shard_map.546 = (f32[288,768]{1,0:T(8,128)S(1)}, bf16[288,768]{1,0:T(8,128)(2,1)S(1)}, bf16[288,2304]{1,0:T(8,128)(2,1)S(1)}, bf16[288,768]{1,0:T(8,128)(2,1)S(1)}) custom-call(s32[5]{0:T(128)S(1)} %pad_add_fusion.place_ref, f32[288,768]{1,0:T(8,128)S(1)} %shard_map.545.values_ref, f32[32,768]{1,0:T(8,128)S(1)} %get-tuple-element.1194.table_ref, ...), custom_call_target="tpu_custom_call" | custom-call | flops 1 | bytes 1 | tf_op jit(solution)/shard_map/pallas_call | solution.py:61
  178.8 12.7 %collective-permute-done.23.p1 = bf16[8,2,96,768]{3,2,1,0:T(8,128)(2,1)S(1)} collective-permute-done((bf16[8,2,96,768]{3,2,1,0:T(8,128)(2,1)S(1)}, bf16[8,2,96,768]{3,2,1,0:T(8,128)(2,1)S(1)}, u32[]{:S(2)}, u32[]{:S(2)}) %collective-permute-start.23) | collective-permute-done | bytes 2359328 | tf_op jit(solution)/shard_map/ppermute | solution.py:36
  192.5 4.2 %collective-permute-done.26.p3 = bf16[8,2,96,768]{3,2,1,0:T(8,128)(2,1)S(1)} collective-permute-done((bf16[8,2,96,768]{3,2,1,0:T(8,128)(2,1)S(1)}, bf16[8,2,96,768]{3,2,1,0:T(8,128)(2,1)S(1)}, u32[]{:S(2)}, u32[]{:S(2)}) %collective-permute-start.26) | collective-permute-done | bytes 2359328 | tf_op jit(solution)/shard_map/ppermute | solution.py:23
  196.6 5.4 %shard_map.547 = (f32[392,768]{1,0:T(8,128)}, bf16[288,1536]{1,0:T(8,128)(2,1)S(1)}, bf16[288,2304]{1,0:T(8,128)(2,1)S(1)}, f32[288,3072]{1,0:T(8,128)S(1)}) custom-call(s32[5]{0:T(128)S(1)} %pad_add_fusion.place_ref, f32[288,768]{1,0:T(8,128)S(1)} %get-tuple-element.958.values_ref, f32[32,768]{1,0:T(8,128)S(1)} %get-tuple-element.1194.table_ref, ...), custom_call_target="tpu_custom_call" | custom-call | flops 1 | bytes 1 | tf_op jit(solution)/shard_map/pallas_call | solution.py:61
  214.4 5.1 %shard_map.549 = (bf16[8,2,96,768]{3,2,1,0:T(8,128)(2,1)S(1)}, bf16[8,2,96,768]{3,2,1,0:T(8,128)(2,1)S(1)}) custom-call(bf16[288,1536]{1,0:T(8,128)(2,1)S(1)} %copy-done.19, bf16[288,2304]{1,0:T(8,128)(2,1)S(1)} %copy-done.11, bf16[288,2304]{1,0:T(8,128)(2,1)S(1)} %copy-done.13, bf16[288,1536]{1,0:T(8,128)(2,1)S(1)} %get-tuple-element.989.hidden_ref, ...), custom_call_target="tpu_custom_call" | custom-call | flops 1 | bytes 1 | tf_op jit(solution)/shard_map/pallas_call | solution.py:61
  220.3 8.6 %shard_map.550 = (f32[288,768]{1,0:T(8,128)S(1)}, bf16[288,2304]{1,0:T(8,128)(2,1)S(1)}, bf16[288,1536]{1,0:T(8,128)(2,1)S(1)}, bf16[288,768]{1,0:T(8,128)(2,1)S...) custom-call(s32[5]{0:T(128)S(1)} %pad_add_fusion.place_ref, f32[288,768]{1,0:T(8,128)S(1)} %get-tuple-element.999.grads_ref, ...), custom_call_target="tpu_custom_call" | custom-call | flops 1 | bytes 1 | tf_op jit(solution)/shard_map/pallas_call | solution.py:61
  234.1 4.0 shard_map.551
  238.1 9.5 %collective-permute-done.31.arrived_ref = bf16[8,2,96,768]{3,2,1,0:T(8,128)(2,1)S(1)} collective-permute-done((bf16[8,2,96,768]{3,2,1,0:T(8,128)(2,1)S(1)}, bf16[8,2,96,768]{3,2,1,0:T(8,128)(2,1)S(1)}, u32[]{:S(2)}, u32[]{:S(2)}) %collective-permute-start.31) | collective-permute-done | bytes 2359328 | tf_op jit(solution)/shard_map/ppermute | solution.py:36
  252.9 4.0 shard_map.554
  256.9 6.6 %collective-permute-done.32.arrived_ref = bf16[4,2,96,768]{3,2,1,0:T(8,128)(2,1)S(1)} collective-permute-done((bf16[4,2,96,768]{3,2,1,0:T(8,128)(2,1)S(1)}, bf16[4,2,96,768]{3,2,1,0:T(8,128)(2,1)S(1)}, u32[]{:S(2)}, u32[]{:S(2)}) %collective-permute-start.32) | collective-permute-done | bytes 1179680 | tf_op jit(solution)/shard_map/ppermute | solution.py:36
  268.3 5.3 %shard_map.556 = (bf16[8,2,96,768]{3,2,1,0:T(8,128)(2,1)S(1)}, bf16[8,2,96,768]{3,2,1,0:T(8,128)(2,1)S(1)}) custom-call(bf16[288,1536]{1,0:T(8,128)(2,1)S(1)} %copy-done.17, bf16[288,2304]{1,0:T(8,128)(2,1)S(1)} %copy-done.5, bf16[288,2304]{1,0:T(8,128)(2,1)S(1)} %copy-done.7, bf16[288,1536]{1,0:T(8,128)(2,1)S(1)} %get-tuple-element.1101.hidden_ref, ...), custom_call_target="tpu_custom_call" | custom-call | flops 1 | bytes 1 | tf_op jit(solution)/shard_map/pallas_call | solution.py:61
  273.7 7.3 %collective-permute-done.34.arrived_ref = bf16[8,4,48,384]{3,2,1,0:T(8,128)(2,1)S(1)} collective-permute-done((bf16[8,4,48,384]{3,2,1,0:T(8,128)(2,1)S(1)}, bf16[8,4,48,384]{3,2,1,0:T(8,128)(2,1)S(1)}, u32[]{:S(2)}, u32[]{:S(2)}) %collective-permute-start.34) | collective-permute-done | bytes 1179680 | tf_op jit(solution)/shard_map/ppermute | solution.py:36
  283.8 12.9 %shard_map.558 = (f32[288,768]{1,0:T(8,128)S(1)}, bf16[288,2304]{1,0:T(8,128)(2,1)S(1)}, bf16[288,1536]{1,0:T(8,128)(2,1)S(1)}, bf16[288,768]{1,0:T(8,128)(2,1)S...) custom-call(s32[5]{0:T(128)S(1)} %pad_add_fusion.place_ref, f32[288,768]{1,0:T(8,128)S(1)} %get-tuple-element.1121.grads_ref, ...), custom_call_target="tpu_custom_call" | custom-call | flops 1 | bytes 1 | tf_op jit(solution)/shard_map/pallas_call | solution.py:61
  296.9 13.9 %collective-permute-done.36.arrived_ref = bf16[2,2,96,768]{3,2,1,0:T(8,128)(2,1)S(1)} collective-permute-done((bf16[2,2,96,768]{3,2,1,0:T(8,128)(2,1)S(1)}, bf16[2,2,96,768]{3,2,1,0:T(8,128)(2,1)S(1)}, u32[]{:S(2)}, u32[]{:S(2)}) %collective-permute-start.36) | collective-permute-done | bytes 589856 | tf_op jit(solution)/shard_map/ppermute | solution.py:23
  316.2 4.0 shard_map.561
  322.1 5.3 %shard_map.563 = (f32[392,768]{1,0:T(8,128)}, f32[10,768]{1,0:T(8,128)S(1)}) custom-call(s32[5]{0:T(128)S(1)} %pad_add_fusion.place_ref, f32[288,768]{1,0:T(8,128)S(1)} %get-tuple-element.1192.grads_ref, f32[288,768]{1,0:T(8,128)S(1)} %copy-done.21, f32[32,768]{1,0:T(8,128)S(1)} %get-tuple-element.1194.table_ref), custom_call_target="tpu_custom_call" | custom-call | flops 1 | bytes 1 | tf_op jit(solution)/shard_map/pallas_call | solution.py:61
  328.2 8.0 %collective-permute-done.42.arrived_ref = bf16[4,2,96,768]{3,2,1,0:T(8,128)(2,1)S(1)} collective-permute-done((bf16[4,2,96,768]{3,2,1,0:T(8,128)(2,1)S(1)}, bf16[4,2,96,768]{3,2,1,0:T(8,128)(2,1)S(1)}, u32[]{:S(2)}, u32[]{:S(2)}) %collective-permute-start.42) | collective-permute-done | bytes 1179680 | tf_op jit(solution)/shard_map/ppermute | solution.py:36
  345.1 6.7 %collective-permute-done.46.arrived_ref = bf16[8,4,48,384]{3,2,1,0:T(8,128)(2,1)S(1)} collective-permute-done((bf16[8,4,48,384]{3,2,1,0:T(8,128)(2,1)S(1)}, bf16[8,4,48,384]{3,2,1,0:T(8,128)(2,1)S(1)}, u32[]{:S(2)}, u32[]{:S(2)}) %collective-permute-start.46) | collective-permute-done | bytes 1179680 | tf_op jit(solution)/shard_map/ppermute | solution.py:36
  352.3 14.4 %collective-permute-done.49.arrived_ref = bf16[2,2,96,768]{3,2,1,0:T(8,128)(2,1)S(1)} collective-permute-done((bf16[2,2,96,768]{3,2,1,0:T(8,128)(2,1)S(1)}, bf16[2,2,96,768]{3,2,1,0:T(8,128)(2,1)S(1)}, u32[]{:S(2)}, u32[]{:S(2)}) %collective-permute-start.49) | collective-permute-done | bytes 589856 | tf_op jit(solution)/shard_map/ppermute | solution.py:23
  374.6 4.8 %collective-permute-done.53.arrived_ref = bf16[1,2,96,768]{3,2,1,0:T(8,128)(2,1)S(1)} collective-permute-done((bf16[1,2,96,768]{3,2,1,0:T(8,128)(2,1)S(1)}, bf16[1,2,96,768]{3,2,1,0:T(8,128)(2,1)S(1)}, u32[]{:S(2)}, u32[]{:S(2)}) %collective-permute-start.53) | collective-permute-done | bytes 294944 | tf_op jit(solution)/shard_map/ppermute | solution.py:23
  385.9 4.8 %collective-permute-start.57 = (f32[4,48,384]{2,1,0:T(8,128)S(1)}, f32[4,48,384]{2,1,0:T(8,128)S(1)}, u32[]{:S(2)}, u32[]{:S(2)}) collective-permute-start(f32[4,48,384]{2,1,0:T(8,128)S(1)} %shard_map.582.own_ref), channel_id=1, source_target_pairs={{0,16},{16,0},{1,17},{17,1},{2,18},{18,2},{3,19},{19,3},{4,20},{20... | collective-permute-start | bytes 884744 | tf_op jit(solution)/shard_map/ppermute | solution.py:23
  393.8 8.8 %collective-permute-done.54.second_ref = f32[64,768]{1,0:T(8,128)S(1)} collective-permute-done((f32[64,768]{1,0:T(8,128)S(1)}, f32[64,768]{1,0:T(8,128)S(1)}, u32[]{:S(2)}, u32[]{:S(2)}) %collective-permute-start.54) | collective-permute-done | bytes 196640 | tf_op jit(solution)/shard_map/ppermute | solution.py:23
  (260 shorter events, 135.9 us)
Async XLA Ops:
  16.4 11.4 %collective-permute-start.3 = (bf16[1,2,96,768]{3,2,1,0:T(8,128)(2,1)S(1)}, bf16[1,2,96,768]{3,2,1,0:T(8,128)(2,1)S(1)}, u32[]{:S(2)}, u32[]{:S(2)}) collective-permute-start(bf16[1,2,96,768]{3,2,1,0:T(8,128)(2,1)S(1)} %get-tuple-element.759.first_ref), channel_id=1, source_target_pairs={{0,1},{1,0},{2,3},{3,2},{4,5},{5,4},{6,7},{7,6},{8,9},{9,8},{10,11... | collective-permute-start | bytes 884744 | tf_op jit(solution)/shard_map/ppermute | solution.py:23
  30.4 28.4 %collective-permute-start.7 = (bf16[2,2,96,768]{3,2,1,0:T(8,128)(2,1)S(1)}, bf16[2,2,96,768]{3,2,1,0:T(8,128)(2,1)S(1)}, u32[]{:S(2)}, u32[]{:S(2)}) collective-permute-start(bf16[2,2,96,768]{3,2,1,0:T(8,128)(2,1)S(1)} %shard_map.531.first_ref), channel_id=1, source_target_pairs={{0,2},{1,3},{2,0},{3,1},{4,6},{5,7},{6,4},{7,5},{8,10},{9,11},{10,... | collective-permute-start | bytes 1769480 | tf_op jit(solution)/shard_map/ppermute | solution.py:23
  37.8 21.1 %collective-permute-start.6 = (bf16[8,4,48,384]{3,2,1,0:T(8,128)(2,1)S(1)}, bf16[8,4,48,384]{3,2,1,0:T(8,128)(2,1)S(1)}, u32[]{:S(2)}, u32[]{:S(2)}) collective-permute-start(bf16[8,4,48,384]{3,2,1,0:T(8,128)(2,1)S(1)} %shard_map.534.p0), channel_id=1, source_target_pairs={{0,8},{4,12},{8,0},{12,4},{16,20},{20,16},{24,28},{28,24},{1,9},{5... | collective-permute-start | bytes 3538952 | tf_op jit(solution)/shard_map/ppermute | solution.py:36
  58.9 12.8 %collective-permute-start.9 = (bf16[8,4,48,384]{3,2,1,0:T(8,128)(2,1)S(1)}, bf16[8,4,48,384]{3,2,1,0:T(8,128)(2,1)S(1)}, u32[]{:S(2)}, u32[]{:S(2)}) collective-permute-start(bf16[8,4,48,384]{3,2,1,0:T(8,128)(2,1)S(1)} %collective-permute-done.6.p1), channel_id=1, source_target_pairs={{0,16},{16,0},{1,17},{17,1},{2,18},{18,2},{3,19},{19,3},{4,20},{20... | collective-permute-start | bytes 3538952 | tf_op jit(solution)/shard_map/ppermute | solution.py:23
  67.3 15.6 %collective-permute-start.11 = (bf16[4,2,96,768]{3,2,1,0:T(8,128)(2,1)S(1)}, bf16[4,2,96,768]{3,2,1,0:T(8,128)(2,1)S(1)}, u32[]{:S(2)}, u32[]{:S(2)}) collective-permute-start(bf16[4,2,96,768]{3,2,1,0:T(8,128)(2,1)S(1)} %shard_map.535.first_ref), channel_id=1, source_target_pairs={{0,4},{4,0},{8,12},{12,8},{16,24},{20,28},{24,16},{28,20},{1,5},{5... | collective-permute-start | bytes 3538952 | tf_op jit(solution)/shard_map/ppermute | solution.py:36
  71.7 16.0 %collective-permute-start.13 = (bf16[2,4,48,384]{3,2,1,0:T(8,128)(2,1)S(1)}, bf16[2,4,48,384]{3,2,1,0:T(8,128)(2,1)S(1)}, u32[]{:S(2)}, u32[]{:S(2)}) collective-permute-start(bf16[2,4,48,384]{3,2,1,0:T(8,128)(2,1)S(1)} %shard_map.536.first_ref), channel_id=1, source_target_pairs={{0,2},{1,3},{2,0},{3,1},{4,6},{5,7},{6,4},{7,5},{8,10},{9,11},{10,... | collective-permute-start | bytes 884744 | tf_op jit(solution)/shard_map/ppermute | solution.py:23
  87.8 45.9 %collective-permute-start.12 = (bf16[8,2,96,768]{3,2,1,0:T(8,128)(2,1)S(1)}, bf16[8,2,96,768]{3,2,1,0:T(8,128)(2,1)S(1)}, u32[]{:S(2)}, u32[]{:S(2)}) collective-permute-start(bf16[8,2,96,768]{3,2,1,0:T(8,128)(2,1)S(1)} %shard_map.538.p0), channel_id=1, source_target_pairs={{0,8},{4,12},{8,0},{12,4},{16,20},{20,16},{24,28},{28,24},{1,9},{5... | collective-permute-start | bytes 7077896 | tf_op jit(solution)/shard_map/ppermute | solution.py:36
  88.2 16.5 %collective-permute-start.16 = (bf16[4,4,48,384]{3,2,1,0:T(8,128)(2,1)S(1)}, bf16[4,4,48,384]{3,2,1,0:T(8,128)(2,1)S(1)}, u32[]{:S(2)}, u32[]{:S(2)}) collective-permute-start(bf16[4,4,48,384]{3,2,1,0:T(8,128)(2,1)S(1)} %shard_map.539.first_ref), channel_id=1, source_target_pairs={{0,4},{4,0},{8,12},{12,8},{16,24},{20,28},{24,16},{28,20},{1,5},{5... | collective-permute-start | bytes 1769480 | tf_op jit(solution)/shard_map/ppermute | solution.py:36
  104.9 30.0 %collective-permute-start.17 = (bf16[8,4,48,384]{3,2,1,0:T(8,128)(2,1)S(1)}, bf16[8,4,48,384]{3,2,1,0:T(8,128)(2,1)S(1)}, u32[]{:S(2)}, u32[]{:S(2)}) collective-permute-start(bf16[8,4,48,384]{3,2,1,0:T(8,128)(2,1)S(1)} %shard_map.541.p0), channel_id=1, source_target_pairs={{0,8},{4,12},{8,0},{12,4},{16,20},{20,16},{24,28},{28,24},{1,9},{5... | collective-permute-start | bytes 3538952 | tf_op jit(solution)/shard_map/ppermute | solution.py:36
  106.0 27.6 %collective-permute-start.15 = (bf16[2,2,96,768]{3,2,1,0:T(8,128)(2,1)S(1)}, bf16[2,2,96,768]{3,2,1,0:T(8,128)(2,1)S(1)}, u32[]{:S(2)}, u32[]{:S(2)}) collective-permute-start(bf16[2,2,96,768]{3,2,1,0:T(8,128)(2,1)S(1)} %shard_map.540.first_ref), channel_id=1, source_target_pairs={{0,2},{1,3},{2,0},{3,1},{4,6},{5,7},{6,4},{7,5},{8,10},{9,11},{10,... | collective-permute-start | bytes 1769480 | tf_op jit(solution)/shard_map/ppermute | solution.py:23
  134.9 17.6 %collective-permute-start.19 = (bf16[8,2,96,768]{3,2,1,0:T(8,128)(2,1)S(1)}, bf16[8,2,96,768]{3,2,1,0:T(8,128)(2,1)S(1)}, u32[]{:S(2)}, u32[]{:S(2)}) collective-permute-start(bf16[8,2,96,768]{3,2,1,0:T(8,128)(2,1)S(1)} %collective-permute-done.12.p1), channel_id=1, source_target_pairs={{0,16},{16,0},{1,17},{17,1},{2,18},{18,2},{3,19},{19,3},{4,20},{20... | collective-permute-start | bytes 7077896 | tf_op jit(solution)/shard_map/ppermute | solution.py:23
  136.9 15.5 %collective-permute-start.18 = (bf16[8,2,96,768]{3,2,1,0:T(8,128)(2,1)S(1)}, bf16[8,2,96,768]{3,2,1,0:T(8,128)(2,1)S(1)}, u32[]{:S(2)}, u32[]{:S(2)}) collective-permute-start(bf16[8,2,96,768]{3,2,1,0:T(8,128)(2,1)S(1)} %shard_map.538.p0), channel_id=1, source_target_pairs={{0,16},{16,0},{1,17},{17,1},{2,18},{18,2},{3,19},{19,3},{4,20},{20... | collective-permute-start | bytes 7077896 | tf_op jit(solution)/shard_map/ppermute | solution.py:23
  136.9 15.3 %collective-permute-start.20 = (bf16[4,2,96,768]{3,2,1,0:T(8,128)(2,1)S(1)}, bf16[4,2,96,768]{3,2,1,0:T(8,128)(2,1)S(1)}, u32[]{:S(2)}, u32[]{:S(2)}) collective-permute-start(bf16[4,2,96,768]{3,2,1,0:T(8,128)(2,1)S(1)} %shard_map.542.first_ref), channel_id=1, source_target_pairs={{0,4},{4,0},{8,12},{12,8},{16,24},{20,28},{24,16},{28,20},{1,5},{5... | collective-permute-start | bytes 3538952 | tf_op jit(solution)/shard_map/ppermute | solution.py:36
  163.5 28.0 %collective-permute-start.23 = (bf16[8,2,96,768]{3,2,1,0:T(8,128)(2,1)S(1)}, bf16[8,2,96,768]{3,2,1,0:T(8,128)(2,1)S(1)}, u32[]{:S(2)}, u32[]{:S(2)}) collective-permute-start(bf16[8,2,96,768]{3,2,1,0:T(8,128)(2,1)S(1)} %shard_map.543.p0), channel_id=1, source_target_pairs={{0,8},{4,12},{8,0},{12,4},{16,20},{20,16},{24,28},{28,24},{1,9},{5... | collective-permute-start | bytes 7077896 | tf_op jit(solution)/shard_map/ppermute | solution.py:36
  219.5 28.1 %collective-permute-start.31 = (bf16[8,2,96,768]{3,2,1,0:T(8,128)(2,1)S(1)}, bf16[8,2,96,768]{3,2,1,0:T(8,128)(2,1)S(1)}, u32[]{:S(2)}, u32[]{:S(2)}) collective-permute-start(bf16[8,2,96,768]{3,2,1,0:T(8,128)(2,1)S(1)} %get-tuple-element.1039), channel_id=1, source_target_pairs={{0,8},{4,12},{8,0},{12,4},{16,20},{20,16},{24,28},{28,24},{1,9},{5... | collective-permute-start | bytes 7077896 | tf_op jit(solution)/shard_map/ppermute | solution.py:36
  248.1 15.4 %collective-permute-start.32 = (bf16[4,2,96,768]{3,2,1,0:T(8,128)(2,1)S(1)}, bf16[4,2,96,768]{3,2,1,0:T(8,128)(2,1)S(1)}, u32[]{:S(2)}, u32[]{:S(2)}) collective-permute-start(bf16[4,2,96,768]{3,2,1,0:T(8,128)(2,1)S(1)} %get-tuple-element.1084), channel_id=1, source_target_pairs={{0,4},{4,0},{8,12},{12,8},{16,24},{20,28},{24,16},{28,20},{1,5},{5... | collective-permute-start | bytes 3538952 | tf_op jit(solution)/shard_map/ppermute | solution.py:36
  265.6 15.3 %collective-permute-start.34 = (bf16[8,4,48,384]{3,2,1,0:T(8,128)(2,1)S(1)}, bf16[8,4,48,384]{3,2,1,0:T(8,128)(2,1)S(1)}, u32[]{:S(2)}, u32[]{:S(2)}) collective-permute-start(bf16[8,4,48,384]{3,2,1,0:T(8,128)(2,1)S(1)} %get-tuple-element.1109), channel_id=1, source_target_pairs={{0,8},{4,12},{8,0},{12,4},{16,20},{20,16},{24,28},{28,24},{1,9},{5... | collective-permute-start | bytes 3538952 | tf_op jit(solution)/shard_map/ppermute | solution.py:36
  281.3 15.5 %collective-permute-start.37 = (bf16[4,4,48,384]{3,2,1,0:T(8,128)(2,1)S(1)}, bf16[4,4,48,384]{3,2,1,0:T(8,128)(2,1)S(1)}, u32[]{:S(2)}, u32[]{:S(2)}) collective-permute-start(bf16[4,4,48,384]{3,2,1,0:T(8,128)(2,1)S(1)} %get-tuple-element.1147), channel_id=1, source_target_pairs={{0,4},{4,0},{8,12},{12,8},{16,24},{20,28},{24,16},{28,20},{1,5},{5... | collective-permute-start | bytes 1769480 | tf_op jit(solution)/shard_map/ppermute | solution.py:36
  282.8 28.0 %collective-permute-start.36 = (bf16[2,2,96,768]{3,2,1,0:T(8,128)(2,1)S(1)}, bf16[2,2,96,768]{3,2,1,0:T(8,128)(2,1)S(1)}, u32[]{:S(2)}, u32[]{:S(2)}) collective-permute-start(bf16[2,2,96,768]{3,2,1,0:T(8,128)(2,1)S(1)} %get-tuple-element.1145), channel_id=1, source_target_pairs={{0,2},{1,3},{2,0},{3,1},{4,6},{5,7},{6,4},{7,5},{8,10},{9,11},{10,... | collective-permute-start | bytes 1769480 | tf_op jit(solution)/shard_map/ppermute | solution.py:23
  282.8 37.4 %collective-permute-start.35 = (bf16[8,2,96,768]{3,2,1,0:T(8,128)(2,1)S(1)}, bf16[8,2,96,768]{3,2,1,0:T(8,128)(2,1)S(1)}, u32[]{:S(2)}, u32[]{:S(2)}) collective-permute-start(bf16[8,2,96,768]{3,2,1,0:T(8,128)(2,1)S(1)} %get-tuple-element.1141), channel_id=1, source_target_pairs={{0,8},{4,12},{8,0},{12,4},{16,20},{20,16},{24,28},{28,24},{1,9},{5... | collective-permute-start | bytes 7077896 | tf_op jit(solution)/shard_map/ppermute | solution.py:36
  320.8 15.4 %collective-permute-start.42 = (bf16[4,2,96,768]{3,2,1,0:T(8,128)(2,1)S(1)}, bf16[4,2,96,768]{3,2,1,0:T(8,128)(2,1)S(1)}, u32[]{:S(2)}, u32[]{:S(2)}) collective-permute-start(bf16[4,2,96,768]{3,2,1,0:T(8,128)(2,1)S(1)} %get-tuple-element.1229), channel_id=1, source_target_pairs={{0,4},{4,0},{8,12},{12,8},{16,24},{20,28},{24,16},{28,20},{1,5},{5... | collective-permute-start | bytes 3538952 | tf_op jit(solution)/shard_map/ppermute | solution.py:36
  320.9 15.5 %collective-permute-start.41 = (bf16[1,2,96,768]{3,2,1,0:T(8,128)(2,1)S(1)}, bf16[1,2,96,768]{3,2,1,0:T(8,128)(2,1)S(1)}, u32[]{:S(2)}, u32[]{:S(2)}) collective-permute-start(bf16[1,2,96,768]{3,2,1,0:T(8,128)(2,1)S(1)} %get-tuple-element.1226), channel_id=1, source_target_pairs={{0,1},{1,0},{2,3},{3,2},{4,5},{5,4},{6,7},{7,6},{8,9},{9,8},{10,11... | collective-permute-start | bytes 884744 | tf_op jit(solution)/shard_map/ppermute | solution.py:23
  320.9 16.6 %collective-permute-start.40 = (bf16[2,4,48,384]{3,2,1,0:T(8,128)(2,1)S(1)}, bf16[2,4,48,384]{3,2,1,0:T(8,128)(2,1)S(1)}, u32[]{:S(2)}, u32[]{:S(2)}) collective-permute-start(bf16[2,4,48,384]{3,2,1,0:T(8,128)(2,1)S(1)} %get-tuple-element.1224), channel_id=1, source_target_pairs={{0,2},{1,3},{2,0},{3,1},{4,6},{5,7},{6,4},{7,5},{8,10},{9,11},{10,... | collective-permute-start | bytes 884744 | tf_op jit(solution)/shard_map/ppermute | solution.py:23
  336.4 15.4 %collective-permute-start.46 = (bf16[8,4,48,384]{3,2,1,0:T(8,128)(2,1)S(1)}, bf16[8,4,48,384]{3,2,1,0:T(8,128)(2,1)S(1)}, u32[]{:S(2)}, u32[]{:S(2)}) collective-permute-start(bf16[8,4,48,384]{3,2,1,0:T(8,128)(2,1)S(1)} %get-tuple-element.1268), channel_id=1, source_target_pairs={{0,8},{4,12},{8,0},{12,4},{16,20},{20,16},{24,28},{28,24},{1,9},{5... | collective-permute-start | bytes 3538952 | tf_op jit(solution)/shard_map/ppermute | solution.py:36
  338.4 28.2 %collective-permute-start.49 = (bf16[2,2,96,768]{3,2,1,0:T(8,128)(2,1)S(1)}, bf16[2,2,96,768]{3,2,1,0:T(8,128)(2,1)S(1)}, u32[]{:S(2)}, u32[]{:S(2)}) collective-permute-start(bf16[2,2,96,768]{3,2,1,0:T(8,128)(2,1)S(1)} %get-tuple-element.1289), channel_id=1, source_target_pairs={{0,2},{1,3},{2,0},{3,1},{4,6},{5,7},{6,4},{7,5},{8,10},{9,11},{10,... | collective-permute-start | bytes 1769480 | tf_op jit(solution)/shard_map/ppermute | solution.py:23
  352.1 14.7 %collective-permute-start.50 = (bf16[4,4,48,384]{3,2,1,0:T(8,128)(2,1)S(1)}, bf16[4,4,48,384]{3,2,1,0:T(8,128)(2,1)S(1)}, u32[]{:S(2)}, u32[]{:S(2)}) collective-permute-start(bf16[4,4,48,384]{3,2,1,0:T(8,128)(2,1)S(1)} %get-tuple-element.1291), channel_id=1, source_target_pairs={{0,4},{4,0},{8,12},{12,8},{16,24},{20,28},{24,16},{28,20},{1,5},{5... | collective-permute-start | bytes 1769480 | tf_op jit(solution)/shard_map/ppermute | solution.py:36
  366.7 12.7 %collective-permute-start.53 = (bf16[1,2,96,768]{3,2,1,0:T(8,128)(2,1)S(1)}, bf16[1,2,96,768]{3,2,1,0:T(8,128)(2,1)S(1)}, u32[]{:S(2)}, u32[]{:S(2)}) collective-permute-start(bf16[1,2,96,768]{3,2,1,0:T(8,128)(2,1)S(1)} %get-tuple-element.1323), channel_id=1, source_target_pairs={{0,1},{1,0},{2,3},{3,2},{4,5},{5,4},{6,7},{7,6},{8,9},{9,8},{10,11... | collective-permute-start | bytes 884744 | tf_op jit(solution)/shard_map/ppermute | solution.py:23
  366.9 12.5 %collective-permute-start.55 = (bf16[2,4,48,384]{3,2,1,0:T(8,128)(2,1)S(1)}, bf16[2,4,48,384]{3,2,1,0:T(8,128)(2,1)S(1)}, u32[]{:S(2)}, u32[]{:S(2)}) collective-permute-start(bf16[2,4,48,384]{3,2,1,0:T(8,128)(2,1)S(1)} %get-tuple-element.1342), channel_id=1, source_target_pairs={{0,2},{1,3},{2,0},{3,1},{4,6},{5,7},{6,4},{7,5},{8,10},{9,11},{10,... | collective-permute-start | bytes 884744 | tf_op jit(solution)/shard_map/ppermute | solution.py:23
  369.2 23.2 %collective-permute-start.51 = (f32[4,48,384]{2,1,0:T(8,128)S(1)}, f32[4,48,384]{2,1,0:T(8,128)S(1)}, u32[]{:S(2)}, u32[]{:S(2)}) collective-permute-start(f32[4,48,384]{2,1,0:T(8,128)S(1)} %shard_map.570.own_ref), channel_id=1, source_target_pairs={{0,16},{16,0},{1,17},{17,1},{2,18},{18,2},{3,19},{19,3},{4,20},{20... | collective-permute-start | bytes 884744 | tf_op jit(solution)/shard_map/ppermute | solution.py:23
  380.7 23.1 %collective-permute-start.58 = (f32[2,96,768]{2,1,0:T(8,128)S(1)}, f32[2,96,768]{2,1,0:T(8,128)S(1)}, u32[]{:S(2)}, u32[]{:S(2)}) collective-permute-start(f32[2,96,768]{2,1,0:T(8,128)S(1)} %shard_map.577.own_ref), channel_id=1, source_target_pairs={{0,16},{16,0},{1,17},{17,1},{2,18},{18,2},{3,19},{19,3},{4,20},{20... | collective-permute-start | bytes 1769480 | tf_op jit(solution)/shard_map/ppermute | solution.py:23
  385.9 19.6 %collective-permute-start.57 = (f32[4,48,384]{2,1,0:T(8,128)S(1)}, f32[4,48,384]{2,1,0:T(8,128)S(1)}, u32[]{:S(2)}, u32[]{:S(2)}) collective-permute-start(f32[4,48,384]{2,1,0:T(8,128)S(1)} %shard_map.582.own_ref), channel_id=1, source_target_pairs={{0,16},{16,0},{1,17},{17,1},{2,18},{18,2},{3,19},{19,3},{4,20},{20... | collective-permute-start | bytes 884744 | tf_op jit(solution)/shard_map/ppermute | solution.py:23
  391.4 11.2 %collective-permute-start.54 = (f32[64,768]{1,0:T(8,128)S(1)}, f32[64,768]{1,0:T(8,128)S(1)}, u32[]{:S(2)}, u32[]{:S(2)}) collective-permute-start(f32[64,768]{1,0:T(8,128)S(1)} %shard_map.578.first_ref), channel_id=1, source_target_pairs={{0,2},{1,3},{2,0},{3,1},{4,6},{5,7},{6,4},{7,5},{8,10},{9,11},{10,... | collective-permute-start | bytes 589832 | tf_op jit(solution)/shard_map/ppermute | solution.py:23
  (83 other events, 468.5 us)

commit v6 on v5

--- a/solution.py
+++ b/solution.py
@@ -50,10 +50,11 @@
 VMEM_LIMIT = 16 * 1024 * 1024
 GROUP = 256
 WAIT = 1_000_000_000
+FOLD = 5
 HEADS = GROUP // HD
 
 
-def call(kernel, outs, operands, spaces=(), scratch=(), flops=1):
+def call(kernel, outs, operands, spaces=(), scratch=(), flops=1, limit=VMEM_LIMIT):
     vmem = pl.BlockSpec(memory_space=pltpu.VMEM)
     specs = [vmem] * len(operands)
     for index, space in spaces:
@@ -64,7 +65,7 @@
         in_specs=specs,
         out_specs=[vmem] * len(outs),
         scratch_shapes=list(scratch),
-        compiler_params=pltpu.CompilerParams(vmem_limit_bytes=VMEM_LIMIT),
+        compiler_params=pltpu.CompilerParams(vmem_limit_bytes=limit),
         cost_estimate=pl.CostEstimate(flops=flops, bytes_accessed=1, transcendentals=0),
     )(*operands)
 
@@ -307,18 +308,17 @@
 
 def mlp_back_kernel(
     base_row, place_ref, grads_ref, values_ref, table_ref, deriv_ref, p0, p1, p2, p3,
-    out_ref, hidden_ref, send_ref, little_ref, bias_ref, total_ref,
+    out_ref, hidden_ref, send_ref, low_ref, little_ref, bias_ref, total_ref,
 ):
-    half = 2 * UNITS
     branch = grads_ref[...] * presence(place_ref, grads_ref.shape[0])
     little_ref[2:3, :] = jnp.sum(branch, axis=0, keepdims=True)
-    send_ref[:, half:] = branch.astype(BF16)
+    low_ref[...] = branch.astype(BF16)
     for index, part in enumerate((p0, p1, p2, p3)):
         target = hidden_ref if index < 2 else send_ref
         base = (index % 2) * UNITS
         here = slice(index * UNITS, (index + 1) * UNITS)
         there = slice(base, base + UNITS)
-        acted = mm_nt(send_ref[:, half:], tile(part, 1))
+        acted = mm_nt(low_ref[...], tile(part, 1))
         hidden = (acted * deriv_ref[:, here]).astype(BF16)
         target[:, there] = hidden
         bias_ref[:, here] = jnp.sum(hidden.astype(F32), axis=0, keepdims=True)
@@ -334,7 +334,8 @@
     outs = [
         struct((rows, width), F32),
         struct((rows, half), BF16),
-        struct((rows, half + width), BF16),
+        struct((rows, half), BF16),
+        struct((rows, width), BF16),
         struct((3, width), F32),
         struct((1, 2 * half), F32),
     ]
@@ -343,22 +344,24 @@
     return call(partial(mlp_back_kernel, base), outs, operands, SMALL, scratch=scratch)
 
 
-def pair_grads_kernel(acted_ref, normed_ref, normed_send_ref, hidden_ref, branch_ref, branch_send_ref, near_ref, far_ref):
+def pair_grads_kernel(
+    acted_ref, normed_ref, normed_send_ref, hidden_ref, branch_ref, hidden_send_ref, branch_send_ref, near_ref, far_ref
+):
     half = 2 * UNITS
     for index, out_ref in enumerate((near_ref, far_ref)):
         cut = slice(index * UNITS, (index + 1) * UNITS)
-        for which, (wide, wide_send, thin, thin_send) in enumerate((
-            (hidden_ref, branch_send_ref, normed_ref, normed_send_ref),
-            (acted_ref, normed_send_ref, branch_ref, branch_send_ref),
-        )):
-            total = mm_tn(wide[:, cut], thin[:, half:]) + mm_tn(wide_send[:, cut], thin_send[:, half:])
-            out_ref[:, which] = total.astype(BF16).reshape(8, -1, total.shape[1])
-
-
-def pair_grads(acted, normed, normed_send, hidden, branch, branch_send):
-    width = normed.shape[1] - 2 * UNITS
+        up = mm_tn(hidden_ref[:, cut], normed_ref[:, half:])
+        up = up + mm_tn(hidden_send_ref[:, cut], normed_send_ref[:, half:])
+        out_ref[:, 0] = up.astype(BF16).reshape(8, -1, up.shape[1])
+        down = mm_tn(acted_ref[:, cut], branch_ref[...])
+        down = down + mm_tn(normed_send_ref[:, cut], branch_send_ref[...])
+        out_ref[:, 1] = down.astype(BF16).reshape(8, -1, down.shape[1])
+
+
+def pair_grads(*operands):
+    width = operands[4].shape[1]
     out = struct((8, 2, UNITS // 8, width), BF16)
-    return call(pair_grads_kernel, [out, out], [acted, normed, normed_send, hidden, branch, branch_send])
+    return call(pair_grads_kernel, [out, out], list(operands))
 
 
 MATS = 4
@@ -376,7 +379,7 @@
             line = 2 * (index % 2) + i
             order = line if side == 0 else SWAP[line]
             for j in range(4):
-                first = pl.multiple_of(order * 192 + jnp.bitwise_xor(wid, j) * 48, 16)
+                first = pl.multiple_of(order * 192 + jnp.bitwise_xor(wid, SWAP[j]) * 48, 16)
                 copies.append(
                     pltpu.make_async_copy(
                         part.at[i * 4 + j],
@@ -590,7 +593,7 @@
         for line in range(4):
             out_ref = near_ref if line < 2 else far_ref
             for j in range(4):
-                inner = jnp.bitwise_xor(wid, j) * 48
+                inner = jnp.bitwise_xor(wid, SWAP[j]) * 48
                 mine = table_ref[pl.ds(pl.multiple_of(line * 192 + inner, 16), 48), :]
                 other = other_ref[pl.ds(pl.multiple_of(SWAP[line] * 192 + inner, 16), 48), :]
                 out_ref[(line % 2) * 4 + j, m] = (mine + other).astype(BF16)
@@ -633,7 +636,9 @@
     units = struct((1, 2, up.shape[0] // 2, up.shape[1]), BF16)
     spaces = SMALL + [(1 + index, pltpu.HBM) for index in range(8)]
     scratch = [pltpu.SemaphoreType.DMA((8,))]
-    return call(pieces_kernel, [heads, units, heads, units], [place, *weights], spaces, scratch)
+    return call(
+        pieces_kernel, [heads, units, heads, units], [place, *weights], spaces, scratch, limit=58 * 1024 * 1024
+    )
 
 
 def table_kernel(*refs):
@@ -673,7 +678,7 @@
             for i in range(4):
                 hid = hids[i if side == 0 else SWAP[i]]
                 for j in range(4):
-                    line = hid[pl.ds(first + jnp.bitwise_xor(wid, j), 1), :]
+                    line = hid[pl.ds(first + jnp.bitwise_xor(wid, SWAP[j]), 1), :]
                     value = jnp.where(core == side, line[:, :half], line[:, half:])
                     lane = side * 16 * half + (i * 4 + j) * half
                     hidden_ref[index : index + 1, lane : lane + half] = value
@@ -711,7 +716,7 @@
                 lane = 16 * half + (SWAP[i] * 4 + j) * half
                 other = ref[0:1, lane : lane + half]
                 parts += [jnp.where(core == 0, mine, other), jnp.where(core == 0, other, mine), gap]
-            line = pl.ds(base + owned * 4 + jnp.bitwise_xor(wid, j), 1)
+            line = pl.ds(base + owned * 4 + jnp.bitwise_xor(wid, SWAP[j]), 1)
             out_ref[line, 0:512] = jnp.concatenate(parts, axis=1)
         for first, heads, kinds in ((base, channel_heads, (0, 1, 2)), (base + BIASES, window_heads, (0, 2))):
             for position, kind in enumerate(kinds):
@@ -776,7 +781,7 @@
 
 def fold(kept, arrived):
     shape = (kept.shape[0] // 2, *kept.shape[1:])
-    return call(fold_kernel, [struct(shape, F32), struct(shape, BF16)], [kept, arrived], flops=5 * WAIT)
+    return call(fold_kernel, [struct(shape, F32), struct(shape, BF16)], [kept, arrived], flops=FOLD * WAIT)
 
 
 def total_kernel(kept_ref, arrived_ref, out_ref):
@@ -784,7 +789,7 @@
 
 
 def fold_last(kept, arrived):
-    return call(total_kernel, [struct(kept.shape[1:], F32)], [kept, arrived], flops=5 * WAIT)[0]
+    return call(total_kernel, [struct(kept.shape[1:], F32)], [kept, arrived], flops=FOLD * WAIT)[0]
 
 
 def rows_kernel(place_ref, own_ref, other_ref, *outs):
@@ -862,9 +867,9 @@
         elif self.step == 1:
             self.flight = cross(self.sent, True)
         elif self.step == 2:
+            self.flight = exchange(self.sent, "wid", 1)
+        elif self.step == 3:
             self.flight = exchange(self.sent, "wid", 2)
-        elif self.step == 3:
-            self.flight = exchange(self.sent, "wid", 1)
         elif self.step == 4:
             self.flight = sibling(gate(self.kept))
         self.step += 1
@@ -912,10 +917,10 @@
         return move(line.gate(values))
 
     def w1(values):
+        return exchange(values, "wid", 2)
+
+    def w2(values):
         return exchange(values, "wid", 1)
-
-    def w2(values):
-        return exchange(values, "wid", 2)
 
     def h1(values):
         return cross(values, True)
@@ -960,14 +965,14 @@
     w2_2 = send(w2, near2)
     s_0 = gate(s_0)
     att_one = [near0, far0, *s_0]
-    after_attn, normed_one, qkv_one, mixed_one = line.run(
-        partial(attention, True), place, after_conv, table, head_bias, att_one
-    )
     near1 = both(near1, h1_1)
     h2_1 = send(h2, near1)
     near2 = both(near2, w2_2)
     h1_2 = send(h1, near2)
     w1_3 = send(w1, own3)
+    after_attn, normed_one, qkv_one, mixed_one = line.run(
+        partial(attention, True), place, after_conv, table, head_bias, att_one
+    )
     near3 = both(own3, w1_3)
     w2_3 = send(w2, near3)
     near2 = both(near2, h1_2)
@@ -975,25 +980,24 @@
     near3 = both(near3, w2_3)
     h1_3 = send(h1, near3)
     far1 = gate(h2_1)
+    s_1 = send(sibling, near1), send(sibling, far1)
     far2 = gate(h2_2)
-    s_1 = send(sibling, near1), send(sibling, far1)
+    s_2 = send(sibling, near2), send(sibling, far2)
+    s_1 = gate(s_1)
+    s_2 = gate(s_2)
     near3 = both(near3, h1_3)
     h2_3 = send(h2, near3)
-    s_1 = gate(s_1)
+    s_3 = send(sibling, near3)
     mlp_two = [near1, far1, *s_1]
     after_mlp, acted_two, fpack_two, deriv_two = line.run(
         partial(mlp, 0), place, after_attn, table, hidden_bias, mlp_two
     )
-    s_2 = send(sibling, near2), send(sibling, far2)
     after_conv_c = line.run(partial(conv, 16), place, after_mlp, table)
-    s_2 = gate(s_2)
-    s_3 = send(sibling, near3)
     att_three = [near2, far2, *s_2]
     after_attn_c, normed_three, qkv_three, mixed_three = line.run(
         partial(attention, False), place, after_conv_c, table, head_bias, att_three
     )
     s_3 = gate(s_3)
-    fpack_two_other = gate(send(sibling, fpack_two))
     far3 = gate(h2_3)
     s_far3 = gate(send(sibling, far3))
     mlp_four = [near3, far3, s_3, s_far3]
@@ -1007,13 +1011,13 @@
         return group
 
     fpack_four_other = send(sibling, fpack_four)
-    flowing, gh_four, bpack_four, little_four, upb_four = line.run(
+    flowing, gh_four, ghs_four, low_four, little_four, upb_four = line.run(
         partial(mlp_back, 16), place, cotangent, after_attn_c, table, deriv_four, mlp_four
     )
     fpack_four_other = gate(fpack_four_other)
-    bpack_four_other = gate(send(sibling, bpack_four))
+    ghs_four_other, low_four_other = gate((send(sibling, ghs_four), send(sibling, low_four)))
     m_four = scatter(
-        *line.run(pair_grads, acted_four, fpack_four, fpack_four_other, gh_four, bpack_four, bpack_four_other), False
+        *line.run(pair_grads, acted_four, fpack_four, fpack_four_other, gh_four, low_four, ghs_four_other, low_four_other), False
     )
     flowing, left_three, rest_three, mine_three, little_three, inb_three = line.run(
         partial(attention_back, False),
@@ -1021,17 +1025,19 @@
     )
     sent_three = gate((send(sibling, left_three), send(sibling, rest_three)))
     near_far = line.run(head_grads, place, left_three, rest_three, *sent_three, mine_three)
+    a_three = scatter(*near_far, True)
     m_four.advance()
-    a_three = scatter(*near_far, True)
+    fpack_two_other = send(sibling, fpack_two)
     flowing, sums_three = line.run(partial(conv_back, 16, False), place, flowing, after_mlp, table)
-    flowing, gh_two, bpack_two, little_two, upb_two = line.run(
+    flowing, gh_two, ghs_two, low_two, little_two, upb_two = line.run(
         partial(mlp_back, 0), place, flowing, after_attn, table, deriv_two, mlp_two
     )
+    ghs_two_other, low_two_other = gate((send(sibling, ghs_two), send(sibling, low_two)))
+    fpack_two_other = gate(fpack_two_other)
+    near_far = line.run(pair_grads, acted_two, fpack_two, fpack_two_other, gh_two, low_two, ghs_two_other, low_two_other)
+    m_two = scatter(*near_far, False)
     m_four.advance()
-    bpack_two_other = gate(send(sibling, bpack_two))
-    near_far = line.run(pair_grads, acted_two, fpack_two, fpack_two_other, gh_two, bpack_two, bpack_two_other)
     a_three.advance()
-    m_two = scatter(*near_far, False)
     flowing, left_one, rest_one, mine_one, little_one, inb_one = line.run(
         partial(attention_back, True),
         place, flowing, after_conv, table, normed_one, qkv_one, mixed_one, att_one,
@@ -1040,33 +1046,33 @@
     m_four.advance()
     sent_one = gate((send(sibling, left_one), send(sibling, rest_one)))
     near_far = line.run(head_grads, place, left_one, rest_one, *sent_one, mine_one)
+    a_one = scatter(*near_far, True)
     m_two.advance()
     input_grad, sums_one = line.run(partial(conv_back, 0, True), place, flowing, start, table)
     small = line.run(
         small_table, place, [sums_one, little_one, little_two, sums_three, little_three, little_four],
         inb_one, inb_three, [upb_two, upb_four],
     )
-    m_two.advance()
-    a_one = scatter(*near_far, True)
-    m_four.advance()
-    a_three.advance()
     small = Small(line, small)
     small.advance()
+    a_three.advance()
     m_four.advance()
     small.advance()
     a_three.advance()
-    a_one.advance()
     small.advance()
-    a_three.advance()
     a_one.advance()
     m_two.advance()
     small.advance()
+    m_four.advance()
+    a_one.advance()
+    small.advance()
     m_two.advance()
+    a_three.advance()
+    a_one.advance()
     small.advance()
+    m_two.advance()
     a_one.advance()
     m_two.advance()
-    a_one.advance()
-    small.advance()
     a_one.advance()
     small = line.run(small_outputs, place, small.table)
 

time: 415 us -> 376 us (0.906)
  waiting for transfers between devices: 215 us -> 182 us
  local copies, waits for them, and re-layouts: 19.5 us -> 8.08 us
  starting transfers between devices: 68.9 us -> 73.3 us
    ppermute x41 -> x43, waiting for transfers between devices: 135 us -> 82 us  [exchange(): return lax.ppermute(values, axis, pairs)]
    ppermute x18, waiting for transfers between devices: 79.1 us -> 100 us  [cross(): return lax.ppermute(values, ('dp', 'hid'), pairs)]
    unnamed x112 -> x106, local copies, waits for them, and re-layouts: 18.8 us -> 7.24 us
    ppermute x41 -> x43, starting transfers between devices: 49.5 us -> 57.3 us  [exchange(): return lax.ppermute(values, axis, pairs)]
  transfers between devices with their start and end apart: 59 -> 61, of which waited for: 34 -> 35; matrix products, arithmetic and copies ran while one was open for 0% -> 0% of each run, Pallas kernels for 20% -> 24%
where the time goes in v6:
time: 376 us; the launch traced here: 371 us
  waiting for transfers between devices  182 us (48%)
  Pallas kernels  105 us (28%)
  starting transfers between devices  73.3 us (19%)
  local copies, waits for them, and re-layouts  8.08 us (2%)
    pallas_call x59, Pallas kernels, call(): pl.pallas_call(kernel, out_shape=list(outs), in_specs=specs, out_specs=[v...  105 us
    ppermute x18, waiting for transfers between devices, cross(): return lax.ppermute(values, ('dp', 'hid'), pairs)  100 us
    ppermute x43, waiting for transfers between devices, exchange(): return lax.ppermute(values, axis, pairs)  82 us
    ppermute x43, starting transfers between devices, exchange(): return lax.ppermute(values, axis, pairs)  57.3 us
    ppermute x18, starting transfers between devices, cross(): return lax.ppermute(values, ('dp', 'hid'), pairs)  16 us
  transfers between devices with their start and end apart: 61, of which 35 were waited for; matrix products, arithmetic and copies ran while one was open for 0% of the time, Pallas kernels for 24%

profile of v6, /device:TPU:1, one launch (start us, length us, event | category | flops | bytes accessed | tf_op | source)
XLA Modules:
  0.0 370.8 jit_solution(10551411425003131954)
XLA Ops:
  8.7 6.7 %collective-permute-done.second_ref = bf16[1,4,48,384]{3,2,1,0:T(8,128)(2,1)S(1)} collective-permute-done((bf16[1,4,48,384]{3,2,1,0:T(8,128)(2,1)}, bf16[1,4,48,384]{3,2,1,0:T(8,128)(2,1)S(1)}, u32[]{:S(2)}, u32[]{:S(2)}) %collective-permute-start) | collective-permute-done | bytes 147488 | tf_op jit(solution)/shard_map/ppermute | solution.py:23
  17.5 4.4 %collective-permute-start.4 = (bf16[2,4,48,384]{3,2,1,0:T(8,128)(2,1)S(1)}, bf16[2,4,48,384]{3,2,1,0:T(8,128)(2,1)S(1)}, u32[]{:S(2)}, u32[]{:S(2)}) collective-permute-start(bf16[2,4,48,384]{3,2,1,0:T(8,128)(2,1)S(1)} %shard_map.528.first_ref), channel_id=1, source_target_pairs={{0,1},{1,0},{2,3},{3,2},{4,5},{5,4},{6,7},{7,6},{8,9},{9,8},{10,11... | collective-permute-start | bytes 884744 | tf_op jit(solution)/shard_map/ppermute | solution.py:23
  26.1 4.8 %collective-permute-done.3.second_ref = bf16[1,2,96,768]{3,2,1,0:T(8,128)(2,1)S(1)} collective-permute-done((bf16[1,2,96,768]{3,2,1,0:T(8,128)(2,1)S(1)}, bf16[1,2,96,768]{3,2,1,0:T(8,128)(2,1)S(1)}, u32[]{:S(2)}, u32[]{:S(2)}) %collective-permute-start.3) | collective-permute-done | bytes 294944 | tf_op jit(solution)/shard_map/ppermute | solution.py:23
  33.0 8.9 %collective-permute-done.5.second_ref = bf16[4,4,48,384]{3,2,1,0:T(8,128)(2,1)S(1)} collective-permute-done((bf16[4,4,48,384]{3,2,1,0:T(8,128)(2,1)S(1)}, bf16[4,4,48,384]{3,2,1,0:T(8,128)(2,1)S(1)}, u32[]{:S(2)}, u32[]{:S(2)}) %collective-permute-start.5) | collective-permute-done | bytes 589856 | tf_op jit(solution)/shard_map/ppermute | solution.py:36
  45.1 12.9 %collective-permute-done.6.p1 = bf16[8,4,48,384]{3,2,1,0:T(8,128)(2,1)S(1)} collective-permute-done((bf16[8,4,48,384]{3,2,1,0:T(8,128)(2,1)S(1)}, bf16[8,4,48,384]{3,2,1,0:T(8,128)(2,1)S(1)}, u32[]{:S(2)}, u32[]{:S(2)}) %collective-permute-start.6) | collective-permute-done | bytes 1179680 | tf_op jit(solution)/shard_map/ppermute | solution.py:36
  62.6 8.2 %collective-permute-done.10.second_ref = bf16[1,4,48,384]{3,2,1,0:T(8,128)(2,1)S(1)} collective-permute-done((bf16[1,4,48,384]{3,2,1,0:T(8,128)(2,1)S(1)}, bf16[1,4,48,384]{3,2,1,0:T(8,128)(2,1)S(1)}, u32[]{:S(2)}, u32[]{:S(2)}) %collective-permute-start.10) | collective-permute-done | bytes 147488 | tf_op jit(solution)/shard_map/ppermute | solution.py:23
  71.0 5.2 %collective-permute-done.12.second_ref = bf16[4,2,96,768]{3,2,1,0:T(8,128)(2,1)S(1)} collective-permute-done((bf16[4,2,96,768]{3,2,1,0:T(8,128)(2,1)S(1)}, bf16[4,2,96,768]{3,2,1,0:T(8,128)(2,1)S(1)}, u32[]{:S(2)}, u32[]{:S(2)}) %collective-permute-start.12) | collective-permute-done | bytes 1179680 | tf_op jit(solution)/shard_map/ppermute | solution.py:36
  81.4 9.6 %shard_map.539 = (f32[288,768]{1,0:T(8,128)S(1)}, bf16[288,768]{1,0:T(8,128)(2,1)S(1)}, bf16[288,2304]{1,0:T(8,128)(2,1)S(1)}, bf16[288,768]{1,0:T(8,128)(2,1)S(1)}) custom-call(s32[5]{0:T(128)S(1)} %copy-done.26, f32[288,768]{1,0:T(8,128)S(1)} %get-tuple-element.1145.values_ref, f32[32,768]{1,0:T(8,128)S(1)} %get-tuple-element.1219.table_ref, ...), custom_call_target="tpu_custom_call" | custom-call | flops 1 | bytes 1 | tf_op jit(solution)/shard_map/pallas_call | solution.py:62
  97.6 10.3 %collective-permute-done.15.second_ref = bf16[2,2,96,768]{3,2,1,0:T(8,128)(2,1)S(1)} collective-permute-done((bf16[2,2,96,768]{3,2,1,0:T(8,128)(2,1)S(1)}, bf16[2,2,96,768]{3,2,1,0:T(8,128)(2,1)S(1)}, u32[]{:S(2)}, u32[]{:S(2)}) %collective-permute-start.15) | collective-permute-done | bytes 589856 | tf_op jit(solution)/shard_map/ppermute | solution.py:23
  113.0 10.4 %collective-permute-done.19.p1 = bf16[8,4,48,384]{3,2,1,0:T(8,128)(2,1)S(1)} collective-permute-done((bf16[8,4,48,384]{3,2,1,0:T(8,128)(2,1)S(1)}, bf16[8,4,48,384]{3,2,1,0:T(8,128)(2,1)S(1)}, u32[]{:S(2)}, u32[]{:S(2)}) %collective-permute-start.19) | collective-permute-done | bytes 1179680 | tf_op jit(solution)/shard_map/ppermute | solution.py:36
  129.8 11.2 %collective-permute-done.20.second_ref = bf16[4,2,96,768]{3,2,1,0:T(8,128)(2,1)S(1)} collective-permute-done((bf16[4,2,96,768]{3,2,1,0:T(8,128)(2,1)S(1)}, bf16[4,2,96,768]{3,2,1,0:T(8,128)(2,1)S(1)}, u32[]{:S(2)}, u32[]{:S(2)}) %collective-permute-start.20) | collective-permute-done | bytes 1179680 | tf_op jit(solution)/shard_map/ppermute | solution.py:36
  143.5 4.3 %shard_map.544 = (f32[288,768]{1,0:T(8,128)S(1)}, bf16[288,1536]{1,0:T(8,128)(2,1)S(1)}, bf16[288,2304]{1,0:T(8,128)(2,1)S(1)}, f32[288,3072]{1,0:T(8,128)S(1)}) custom-call(s32[5]{0:T(128)S(1)} %copy-done.26, f32[288,768]{1,0:T(8,128)S(1)} %get-tuple-element.1077.values_ref, f32[32,768]{1,0:T(8,128)S(1)} %get-tuple-element.1219.table_ref, ...), custom_call_target="tpu_custom_call" | custom-call | flops 1 | bytes 1 | tf_op jit(solution)/shard_map/pallas_call | solution.py:62
  150.6 7.8 %shard_map.546 = (f32[288,768]{1,0:T(8,128)S(1)}, bf16[288,768]{1,0:T(8,128)(2,1)S(1)}, bf16[288,2304]{1,0:T(8,128)(2,1)S(1)}, bf16[288,768]{1,0:T(8,128)(2,1)S(1)}) custom-call(s32[5]{0:T(128)S(1)} %copy-done.26, f32[288,768]{1,0:T(8,128)S(1)} %shard_map.545.values_ref, f32[32,768]{1,0:T(8,128)S(1)} %get-tuple-element.1219.table_ref, ...), custom_call_target="tpu_custom_call" | custom-call | flops 1 | bytes 1 | tf_op jit(solution)/shard_map/pallas_call | solution.py:62
  158.4 12.1 %collective-permute-done.23.p1 = bf16[8,2,96,768]{3,2,1,0:T(8,128)(2,1)S(1)} collective-permute-done((bf16[8,2,96,768]{3,2,1,0:T(8,128)(2,1)S(1)}, bf16[8,2,96,768]{3,2,1,0:T(8,128)(2,1)S(1)}, u32[]{:S(2)}, u32[]{:S(2)}) %collective-permute-start.23) | collective-permute-done | bytes 2359328 | tf_op jit(solution)/shard_map/ppermute | solution.py:36
  171.5 4.2 %collective-permute-done.25.p3 = bf16[8,2,96,768]{3,2,1,0:T(8,128)(2,1)S(1)} collective-permute-done((bf16[8,2,96,768]{3,2,1,0:T(8,128)(2,1)S(1)}, bf16[8,2,96,768]{3,2,1,0:T(8,128)(2,1)S(1)}, u32[]{:S(2)}, u32[]{:S(2)}) %collective-permute-start.25) | collective-permute-done | bytes 2359328 | tf_op jit(solution)/shard_map/ppermute | solution.py:23
  175.6 5.4 %shard_map.547 = (f32[392,768]{1,0:T(8,128)}, bf16[288,1536]{1,0:T(8,128)(2,1)S(1)}, bf16[288,2304]{1,0:T(8,128)(2,1)S(1)}, f32[288,3072]{1,0:T(8,128)S(1)}) custom-call(s32[5]{0:T(128)S(1)} %copy-done.26, f32[288,768]{1,0:T(8,128)S(1)} %get-tuple-element.965.values_ref, f32[32,768]{1,0:T(8,128)S(1)} %get-tuple-element.1219.table_ref, ...), custom_call_target="tpu_custom_call" | custom-call | flops 1 | bytes 1 | tf_op jit(solution)/shard_map/pallas_call | solution.py:62
  191.2 5.1 %shard_map.549 = (bf16[8,2,96,768]{3,2,1,0:T(8,128)(2,1)S(1)}, bf16[8,2,96,768]{3,2,1,0:T(8,128)(2,1)S(1)}) custom-call(bf16[288,1536]{1,0:T(8,128)(2,1)S(1)} %copy-done.15, bf16[288,2304]{1,0:T(8,128)(2,1)S(1)} %copy-done.9, bf16[288,2304]{1,0:T(8,128)(2,1)S(1)} %collective-permute-done.26.normed_send_ref, ...), custom_call_target="tpu_custom_call" | custom-call | flops 1 | bytes 1 | tf_op jit(solution)/shard_map/pallas_call | solution.py:62
  197.3 8.6 %shard_map.550 = (f32[288,768]{1,0:T(8,128)S(1)}, bf16[288,2304]{1,0:T(8,128)(2,1)S(1)}, bf16[288,1536]{1,0:T(8,128)(2,1)S(1)}, bf16[288,768]{1,0:T(8,128)(2,1)S...) custom-call(s32[5]{0:T(128)S(1)} %copy-done.26, f32[288,768]{1,0:T(8,128)S(1)} %get-tuple-element.1012.grads_ref, ...), custom_call_target="tpu_custom_call" | custom-call | flops 1 | bytes 1 | tf_op jit(solution)/shard_map/pallas_call | solution.py:62
  210.3 4.9 %shard_map.551 = (bf16[8,4,48,384]{3,2,1,0:T(8,128)(2,1)S(1)}, bf16[8,4,48,384]{3,2,1,0:T(8,128)(2,1)}) custom-call(s32[5]{0:T(128)S(1)} %copy-done.26, bf16[288,2304]{1,0:T(8,128)(2,1)S(1)} %get-tuple-element.1045.left_ref, bf16[288,1536]{1,0:T(8,128)(2,1)S(1)} %get-tuple-element.1046.rest_ref, bf16[288,2304]{1,0:T(8,128)(2,1)S(1)} %collective-permute-done.30.left_send_ref, ...), custom_call_target="tpu_custom_call" | custom-call | flops 1 | bytes 1 | tf_op jit(solution)/shard_map/pallas_call | solution.py:62
  216.2 8.1 %collective-permute-done.29.arrived_ref = bf16[8,2,96,768]{3,2,1,0:T(8,128)(2,1)S(1)} collective-permute-done((bf16[8,2,96,768]{3,2,1,0:T(8,128)(2,1)S(1)}, bf16[8,2,96,768]{3,2,1,0:T(8,128)(2,1)S(1)}, u32[]{:S(2)}, u32[]{:S(2)}) %collective-permute-start.29) | collective-permute-done | bytes 2359328 | tf_op jit(solution)/shard_map/ppermute | solution.py:36
  237.2 5.3 %shard_map.555 = (bf16[8,2,96,768]{3,2,1,0:T(8,128)(2,1)S(1)}, bf16[8,2,96,768]{3,2,1,0:T(8,128)(2,1)S(1)}) custom-call(bf16[288,1536]{1,0:T(8,128)(2,1)S(1)} %copy-done.13, bf16[288,2304]{1,0:T(8,128)(2,1)S(1)} %copy-done.7, bf16[288,2304]{1,0:T(8,128)(2,1)S(1)} %collective-permute-done.34.normed_send_ref, ...), custom_call_target="tpu_custom_call" | custom-call | flops 1 | bytes 1 | tf_op jit(solution)/shard_map/pallas_call | solution.py:62
  244.7 9.4 %collective-permute-done.32.arrived_ref = bf16[8,4,48,384]{3,2,1,0:T(8,128)(2,1)S(1)} collective-permute-done((bf16[8,4,48,384]{3,2,1,0:T(8,128)(2,1)}, bf16[8,4,48,384]{3,2,1,0:T(8,128)(2,1)S(1)}, u32[]{:S(2)}, u32[]{:S(2)}) %collective-permute-start.32) | collective-permute-done | bytes 1179680 | tf_op jit(solution)/shard_map/ppermute | solution.py:36
  256.3 12.9 %shard_map.558 = (f32[288,768]{1,0:T(8,128)S(1)}, bf16[288,2304]{1,0:T(8,128)(2,1)S(1)}, bf16[288,1536]{1,0:T(8,128)(2,1)S(1)}, bf16[288,768]{1,0:T(8,128)(2,1)S...) custom-call(s32[5]{0:T(128)S(1)} %copy-done.26, f32[288,768]{1,0:T(8,128)S(1)} %get-tuple-element.1144.grads_ref, ...), custom_call_target="tpu_custom_call" | custom-call | flops 1 | bytes 1 | tf_op jit(solution)/shard_map/pallas_call | solution.py:62
  280.2 9.1 %collective-permute-done.37.arrived_ref = bf16[8,2,96,768]{3,2,1,0:T(8,128)(2,1)S(1)} collective-permute-done((bf16[8,2,96,768]{3,2,1,0:T(8,128)(2,1)S(1)}, bf16[8,2,96,768]{3,2,1,0:T(8,128)(2,1)S(1)}, u32[]{:S(2)}, u32[]{:S(2)}) %collective-permute-start.37) | collective-permute-done | bytes 2359328 | tf_op jit(solution)/shard_map/ppermute | solution.py:36
  289.9 5.3 %shard_map.563 = (f32[392,768]{1,0:T(8,128)}, f32[10,768]{1,0:T(8,128)S(1)}) custom-call(s32[5]{0:T(128)S(1)} %copy-done.26, f32[288,768]{1,0:T(8,128)S(1)} %get-tuple-element.1217.grads_ref, f32[288,768]{1,0:T(8,128)S(1)} %copy-done.17, f32[32,768]{1,0:T(8,128)S(1)} %get-tuple-element.1219.table_ref), custom_call_target="tpu_custom_call" | custom-call | flops 1 | bytes 1 | tf_op jit(solution)/shard_map/pallas_call | solution.py:62
  298.6 7.1 %collective-permute-done.46.arrived_ref = bf16[1,4,48,384]{3,2,1,0:T(8,128)(2,1)S(1)} collective-permute-done((bf16[1,4,48,384]{3,2,1,0:T(8,128)(2,1)S(1)}, bf16[1,4,48,384]{3,2,1,0:T(8,128)(2,1)S(1)}, u32[]{:S(2)}, u32[]{:S(2)}) %collective-permute-start.46) | collective-permute-done | bytes 147488 | tf_op jit(solution)/shard_map/ppermute | solution.py:23
  306.8 5.9 %collective-permute-done.45.second_ref = f32[64,768]{1,0:T(8,128)S(1)} collective-permute-done((f32[64,768]{1,0:T(8,128)S(1)}, f32[64,768]{1,0:T(8,128)S(1)}, u32[]{:S(2)}, u32[]{:S(2)}) %collective-permute-start.45) | collective-permute-done | bytes 196640 | tf_op jit(solution)/shard_map/ppermute | solution.py:23
  315.1 6.6 %collective-permute-done.51.arrived_ref = bf16[4,4,48,384]{3,2,1,0:T(8,128)(2,1)S(1)} collective-permute-done((bf16[4,4,48,384]{3,2,1,0:T(8,128)(2,1)S(1)}, bf16[4,4,48,384]{3,2,1,0:T(8,128)(2,1)S(1)}, u32[]{:S(2)}, u32[]{:S(2)}) %collective-permute-start.51) | collective-permute-done | bytes 589856 | tf_op jit(solution)/shard_map/ppermute | solution.py:36
  322.7 8.3 %collective-permute-done.54.arrived_ref = bf16[2,4,48,384]{3,2,1,0:T(8,128)(2,1)S(1)} collective-permute-done((bf16[2,4,48,384]{3,2,1,0:T(8,128)(2,1)S(1)}, bf16[2,4,48,384]{3,2,1,0:T(8,128)(2,1)S(1)}, u32[]{:S(2)}, u32[]{:S(2)}) %collective-permute-start.54) | collective-permute-done | bytes 294944 | tf_op jit(solution)/shard_map/ppermute | solution.py:23
  333.6 9.4 %collective-permute-start.52 = (f32[2,96,768]{2,1,0:T(8,128)S(1)}, f32[2,96,768]{2,1,0:T(8,128)S(1)}, u32[]{:S(2)}, u32[]{:S(2)}) collective-permute-start(f32[2,96,768]{2,1,0:T(8,128)S(1)} %shard_map.566.own_ref), channel_id=1, source_target_pairs={{0,16},{16,0},{1,17},{17,1},{2,18},{18,2},{3,19},{19,3},{4,20},{20... | collective-permute-start | bytes 1769480 | tf_op jit(solution)/shard_map/ppermute | solution.py:23
  343.9 10.3 %collective-permute-start.60 = (f32[2,96,768]{2,1,0:T(8,128)S(1)}, f32[2,96,768]{2,1,0:T(8,128)S(1)}, u32[]{:S(2)}, u32[]{:S(2)}) collective-permute-start(f32[2,96,768]{2,1,0:T(8,128)S(1)} %shard_map.583.own_ref), channel_id=1, source_target_pairs={{0,16},{16,0},{1,17},{17,1},{2,18},{18,2},{3,19},{19,3},{4,20},{20... | collective-permute-start | bytes 1769480 | tf_op jit(solution)/shard_map/ppermute | solution.py:23
  357.5 8.7 %collective-permute-done.53.second_ref = f32[64,768]{1,0:T(8,128)S(1)} collective-permute-done((f32[64,768]{1,0:T(8,128)S(1)}, f32[64,768]{1,0:T(8,128)S(1)}, u32[]{:S(2)}, u32[]{:S(2)}) %collective-permute-start.53) | collective-permute-done | bytes 196640 | tf_op jit(solution)/shard_map/ppermute | solution.py:23
  (258 shorter events, 117.4 us)
Async XLA Ops:
  16.3 14.6 %collective-permute-start.3 = (bf16[1,2,96,768]{3,2,1,0:T(8,128)(2,1)S(1)}, bf16[1,2,96,768]{3,2,1,0:T(8,128)(2,1)S(1)}, u32[]{:S(2)}, u32[]{:S(2)}) collective-permute-start(bf16[1,2,96,768]{3,2,1,0:T(8,128)(2,1)S(1)} %copy-done.50), channel_id=1, source_target_pairs={{0,2},{1,3},{2,0},{3,1},{4,6},{5,7},{6,4},{7,5},{8,10},{9,11},{10,... | collective-permute-start | bytes 884744 | tf_op jit(solution)/shard_map/ppermute | solution.py:23
  17.5 15.4 %collective-permute-start.4 = (bf16[2,4,48,384]{3,2,1,0:T(8,128)(2,1)S(1)}, bf16[2,4,48,384]{3,2,1,0:T(8,128)(2,1)S(1)}, u32[]{:S(2)}, u32[]{:S(2)}) collective-permute-start(bf16[2,4,48,384]{3,2,1,0:T(8,128)(2,1)S(1)} %shard_map.528.first_ref), channel_id=1, source_target_pairs={{0,1},{1,0},{2,3},{3,2},{4,5},{5,4},{6,7},{7,6},{8,9},{9,8},{10,11... | collective-permute-start | bytes 884744 | tf_op jit(solution)/shard_map/ppermute | solution.py:23
  42.1 15.9 %collective-permute-start.6 = (bf16[8,4,48,384]{3,2,1,0:T(8,128)(2,1)S(1)}, bf16[8,4,48,384]{3,2,1,0:T(8,128)(2,1)S(1)}, u32[]{:S(2)}, u32[]{:S(2)}) collective-permute-start(bf16[8,4,48,384]{3,2,1,0:T(8,128)(2,1)S(1)} %shard_map.534.p0), channel_id=1, source_target_pairs={{0,8},{4,12},{8,0},{12,4},{16,20},{20,16},{24,28},{28,24},{1,9},{5... | collective-permute-start | bytes 3538952 | tf_op jit(solution)/shard_map/ppermute | solution.py:36
  58.0 13.0 %collective-permute-start.9 = (bf16[8,4,48,384]{3,2,1,0:T(8,128)(2,1)S(1)}, bf16[8,4,48,384]{3,2,1,0:T(8,128)(2,1)S(1)}, u32[]{:S(2)}, u32[]{:S(2)}) collective-permute-start(bf16[8,4,48,384]{3,2,1,0:T(8,128)(2,1)S(1)} %collective-permute-done.6.p1), channel_id=1, source_target_pairs={{0,16},{16,0},{1,17},{17,1},{2,18},{18,2},{3,19},{19,3},{4,20},{20... | collective-permute-start | bytes 3538952 | tf_op jit(solution)/shard_map/ppermute | solution.py:23
  60.9 15.3 %collective-permute-start.12 = (bf16[4,2,96,768]{3,2,1,0:T(8,128)(2,1)S(1)}, bf16[4,2,96,768]{3,2,1,0:T(8,128)(2,1)S(1)}, u32[]{:S(2)}, u32[]{:S(2)}) collective-permute-start(bf16[4,2,96,768]{3,2,1,0:T(8,128)(2,1)S(1)} %shard_map.535.first_ref), channel_id=1, source_target_pairs={{0,4},{4,0},{8,12},{12,8},{16,24},{20,28},{24,16},{28,20},{1,5},{5... | collective-permute-start | bytes 3538952 | tf_op jit(solution)/shard_map/ppermute | solution.py:36
  76.4 34.4 %collective-permute-start.13 = (bf16[8,2,96,768]{3,2,1,0:T(8,128)(2,1)S(1)}, bf16[8,2,96,768]{3,2,1,0:T(8,128)(2,1)S(1)}, u32[]{:S(2)}, u32[]{:S(2)}) collective-permute-start(bf16[8,2,96,768]{3,2,1,0:T(8,128)(2,1)S(1)} %shard_map.537.p0), channel_id=1, source_target_pairs={{0,8},{4,12},{8,0},{12,4},{16,20},{20,16},{24,28},{28,24},{1,9},{5... | collective-permute-start | bytes 7077896 | tf_op jit(solution)/shard_map/ppermute | solution.py:36
  78.7 15.6 %collective-permute-start.14 = (bf16[1,2,96,768]{3,2,1,0:T(8,128)(2,1)S(1)}, bf16[1,2,96,768]{3,2,1,0:T(8,128)(2,1)S(1)}, u32[]{:S(2)}, u32[]{:S(2)}) collective-permute-start(bf16[1,2,96,768]{3,2,1,0:T(8,128)(2,1)S(1)} %copy-done.49), channel_id=1, source_target_pairs={{0,2},{1,3},{2,0},{3,1},{4,6},{5,7},{6,4},{7,5},{8,10},{9,11},{10,... | collective-permute-start | bytes 884744 | tf_op jit(solution)/shard_map/ppermute | solution.py:23
  80.7 15.4 %collective-permute-start.16 = (bf16[4,4,48,384]{3,2,1,0:T(8,128)(2,1)S(1)}, bf16[4,4,48,384]{3,2,1,0:T(8,128)(2,1)S(1)}, u32[]{:S(2)}, u32[]{:S(2)}) collective-permute-start(bf16[4,4,48,384]{3,2,1,0:T(8,128)(2,1)S(1)} %shard_map.538.first_ref), channel_id=1, source_target_pairs={{0,4},{4,0},{8,12},{12,8},{16,24},{20,28},{24,16},{28,20},{1,5},{5... | collective-permute-start | bytes 1769480 | tf_op jit(solution)/shard_map/ppermute | solution.py:36
  94.4 13.5 %collective-permute-start.15 = (bf16[2,2,96,768]{3,2,1,0:T(8,128)(2,1)S(1)}, bf16[2,2,96,768]{3,2,1,0:T(8,128)(2,1)S(1)}, u32[]{:S(2)}, u32[]{:S(2)}) collective-permute-start(bf16[2,2,96,768]{3,2,1,0:T(8,128)(2,1)S(1)} %shard_map.540.first_ref), channel_id=1, source_target_pairs={{0,1},{1,0},{2,3},{3,2},{4,5},{5,4},{6,7},{7,6},{8,9},{9,8},{10,11... | collective-permute-start | bytes 1769480 | tf_op jit(solution)/shard_map/ppermute | solution.py:23
  96.3 27.1 %collective-permute-start.19 = (bf16[8,4,48,384]{3,2,1,0:T(8,128)(2,1)S(1)}, bf16[8,4,48,384]{3,2,1,0:T(8,128)(2,1)S(1)}, u32[]{:S(2)}, u32[]{:S(2)}) collective-permute-start(bf16[8,4,48,384]{3,2,1,0:T(8,128)(2,1)S(1)} %shard_map.541.p0), channel_id=1, source_target_pairs={{0,8},{4,12},{8,0},{12,4},{16,20},{20,16},{24,28},{28,24},{1,9},{5... | collective-permute-start | bytes 3538952 | tf_op jit(solution)/shard_map/ppermute | solution.py:36
  110.7 15.4 %collective-permute-start.18 = (bf16[8,2,96,768]{3,2,1,0:T(8,128)(2,1)S(1)}, bf16[8,2,96,768]{3,2,1,0:T(8,128)(2,1)S(1)}, u32[]{:S(2)}, u32[]{:S(2)}) collective-permute-start(bf16[8,2,96,768]{3,2,1,0:T(8,128)(2,1)S(1)} %collective-permute-done.13.p1), channel_id=1, source_target_pairs={{0,16},{16,0},{1,17},{17,1},{2,18},{18,2},{3,19},{19,3},{4,20},{20... | collective-permute-start | bytes 7077896 | tf_op jit(solution)/shard_map/ppermute | solution.py:23
  113.0 13.2 %collective-permute-start.17 = (bf16[8,2,96,768]{3,2,1,0:T(8,128)(2,1)S(1)}, bf16[8,2,96,768]{3,2,1,0:T(8,128)(2,1)S(1)}, u32[]{:S(2)}, u32[]{:S(2)}) collective-permute-start(bf16[8,2,96,768]{3,2,1,0:T(8,128)(2,1)S(1)} %shard_map.537.p0), channel_id=1, source_target_pairs={{0,16},{16,0},{1,17},{17,1},{2,18},{18,2},{3,19},{19,3},{4,20},{20... | collective-permute-start | bytes 7077896 | tf_op jit(solution)/shard_map/ppermute | solution.py:23
  125.6 15.3 %collective-permute-start.20 = (bf16[4,2,96,768]{3,2,1,0:T(8,128)(2,1)S(1)}, bf16[4,2,96,768]{3,2,1,0:T(8,128)(2,1)S(1)}, u32[]{:S(2)}, u32[]{:S(2)}) collective-permute-start(bf16[4,2,96,768]{3,2,1,0:T(8,128)(2,1)S(1)} %shard_map.542.first_ref), channel_id=1, source_target_pairs={{0,4},{4,0},{8,12},{12,8},{16,24},{20,28},{24,16},{28,20},{1,5},{5... | collective-permute-start | bytes 3538952 | tf_op jit(solution)/shard_map/ppermute | solution.py:36
  141.1 17.3 %collective-permute-start.24 = (bf16[8,2,96,768]{3,2,1,0:T(8,128)(2,1)S(1)}, bf16[8,2,96,768]{3,2,1,0:T(8,128)(2,1)S(1)}, u32[]{:S(2)}, u32[]{:S(2)}) collective-permute-start(bf16[8,2,96,768]{3,2,1,0:T(8,128)(2,1)S(1)} %shard_map.543.p0), channel_id=1, source_target_pairs={{0,16},{16,0},{1,17},{17,1},{2,18},{18,2},{3,19},{19,3},{4,20},{20... | collective-permute-start | bytes 7077896 | tf_op jit(solution)/shard_map/ppermute | solution.py:23
  142.5 28.0 %collective-permute-start.23 = (bf16[8,2,96,768]{3,2,1,0:T(8,128)(2,1)S(1)}, bf16[8,2,96,768]{3,2,1,0:T(8,128)(2,1)S(1)}, u32[]{:S(2)}, u32[]{:S(2)}) collective-permute-start(bf16[8,2,96,768]{3,2,1,0:T(8,128)(2,1)S(1)} %shard_map.543.p0), channel_id=1, source_target_pairs={{0,8},{4,12},{8,0},{12,4},{16,20},{20,16},{24,28},{28,24},{1,9},{5... | collective-permute-start | bytes 7077896 | tf_op jit(solution)/shard_map/ppermute | solution.py:36
  196.3 28.1 %collective-permute-start.29 = (bf16[8,2,96,768]{3,2,1,0:T(8,128)(2,1)S(1)}, bf16[8,2,96,768]{3,2,1,0:T(8,128)(2,1)S(1)}, u32[]{:S(2)}, u32[]{:S(2)}) collective-permute-start(bf16[8,2,96,768]{3,2,1,0:T(8,128)(2,1)S(1)} %get-tuple-element.1032), channel_id=1, source_target_pairs={{0,8},{4,12},{8,0},{12,4},{16,20},{20,16},{24,28},{28,24},{1,9},{5... | collective-permute-start | bytes 7077896 | tf_op jit(solution)/shard_map/ppermute | solution.py:36
  224.8 12.4 %collective-permute-start.34 = (bf16[288,2304]{1,0:T(8,128)(2,1)S(1)}, bf16[288,2304]{1,0:T(8,128)(2,1)S(1)}, u32[]{:S(2)}, u32[]{:S(2)}) collective-permute-start(bf16[288,2304]{1,0:T(8,128)(2,1)S(1)} %copy-done.7), channel_id=1, source_target_pairs={{0,16},{16,0},{1,17},{17,1},{2,18},{18,2},{3,19},{19,3},{4,20},{20... | collective-permute-start | bytes 3981320 | tf_op jit(solution)/shard_map/ppermute | solution.py:23
  225.9 18.5 %collective-permute-start.33 = (bf16[4,2,96,768]{3,2,1,0:T(8,128)(2,1)S(1)}, bf16[4,2,96,768]{3,2,1,0:T(8,128)(2,1)S(1)}, u32[]{:S(2)}, u32[]{:S(2)}) collective-permute-start(bf16[4,2,96,768]{3,2,1,0:T(8,128)(2,1)S(1)} %get-tuple-element.1098), channel_id=1, source_target_pairs={{0,4},{4,0},{8,12},{12,8},{16,24},{20,28},{24,16},{28,20},{1,5},{5... | collective-permute-start | bytes 3538952 | tf_op jit(solution)/shard_map/ppermute | solution.py:36
  234.5 19.6 %collective-permute-start.32 = (bf16[8,4,48,384]{3,2,1,0:T(8,128)(2,1)}, bf16[8,4,48,384]{3,2,1,0:T(8,128)(2,1)S(1)}, u32[]{:S(2)}, u32[]{:S(2)}) collective-permute-start(bf16[8,4,48,384]{3,2,1,0:T(8,128)(2,1)} %get-tuple-element.1096), channel_id=1, source_target_pairs={{0,8},{4,12},{8,0},{12,4},{16,20},{20,16},{24,28},{28,24},{1,9},{5... | collective-permute-start | bytes 3538952 | tf_op jit(solution)/shard_map/ppermute | solution.py:36
  254.4 14.8 %collective-permute-start.39 = (bf16[4,4,48,384]{3,2,1,0:T(8,128)(2,1)S(1)}, bf16[4,4,48,384]{3,2,1,0:T(8,128)(2,1)S(1)}, u32[]{:S(2)}, u32[]{:S(2)}) collective-permute-start(bf16[4,4,48,384]{3,2,1,0:T(8,128)(2,1)S(1)} %get-tuple-element.1170), channel_id=1, source_target_pairs={{0,4},{4,0},{8,12},{12,8},{16,24},{20,28},{24,16},{28,20},{1,5},{5... | collective-permute-start | bytes 1769480 | tf_op jit(solution)/shard_map/ppermute | solution.py:36
  255.0 14.3 %collective-permute-start.38 = (bf16[2,2,96,768]{3,2,1,0:T(8,128)(2,1)S(1)}, bf16[2,2,96,768]{3,2,1,0:T(8,128)(2,1)S(1)}, u32[]{:S(2)}, u32[]{:S(2)}) collective-permute-start(bf16[2,2,96,768]{3,2,1,0:T(8,128)(2,1)S(1)} %get-tuple-element.1168), channel_id=1, source_target_pairs={{0,1},{1,0},{2,3},{3,2},{4,5},{5,4},{6,7},{7,6},{8,9},{9,8},{10,11... | collective-permute-start | bytes 1769480 | tf_op jit(solution)/shard_map/ppermute | solution.py:23
  255.1 34.3 %collective-permute-start.37 = (bf16[8,2,96,768]{3,2,1,0:T(8,128)(2,1)S(1)}, bf16[8,2,96,768]{3,2,1,0:T(8,128)(2,1)S(1)}, u32[]{:S(2)}, u32[]{:S(2)}) collective-permute-start(bf16[8,2,96,768]{3,2,1,0:T(8,128)(2,1)S(1)} %get-tuple-element.1164), channel_id=1, source_target_pairs={{0,8},{4,12},{8,0},{12,4},{16,20},{20,16},{24,28},{28,24},{1,9},{5... | collective-permute-start | bytes 7077896 | tf_op jit(solution)/shard_map/ppermute | solution.py:36
  271.3 24.7 %collective-permute-start.44 = (bf16[2,4,48,384]{3,2,1,0:T(8,128)(2,1)S(1)}, bf16[2,4,48,384]{3,2,1,0:T(8,128)(2,1)S(1)}, u32[]{:S(2)}, u32[]{:S(2)}) collective-permute-start(bf16[2,4,48,384]{3,2,1,0:T(8,128)(2,1)S(1)} %get-tuple-element.1251), channel_id=1, source_target_pairs={{0,1},{1,0},{2,3},{3,2},{4,5},{5,4},{6,7},{7,6},{8,9},{9,8},{10,11... | collective-permute-start | bytes 884744 | tf_op jit(solution)/shard_map/ppermute | solution.py:23
  272.1 23.9 %collective-permute-start.43 = (bf16[1,2,96,768]{3,2,1,0:T(8,128)(2,1)S(1)}, bf16[1,2,96,768]{3,2,1,0:T(8,128)(2,1)S(1)}, u32[]{:S(2)}, u32[]{:S(2)}) collective-permute-start(bf16[1,2,96,768]{3,2,1,0:T(8,128)(2,1)S(1)} %get-tuple-element.1249), channel_id=1, source_target_pairs={{0,2},{1,3},{2,0},{3,1},{4,6},{5,7},{6,4},{7,5},{8,10},{9,11},{10,... | collective-permute-start | bytes 884744 | tf_op jit(solution)/shard_map/ppermute | solution.py:23
  279.2 33.5 %collective-permute-start.49 = (bf16[8,4,48,384]{3,2,1,0:T(8,128)(2,1)S(1)}, bf16[8,4,48,384]{3,2,1,0:T(8,128)(2,1)S(1)}, u32[]{:S(2)}, u32[]{:S(2)}) collective-permute-start(bf16[8,4,48,384]{3,2,1,0:T(8,128)(2,1)S(1)} %get-tuple-element.1283), channel_id=1, source_target_pairs={{0,8},{4,12},{8,0},{12,4},{16,20},{20,16},{24,28},{28,24},{1,9},{5... | collective-permute-start | bytes 3538952 | tf_op jit(solution)/shard_map/ppermute | solution.py:36
  297.2 16.8 %collective-permute-start.48 = (bf16[4,2,96,768]{3,2,1,0:T(8,128)(2,1)S(1)}, bf16[4,2,96,768]{3,2,1,0:T(8,128)(2,1)S(1)}, u32[]{:S(2)}, u32[]{:S(2)}) collective-permute-start(bf16[4,2,96,768]{3,2,1,0:T(8,128)(2,1)S(1)} %get-tuple-element.1281), channel_id=1, source_target_pairs={{0,4},{4,0},{8,12},{12,8},{16,24},{20,28},{24,16},{28,20},{1,5},{5... | collective-permute-start | bytes 3538952 | tf_op jit(solution)/shard_map/ppermute | solution.py:36
  314.4 16.6 %collective-permute-start.56 = (bf16[2,2,96,768]{3,2,1,0:T(8,128)(2,1)S(1)}, bf16[2,2,96,768]{3,2,1,0:T(8,128)(2,1)S(1)}, u32[]{:S(2)}, u32[]{:S(2)}) collective-permute-start(bf16[2,2,96,768]{3,2,1,0:T(8,128)(2,1)S(1)} %get-tuple-element.1342), channel_id=1, source_target_pairs={{0,1},{1,0},{2,3},{3,2},{4,5},{5,4},{6,7},{7,6},{8,9},{9,8},{10,11... | collective-permute-start | bytes 1769480 | tf_op jit(solution)/shard_map/ppermute | solution.py:23
  322.0 21.2 %collective-permute-start.47 = (f32[64,768]{1,0:T(8,128)S(1)}, f32[64,768]{1,0:T(8,128)S(1)}, u32[]{:S(2)}, u32[]{:S(2)}) collective-permute-start(f32[64,768]{1,0:T(8,128)S(1)} %shard_map.569.first_ref), channel_id=1, source_target_pairs={{0,8},{4,12},{8,0},{12,4},{1,9},{5,13},{9,1},{13,5},{2,10},{6,14},... | collective-permute-start | bytes 589832 | tf_op jit(solution)/shard_map/ppermute | solution.py:23
  331.1 12.7 %collective-permute-start.59 = (bf16[1,2,96,768]{3,2,1,0:T(8,128)(2,1)S(1)}, bf16[1,2,96,768]{3,2,1,0:T(8,128)(2,1)S(1)}, u32[]{:S(2)}, u32[]{:S(2)}) collective-permute-start(bf16[1,2,96,768]{3,2,1,0:T(8,128)(2,1)S(1)} %get-tuple-element.1378), channel_id=1, source_target_pairs={{0,2},{1,3},{2,0},{3,1},{4,6},{5,7},{6,4},{7,5},{8,10},{9,11},{10,... | collective-permute-start | bytes 884744 | tf_op jit(solution)/shard_map/ppermute | solution.py:23
  333.6 22.2 %collective-permute-start.52 = (f32[2,96,768]{2,1,0:T(8,128)S(1)}, f32[2,96,768]{2,1,0:T(8,128)S(1)}, u32[]{:S(2)}, u32[]{:S(2)}) collective-permute-start(f32[2,96,768]{2,1,0:T(8,128)S(1)} %shard_map.566.own_ref), channel_id=1, source_target_pairs={{0,16},{16,0},{1,17},{17,1},{2,18},{18,2},{3,19},{19,3},{4,20},{20... | collective-permute-start | bytes 1769480 | tf_op jit(solution)/shard_map/ppermute | solution.py:23
  343.9 25.0 %collective-permute-start.60 = (f32[2,96,768]{2,1,0:T(8,128)S(1)}, f32[2,96,768]{2,1,0:T(8,128)S(1)}, u32[]{:S(2)}, u32[]{:S(2)}) collective-permute-start(f32[2,96,768]{2,1,0:T(8,128)S(1)} %shard_map.583.own_ref), channel_id=1, source_target_pairs={{0,16},{16,0},{1,17},{17,1},{2,18},{18,2},{3,19},{19,3},{4,20},{20... | collective-permute-start | bytes 1769480 | tf_op jit(solution)/shard_map/ppermute | solution.py:23
  354.2 13.2 %collective-permute-start.58 = (f32[4,48,384]{2,1,0:T(8,128)S(1)}, f32[4,48,384]{2,1,0:T(8,128)S(1)}, u32[]{:S(2)}, u32[]{:S(2)}) collective-permute-start(f32[4,48,384]{2,1,0:T(8,128)S(1)} %shard_map.581.own_ref), channel_id=1, source_target_pairs={{0,16},{16,0},{1,17},{17,1},{2,18},{18,2},{3,19},{19,3},{4,20},{20... | collective-permute-start | bytes 884744 | tf_op jit(solution)/shard_map/ppermute | solution.py:23
  (82 other events, 676.5 us)
